TPU v7x, 32 devices: a whole 2x2x4 slice. The times are simulated.
32 devices in a mesh: groups: 2 (over x), space: 16 (over z, y, core).
Axes of the slice: x: 2, y: 2, z: 4, core: 2. Of those that a mesh axis runs over, the one named last changes fastest.
Arguments:
- lifted_field: float32 [64, 16, 128, 256], P('groups', 'space'), parts along dimension 0, may hold values from -6 to 6
- cotangent: bfloat16 [64, 16, 128, 256], P('groups', 'space'), parts along dimension 0, may hold values from -6 to 6
- spectral_weights: float32 [2, 32, 1024, 32, 32], P(None, None, 'space'), may hold values from -4 to 4
- point_weights: float32 [32, 32], replicated, may hold values from -1 to 1
- point_bias: float32 [32], replicated, may hold values from -3 to 3
Outputs:
- activated: bfloat16 [64, 16, 128, 256], P('groups', 'space'), parts along dimension 0
- grad_spectral: float32 [4, 32, 1024, 32, 32], P('groups', None, 'space'), parts along dimension 0
- grad_point: float32 [64, 32], P('groups'), parts along dimension 0
- grad_bias: float32 [64], P('groups'), parts along dimension 0
There are 2 independent parts, one for each index of `groups`. A program takes and returns all parts, laid end to end along the dimension named above; an argument that names none is the same for every part. Nothing has to cross between parts.
All inputs are finite; a program needn't handle non-finite values.
Results may differ from a plain program's by a relative error of at most 0.001.
Values sent between devices are 32-bit elements; how exact they have to be, the bound alone decides.
No kernel may reach another device: no remote copies, remote signals or barrier semaphores. Data moves between devices by JAX's collectives and lax.ppermute only.
A program may use at most 192 MiB of HBM per device.

v0:
```python
import functools

import jax
import jax.numpy as jnp
import ml_dtypes
import numpy as np
from jax import lax
from jax.experimental import pallas as pl
from jax.experimental.pallas import tpu as pltpu
from jax.sharding import PartitionSpec as P

MX = 32
MY = 32
MZ = 32
NY = 128
NZ = 256

F32 = jnp.float32
BF16 = jnp.bfloat16
INV_SQRT_TWO = 0.7071067811865476
INV_SQRT_TWO_PI = 0.3989422804014327
MIB = 1 << 20
LANES = 128
GROUP = 4


def kept(kept_count, length):
    index = np.arange(kept_count)
    return np.where(index < kept_count // 2, index, length - kept_count + index)


def angles(positions, frequency, length):
    product = positions[:, None] * frequency[None, :] % length
    return 2.0 * np.pi / length * product


def split_table(table):
    high = table.astype(ml_dtypes.bfloat16)
    return high, (table - high.astype(np.float64)).astype(ml_dtypes.bfloat16)


def lane_spread(first, second, real_table, imag_table):
    return np.concatenate(
        [real_table * first, real_table * second, imag_table * first, imag_table * second], axis=1
    )


def forward_tables():
    theta = angles(np.arange(NZ), np.arange(MZ), NZ)
    cos_z, sin_z = np.cos(theta), np.sin(theta)
    plain = [lane_spread(f, s, cos_z, -sin_z) for f, s in ((1, 0), (0, 1))]
    turned = [lane_spread(f, s, -sin_z, -cos_z) for f, s in ((1, 0), (0, 1))]
    table_z = np.concatenate([np.concatenate(plain, 0), np.concatenate(turned, 0)], axis=1)
    theta = angles(np.arange(NY), kept(MY, NY), NY)
    both = np.concatenate([np.cos(theta).T, np.sin(theta).T], axis=1)
    table_y = np.concatenate([both[0::2], both[1::2]], axis=0)
    z_high, z_low = split_table(table_z)
    y_high, y_low = split_table(table_y)
    return z_high, z_low, np.concatenate([y_high, y_low], axis=0)


def inverse_tables(norm):
    theta = angles(np.arange(NY), kept(MY, NY), NY)
    cos_y, sin_y = np.cos(theta), np.sin(theta)
    table_y = np.concatenate([cos_y[:, 0::2], cos_y[:, 1::2], sin_y[:, 0::2], sin_y[:, 1::2]], axis=1)
    y_high, y_low = split_table(table_y)
    theta = angles(np.arange(NZ), np.arange(MZ), NZ)
    weight = np.where(np.arange(MZ) == 0, 1.0, 2.0) * norm
    cos_z, sin_z = np.cos(theta) * weight, -np.sin(theta) * weight
    table_z = np.concatenate([lane_spread(f, s, cos_z, sin_z).T for f, s in ((1, 0), (0, 1))], axis=1)
    z_high, z_low = split_table(table_z)
    return (
        np.concatenate([y_high, y_high, y_low], axis=1),
        np.concatenate([z_high, z_high], axis=0),
        z_low,
    )


def dot(left, right):
    return jnp.dot(left, right, preferred_element_type=F32)


def split(values):
    high = values.astype(BF16)
    return high, (values - high.astype(F32)).astype(BF16)


def lane_index(shape):
    return lax.broadcasted_iota(jnp.int32, shape, len(shape) - 1)


def roll(values, shift):
    return pltpu.roll(values, shift % LANES, len(values.shape) - 1)


def forward_group(fields, z_high, z_low, y_both, out_ref, first, rows):
    left = jnp.concatenate(
        [jnp.concatenate([fields[q], fields[q + 1]], axis=1) for q in range(0, GROUP, 2)], axis=0
    )
    high, low = split(left)
    lines = dot(high, z_high) + dot(high, z_low) + dot(low, z_high)
    pairs = []
    for q in range(GROUP // 2):
        part = lines[q * NY : (q + 1) * NY]
        pairs.append(jnp.concatenate([part[:, :LANES], part[:, LANES:]], axis=0))
    high, low = split(jnp.concatenate(pairs, axis=1))
    wide = dot(y_both, high)
    modes = wide[:MY] + wide[MY:] + dot(y_both[:MY], low)
    half = MY // 2
    for q in range(GROUP // 2):
        even = modes[:half, q * LANES : (q + 1) * LANES]
        odd = modes[half:, q * LANES : (q + 1) * LANES]
        at_even = (lane_index(even.shape) // MZ) % 2 == 0
        out_ref[pl.ds(first + 2 * q, half, stride=rows), :] = jnp.where(at_even, even, roll(odd, MZ))
        out_ref[pl.ds(first + 2 * q + 1, half, stride=rows), :] = jnp.where(at_even, roll(even, -MZ), odd)


def inverse_y_group(modes_ref, y_table, first, rows):
    half = MY // 2
    pairs = []
    for q in range(GROUP // 2):
        c0 = modes_ref[pl.ds(first + 2 * q, half, stride=rows), :]
        c1 = modes_ref[pl.ds(first + 2 * q + 1, half, stride=rows), :]
        lane = lane_index(c0.shape)
        at_even = (lane // MZ) % 2 == 0
        even = jnp.where(at_even, c0, roll(c1, MZ))
        odd = jnp.where(at_even, roll(c0, -MZ), c1)
        both = jnp.concatenate([even, odd], axis=0)
        turned = jnp.where(lane_index(both.shape) < LANES // 2, -roll(both, 64), roll(both, 64))
        pairs.append(jnp.concatenate([both, turned], axis=0))
    high, low = split(jnp.concatenate(pairs, axis=1))
    return dot(y_table, jnp.concatenate([high, low, high], axis=0))


def full(shape):
    return pl.BlockSpec(shape, lambda *_: (0,) * len(shape))


def params(limit):
    return pltpu.CompilerParams(vmem_limit_bytes=limit * MIB)


def forward_kernel(z_high, z_low, y_both, field_ref, out_ref, *, channels, step_channels):
    step = pl.program_id(0)
    for g in range(0, step_channels, GROUP):
        fields = [field_ref[g + q] for q in range(GROUP)]
        first = step * step_channels + g
        forward_group(fields, z_high[...], z_low[...], y_both[...], out_ref, first, channels)


def forward_modes(field, tables):
    channels = field.shape[0]
    step_channels = min(channels, 8)
    z_high, z_low, y_both = tables
    owners = MY // 2
    out = pl.pallas_call(
        functools.partial(forward_kernel, channels=channels, step_channels=step_channels),
        grid=(channels // step_channels,),
        in_specs=[
            full(z_high.shape),
            full(z_low.shape),
            full(y_both.shape),
            pl.BlockSpec((step_channels, NY, NZ), lambda s: (s, 0, 0)),
        ],
        out_specs=full((owners * channels, LANES)),
        out_shape=jax.ShapeDtypeStruct((owners * channels, LANES), F32),
        compiler_params=params(24),
        cost_estimate=pl.CostEstimate(flops=2 * 10**9, bytes_accessed=8 * MIB, transcendentals=0),
        name="forward_yz",
    )(z_high, z_low, y_both, field)
    return out.reshape(owners, channels, LANES)


def fold_kernel(first_ref, *refs):
    *others, out_ref = refs
    real, imag = first_ref[0, 0], first_ref[1, 0]
    for other in others:
        real, imag = real + other[0, 0], imag + other[1, 0]
    modes = real.shape[-1]
    out_ref[0, :, :, :modes] = real
    out_ref[0, :, :, modes:] = imag


def fold_weights(weights, unique):
    _, kept_x, channels, outputs, modes = weights.shape
    block = (2, 1, channels, outputs, modes)
    copies = kept_x // unique
    return pl.pallas_call(
        fold_kernel,
        grid=(unique,),
        in_specs=[pl.BlockSpec(block, functools.partial(lambda a, r: (0, a + r, 0, 0, 0), r=r * unique)) for r in range(copies)],
        out_specs=pl.BlockSpec((1, channels, outputs, 2 * modes), lambda a: (a, 0, 0, 0)),
        out_shape=jax.ShapeDtypeStruct((unique, channels, outputs, 2 * modes), F32),
        compiler_params=params(16),
        cost_estimate=pl.CostEstimate(flops=8 * 10**6, bytes_accessed=44 * MIB, transcendentals=0),
        name="fold_weights",
    )(*([weights] * copies))


def spectrum_row(cos_ref, sin_ref, lines_ref, turned_ref, at, points):
    total = cos_ref[at, 0] * lines_ref[0] + sin_ref[at, 0] * turned_ref[0]
    for x in range(1, points):
        total += cos_ref[at, x] * lines_ref[x] + sin_ref[at, x] * turned_ref[x]
    return total


def turn_lines(lines_ref, turned_ref, points, channels):
    sign = jnp.where(lane_index((channels, LANES)) < LANES // 2, 1.0, -1.0)
    for x in range(points):
        turned_ref[x] = sign * roll(lines_ref[x, :channels], 64)


def doubled(values):
    other = roll(values, 64)
    low = lane_index(values.shape) < LANES // 2
    return jnp.where(low, values, other), jnp.where(low, other, values)


def mix_kernel(cos_ref, sin_ref, lines_ref, weights_ref, spec_ref, out_ref, turned_ref, real_ref, imag_ref, *, points, channels, per_step, norm):
    step = pl.program_id(0)

    @pl.when(step == 0)
    def _():
        turn_lines(lines_ref, turned_ref, points, channels)
        out_ref[...] = jnp.zeros_like(out_ref)

    low = lane_index((channels, LANES)) < LANES // 2

    @pl.loop(0, per_step)
    def _(q):
        at = step * per_step + q
        spec = norm * spectrum_row(cos_ref, sin_ref, lines_ref, turned_ref, at, points)
        spec_ref[q] = spec
        real_ref[...], imag_ref[...] = doubled(spec)
        by_real = jnp.zeros((channels, LANES), F32)
        by_imag = jnp.zeros((channels, LANES), F32)
        for i in range(channels):
            weight = weights_ref[q, i]
            by_real += real_ref[pl.ds(i, 1), :] * weight
            by_imag += imag_ref[pl.ds(i, 1), :] * weight
        other = roll(by_imag, 64)
        mixed = by_real + jnp.where(low, -other, other)
        other = roll(mixed, 64)
        turned = jnp.where(low, -other, other)
        for x in range(points):
            out_ref[x] += cos_ref[at, x] * mixed + sin_ref[at, x] * turned


def smem():
    return pl.BlockSpec(memory_space=pltpu.SMEM)


def mix(cos_x, sin_x, lines, weights, norm):
    points, channels, _ = lines.shape
    unique = weights.shape[0]
    per_step = min(unique, 4)
    shape = (points, channels, LANES)
    return pl.pallas_call(
        functools.partial(mix_kernel, points=points, channels=channels, per_step=per_step, norm=norm),
        grid=(unique // per_step,),
        in_specs=[
            smem(),
            smem(),
            full(shape),
            pl.BlockSpec((per_step,) + weights.shape[1:], lambda s: (s, 0, 0, 0)),
        ],
        out_specs=[
            pl.BlockSpec((per_step, channels, LANES), lambda s: (s, 0, 0)),
            full(shape),
        ],
        out_shape=[
            jax.ShapeDtypeStruct((unique, channels, LANES), F32),
            jax.ShapeDtypeStruct(shape, F32),
        ],
        scratch_shapes=[
            pltpu.VMEM(shape, F32),
            pltpu.VMEM((channels, LANES), F32),
            pltpu.VMEM((channels, LANES), F32),
        ],
        compiler_params=params(16),
        cost_estimate=pl.CostEstimate(flops=2 * 10**7, bytes_accessed=9 * MIB, transcendentals=0),
        name="mix_modes",
    )(cos_x, sin_x, lines, weights)


def pointwise_kernel(mixer_ref, bias_ref, field_ref, out_ref, *, channels, blocks):
    size = 8 * channels
    mixer = mixer_ref[...]
    bias = bias_ref[...]
    for b in range(blocks):
        high, low = split(field_ref[:, 8 * b : 8 * b + 8, :].reshape(size, NZ))
        wide = dot(mixer, high)
        values = wide[:size] + wide[size:] + dot(mixer[:size], low) + bias
        out_ref[:, 8 * b : 8 * b + 8, :] = values.reshape(channels, 8, NZ)


def pointwise(field, mixer, bias):
    channels = field.shape[0]
    blocks = 2
    block = pl.BlockSpec((channels, 8 * blocks, NZ), lambda s: (0, s, 0))
    return pl.pallas_call(
        functools.partial(pointwise_kernel, channels=channels, blocks=blocks),
        grid=(NY // (8 * blocks),),
        in_specs=[full(mixer.shape), full(bias.shape), block],
        out_specs=block,
        out_shape=jax.ShapeDtypeStruct(field.shape, F32),
        compiler_params=params(16),
        cost_estimate=pl.CostEstimate(flops=4 * 10**9, bytes_accessed=24 * MIB, transcendentals=0),
        name="pointwise",
    )(mixer, bias, field)


def cell_kernel(
    inv_y, inv_z, inv_z_low, z_high, z_low, y_both, sum_ref, modes_ref, pre_ref, cot_ref, field_hbm,
    act_ref, out_ref, field_ref, slope_high, slope_low, sem, *, channels, rows, owners,
):
    step = pl.program_id(0)
    copy = pltpu.make_async_copy(field_hbm, field_ref, sem)

    @pl.when(step == 0)
    def _():
        copy.start()

    first = step * GROUP
    lines = inverse_y_group(modes_ref, inv_y[...], first, channels)
    lines = jnp.concatenate([lines[:, q * LANES : (q + 1) * LANES] for q in range(GROUP // 2)], axis=0)
    high, low = split(lines)
    spectral = dot(jnp.concatenate([high, low], axis=1), inv_z[...]) + dot(high, inv_z_low[...])
    slopes = []
    for q in range(GROUP):
        r = q // 2 * NY
        c = q % 2 * NZ
        before = spectral[r : r + NY, c : c + NZ] + pre_ref[q]
        cdf = 0.5 + 0.5 * lax.erf(before * INV_SQRT_TWO)
        act_ref[q] = (before * cdf).astype(BF16)
        pdf = jnp.exp(-0.5 * before * before) * INV_SQRT_TWO_PI
        slope = cot_ref[q].astype(F32) * (cdf + before * pdf)
        slopes.append(slope)
        high, low = split(slope)
        slope_high[first + q] = high
        slope_low[first + q] = low
    forward_group(slopes, z_high[...], z_low[...], y_both[...], out_ref, first, rows)

    @pl.when(step == pl.num_programs(0) - 1)
    def _():
        copy.wait()
        size = 8 * channels
        total = jnp.zeros((size, size), F32)
        nt = (((1,), (1,)), ((), ()))
        for b in range(NY // 16):
            at = pl.ds(16 * b, 16)
            field_high, field_low = split(field_ref[:, at, :])
            s_high, s_low = slope_high[:, at, :], slope_low[:, at, :]
            for h in range(2):
                part = slice(8 * h, 8 * h + 8)
                f_h = field_high[:, part].reshape(size, NZ)
                f_l = field_low[:, part].reshape(size, NZ)
                s_h = s_high[:, part].reshape(size, NZ)
                s_l = s_low[:, part].reshape(size, NZ)
                total += lax.dot_general(f_h, s_h, nt, preferred_element_type=F32)
                total += lax.dot_general(f_h, s_l, nt, preferred_element_type=F32)
                total += lax.dot_general(f_l, s_h, nt, preferred_element_type=F32)
        row = lax.broadcasted_iota(jnp.int32, (size, size), 0) % 8
        total = jnp.where(row == lane_index((size, size)) % 8, total, 0.0)
        folded = jnp.sum(total.reshape(channels, 8, size), axis=1)
        point = jnp.dot(folded, sum_ref[...], precision=lax.Precision.HIGHEST, preferred_element_type=F32)
        packed = jnp.concatenate([point[8 * q : 8 * q + 8] for q in range(channels // 8)], axis=1)
        dc = jnp.broadcast_to(out_ref[0:channels, 0:1], (channels, LANES))
        eye = lax.broadcasted_iota(jnp.int32, (channels, LANES), 0) == lane_index((channels, LANES))
        bias = jnp.sum(jnp.where(eye, dc, 0.0), axis=0, keepdims=True)
        extra = jnp.where(lax.broadcasted_iota(jnp.int32, (8, LANES), 0) == 0, jnp.broadcast_to(bias, (8, LANES)), 0.0)
        for d in range(owners):
            out_ref[d * rows + channels : d * rows + channels + 8, :] = packed
            out_ref[d * rows + channels + 8 : (d + 1) * rows, :] = extra


def cell_stage(inverse, forward, summing, modes, pre, cotangent, field):
    channels = field.shape[0]
    owners = MY // 2
    rows = channels + 16
    block = pl.BlockSpec((GROUP, NY, NZ), lambda s: (s, 0, 0))
    tables = (*inverse, *forward, summing)
    act, out = pl.pallas_call(
        functools.partial(cell_kernel, channels=channels, rows=rows, owners=owners),
        grid=(channels // GROUP,),
        in_specs=[full(t.shape) for t in tables]
        + [full((owners * channels, LANES)), block, block, pl.BlockSpec(memory_space=pl.ANY)],
        out_specs=[block, full((owners * rows, LANES))],
        out_shape=[
            jax.ShapeDtypeStruct((channels, NY, NZ), BF16),
            jax.ShapeDtypeStruct((owners * rows, LANES), F32),
        ],
        scratch_shapes=[
            pltpu.VMEM((channels, NY, NZ), F32),
            pltpu.VMEM((channels, NY, NZ), BF16),
            pltpu.VMEM((channels, NY, NZ), BF16),
            pltpu.SemaphoreType.DMA,
        ],
        compiler_params=params(36),
        cost_estimate=pl.CostEstimate(flops=8 * 10**9, bytes_accessed=12 * MIB, transcendentals=2 * 10**6),
        name="cells",
    )(*tables, modes.reshape(owners * channels, LANES), pre, cotangent, field)
    return act, out.reshape(owners, rows, LANES)


def gradient_kernel(
    cos_ref, sin_ref, spec_ref, lines_ref, out_hbm, point_ref, bias_ref,
    turned_ref, slope_ref, flip_ref, real_ref, imag_ref, buffer, sems, *, points, channels, unique, copies, norm,
):
    turn_lines(lines_ref, turned_ref, points, channels)
    half = LANES // 2
    lane = lane_index((channels, LANES))
    scale = jnp.where(lane % MZ == 0, norm, 2.0 * norm)
    packed = lines_ref[0, channels : channels + 16, :]
    for x in range(1, points):
        packed += lines_ref[x, channels : channels + 16, :]
    packed = norm * packed
    for q in range(channels // 8):
        point_ref[8 * q : 8 * q + 8, :] = packed[:8, q * channels : (q + 1) * channels]
    bias_ref[...] = packed[8:9, :channels]

    def writes(at, slot):
        return [
            pltpu.make_async_copy(buffer.at[slot], out_hbm.at[:, at + r * unique], sems.at[slot, r])
            for r in range(copies)
        ]

    @pl.loop(0, unique)
    def _(at):
        slot = at % 2

        @pl.when(at >= 2)
        def _():
            for copy in writes(at - 2, slot):
                copy.wait()

        total = cos_ref[at, 0] * lines_ref[0, :channels] + sin_ref[at, 0] * turned_ref[0]
        for x in range(1, points):
            total += cos_ref[at, x] * lines_ref[x, :channels] + sin_ref[at, x] * turned_ref[x]
        slope = scale * total
        other = roll(slope, 64)
        flipped = jnp.where(lane < half, other, -other)
        real_ref[...], imag_ref[...] = doubled(spec_ref[at])
        for i in range(channels):
            both = real_ref[pl.ds(i, 1), :] * slope + imag_ref[pl.ds(i, 1), :] * flipped
            buffer[slot, 0, i] = both[:, :half]
            buffer[slot, 1, i] = both[:, half:]
        for copy in writes(at, slot):
            copy.start()

    for at in range(max(unique - 2, 0), unique):
        for copy in writes(at, at % 2):
            copy.wait()


def gradient(cos_x, sin_x, spectrum, lines, norm, kept_x):
    points, rows, _ = lines.shape
    unique, channels, _ = spectrum.shape
    half = LANES // 2
    copies = kept_x // unique
    flat = (channels, LANES)
    return pl.pallas_call(
        functools.partial(gradient_kernel, points=points, channels=channels, unique=unique, copies=copies, norm=norm),
        in_specs=[smem(), smem(), full(spectrum.shape), full(lines.shape)],
        out_specs=[pl.BlockSpec(memory_space=pl.ANY), full((channels, channels)), full((1, channels))],
        out_shape=[
            jax.ShapeDtypeStruct((2, kept_x, channels, channels, half), F32),
            jax.ShapeDtypeStruct((channels, channels), F32),
            jax.ShapeDtypeStruct((1, channels), F32),
        ],
        scratch_shapes=[
            pltpu.VMEM((points, channels, LANES), F32),
            pltpu.VMEM(flat, F32),
            pltpu.VMEM(flat, F32),
            pltpu.VMEM(flat, F32),
            pltpu.VMEM(flat, F32),
            pltpu.VMEM((2, 2, channels, channels, half), F32),
            pltpu.SemaphoreType.DMA((2, copies)),
        ],
        compiler_params=params(16),
        cost_estimate=pl.CostEstimate(flops=10**7, bytes_accessed=40 * MIB, transcendentals=0),
        name="weight_gradient",
    )(cos_x, sin_x, spectrum, lines)


def swap(lines):
    return lax.all_to_all(lines, "space", split_axis=0, concat_axis=0, tiled=True)


def suits(width_x, length_x, devices, channels, weights):
    held = weights.shape[2]
    even = np.array_equal(kept(MX, length_x) % length_x, np.arange(MX) % length_x)
    return (
        width_x == 1
        and held == 2 * MZ
        and devices * 2 == MY
        and 2 * held == LANES
        and MX % length_x == 0
        and even
        and channels == MZ
    )


def body(lifted_field, cotangent, spectral_weights, point_weights, point_bias):
    devices = lax.axis_size("space")
    channels, width_x = lifted_field.shape[:2]
    length_x = width_x * devices
    if not suits(width_x, length_x, devices, channels, spectral_weights):
        return general_body(lifted_field, cotangent, spectral_weights, point_weights, point_bias)
    norm = float(length_x * NY * NZ) ** -0.5
    theta = angles(np.arange(length_x), np.arange(length_x), length_x)
    cos_x, sin_x = jnp.asarray(np.cos(theta), F32), jnp.asarray(np.sin(theta), F32)
    forward = forward_tables()
    inverse = inverse_tables(norm)
    summing = jnp.asarray(np.repeat(np.eye(channels), 8, axis=0), F32)

    field = lifted_field.reshape(channels, NY, NZ)
    slopes_in = cotangent.reshape(channels, NY, NZ)
    weights = jnp.transpose(spectral_weights, (0, 1, 3, 4, 2))
    mixer = jnp.kron(point_weights.T, jnp.eye(8, dtype=F32))
    high = lax.reduce_precision(mixer, 8, 7)
    mixer = jnp.concatenate([high, mixer - high], axis=0).astype(BF16)
    bias = jnp.repeat(point_bias, 8)[:, None]

    lines = swap(forward_modes(field, forward))
    folded = fold_weights(weights, length_x)
    spectrum, mixed = mix(cos_x, sin_x, lines, folded, norm)
    modes = swap(mixed)
    pre = pointwise(field, mixer, bias)
    activated, slope_lines = cell_stage(inverse, forward, summing, modes, pre, slopes_in, field)
    slope_lines = swap(slope_lines)
    grad, grad_point, grad_bias = gradient(cos_x, sin_x, spectrum, slope_lines, norm, MX)
    return (
        activated.reshape(cotangent.shape),
        jnp.transpose(grad, (0, 1, 4, 2, 3)),
        grad_point,
        grad_bias.reshape(channels),
    )


HIGHEST = lax.Precision.HIGHEST


def trig_tables(positions, frequency, length):
    product = positions[:, None] * frequency[None, :] % length
    phase_angle = 2.0 * jnp.pi / length * product.astype(jnp.float32)
    return (jnp.cos(phase_angle), jnp.sin(phase_angle))


def kept_frequencies(kept_count, length):
    mode_index = jnp.arange(kept_count, dtype=jnp.int32)
    return jnp.where(mode_index < kept_count // 2, mode_index, length - kept_count + mode_index)


def forward_local(field_in):
    channels = field_in.shape[0]
    width_x = field_in.shape[1]
    cos_z, sin_z = trig_tables(jnp.arange(NZ, dtype=jnp.int32), jnp.arange(MZ, dtype=jnp.int32), NZ)
    table_z = jnp.concatenate([cos_z, -sin_z], axis=1)
    along_z = jnp.einsum("cxyz,zk->cxyk", field_in, table_z, precision=HIGHEST)
    z_real = along_z[..., :MZ]
    z_imag = along_z[..., MZ:]
    cos_y, sin_y = trig_tables(jnp.arange(NY, dtype=jnp.int32), kept_frequencies(MY, NY), NY)
    y_real = jnp.einsum("cxyk,yj->xcjk", z_real, cos_y, precision=HIGHEST) + jnp.einsum(
        "cxyk,yj->xcjk", z_imag, sin_y, precision=HIGHEST
    )
    y_imag = jnp.einsum("cxyk,yj->xcjk", z_imag, cos_y, precision=HIGHEST) - jnp.einsum(
        "cxyk,yj->xcjk", z_real, sin_y, precision=HIGHEST
    )
    stacked = jnp.stack([y_real, y_imag], axis=1)
    return stacked.reshape(width_x, 2, channels, MY * MZ)


def transform_x(x_lines):
    length_x = x_lines.shape[0]
    cos_x, sin_x = trig_tables(
        jnp.arange(length_x, dtype=jnp.int32), kept_frequencies(MX, length_x), length_x
    )
    norm_scale = 1.0 / float(length_x * NY * NZ) ** 0.5
    part_real = x_lines[:, 0]
    part_imag = x_lines[:, 1]
    x_real = jnp.einsum("xcm,xk->kcm", part_real, cos_x, precision=HIGHEST) + jnp.einsum(
        "xcm,xk->kcm", part_imag, sin_x, precision=HIGHEST
    )
    x_imag = jnp.einsum("xcm,xk->kcm", part_imag, cos_x, precision=HIGHEST) - jnp.einsum(
        "xcm,xk->kcm", part_real, sin_x, precision=HIGHEST
    )
    return norm_scale * jnp.stack([x_real, x_imag], axis=1)


def mix_modes(spectrum, weights):
    spec_real = spectrum[:, 0]
    spec_imag = spectrum[:, 1]
    out_real = jnp.einsum("kim,kmio->kom", spec_real, weights[0], precision=HIGHEST) - jnp.einsum(
        "kim,kmio->kom", spec_imag, weights[1], precision=HIGHEST
    )
    out_imag = jnp.einsum("kim,kmio->kom", spec_real, weights[1], precision=HIGHEST) + jnp.einsum(
        "kim,kmio->kom", spec_imag, weights[0], precision=HIGHEST
    )
    return jnp.stack([out_real, out_imag], axis=1)


def inverse_x(spectrum, positions, length_x):
    cos_x, sin_x = trig_tables(positions, kept_frequencies(MX, length_x), length_x)
    spec_real = spectrum[:, 0]
    spec_imag = spectrum[:, 1]
    a_real = jnp.einsum("kcm,xk->xcm", spec_real, cos_x, precision=HIGHEST) - jnp.einsum(
        "kcm,xk->xcm", spec_imag, sin_x, precision=HIGHEST
    )
    a_imag = jnp.einsum("kcm,xk->xcm", spec_imag, cos_x, precision=HIGHEST) + jnp.einsum(
        "kcm,xk->xcm", spec_real, sin_x, precision=HIGHEST
    )
    return jnp.stack([a_real, a_imag], axis=1)


def inverse_yz(x_lines, length_x):
    width_x = x_lines.shape[0]
    channels = x_lines.shape[2]
    mode_grid = x_lines.reshape(width_x, 2, channels, MY, MZ)
    cos_y, sin_y = trig_tables(jnp.arange(NY, dtype=jnp.int32), kept_frequencies(MY, NY), NY)
    b_real = jnp.einsum("xcjk,yj->cxyk", mode_grid[:, 0], cos_y, precision=HIGHEST) - jnp.einsum(
        "xcjk,yj->cxyk", mode_grid[:, 1], sin_y, precision=HIGHEST
    )
    b_imag = jnp.einsum("xcjk,yj->cxyk", mode_grid[:, 1], cos_y, precision=HIGHEST) + jnp.einsum(
        "xcjk,yj->cxyk", mode_grid[:, 0], sin_y, precision=HIGHEST
    )
    cos_z, sin_z = trig_tables(jnp.arange(NZ, dtype=jnp.int32), jnp.arange(MZ, dtype=jnp.int32), NZ)
    weight_z = jnp.where(jnp.arange(MZ, dtype=jnp.int32) == 0, 1.0, 2.0).astype(jnp.float32)
    table_z = jnp.concatenate([cos_z * weight_z[None, :], -sin_z * weight_z[None, :]], axis=1)
    stacked = jnp.concatenate([b_real, b_imag], axis=-1)
    result = jnp.einsum("cxyk,zk->cxyz", stacked, table_z, precision=HIGHEST)
    return result * (1.0 / float(length_x * NY * NZ) ** 0.5)


def gelu_slope(values):
    return (
        0.5 * (1.0 + lax.erf(values * INV_SQRT_TWO))
        + values * jnp.exp(-0.5 * values * values) * INV_SQRT_TWO_PI
    )


def weight_gradient(spectrum, slope_modes, first_mode):
    mode_ids = first_mode + jnp.arange(spectrum.shape[3], dtype=jnp.int32)
    weight_modes = jnp.where(mode_ids % MZ == 0, 1.0, 2.0).astype(jnp.float32)
    grad_real = jnp.einsum(
        "kim,kom->kmio", spectrum[:, 0], slope_modes[:, 0], precision=HIGHEST
    ) + jnp.einsum("kim,kom->kmio", spectrum[:, 1], slope_modes[:, 1], precision=HIGHEST)
    grad_imag = jnp.einsum(
        "kim,kom->kmio", spectrum[:, 0], slope_modes[:, 1], precision=HIGHEST
    ) - jnp.einsum("kim,kom->kmio", spectrum[:, 1], slope_modes[:, 0], precision=HIGHEST)
    stacked = jnp.stack([grad_real, grad_imag], axis=0)
    return stacked * weight_modes[None, None, :, None, None]


def to_modes(field_in):
    return transform_x(
        lax.all_to_all(forward_local(field_in), "space", split_axis=3, concat_axis=0, tiled=True)
    )


def general_body(lifted_field, cotangent, spectral_weights, point_weights, point_bias):
    devices = lax.axis_size("space")
    width_x = lifted_field.shape[1]
    length_x = width_x * devices
    spectrum = to_modes(lifted_field)
    mixed_modes = mix_modes(spectrum, spectral_weights)
    full_lines = inverse_x(mixed_modes, jnp.arange(length_x, dtype=jnp.int32), length_x)
    spectral = inverse_yz(
        lax.all_to_all(full_lines, "space", split_axis=0, concat_axis=3, tiled=True), length_x
    )
    pointwise = (
        jnp.einsum("ixyz,io->oxyz", lifted_field, point_weights, precision=HIGHEST)
        + point_bias[:, None, None, None]
    )
    before = spectral + pointwise
    activated = jax.nn.gelu(before, approximate=False).astype(jnp.bfloat16)
    slope_field = cotangent.astype(jnp.float32) * gelu_slope(before)
    local_point = jnp.einsum("ixyz,oxyz->io", lifted_field, slope_field, precision=HIGHEST)
    local_bias = jnp.sum(slope_field, axis=(1, 2, 3))
    partial = jnp.concatenate([local_point, local_bias[None, :]], axis=0)
    gathered = lax.all_gather(partial, "space", axis=0, tiled=False)
    summed = jnp.sum(gathered, axis=0)
    summed_point, summed_bias = summed[:-1], summed[-1]
    root_cells = float(length_x * NY * NZ) ** 0.5
    slope_spectrum = to_modes(slope_field)
    first_mode = lax.axis_index("space") * spectrum.shape[3]
    grad_spectral = weight_gradient(spectrum, slope_spectrum, first_mode)
    return (activated, grad_spectral, summed_point / root_cells, summed_bias / root_cells)


def solution(mesh):
    placed = (
        P("groups", "space", None, None),
        P("groups", "space", None, None),
        P(None, None, "space", None, None),
        P(),
        P(),
    )
    return jax.shard_map(
        body,
        mesh=mesh,
        in_specs=placed,
        out_specs=(
            P("groups", "space", None, None),
            P("groups", None, "space", None, None),
            P("groups", None),
            P("groups"),
        ),
        check_vma=False,
    )
```

profile of v0, /device:TPU:0, one launch (start us, length us, event | category | flops | bytes accessed | tf_op | source)
XLA Modules:
  0.0 125.9 jit_solution(18341760263749243245)
XLA Ops:
  0.6 0.0 copy-start.21
  0.6 0.0 copy-start.4
  0.7 2.2 %copy-done.4 = f32[32,1,128,256]{3,2,1,0:T(8,128)S(1)} copy-done((f32[32,1,128,256]{3,2,1,0:T(8,128)S(1)}, f32[32,1,128,256]{3,2,1,0:T(8,128)}, u32[]{:S(2)}) %copy-start.4) | copy-done | bytes 4194328
  2.8 0.0 copy-start.8
  2.8 0.9 copy-done.8
  3.8 0.9 copy-done.10
  4.7 0.8 copy-done.16
  5.5 6.4 %forward_yz.1 = f32[512,128]{1,0:T(8,128)} custom-call(bf16[512,256]{1,0:T(8,128)(2,1)S(1)} %copy-done.10, bf16[512,256]{1,0:T(8,128)(2,1)S(1)} %copy-done.8, bf16[64,256]{1,0:T(8,128)(2,1)S(1)} %copy-done.16, f32[32,128,256]{2,1,0:T(8,128)S(1)} %bitcast.16), custom_call_target="tpu_custom_call" | custom-call | flops 2000000000 | bytes 8388608 | tf_op jit(solution)/shard_map/forward_yz/pallas_call | solution.py:156
  11.9 7.4 %all-to-all-start = ((f32[16,32,128]{2,1,0:T(8,128)}), f32[16,32,128]{2,1,0:T(8,128)S(1)}, u32[]{:S(2)}, u32[]{:S(2)}) async-start(f32[16,32,128]{2,1,0:T(8,128)} %bitcast.1), calls=%async_computation | async-start | bytes 524288 | tf_op jit(solution)/shard_map/all_to_all | solution.py:487
  19.3 0.0 copy-done.20
  19.3 0.1 copy.20
  19.4 0.0 copy-done.21
  19.4 0.1 broadcast_in_dim.7
  19.5 0.1 broadcast_in_dim_reshape.4.bias_ref
  19.6 2.6 %broadcast_multiply_fusion = f32[32,8,32,8]{3,2,1,0:T(8,128)} fusion(f32[8,8]{1,0:T(8,128)S(1)} %fusion.1, f32[32,32]{1,0:T(8,128)S(1)} %copy.20), kind=kLoop, calls=%fused_computation | loop fusion | flops 65536 | bytes 266496 | tf_op jit(solution)/shard_map/jit(kron)/mul | solution.py:520
  22.2 4.0 %mul.27 = f32[256,256]{1,0:T(8,128)S(1)} reshape(f32[32,8,32,8]{3,2,1,0:T(8,128)} %broadcast_multiply_fusion) | data formatting | bytes 524288 | tf_op jit(solution)/shard_map/jit(kron)/mul | solution.py:520
  26.2 0.0 copy-start.2
  26.2 0.0 copy-start.3
  26.3 15.7 %fold_weights.1.weights_ref = f32[16,32,32,128]{3,2,1,0:T(8,128)S(1)} custom-call(f32[2,32,32,32,64]{4,3,2,1,0:T(8,128)} %bitcast.20, f32[2,32,32,32,64]{4,3,2,1,0:T(8,128)} %bitcast.21), custom_call_target="tpu_custom_call" | custom-call | flops 8000000 | bytes 46137344 | tf_op jit(solution)/shard_map/fold_weights/pallas_call | solution.py:188
  42.0 0.0 copy-start
  42.0 3.4 %copy-done = f32[16,32,32,128]{3,2,1,0:T(8,128)} copy-done((f32[16,32,32,128]{3,2,1,0:T(8,128)}, f32[16,32,32,128]{3,2,1,0:T(8,128)S(1)}, u32[]{:S(2)}) %copy-start) | copy-done | bytes 8388632
  45.4 0.0 all-to-all-done.lines_ref
  45.4 0.0 copy-done.2
  45.4 0.0 copy-done.3
  45.4 0.0 copy-start.1
  45.5 3.4 %copy-done.1 = f32[16,32,32,128]{3,2,1,0:T(8,128)S(1)} copy-done((f32[16,32,32,128]{3,2,1,0:T(8,128)S(1)}, f32[16,32,32,128]{3,2,1,0:T(8,128)}, u32[]{:S(2)}) %copy-start.1) | copy-done | bytes 8388632
  48.8 6.8 %mix_modes.1 = (f32[16,32,128]{2,1,0:T(8,128)S(1)}, f32[16,32,128]{2,1,0:T(8,128)}) custom-call(f32[16,16]{1,0:T(8,128)S(1)} %copy-done.3, f32[16,16]{1,0:T(8,128)S(1)} %copy-done.2, f32[16,32,128]{2,1,0:T(8,128)S(1)} %all-to-all-done.lines_ref, f32[16,32,32,128]{3,2,1,0:T(8,128)S(1)} %copy-done.1), custom_call_target="tpu_custom_call" | custom-call | flops 20000000 | bytes 9437184 | tf_op jit(solution)/shard_map/mix_modes/pallas_call | solution.py:258
  55.7 6.0 %all-to-all-start.1 = ((f32[16,32,128]{2,1,0:T(8,128)}), f32[16,32,128]{2,1,0:T(8,128)S(1)}, u32[]{:S(2)}, u32[]{:S(2)}) async-start(f32[16,32,128]{2,1,0:T(8,128)} %get-tuple-element.11), calls=%async_computation.1 | async-start | bytes 524288 | tf_op jit(solution)/shard_map/all_to_all | solution.py:487
  61.7 0.0 copy-start.5
  61.7 2.2 %copy-done.5 = f32[32,1,128,256]{3,2,1,0:T(8,128)S(1)} copy-done((f32[32,1,128,256]{3,2,1,0:T(8,128)S(1)}, f32[32,1,128,256]{3,2,1,0:T(8,128)}, u32[]{:S(2)}) %copy-start.5) | copy-done | bytes 4194328
  63.9 3.7 %pointwise.1.pre_ref = f32[32,128,256]{2,1,0:T(8,128)S(1)} custom-call(bf16[512,256]{1,0:T(8,128)(2,1)S(1)} %pad_maximum_fusion.mixer_ref, f32[256,1]{1,0:T(8,128)S(1)} %broadcast_in_dim_reshape.4.bias_ref, f32[32,128,256]{2,1,0:T(8,128)S(1)} %bitcast.17), custom_call_target="tpu_custom_call" | custom-call | flops 4000000000 | bytes 25165824 | tf_op jit(solution)/shard_map/pointwise/pallas_call | solution.py:301
  67.6 0.0 copy-start.18
  67.6 2.0 %copy-done.18 = f32[32,128,256]{2,1,0:T(8,128)} copy-done((f32[32,128,256]{2,1,0:T(8,128)}, f32[32,128,256]{2,1,0:T(8,128)S(1)}, u32[]{:S(2)}) %copy-start.18) | copy-done | bytes 4194328
  69.6 2.1 %all-to-all-done.1 = f32[16,32,128]{2,1,0:T(8,128)S(1)} async-done(((f32[16,32,128]{2,1,0:T(8,128)}), f32[16,32,128]{2,1,0:T(8,128)S(1)}, u32[]{:S(2)}, u32[]{:S(2)}) %all-to-all-start.1) | async-done | bytes 262176 | tf_op jit(solution)/shard_map/all_to_all | solution.py:487
  71.7 0.0 copy-done.7
  71.7 0.0 copy-done.9
  71.7 0.0 copy-done.11
  71.7 0.0 copy-done.12
  71.7 0.0 copy-start.6
  71.8 2.2 %copy-done.6 = f32[32,1,128,256]{3,2,1,0:T(8,128)S(1)} copy-done((f32[32,1,128,256]{3,2,1,0:T(8,128)S(1)}, f32[32,1,128,256]{3,2,1,0:T(8,128)}, u32[]{:S(2)}) %copy-start.6) | copy-done | bytes 4194328
  73.9 0.9 copy-done.13
  74.8 0.9 copy-done.14
  75.7 0.8 copy-done.15
  76.6 0.8 copy-done.17
  77.3 2.2 %copy-done.19 = f32[32,128,256]{2,1,0:T(8,128)S(1)} copy-done((f32[32,128,256]{2,1,0:T(8,128)S(1)}, f32[32,128,256]{2,1,0:T(8,128)}, u32[]{:S(2)}) %copy-start.19) | copy-done | bytes 4194328
  79.5 14.9 %cells.1 = (bf16[32,128,256]{2,1,0:T(8,128)(2,1)}, f32[768,128]{1,0:T(8,128)S(1)}) custom-call(bf16[128,192]{1,0:T(8,128)(2,1)S(1)} %copy-done.15, bf16[256,512]{1,0:T(8,128)(2,1)S(1)} %copy-done.12, bf16[128,512]{1,0:T(8,128)(2,1)S(1)} %copy-done.13, bf16[512,256]{1,0:T(8,128)(2,1)S(1)} %copy-done.11, bf16[512,256]{1,0:T(8,128)(2,1)S(1)} %copy-done.9, ...), custom_call_target="tpu_custom_call" | custom-call | flops 8000000000 | bytes 12582912 | tf_op jit(solution)/shard_map/cells/pallas_call | solution.py:383
  94.5 15.9 %all_to_all.15.lines_ref = f32[16,48,128]{2,1,0:T(8,128)S(1)} all-to-all(f32[16,48,128]{2,1,0:T(8,128)S(1)} %bitcast.14), channel_id=1, replica_groups=mesh['groups'=2,'space'=16] {'space'}, dimensions={0} | all-to-all | bytes 786432 | tf_op jit(solution)/shard_map/all_to_all | solution.py:487
  110.4 15.5 %weight_gradient.1 = (f32[2,32,32,32,64]{4,3,2,1,0:T(8,128)}, f32[32,32]{1,0:T(8,128)}, f32[1,32]{1,0:T(1,128)}) custom-call(f32[16,16]{1,0:T(8,128)S(1)} %copy-done.3, f32[16,16]{1,0:T(8,128)S(1)} %copy-done.2, f32[16,32,128]{2,1,0:T(8,128)S(1)} %get-tuple-element.13.spec_ref, f32[16,48,128]{2,1,0:T(8,128)S(1)} %all_to_all.15.lines_ref), custom_call_target="tpu_custom_call" | custom-call | flops 10000000 | bytes 41943040 | tf_op jit(solution)/shard_map/weight_gradient/pallas_call | solution.py:462
  (15 shorter events, 0.1 us)
Async XLA Ops:
  0.6 18.8 %copy-start.21 = (f32[32]{0:T(128)S(1)}, f32[32]{0:T(128)}, u32[]{:S(2)}) copy-start(f32[32]{0:T(128)} %param.18) | copy-start | bytes 388
  0.6 2.2 %copy-start.4 = (f32[32,1,128,256]{3,2,1,0:T(8,128)S(1)}, f32[32,1,128,256]{3,2,1,0:T(8,128)}, u32[]{:S(2)}) copy-start(f32[32,1,128,256]{3,2,1,0:T(8,128)} %param.14) | copy-start | bytes 12582916
  2.8 0.9 copy-start.8
  3.8 0.9 copy-start.10
  4.7 0.8 copy-start.16
  5.5 13.8 %copy-start.20 = (f32[32,32]{1,0:T(8,128)S(1)}, f32[32,32]{1,0:T(8,128)}, u32[]{:S(2)}) copy-start(f32[32,32]{1,0:T(8,128)} %param.17) | copy-start | bytes 12292
  11.9 33.5 %all-to-all-start = ((f32[16,32,128]{2,1,0:T(8,128)}), f32[16,32,128]{2,1,0:T(8,128)S(1)}, u32[]{:S(2)}, u32[]{:S(2)}) async-start(f32[16,32,128]{2,1,0:T(8,128)} %bitcast.1), calls=%async_computation | async-start | bytes 524288 | tf_op jit(solution)/shard_map/all_to_all | solution.py:487
  26.2 19.2 %copy-start.2 = (f32[16,16]{1,0:T(8,128)S(1)}, f32[16,16]{1,0:T(8,128)}, u32[]{:S(2)}) copy-start(f32[16,16]{1,0:T(8,128)} %constant.19.clone.sin_ref) | copy-start | bytes 3076
  26.2 19.2 %copy-start.3 = (f32[16,16]{1,0:T(8,128)S(1)}, f32[16,16]{1,0:T(8,128)}, u32[]{:S(2)}) copy-start(f32[16,16]{1,0:T(8,128)} %constant.18.clone.cos_ref) | copy-start | bytes 3076
  42.0 3.4 %copy-start = (f32[16,32,32,128]{3,2,1,0:T(8,128)}, f32[16,32,32,128]{3,2,1,0:T(8,128)S(1)}, u32[]{:S(2)}) copy-start(f32[16,32,32,128]{3,2,1,0:T(8,128)S(1)} %fold_weights.1.weights_ref) | copy-start | bytes 25165828
  45.4 3.4 %copy-start.1 = (f32[16,32,32,128]{3,2,1,0:T(8,128)S(1)}, f32[16,32,32,128]{3,2,1,0:T(8,128)}, u32[]{:S(2)}) copy-start(f32[16,32,32,128]{3,2,1,0:T(8,128)} %copy-done) | copy-start | bytes 25165828
  55.7 16.1 %all-to-all-start.1 = ((f32[16,32,128]{2,1,0:T(8,128)}), f32[16,32,128]{2,1,0:T(8,128)S(1)}, u32[]{:S(2)}, u32[]{:S(2)}) async-start(f32[16,32,128]{2,1,0:T(8,128)} %get-tuple-element.11), calls=%async_computation.1 | async-start | bytes 524288 | tf_op jit(solution)/shard_map/all_to_all | solution.py:487
  61.7 2.2 %copy-start.5 = (f32[32,1,128,256]{3,2,1,0:T(8,128)S(1)}, f32[32,1,128,256]{3,2,1,0:T(8,128)}, u32[]{:S(2)}) copy-start(f32[32,1,128,256]{3,2,1,0:T(8,128)} %param.14) | copy-start | bytes 12582916
  63.9 7.8 %copy-start.7 = (bf16[32,1,128,256]{3,2,1,0:T(8,128)(2,1)S(1)}, bf16[32,1,128,256]{3,2,1,0:T(8,128)(2,1)}, u32[]{:S(2)}) copy-start(bf16[32,1,128,256]{3,2,1,0:T(8,128)(2,1)} %param.15) | copy-start | bytes 6291460
  63.9 7.8 %copy-start.9 = (bf16[512,256]{1,0:T(8,128)(2,1)S(1)}, bf16[512,256]{1,0:T(8,128)(2,1)}, u32[]{:S(2)}) copy-start(bf16[512,256]{1,0:T(8,128)(2,1)} %constant.22.clone.z_low) | copy-start | bytes 786436
  63.9 7.8 %copy-start.11 = (bf16[512,256]{1,0:T(8,128)(2,1)S(1)}, bf16[512,256]{1,0:T(8,128)(2,1)}, u32[]{:S(2)}) copy-start(bf16[512,256]{1,0:T(8,128)(2,1)} %constant.21.clone.z_high) | copy-start | bytes 786436
  63.9 7.8 %copy-start.12 = (bf16[256,512]{1,0:T(8,128)(2,1)S(1)}, bf16[256,512]{1,0:T(8,128)(2,1)}, u32[]{:S(2)}) copy-start(bf16[256,512]{1,0:T(8,128)(2,1)} %constant.25.clone.inv_z) | copy-start | bytes 786436
  67.6 2.0 %copy-start.18 = (f32[32,128,256]{2,1,0:T(8,128)}, f32[32,128,256]{2,1,0:T(8,128)S(1)}, u32[]{:S(2)}) copy-start(f32[32,128,256]{2,1,0:T(8,128)S(1)} %pointwise.1.pre_ref) | copy-start | bytes 12582916
  71.7 2.2 %copy-start.6 = (f32[32,1,128,256]{3,2,1,0:T(8,128)S(1)}, f32[32,1,128,256]{3,2,1,0:T(8,128)}, u32[]{:S(2)}) copy-start(f32[32,1,128,256]{3,2,1,0:T(8,128)} %param.14) | copy-start | bytes 12582916
  73.9 0.9 copy-start.13
  74.8 0.9 copy-start.14
  75.7 0.8 copy-start.15
  76.6 0.8 copy-start.17
  77.3 2.2 %copy-start.19 = (f32[32,128,256]{2,1,0:T(8,128)S(1)}, f32[32,128,256]{2,1,0:T(8,128)}, u32[]{:S(2)}) copy-start(f32[32,128,256]{2,1,0:T(8,128)} %copy-done.18) | copy-start | bytes 12582916
where the time goes:
time: 127 us; the launch traced here: 126 us
  Pallas kernels  63.1 us (50%)
  local copies, waits for them, and re-layouts  27.9 us (22%)
  blocking collectives  15.9 us (13%)
  starting transfers between devices  13.4 us (11%)
  other arithmetic  2.67 us (2%)
  waiting for transfers between devices  2.12 us (2%)
    unnamed x44, local copies, waits for them, and re-layouts  23.6 us
    all_to_all x1, blocking collectives, swap(): lax.all_to_all(lines, 'space', split_axis=0, concat_axis=0, tiled=True)  15.9 us
    pallas_call x1, Pallas kernels, fold_weights(): pl.pallas_call(fold_kernel, grid=(unique,), in_specs=[pl.BlockSpec(block,...  15.7 us
    pallas_call x1, Pallas kernels, gradient(): pl.pallas_call(functools.partial(gradient_kernel, points=points, channels...  15.5 us
    pallas_call x1, Pallas kernels, cell_stage(): pl.pallas_call(functools.partial(cell_kernel, channels=channels, rows=row...  14.9 us
    all_to_all x2, starting transfers between devices, swap(): lax.all_to_all(lines, 'space', split_axis=0, concat_axis=0, tiled=True)  13.4 us
    pallas_call x1, Pallas kernels, mix(): pl.pallas_call(functools.partial(mix_kernel, points=points, channels=chan...  6.83 us
    pallas_call x1, Pallas kernels, forward_modes(): pl.pallas_call(functools.partial(forward_kernel, channels=channels, step_...  6.42 us
  transfers between devices with their start and end apart: 2, of which 1 were waited for; matrix products, arithmetic and copies ran while one was open for 6% of the time, Pallas kernels for 15%

commit v1 on v0

--- a/solution.py
+++ b/solution.py
@@ -140,61 +140,78 @@
     return pltpu.CompilerParams(vmem_limit_bytes=limit * MIB)
 
 
-def forward_kernel(z_high, z_low, y_both, field_ref, out_ref, *, channels, step_channels):
+def fold_block(pieces, out_ref, at):
+    real, imag = pieces[0][0, at], pieces[0][1, at]
+    for piece in pieces[1:]:
+        real, imag = real + piece[0, at], imag + piece[1, at]
+    modes = real.shape[-1]
+    out_ref[at, :, :, :modes] = real
+    out_ref[at, :, :, modes:] = imag
+
+
+def fold_specs(weights, unique, per_step, first):
+    block = (2, per_step) + weights.shape[2:]
+    pieces = [
+        pl.BlockSpec(block, functools.partial(lambda s, r: (0, first + s + r, 0, 0, 0), r=r * (unique // per_step)))
+        for r in range(weights.shape[1] // unique)
+    ]
+    shape = (unique,) + weights.shape[2:4] + (2 * weights.shape[4],)
+    out = pl.BlockSpec((per_step,) + shape[1:], lambda s: (first + s, 0, 0, 0))
+    return pieces, out, jax.ShapeDtypeStruct(shape, F32)
+
+
+def forward_kernel(z_high, z_low, y_both, field_ref, *refs, channels, step_channels, per_step):
+    *pieces, out_ref, folded_ref = refs
     step = pl.program_id(0)
+    for at in range(per_step):
+        fold_block(pieces, folded_ref, at)
     for g in range(0, step_channels, GROUP):
         fields = [field_ref[g + q] for q in range(GROUP)]
         first = step * step_channels + g
         forward_group(fields, z_high[...], z_low[...], y_both[...], out_ref, first, channels)
 
 
-def forward_modes(field, tables):
+def forward_modes(field, tables, weights, unique):
     channels = field.shape[0]
-    step_channels = min(channels, 8)
-    z_high, z_low, y_both = tables
+    step_channels = 8
+    steps = channels // step_channels
+    per_step = unique // 2 // steps
+    pieces, folded, folded_shape = fold_specs(weights, unique, per_step, 0)
     owners = MY // 2
-    out = pl.pallas_call(
-        functools.partial(forward_kernel, channels=channels, step_channels=step_channels),
-        grid=(channels // step_channels,),
-        in_specs=[
-            full(z_high.shape),
-            full(z_low.shape),
-            full(y_both.shape),
-            pl.BlockSpec((step_channels, NY, NZ), lambda s: (s, 0, 0)),
-        ],
-        out_specs=full((owners * channels, LANES)),
-        out_shape=jax.ShapeDtypeStruct((owners * channels, LANES), F32),
-        compiler_params=params(24),
-        cost_estimate=pl.CostEstimate(flops=2 * 10**9, bytes_accessed=8 * MIB, transcendentals=0),
+    out, half = pl.pallas_call(
+        functools.partial(forward_kernel, channels=channels, step_channels=step_channels, per_step=per_step),
+        grid=(steps,),
+        in_specs=[full(t.shape) for t in tables]
+        + [pl.BlockSpec((step_channels, NY, NZ), lambda s: (s, 0, 0))]
+        + pieces,
+        out_specs=[full((owners * channels, LANES)), folded],
+        out_shape=[jax.ShapeDtypeStruct((owners * channels, LANES), F32), folded_shape],
+        compiler_params=params(60),
+        cost_estimate=pl.CostEstimate(flops=2 * 10**9, bytes_accessed=26 * MIB, transcendentals=0),
         name="forward_yz",
-    )(z_high, z_low, y_both, field)
-    return out.reshape(owners, channels, LANES)
-
-
-def fold_kernel(first_ref, *refs):
-    *others, out_ref = refs
-    real, imag = first_ref[0, 0], first_ref[1, 0]
-    for other in others:
-        real, imag = real + other[0, 0], imag + other[1, 0]
-    modes = real.shape[-1]
-    out_ref[0, :, :, :modes] = real
-    out_ref[0, :, :, modes:] = imag
-
-
-def fold_weights(weights, unique):
-    _, kept_x, channels, outputs, modes = weights.shape
-    block = (2, 1, channels, outputs, modes)
-    copies = kept_x // unique
+    )(*tables, field, *([weights] * len(pieces)))
+    return out.reshape(owners, channels, LANES), half
+
+
+def fold_kernel(*refs):
+    *pieces, _, out_ref = refs
+    fold_block(pieces, out_ref, 0)
+
+
+def fold_rest(weights, half, unique):
+    first = unique // 2
+    pieces, folded, folded_shape = fold_specs(weights, unique, 1, first)
     return pl.pallas_call(
         fold_kernel,
-        grid=(unique,),
-        in_specs=[pl.BlockSpec(block, functools.partial(lambda a, r: (0, a + r, 0, 0, 0), r=r * unique)) for r in range(copies)],
-        out_specs=pl.BlockSpec((1, channels, outputs, 2 * modes), lambda a: (a, 0, 0, 0)),
-        out_shape=jax.ShapeDtypeStruct((unique, channels, outputs, 2 * modes), F32),
-        compiler_params=params(16),
-        cost_estimate=pl.CostEstimate(flops=8 * 10**6, bytes_accessed=44 * MIB, transcendentals=0),
+        grid=(unique - first,),
+        in_specs=pieces + [pl.BlockSpec(memory_space=pl.ANY)],
+        out_specs=folded,
+        out_shape=folded_shape,
+        input_output_aliases={len(pieces): 0},
+        compiler_params=params(60),
+        cost_estimate=pl.CostEstimate(flops=4 * 10**6, bytes_accessed=20 * MIB, transcendentals=0),
         name="fold_weights",
-    )(*([weights] * copies))
+    )(*([weights] * len(pieces)), half)
 
 
 def spectrum_row(cos_ref, sin_ref, lines_ref, turned_ref, at, points):
@@ -277,37 +294,56 @@
             pltpu.VMEM((channels, LANES), F32),
             pltpu.VMEM((channels, LANES), F32),
         ],
-        compiler_params=params(16),
+        compiler_params=params(60),
         cost_estimate=pl.CostEstimate(flops=2 * 10**7, bytes_accessed=9 * MIB, transcendentals=0),
         name="mix_modes",
     )(cos_x, sin_x, lines, weights)
 
 
-def pointwise_kernel(mixer_ref, bias_ref, field_ref, out_ref, *, channels, blocks):
+def exact_dot(left, right):
+    return jnp.dot(left, right, precision=lax.Precision.HIGHEST, preferred_element_type=F32)
+
+
+def pointwise_kernel(sum_ref, turned_ref, bias_in_ref, field_ref, out_ref, mixer_ref, bias_ref, *, channels, blocks):
     size = 8 * channels
-    mixer = mixer_ref[...]
-    bias = bias_ref[...]
+
+    @pl.when(pl.program_id(0) == 0)
+    def _():
+        wide = exact_dot(sum_ref[...], turned_ref[...])
+        wide = lax.dot_general(
+            wide, sum_ref[...], (((1,), (1,)), ((), ())), precision=lax.Precision.HIGHEST, preferred_element_type=F32
+        )
+        row = lax.broadcasted_iota(jnp.int32, (size, size), 0) % 8
+        high, low = split(jnp.where(row == lane_index((size, size)) % 8, wide, 0.0))
+        mixer_ref[:size] = high
+        mixer_ref[size:] = low
+        bias_ref[...] = exact_dot(sum_ref[...], bias_in_ref[...])
+
     for b in range(blocks):
         high, low = split(field_ref[:, 8 * b : 8 * b + 8, :].reshape(size, NZ))
-        wide = dot(mixer, high)
-        values = wide[:size] + wide[size:] + dot(mixer[:size], low) + bias
+        wide = dot(mixer_ref[...], high)
+        values = wide[:size] + wide[size:] + dot(mixer_ref[:size], low) + bias_ref[...]
         out_ref[:, 8 * b : 8 * b + 8, :] = values.reshape(channels, 8, NZ)
 
 
-def pointwise(field, mixer, bias):
+def pointwise(field, summing, point_weights, point_bias):
     channels = field.shape[0]
     blocks = 2
+    turned = point_weights.T
+    bias = point_bias[:, None]
+    size = 8 * channels
     block = pl.BlockSpec((channels, 8 * blocks, NZ), lambda s: (0, s, 0))
     return pl.pallas_call(
         functools.partial(pointwise_kernel, channels=channels, blocks=blocks),
         grid=(NY // (8 * blocks),),
-        in_specs=[full(mixer.shape), full(bias.shape), block],
+        in_specs=[full(summing.shape), full(turned.shape), full(bias.shape), block],
         out_specs=block,
         out_shape=jax.ShapeDtypeStruct(field.shape, F32),
-        compiler_params=params(16),
+        scratch_shapes=[pltpu.VMEM((2 * size, size), BF16), pltpu.VMEM((size, 1), F32)],
+        compiler_params=params(60),
         cost_estimate=pl.CostEstimate(flops=4 * 10**9, bytes_accessed=24 * MIB, transcendentals=0),
         name="pointwise",
-    )(mixer, bias, field)
+    )(summing, turned, bias, field)
 
 
 def cell_kernel(
@@ -363,7 +399,7 @@
         row = lax.broadcasted_iota(jnp.int32, (size, size), 0) % 8
         total = jnp.where(row == lane_index((size, size)) % 8, total, 0.0)
         folded = jnp.sum(total.reshape(channels, 8, size), axis=1)
-        point = jnp.dot(folded, sum_ref[...], precision=lax.Precision.HIGHEST, preferred_element_type=F32)
+        point = exact_dot(folded, sum_ref[...])
         packed = jnp.concatenate([point[8 * q : 8 * q + 8] for q in range(channels // 8)], axis=1)
         dc = jnp.broadcast_to(out_ref[0:channels, 0:1], (channels, LANES))
         eye = lax.broadcasted_iota(jnp.int32, (channels, LANES), 0) == lane_index((channels, LANES))
@@ -396,7 +432,7 @@
             pltpu.VMEM((channels, NY, NZ), BF16),
             pltpu.SemaphoreType.DMA,
         ],
-        compiler_params=params(36),
+        compiler_params=params(60),
         cost_estimate=pl.CostEstimate(flops=8 * 10**9, bytes_accessed=12 * MIB, transcendentals=2 * 10**6),
         name="cells",
     )(*tables, modes.reshape(owners * channels, LANES), pre, cotangent, field)
@@ -477,7 +513,7 @@
             pltpu.VMEM((2, 2, channels, channels, half), F32),
             pltpu.SemaphoreType.DMA((2, copies)),
         ],
-        compiler_params=params(16),
+        compiler_params=params(60),
         cost_estimate=pl.CostEstimate(flops=10**7, bytes_accessed=40 * MIB, transcendentals=0),
         name="weight_gradient",
     )(cos_x, sin_x, spectrum, lines)
@@ -517,16 +553,14 @@
     field = lifted_field.reshape(channels, NY, NZ)
     slopes_in = cotangent.reshape(channels, NY, NZ)
     weights = jnp.transpose(spectral_weights, (0, 1, 3, 4, 2))
-    mixer = jnp.kron(point_weights.T, jnp.eye(8, dtype=F32))
-    high = lax.reduce_precision(mixer, 8, 7)
-    mixer = jnp.concatenate([high, mixer - high], axis=0).astype(BF16)
-    bias = jnp.repeat(point_bias, 8)[:, None]
-
-    lines = swap(forward_modes(field, forward))
-    folded = fold_weights(weights, length_x)
+
+    lines, half = forward_modes(field, forward, weights, length_x)
+    lines = swap(lines)
+    folded = fold_rest(weights, half, length_x)
     spectrum, mixed = mix(cos_x, sin_x, lines, folded, norm)
+    field_late, mixed = lax.optimization_barrier((field, mixed))
     modes = swap(mixed)
-    pre = pointwise(field, mixer, bias)
+    pre = pointwise(field_late, summing, point_weights, point_bias)
     activated, slope_lines = cell_stage(inverse, forward, summing, modes, pre, slopes_in, field)
     slope_lines = swap(slope_lines)
     grad, grad_point, grad_bias = gradient(cos_x, sin_x, spectrum, slope_lines, norm, MX)

time: 127 us -> 106 us (0.83)
  local copies, waits for them, and re-layouts: 27.9 us -> 2.77 us
  Pallas kernels: 63.1 us -> 70.4 us
  other arithmetic: 2.67 us -> 0 us
  blocking collectives: 15.9 us -> 18.3 us
  waiting for transfers between devices: 2.12 us -> 0.18 us
    unnamed x44 -> x9, local copies, waits for them, and re-layouts: 23.6 us -> 2.08 us
    pallas_call x1, Pallas kernels: 15.7 us -> 9.87 us  [fold_rest(): pl.pallas_call(fold_kernel, grid=(unique - first,), in_specs=pieces + [pl...]
    pallas_call x1, Pallas kernels: 6.42 us -> 11.5 us  [forward_modes(): pl.pallas_call(functools.partial(forward_kernel, channels=channels, step_...]
    pallas_call x1, Pallas kernels: 3.67 us -> 8.65 us  [pointwise(): pl.pallas_call(functools.partial(pointwise_kernel, channels=channels, blo...]
    mul x1 -> x0, local copies, waits for them, and re-layouts: 4.02 us -> none  [body(): mixer = jnp.kron(point_weights.T, jnp.eye(8, dtype=F32))]
    mul x1 -> x0, other arithmetic: 2.61 us -> none  [body(): mixer = jnp.kron(point_weights.T, jnp.eye(8, dtype=F32))]
    all_to_all x1, blocking collectives: 15.9 us -> 18.3 us  [swap(): lax.all_to_all(lines, 'space', split_axis=0, concat_axis=0, tiled=True)]
    all_to_all x2, waiting for transfers between devices: 2.12 us -> 0.18 us  [swap(): lax.all_to_all(lines, 'space', split_axis=0, concat_axis=0, tiled=True)]
  transfers between devices with their start and end apart: 2 -> 2, of which waited for: 1 -> 1; matrix products, arithmetic and copies ran while one was open for 6% -> 1% of each run, Pallas kernels for 15% -> 18%
where the time goes in v1:
time: 106 us
  Pallas kernels  70.4 us (66%)
  blocking collectives  18.3 us (17%)
  starting transfers between devices  13.2 us (12%)
  local copies, waits for them, and re-layouts  2.77 us (3%)
    all_to_all x1, blocking collectives, swap(): lax.all_to_all(lines, 'space', split_axis=0, concat_axis=0, tiled=True)  18.3 us
    pallas_call x1, Pallas kernels, cell_stage(): pl.pallas_call(functools.partial(cell_kernel, channels=channels, rows=row...  16.5 us
    pallas_call x1, Pallas kernels, gradient(): pl.pallas_call(functools.partial(gradient_kernel, points=points, channels...  15.8 us
    all_to_all x2, starting transfers between devices, swap(): lax.all_to_all(lines, 'space', split_axis=0, concat_axis=0, tiled=True)  13.2 us
    pallas_call x1, Pallas kernels, forward_modes(): pl.pallas_call(functools.partial(forward_kernel, channels=channels, step_...  11.5 us
    pallas_call x1, Pallas kernels, fold_rest(): pl.pallas_call(fold_kernel, grid=(unique - first,), in_specs=pieces + [pl...  9.87 us
    pallas_call x1, Pallas kernels, pointwise(): pl.pallas_call(functools.partial(pointwise_kernel, channels=channels, blo...  8.65 us
    pallas_call x1, Pallas kernels, mix(): pl.pallas_call(functools.partial(mix_kernel, points=points, channels=chan...  8.05 us
  transfers between devices with their start and end apart: 2, of which 1 were waited for; matrix products, arithmetic and copies ran while one was open for 1% of the time, Pallas kernels for 18%

profile of v1, /device:TPU:0, one launch (start us, length us, event | category | flops | bytes accessed | tf_op | source)
XLA Modules:
  0.0 105.5 jit_solution(6489445357655211919)
XLA Ops:
  0.6 11.5 %forward_yz.1 = (f32[512,128]{1,0:T(8,128)}, f32[16,32,32,128]{3,2,1,0:T(8,128)}) custom-call(bf16[512,256]{1,0:T(8,128)(2,1)} %constant.21.clone.z_high, bf16[512,256]{1,0:T(8,128)(2,1)} %constant.22.clone.z_low, bf16[64,256]{1,0:T(8,128)(2,1)} %constant.23.clone.y_both, f32[32,128,256]{2,1,0:T(8,128)} %bitcast.17, f32[2,32,32,32,64]{4,3,2,1,0:T(8,128)} %bitcast.13, ...), custom_call_target="tpu_custom_call" | custom-call | flops 2000000000 | bytes 27262976 | tf_op jit(solution)/shard_map/forward_yz/pallas_call | solution.py:181
  12.2 7.4 %all-to-all-start = ((f32[16,32,128]{2,1,0:T(8,128)}), f32[16,32,128]{2,1,0:T(8,128)S(1)}, u32[]{:S(2)}, u32[]{:S(2)}) async-start(f32[16,32,128]{2,1,0:T(8,128)} %bitcast.22), calls=%async_computation | async-start | bytes 524288 | tf_op jit(solution)/shard_map/all_to_all | solution.py:523
  19.6 9.9 %fold_weights.1.weights_ref = f32[16,32,32,128]{3,2,1,0:T(8,128)} custom-call(f32[2,32,32,32,64]{4,3,2,1,0:T(8,128)} %bitcast.15, f32[2,32,32,32,64]{4,3,2,1,0:T(8,128)} %bitcast.16, f32[16,32,32,128]{3,2,1,0:T(8,128)} %get-tuple-element.16.refs_2_), custom_call_target="tpu_custom_call", output_to_operand_aliasing={{}: (2, {})} | custom-call | flops 4000000 | bytes 20971520 | tf_op jit(solution)/shard_map/fold_weights/pallas_call | solution.py:204
  29.4 0.0 copy-start.2
  29.4 0.0 copy-start.3
  29.4 0.2 all-to-all-done.lines_ref
  29.6 0.0 copy-start
  29.6 0.7 copy-done
  30.3 8.1 %mix_modes.1 = (f32[16,32,128]{2,1,0:T(8,128)}, f32[16,32,128]{2,1,0:T(8,128)}) custom-call(f32[16,16]{1,0:T(8,128)} %constant.18.clone.cos_ref, f32[16,16]{1,0:T(8,128)} %constant.19.clone.sin_ref, f32[16,32,128]{2,1,0:T(8,128)} %copy-done, f32[16,32,32,128]{3,2,1,0:T(8,128)} %fold_weights.1.weights_ref), custom_call_target="tpu_custom_call" | custom-call | flops 20000000 | bytes 9437184 | tf_op jit(solution)/shard_map/mix_modes/pallas_call | solution.py:275
  38.4 5.8 %all-to-all-start.1 = ((f32[16,32,128]{2,1,0:T(8,128)}), f32[16,32,128]{2,1,0:T(8,128)S(1)}, u32[]{:S(2)}, u32[]{:S(2)}) async-start(f32[16,32,128]{2,1,0:T(8,128)} %get-tuple-element.18), calls=%async_computation.1 | async-start | bytes 524288 | tf_op jit(solution)/shard_map/all_to_all | solution.py:523
  44.2 0.0 copy-done.2
  44.2 0.7 copy.19
  44.9 0.0 copy-done.3
  44.9 0.7 copy.20.bias_in_ref
  45.6 8.7 %pointwise.1.pre_ref = f32[32,128,256]{2,1,0:T(8,128)} custom-call(f32[256,32]{1,0:T(8,128)} %constant.20.clone.sum_ref, f32[32,32]{1,0:T(8,128)} %bitcast.23, f32[32,1]{1,0:T(8,128)} %copy.20.bias_in_ref, f32[32,128,256]{2,1,0:T(8,128)} %bitcast.18), custom_call_target="tpu_custom_call" | custom-call | flops 4000000000 | bytes 25165824 | tf_op jit(solution)/shard_map/pointwise/pallas_call | solution.py:336
  54.3 0.0 all-to-all-done.1
  54.3 0.0 copy-start.1
  54.3 0.7 copy-done.1
  55.0 16.5 %cells.1 = (bf16[32,128,256]{2,1,0:T(8,128)(2,1)}, f32[768,128]{1,0:T(8,128)}) custom-call(bf16[128,192]{1,0:T(8,128)(2,1)} %constant.24.clone.inv_y, bf16[256,512]{1,0:T(8,128)(2,1)} %constant.25.clone.inv_z, bf16[128,512]{1,0:T(8,128)(2,1)} %constant.26.clone.inv_z_low, bf16[512,256]{1,0:T(8,128)(2,1)} %constant.21.clone.z_high, ...), custom_call_target="tpu_custom_call" | custom-call | flops 8000000000 | bytes 12582912 | tf_op jit(solution)/shard_map/cells/pallas_call | solution.py:419
  71.4 18.3 %all_to_all.15.lines_ref = f32[16,48,128]{2,1,0:T(8,128)} all-to-all(f32[16,48,128]{2,1,0:T(8,128)} %bitcast.20), channel_id=1, replica_groups=mesh['groups'=2,'space'=16] {'space'}, dimensions={0} | all-to-all | bytes 786432 | tf_op jit(solution)/shard_map/all_to_all | solution.py:523
  89.8 15.8 %weight_gradient.1 = (f32[2,32,32,32,64]{4,3,2,1,0:T(8,128)}, f32[32,32]{1,0:T(8,128)}, f32[1,32]{1,0:T(1,128)}) custom-call(f32[16,16]{1,0:T(8,128)} %constant.18.clone.cos_ref, f32[16,16]{1,0:T(8,128)} %constant.19.clone.sin_ref, f32[16,32,128]{2,1,0:T(8,128)} %get-tuple-element.21.spec_ref, f32[16,48,128]{2,1,0:T(8,128)} %all_to_all.15.lines_ref), custom_call_target="tpu_custom_call" | custom-call | flops 10000000 | bytes 41943040 | tf_op jit(solution)/shard_map/weight_gradient/pallas_call | solution.py:498
Async XLA Ops:
  12.2 17.4 %all-to-all-start = ((f32[16,32,128]{2,1,0:T(8,128)}), f32[16,32,128]{2,1,0:T(8,128)S(1)}, u32[]{:S(2)}, u32[]{:S(2)}) async-start(f32[16,32,128]{2,1,0:T(8,128)} %bitcast.22), calls=%async_computation | async-start | bytes 524288 | tf_op jit(solution)/shard_map/all_to_all | solution.py:523
  29.4 14.8 %copy-start.2 = (f32[32,32]{1,0:T(8,128)S(1)}, f32[32,32]{1,0:T(8,128)}, u32[]{:S(2)}) copy-start(f32[32,32]{1,0:T(8,128)} %param.17) | copy-start | bytes 12292
  29.4 15.5 %copy-start.3 = (f32[32]{0:T(128)S(1)}, f32[32]{0:T(128)}, u32[]{:S(2)}) copy-start(f32[32]{0:T(128)} %param.18) | copy-start | bytes 388
  29.6 0.7 copy-start
  38.4 15.9 %all-to-all-start.1 = ((f32[16,32,128]{2,1,0:T(8,128)}), f32[16,32,128]{2,1,0:T(8,128)S(1)}, u32[]{:S(2)}, u32[]{:S(2)}) async-start(f32[16,32,128]{2,1,0:T(8,128)} %get-tuple-element.18), calls=%async_computation.1 | async-start | bytes 524288 | tf_op jit(solution)/shard_map/all_to_all | solution.py:523
  54.3 0.7 copy-start.1

commit v2 on v1

--- a/solution.py
+++ b/solution.py
@@ -22,6 +22,7 @@
 MIB = 1 << 20
 LANES = 128
 GROUP = 4
+STEP = 16
 
 
 def kept(kept_count, length):
@@ -95,24 +96,26 @@
 
 def forward_group(fields, z_high, z_low, y_both, out_ref, first, rows):
     left = jnp.concatenate(
-        [jnp.concatenate([fields[q], fields[q + 1]], axis=1) for q in range(0, GROUP, 2)], axis=0
+        [jnp.concatenate([fields[q], fields[q + 1]], axis=1) for q in range(0, len(fields), 2)], axis=0
     )
     high, low = split(left)
     lines = dot(high, z_high) + dot(high, z_low) + dot(low, z_high)
-    pairs = []
-    for q in range(GROUP // 2):
-        part = lines[q * NY : (q + 1) * NY]
-        pairs.append(jnp.concatenate([part[:, :LANES], part[:, LANES:]], axis=0))
-    high, low = split(jnp.concatenate(pairs, axis=1))
-    wide = dot(y_both, high)
-    modes = wide[:MY] + wide[MY:] + dot(y_both[:MY], low)
     half = MY // 2
-    for q in range(GROUP // 2):
-        even = modes[:half, q * LANES : (q + 1) * LANES]
-        odd = modes[half:, q * LANES : (q + 1) * LANES]
-        at_even = (lane_index(even.shape) // MZ) % 2 == 0
-        out_ref[pl.ds(first + 2 * q, half, stride=rows), :] = jnp.where(at_even, even, roll(odd, MZ))
-        out_ref[pl.ds(first + 2 * q + 1, half, stride=rows), :] = jnp.where(at_even, roll(even, -MZ), odd)
+    for g in range(0, len(fields) // 2, GROUP // 2):
+        pairs = []
+        for q in range(g, g + GROUP // 2):
+            part = lines[q * NY : (q + 1) * NY]
+            pairs.append(jnp.concatenate([part[:, :LANES], part[:, LANES:]], axis=0))
+        high, low = split(jnp.concatenate(pairs, axis=1))
+        wide = dot(y_both, high)
+        modes = wide[:MY] + wide[MY:] + dot(y_both[:MY], low)
+        for q in range(GROUP // 2):
+            even = modes[:half, q * LANES : (q + 1) * LANES]
+            odd = modes[half:, q * LANES : (q + 1) * LANES]
+            at_even = (lane_index(even.shape) // MZ) % 2 == 0
+            at = first + 2 * (g + q)
+            out_ref[pl.ds(at, half, stride=rows), :] = jnp.where(at_even, even, roll(odd, MZ))
+            out_ref[pl.ds(at + 1, half, stride=rows), :] = jnp.where(at_even, roll(even, -MZ), odd)
 
 
 def inverse_y_group(modes_ref, y_table, first, rows):
@@ -121,15 +124,16 @@
     for q in range(GROUP // 2):
         c0 = modes_ref[pl.ds(first + 2 * q, half, stride=rows), :]
         c1 = modes_ref[pl.ds(first + 2 * q + 1, half, stride=rows), :]
-        lane = lane_index(c0.shape)
-        at_even = (lane // MZ) % 2 == 0
+        at_even = (lane_index(c0.shape) // MZ) % 2 == 0
         even = jnp.where(at_even, c0, roll(c1, MZ))
         odd = jnp.where(at_even, roll(c0, -MZ), c1)
         both = jnp.concatenate([even, odd], axis=0)
-        turned = jnp.where(lane_index(both.shape) < LANES // 2, -roll(both, 64), roll(both, 64))
+        other = roll(both, 64)
+        turned = jnp.where(lane_index(both.shape) < LANES // 2, -other, other)
         pairs.append(jnp.concatenate([both, turned], axis=0))
     high, low = split(jnp.concatenate(pairs, axis=1))
-    return dot(y_table, jnp.concatenate([high, low, high], axis=0))
+    lines = dot(y_table, jnp.concatenate([high, low, high], axis=0))
+    return [lines[:, q * LANES : (q + 1) * LANES] for q in range(GROUP // 2)]
 
 
 def full(shape):
@@ -165,10 +169,8 @@
     step = pl.program_id(0)
     for at in range(per_step):
         fold_block(pieces, folded_ref, at)
-    for g in range(0, step_channels, GROUP):
-        fields = [field_ref[g + q] for q in range(GROUP)]
-        first = step * step_channels + g
-        forward_group(fields, z_high[...], z_low[...], y_both[...], out_ref, first, channels)
+    fields = [field_ref[q] for q in range(step_channels)]
+    forward_group(fields, z_high[...], z_low[...], y_both[...], out_ref, step * step_channels, channels)
 
 
 def forward_modes(field, tables, weights, unique):
@@ -214,17 +216,21 @@
     )(*([weights] * len(pieces)), half)
 
 
-def spectrum_row(cos_ref, sin_ref, lines_ref, turned_ref, at, points):
-    total = cos_ref[at, 0] * lines_ref[0] + sin_ref[at, 0] * turned_ref[0]
-    for x in range(1, points):
-        total += cos_ref[at, x] * lines_ref[x] + sin_ref[at, x] * turned_ref[x]
+def halve_lines(lines_ref, sums_ref, points, channels):
+    half = points // 2
+    sign = jnp.where(lane_index((channels, LANES)) < LANES // 2, 1.0, -1.0)
+    for x in range(half):
+        near, far = lines_ref[x, :channels], lines_ref[x + half, :channels]
+        for parity, value in enumerate((near + far, near - far)):
+            sums_ref[parity, 0, x] = value
+            sums_ref[parity, 1, x] = sign * roll(value, 64)
+
+
+def spectrum_row(cos_ref, sin_ref, sums_ref, at, parity, half):
+    total = cos_ref[at, 0] * sums_ref[parity, 0, 0] + sin_ref[at, 0] * sums_ref[parity, 1, 0]
+    for x in range(1, half):
+        total += cos_ref[at, x] * sums_ref[parity, 0, x] + sin_ref[at, x] * sums_ref[parity, 1, x]
     return total
-
-
-def turn_lines(lines_ref, turned_ref, points, channels):
-    sign = jnp.where(lane_index((channels, LANES)) < LANES // 2, 1.0, -1.0)
-    for x in range(points):
-        turned_ref[x] = sign * roll(lines_ref[x, :channels], 64)
 
 
 def doubled(values):
@@ -233,34 +239,43 @@
     return jnp.where(low, values, other), jnp.where(low, other, values)
 
 
-def mix_kernel(cos_ref, sin_ref, lines_ref, weights_ref, spec_ref, out_ref, turned_ref, real_ref, imag_ref, *, points, channels, per_step, norm):
+def mix_kernel(
+    cos_ref, sin_ref, lines_ref, weights_ref, spec_ref, out_ref, sums_ref, total_ref, real_ref, imag_ref,
+    *, points, channels, per_step, norm,
+):
     step = pl.program_id(0)
+    half = points // 2
 
     @pl.when(step == 0)
     def _():
-        turn_lines(lines_ref, turned_ref, points, channels)
-        out_ref[...] = jnp.zeros_like(out_ref)
+        halve_lines(lines_ref, sums_ref, points, channels)
+        total_ref[...] = jnp.zeros_like(total_ref)
 
     low = lane_index((channels, LANES)) < LANES // 2
-
-    @pl.loop(0, per_step)
-    def _(q):
+    for q in range(per_step):
         at = step * per_step + q
-        spec = norm * spectrum_row(cos_ref, sin_ref, lines_ref, turned_ref, at, points)
+        parity = q % 2
+        spec = norm * spectrum_row(cos_ref, sin_ref, sums_ref, at, parity, half)
         spec_ref[q] = spec
-        real_ref[...], imag_ref[...] = doubled(spec)
+        real_ref[q], imag_ref[q] = doubled(spec)
         by_real = jnp.zeros((channels, LANES), F32)
         by_imag = jnp.zeros((channels, LANES), F32)
         for i in range(channels):
             weight = weights_ref[q, i]
-            by_real += real_ref[pl.ds(i, 1), :] * weight
-            by_imag += imag_ref[pl.ds(i, 1), :] * weight
+            by_real += real_ref[q, pl.ds(i, 1), :] * weight
+            by_imag += imag_ref[q, pl.ds(i, 1), :] * weight
         other = roll(by_imag, 64)
         mixed = by_real + jnp.where(low, -other, other)
         other = roll(mixed, 64)
         turned = jnp.where(low, -other, other)
-        for x in range(points):
-            out_ref[x] += cos_ref[at, x] * mixed + sin_ref[at, x] * turned
+        for x in range(half):
+            total_ref[parity, x] += cos_ref[at, x] * mixed + sin_ref[at, x] * turned
+
+    @pl.when(step == pl.num_programs(0) - 1)
+    def _():
+        for x in range(half):
+            out_ref[x] = total_ref[0, x] + total_ref[1, x]
+            out_ref[x + half] = total_ref[0, x] - total_ref[1, x]
 
 
 def smem():
@@ -290,9 +305,10 @@
             jax.ShapeDtypeStruct(shape, F32),
         ],
         scratch_shapes=[
-            pltpu.VMEM(shape, F32),
-            pltpu.VMEM((channels, LANES), F32),
-            pltpu.VMEM((channels, LANES), F32),
+            pltpu.VMEM((2, 2, points // 2, channels, LANES), F32),
+            pltpu.VMEM((2, points // 2, channels, LANES), F32),
+            pltpu.VMEM((per_step, channels, LANES), F32),
+            pltpu.VMEM((per_step, channels, LANES), F32),
         ],
         compiler_params=params(60),
         cost_estimate=pl.CostEstimate(flops=2 * 10**7, bytes_accessed=9 * MIB, transcendentals=0),
@@ -348,7 +364,7 @@
 
 def cell_kernel(
     inv_y, inv_z, inv_z_low, z_high, z_low, y_both, sum_ref, modes_ref, pre_ref, cot_ref, field_hbm,
-    act_ref, out_ref, field_ref, slope_high, slope_low, sem, *, channels, rows, owners,
+    act_ref, out_ref, field_ref, slope_ref, sem, *, channels, step_channels, rows, owners,
 ):
     step = pl.program_id(0)
     copy = pltpu.make_async_copy(field_hbm, field_ref, sem)
@@ -357,13 +373,14 @@
     def _():
         copy.start()
 
-    first = step * GROUP
-    lines = inverse_y_group(modes_ref, inv_y[...], first, channels)
-    lines = jnp.concatenate([lines[:, q * LANES : (q + 1) * LANES] for q in range(GROUP // 2)], axis=0)
-    high, low = split(lines)
+    first = step * step_channels
+    lines = []
+    for g in range(0, step_channels, GROUP):
+        lines += inverse_y_group(modes_ref, inv_y[...], first + g, channels)
+    high, low = split(jnp.concatenate(lines, axis=0))
     spectral = dot(jnp.concatenate([high, low], axis=1), inv_z[...]) + dot(high, inv_z_low[...])
     slopes = []
-    for q in range(GROUP):
+    for q in range(step_channels):
         r = q // 2 * NY
         c = q % 2 * NZ
         before = spectral[r : r + NY, c : c + NZ] + pre_ref[q]
@@ -372,9 +389,7 @@
         pdf = jnp.exp(-0.5 * before * before) * INV_SQRT_TWO_PI
         slope = cot_ref[q].astype(F32) * (cdf + before * pdf)
         slopes.append(slope)
-        high, low = split(slope)
-        slope_high[first + q] = high
-        slope_low[first + q] = low
+        slope_ref[first + q] = slope
     forward_group(slopes, z_high[...], z_low[...], y_both[...], out_ref, first, rows)
 
     @pl.when(step == pl.num_programs(0) - 1)
@@ -382,20 +397,16 @@
         copy.wait()
         size = 8 * channels
         total = jnp.zeros((size, size), F32)
-        nt = (((1,), (1,)), ((), ()))
-        for b in range(NY // 16):
-            at = pl.ds(16 * b, 16)
-            field_high, field_low = split(field_ref[:, at, :])
-            s_high, s_low = slope_high[:, at, :], slope_low[:, at, :]
-            for h in range(2):
-                part = slice(8 * h, 8 * h + 8)
-                f_h = field_high[:, part].reshape(size, NZ)
-                f_l = field_low[:, part].reshape(size, NZ)
-                s_h = s_high[:, part].reshape(size, NZ)
-                s_l = s_low[:, part].reshape(size, NZ)
-                total += lax.dot_general(f_h, s_h, nt, preferred_element_type=F32)
-                total += lax.dot_general(f_h, s_l, nt, preferred_element_type=F32)
-                total += lax.dot_general(f_l, s_h, nt, preferred_element_type=F32)
+        for b in range(NY // 8):
+            at = slice(8 * b, 8 * b + 8)
+            f_h, f_l = split(field_ref[:, at, :].reshape(size, NZ))
+            s_h, s_l = split(slope_ref[:, at, :].reshape(size, NZ))
+            total += lax.dot_general(
+                jnp.concatenate([f_h, f_h, f_l], axis=1),
+                jnp.concatenate([s_h, s_l, s_h], axis=1),
+                (((1,), (1,)), ((), ())),
+                preferred_element_type=F32,
+            )
         row = lax.broadcasted_iota(jnp.int32, (size, size), 0) % 8
         total = jnp.where(row == lane_index((size, size)) % 8, total, 0.0)
         folded = jnp.sum(total.reshape(channels, 8, size), axis=1)
@@ -414,11 +425,12 @@
     channels = field.shape[0]
     owners = MY // 2
     rows = channels + 16
-    block = pl.BlockSpec((GROUP, NY, NZ), lambda s: (s, 0, 0))
+    step_channels = STEP
+    block = pl.BlockSpec((step_channels, NY, NZ), lambda s: (s, 0, 0))
     tables = (*inverse, *forward, summing)
     act, out = pl.pallas_call(
-        functools.partial(cell_kernel, channels=channels, rows=rows, owners=owners),
-        grid=(channels // GROUP,),
+        functools.partial(cell_kernel, channels=channels, step_channels=step_channels, rows=rows, owners=owners),
+        grid=(channels // step_channels,),
         in_specs=[full(t.shape) for t in tables]
         + [full((owners * channels, LANES)), block, block, pl.BlockSpec(memory_space=pl.ANY)],
         out_specs=[block, full((owners * rows, LANES))],
@@ -428,8 +440,7 @@
         ],
         scratch_shapes=[
             pltpu.VMEM((channels, NY, NZ), F32),
-            pltpu.VMEM((channels, NY, NZ), BF16),
-            pltpu.VMEM((channels, NY, NZ), BF16),
+            pltpu.VMEM((channels, NY, NZ), F32),
             pltpu.SemaphoreType.DMA,
         ],
         compiler_params=params(60),
@@ -441,9 +452,9 @@
 
 def gradient_kernel(
     cos_ref, sin_ref, spec_ref, lines_ref, out_hbm, point_ref, bias_ref,
-    turned_ref, slope_ref, flip_ref, real_ref, imag_ref, buffer, sems, *, points, channels, unique, copies, norm,
+    sums_ref, real_ref, imag_ref, buffer, sems, *, points, channels, unique, copies, norm,
 ):
-    turn_lines(lines_ref, turned_ref, points, channels)
+    halve_lines(lines_ref, sums_ref, points, channels)
     half = LANES // 2
     lane = lane_index((channels, LANES))
     scale = jnp.where(lane % MZ == 0, norm, 2.0 * norm)
@@ -461,30 +472,28 @@
             for r in range(copies)
         ]
 
-    @pl.loop(0, unique)
-    def _(at):
-        slot = at % 2
-
-        @pl.when(at >= 2)
-        def _():
-            for copy in writes(at - 2, slot):
-                copy.wait()
-
-        total = cos_ref[at, 0] * lines_ref[0, :channels] + sin_ref[at, 0] * turned_ref[0]
-        for x in range(1, points):
-            total += cos_ref[at, x] * lines_ref[x, :channels] + sin_ref[at, x] * turned_ref[x]
-        slope = scale * total
-        other = roll(slope, 64)
-        flipped = jnp.where(lane < half, other, -other)
-        real_ref[...], imag_ref[...] = doubled(spec_ref[at])
-        for i in range(channels):
-            both = real_ref[pl.ds(i, 1), :] * slope + imag_ref[pl.ds(i, 1), :] * flipped
-            buffer[slot, 0, i] = both[:, :half]
-            buffer[slot, 1, i] = both[:, half:]
-        for copy in writes(at, slot):
-            copy.start()
-
-    for at in range(max(unique - 2, 0), unique):
+    @pl.loop(0, unique // 2)
+    def _(pair):
+        for slot in range(2):
+            at = 2 * pair + slot
+
+            @pl.when(pair > 0)
+            def _():
+                for copy in writes(at - 2, slot):
+                    copy.wait()
+
+            slope = scale * spectrum_row(cos_ref, sin_ref, sums_ref, at, slot, points // 2)
+            other = roll(slope, 64)
+            flipped = jnp.where(lane < half, other, -other)
+            real_ref[slot], imag_ref[slot] = doubled(spec_ref[at])
+            for i in range(channels):
+                both = real_ref[slot, pl.ds(i, 1), :] * slope + imag_ref[slot, pl.ds(i, 1), :] * flipped
+                buffer[slot, 0, i] = both[:, :half]
+                buffer[slot, 1, i] = both[:, half:]
+            for copy in writes(at, slot):
+                copy.start()
+
+    for at in range(unique - 2, unique):
         for copy in writes(at, at % 2):
             copy.wait()
 
@@ -505,11 +514,9 @@
             jax.ShapeDtypeStruct((1, channels), F32),
         ],
         scratch_shapes=[
-            pltpu.VMEM((points, channels, LANES), F32),
-            pltpu.VMEM(flat, F32),
-            pltpu.VMEM(flat, F32),
-            pltpu.VMEM(flat, F32),
-            pltpu.VMEM(flat, F32),
+            pltpu.VMEM((2, 2, points // 2, channels, LANES), F32),
+            pltpu.VMEM((2,) + flat, F32),
+            pltpu.VMEM((2,) + flat, F32),
             pltpu.VMEM((2, 2, channels, channels, half), F32),
             pltpu.SemaphoreType.DMA((2, copies)),
         ],
@@ -532,6 +539,7 @@
         and devices * 2 == MY
         and 2 * held == LANES
         and MX % length_x == 0
+        and length_x % 8 == 0
         and even
         and channels == MZ
     )

time: 106 us -> 98.9 us (0.933)
  Pallas kernels: 70.4 us -> 63 us
    pallas_call x1, Pallas kernels: 16.5 us -> 12.7 us  [cell_stage(): pl.pallas_call(functools.partial(cell_kernel, channels=channels, step_cha...]
    pallas_call x1, Pallas kernels: 8.05 us -> 5.89 us  [mix(): pl.pallas_call(functools.partial(mix_kernel, points=points, channels=chan...]
  transfers between devices with their start and end apart: 2 -> 2, of which waited for: 1 -> 1; matrix products, arithmetic and copies ran while one was open for 1% -> 1% of each run, Pallas kernels for 18% -> 19%
where the time goes in v2:
time: 98.9 us; the launch traced here: 98.2 us
  Pallas kernels  63 us (64%)
  blocking collectives  18.3 us (19%)
  starting transfers between devices  13.2 us (13%)
  local copies, waits for them, and re-layouts  2.77 us (3%)
    all_to_all x1, blocking collectives, swap(): lax.all_to_all(lines, 'space', split_axis=0, concat_axis=0, tiled=True)  18.3 us
    pallas_call x1, Pallas kernels, gradient(): pl.pallas_call(functools.partial(gradient_kernel, points=points, channels...  15.4 us
    all_to_all x2, starting transfers between devices, swap(): lax.all_to_all(lines, 'space', split_axis=0, concat_axis=0, tiled=True)  13.2 us
    pallas_call x1, Pallas kernels, cell_stage(): pl.pallas_call(functools.partial(cell_kernel, channels=channels, step_cha...  12.7 us
    pallas_call x1, Pallas kernels, forward_modes(): pl.pallas_call(functools.partial(forward_kernel, channels=channels, step_...  10.5 us
    pallas_call x1, Pallas kernels, fold_rest(): pl.pallas_call(fold_kernel, grid=(unique - first,), in_specs=pieces + [pl...  9.87 us
    pallas_call x1, Pallas kernels, pointwise(): pl.pallas_call(functools.partial(pointwise_kernel, channels=channels, blo...  8.67 us
    pallas_call x1, Pallas kernels, mix(): pl.pallas_call(functools.partial(mix_kernel, points=points, channels=chan...  5.89 us
  transfers between devices with their start and end apart: 2, of which 1 were waited for; matrix products, arithmetic and copies ran while one was open for 1% of the time, Pallas kernels for 19%

profile of v2, /device:TPU:0, one launch (start us, length us, event | category | flops | bytes accessed | tf_op | source)
XLA Modules:
  0.0 98.2 jit_solution(18232393389377270924)
XLA Ops:
  0.6 10.5 %forward_yz.1 = (f32[512,128]{1,0:T(8,128)}, f32[16,32,32,128]{3,2,1,0:T(8,128)}) custom-call(bf16[512,256]{1,0:T(8,128)(2,1)} %constant.21.clone.z_high, bf16[512,256]{1,0:T(8,128)(2,1)} %constant.22.clone.z_low, bf16[64,256]{1,0:T(8,128)(2,1)} %constant.23.clone.y_both, f32[32,128,256]{2,1,0:T(8,128)} %bitcast.17, f32[2,32,32,32,64]{4,3,2,1,0:T(8,128)} %bitcast.13, ...), custom_call_target="tpu_custom_call" | custom-call | flops 2000000000 | bytes 27262976 | tf_op jit(solution)/shard_map/forward_yz/pallas_call | solution.py:183
  11.1 7.4 %all-to-all-start = ((f32[16,32,128]{2,1,0:T(8,128)}), f32[16,32,128]{2,1,0:T(8,128)S(1)}, u32[]{:S(2)}, u32[]{:S(2)}) async-start(f32[16,32,128]{2,1,0:T(8,128)} %bitcast.22), calls=%async_computation | async-start | bytes 524288 | tf_op jit(solution)/shard_map/all_to_all | solution.py:530
  18.5 9.9 %fold_weights.1.weights_ref = f32[16,32,32,128]{3,2,1,0:T(8,128)} custom-call(f32[2,32,32,32,64]{4,3,2,1,0:T(8,128)} %bitcast.15, f32[2,32,32,32,64]{4,3,2,1,0:T(8,128)} %bitcast.16, f32[16,32,32,128]{3,2,1,0:T(8,128)} %get-tuple-element.16.refs_2_), custom_call_target="tpu_custom_call", output_to_operand_aliasing={{}: (2, {})} | custom-call | flops 4000000 | bytes 20971520 | tf_op jit(solution)/shard_map/fold_weights/pallas_call | solution.py:206
  28.4 0.0 copy-start.2
  28.4 0.0 copy-start.3
  28.4 0.2 all-to-all-done.lines_ref
  28.6 0.0 copy-start
  28.6 0.7 copy-done
  29.3 5.9 %mix_modes.1 = (f32[16,32,128]{2,1,0:T(8,128)}, f32[16,32,128]{2,1,0:T(8,128)}) custom-call(f32[16,16]{1,0:T(8,128)} %constant.18.clone.cos_ref, f32[16,16]{1,0:T(8,128)} %constant.19.clone.sin_ref, f32[16,32,128]{2,1,0:T(8,128)} %copy-done, f32[16,32,32,128]{3,2,1,0:T(8,128)} %fold_weights.1.weights_ref), custom_call_target="tpu_custom_call" | custom-call | flops 20000000 | bytes 9437184 | tf_op jit(solution)/shard_map/mix_modes/pallas_call | solution.py:290
  35.1 5.8 %all-to-all-start.1 = ((f32[16,32,128]{2,1,0:T(8,128)}), f32[16,32,128]{2,1,0:T(8,128)S(1)}, u32[]{:S(2)}, u32[]{:S(2)}) async-start(f32[16,32,128]{2,1,0:T(8,128)} %get-tuple-element.18), calls=%async_computation.1 | async-start | bytes 524288 | tf_op jit(solution)/shard_map/all_to_all | solution.py:530
  41.0 0.0 copy-done.2
  41.0 0.7 copy.19
  41.7 0.0 copy-done.3
  41.7 0.7 copy.20.bias_in_ref
  42.4 8.7 %pointwise.1.pre_ref = f32[32,128,256]{2,1,0:T(8,128)} custom-call(f32[256,32]{1,0:T(8,128)} %constant.20.clone.sum_ref, f32[32,32]{1,0:T(8,128)} %bitcast.23, f32[32,1]{1,0:T(8,128)} %copy.20.bias_in_ref, f32[32,128,256]{2,1,0:T(8,128)} %bitcast.18), custom_call_target="tpu_custom_call" | custom-call | flops 4000000000 | bytes 25165824 | tf_op jit(solution)/shard_map/pointwise/pallas_call | solution.py:352
  51.0 0.0 all-to-all-done.1
  51.0 0.0 copy-start.1
  51.0 0.7 copy-done.1
  51.7 12.7 %cells.1 = (bf16[32,128,256]{2,1,0:T(8,128)(2,1)}, f32[768,128]{1,0:T(8,128)}) custom-call(bf16[128,192]{1,0:T(8,128)(2,1)} %constant.24.clone.inv_y, bf16[256,512]{1,0:T(8,128)(2,1)} %constant.25.clone.inv_z, bf16[128,512]{1,0:T(8,128)(2,1)} %constant.26.clone.inv_z_low, bf16[512,256]{1,0:T(8,128)(2,1)} %constant.21.clone.z_high, ...), custom_call_target="tpu_custom_call" | custom-call | flops 8000000000 | bytes 12582912 | tf_op jit(solution)/shard_map/cells/pallas_call | solution.py:431
  64.5 18.3 %all_to_all.15.lines_ref = f32[16,48,128]{2,1,0:T(8,128)} all-to-all(f32[16,48,128]{2,1,0:T(8,128)} %bitcast.20), channel_id=1, replica_groups=mesh['groups'=2,'space'=16] {'space'}, dimensions={0} | all-to-all | bytes 786432 | tf_op jit(solution)/shard_map/all_to_all | solution.py:530
  82.8 15.4 %weight_gradient.1 = (f32[2,32,32,32,64]{4,3,2,1,0:T(8,128)}, f32[32,32]{1,0:T(8,128)}, f32[1,32]{1,0:T(1,128)}) custom-call(f32[16,16]{1,0:T(8,128)} %constant.18.clone.cos_ref, f32[16,16]{1,0:T(8,128)} %constant.19.clone.sin_ref, f32[16,32,128]{2,1,0:T(8,128)} %get-tuple-element.21.spec_ref, f32[16,48,128]{2,1,0:T(8,128)} %all_to_all.15.lines_ref), custom_call_target="tpu_custom_call" | custom-call | flops 10000000 | bytes 41943040 | tf_op jit(solution)/shard_map/weight_gradient/pallas_call | solution.py:507
Async XLA Ops:
  11.1 17.4 %all-to-all-start = ((f32[16,32,128]{2,1,0:T(8,128)}), f32[16,32,128]{2,1,0:T(8,128)S(1)}, u32[]{:S(2)}, u32[]{:S(2)}) async-start(f32[16,32,128]{2,1,0:T(8,128)} %bitcast.22), calls=%async_computation | async-start | bytes 524288 | tf_op jit(solution)/shard_map/all_to_all | solution.py:530
  28.4 12.6 %copy-start.2 = (f32[32,32]{1,0:T(8,128)S(1)}, f32[32,32]{1,0:T(8,128)}, u32[]{:S(2)}) copy-start(f32[32,32]{1,0:T(8,128)} %param.17) | copy-start | bytes 12292
  28.4 13.3 %copy-start.3 = (f32[32]{0:T(128)S(1)}, f32[32]{0:T(128)}, u32[]{:S(2)}) copy-start(f32[32]{0:T(128)} %param.18) | copy-start | bytes 388
  28.6 0.7 copy-start
  35.1 15.9 %all-to-all-start.1 = ((f32[16,32,128]{2,1,0:T(8,128)}), f32[16,32,128]{2,1,0:T(8,128)S(1)}, u32[]{:S(2)}, u32[]{:S(2)}) async-start(f32[16,32,128]{2,1,0:T(8,128)} %get-tuple-element.18), calls=%async_computation.1 | async-start | bytes 524288 | tf_op jit(solution)/shard_map/all_to_all | solution.py:530
  51.0 0.7 copy-start.1

commit v3 on v2

--- a/solution.py
+++ b/solution.py
@@ -240,7 +240,8 @@
 
 
 def mix_kernel(
-    cos_ref, sin_ref, lines_ref, weights_ref, spec_ref, out_ref, sums_ref, total_ref, real_ref, imag_ref,
+    core_ref, cos_ref, sin_ref, near_ref, far_ref, weights_ref, spec_ref, out_ref,
+    lines_ref, sums_ref, total_ref, real_ref, imag_ref,
     *, points, channels, per_step, norm,
 ):
     step = pl.program_id(0)
@@ -248,6 +249,7 @@
 
     @pl.when(step == 0)
     def _():
+        join(core_ref[0], near_ref, far_ref, lines_ref)
         halve_lines(lines_ref, sums_ref, points, channels)
         total_ref[...] = jnp.zeros_like(total_ref)
 
@@ -282,8 +284,10 @@
     return pl.BlockSpec(memory_space=pltpu.SMEM)
 
 
-def mix(cos_x, sin_x, lines, weights, norm):
-    points, channels, _ = lines.shape
+def mix(core, cos_x, sin_x, lines, weights, norm):
+    near, far = lines
+    chips, cores, channels, _ = near.shape
+    points = chips * cores
     unique = weights.shape[0]
     per_step = min(unique, 4)
     shape = (points, channels, LANES)
@@ -293,7 +297,9 @@
         in_specs=[
             smem(),
             smem(),
-            full(shape),
+            smem(),
+            full(near.shape),
+            full(far.shape),
             pl.BlockSpec((per_step,) + weights.shape[1:], lambda s: (s, 0, 0, 0)),
         ],
         out_specs=[
@@ -305,6 +311,7 @@
             jax.ShapeDtypeStruct(shape, F32),
         ],
         scratch_shapes=[
+            pltpu.VMEM(shape, F32),
             pltpu.VMEM((2, 2, points // 2, channels, LANES), F32),
             pltpu.VMEM((2, points // 2, channels, LANES), F32),
             pltpu.VMEM((per_step, channels, LANES), F32),
@@ -313,7 +320,7 @@
         compiler_params=params(60),
         cost_estimate=pl.CostEstimate(flops=2 * 10**7, bytes_accessed=9 * MIB, transcendentals=0),
         name="mix_modes",
-    )(cos_x, sin_x, lines, weights)
+    )(core, cos_x, sin_x, near, far, weights)
 
 
 def exact_dot(left, right):
@@ -363,8 +370,8 @@
 
 
 def cell_kernel(
-    inv_y, inv_z, inv_z_low, z_high, z_low, y_both, sum_ref, modes_ref, pre_ref, cot_ref, field_hbm,
-    act_ref, out_ref, field_ref, slope_ref, sem, *, channels, step_channels, rows, owners,
+    core_ref, inv_y, inv_z, inv_z_low, z_high, z_low, y_both, sum_ref, near_ref, far_ref, pre_ref, cot_ref, field_hbm,
+    act_ref, out_ref, field_ref, slope_ref, lines_ref, sem, *, channels, step_channels, rows, owners,
 ):
     step = pl.program_id(0)
     copy = pltpu.make_async_copy(field_hbm, field_ref, sem)
@@ -372,7 +379,9 @@
     @pl.when(step == 0)
     def _():
         copy.start()
-
+        join(core_ref[0], near_ref, far_ref, lines_ref)
+
+    modes_ref = lines_ref.reshape(owners * channels, LANES)
     first = step * step_channels
     lines = []
     for g in range(0, step_channels, GROUP):
@@ -421,18 +430,20 @@
             out_ref[d * rows + channels + 8 : (d + 1) * rows, :] = extra
 
 
-def cell_stage(inverse, forward, summing, modes, pre, cotangent, field):
+def cell_stage(core, inverse, forward, summing, modes, pre, cotangent, field):
     channels = field.shape[0]
     owners = MY // 2
     rows = channels + 16
     step_channels = STEP
+    near, far = modes
     block = pl.BlockSpec((step_channels, NY, NZ), lambda s: (s, 0, 0))
     tables = (*inverse, *forward, summing)
     act, out = pl.pallas_call(
         functools.partial(cell_kernel, channels=channels, step_channels=step_channels, rows=rows, owners=owners),
         grid=(channels // step_channels,),
-        in_specs=[full(t.shape) for t in tables]
-        + [full((owners * channels, LANES)), block, block, pl.BlockSpec(memory_space=pl.ANY)],
+        in_specs=[smem()]
+        + [full(t.shape) for t in tables]
+        + [full(near.shape), full(far.shape), block, block, pl.BlockSpec(memory_space=pl.ANY)],
         out_specs=[block, full((owners * rows, LANES))],
         out_shape=[
             jax.ShapeDtypeStruct((channels, NY, NZ), BF16),
@@ -441,19 +452,21 @@
         scratch_shapes=[
             pltpu.VMEM((channels, NY, NZ), F32),
             pltpu.VMEM((channels, NY, NZ), F32),
+            pltpu.VMEM((owners, channels, LANES), F32),
             pltpu.SemaphoreType.DMA,
         ],
         compiler_params=params(60),
         cost_estimate=pl.CostEstimate(flops=8 * 10**9, bytes_accessed=12 * MIB, transcendentals=2 * 10**6),
         name="cells",
-    )(*tables, modes.reshape(owners * channels, LANES), pre, cotangent, field)
+    )(core, *tables, near, far, pre, cotangent, field)
     return act, out.reshape(owners, rows, LANES)
 
 
 def gradient_kernel(
-    cos_ref, sin_ref, spec_ref, lines_ref, out_hbm, point_ref, bias_ref,
-    sums_ref, real_ref, imag_ref, buffer, sems, *, points, channels, unique, copies, norm,
+    core_ref, cos_ref, sin_ref, spec_ref, near_ref, far_ref, out_hbm, point_ref, bias_ref,
+    lines_ref, sums_ref, real_ref, imag_ref, buffer, sems, *, points, channels, unique, copies, norm,
 ):
+    join(core_ref[0], near_ref, far_ref, lines_ref)
     halve_lines(lines_ref, sums_ref, points, channels)
     half = LANES // 2
     lane = lane_index((channels, LANES))
@@ -498,15 +511,17 @@
             copy.wait()
 
 
-def gradient(cos_x, sin_x, spectrum, lines, norm, kept_x):
-    points, rows, _ = lines.shape
+def gradient(core, cos_x, sin_x, spectrum, lines, norm, kept_x):
+    near, far = lines
+    chips, cores, rows, _ = near.shape
+    points = chips * cores
     unique, channels, _ = spectrum.shape
     half = LANES // 2
     copies = kept_x // unique
     flat = (channels, LANES)
     return pl.pallas_call(
         functools.partial(gradient_kernel, points=points, channels=channels, unique=unique, copies=copies, norm=norm),
-        in_specs=[smem(), smem(), full(spectrum.shape), full(lines.shape)],
+        in_specs=[smem(), smem(), smem(), full(spectrum.shape), full(near.shape), full(far.shape)],
         out_specs=[pl.BlockSpec(memory_space=pl.ANY), full((channels, channels)), full((1, channels))],
         out_shape=[
             jax.ShapeDtypeStruct((2, kept_x, channels, channels, half), F32),
@@ -514,6 +529,7 @@
             jax.ShapeDtypeStruct((1, channels), F32),
         ],
         scratch_shapes=[
+            pltpu.VMEM((points, rows, LANES), F32),
             pltpu.VMEM((2, 2, points // 2, channels, LANES), F32),
             pltpu.VMEM((2,) + flat, F32),
             pltpu.VMEM((2,) + flat, F32),
@@ -523,11 +539,29 @@
         compiler_params=params(60),
         cost_estimate=pl.CostEstimate(flops=10**7, bytes_accessed=40 * MIB, transcendentals=0),
         name="weight_gradient",
-    )(cos_x, sin_x, spectrum, lines)
-
-
-def swap(lines):
-    return lax.all_to_all(lines, "space", split_axis=0, concat_axis=0, tiled=True)
+    )(core, cos_x, sin_x, spectrum, near, far)
+
+
+CORES = 2
+
+
+def swap(lines, core):
+    devices, rows, lanes = lines.shape
+    chips = devices // CORES
+    groups = [[p * CORES + q for p in range(chips)] for q in range(CORES)]
+    near = lax.all_to_all(
+        lines.reshape(chips, CORES * rows, lanes), "space", split_axis=0, concat_axis=0, tiled=True, axis_index_groups=groups
+    ).reshape(chips, CORES, rows, lanes)
+    give = lax.dynamic_index_in_dim(near, 1 - core, axis=1, keepdims=False)
+    far = lax.ppermute(give, "space", [(d, d ^ 1) for d in range(devices)])
+    return near, far
+
+
+def join(core, near_ref, far_ref, lines_ref):
+    chips, _, rows, _ = near_ref.shape
+    for p in range(chips):
+        lines_ref[CORES * p + core] = near_ref[p, core]
+        lines_ref[CORES * p + 1 - core] = far_ref[p]
 
 
 def suits(width_x, length_x, devices, channels, weights):
@@ -552,6 +586,7 @@
     if not suits(width_x, length_x, devices, channels, spectral_weights):
         return general_body(lifted_field, cotangent, spectral_weights, point_weights, point_bias)
     norm = float(length_x * NY * NZ) ** -0.5
+    core = lax.axis_index("space") % CORES
     theta = angles(np.arange(length_x), np.arange(length_x), length_x)
     cos_x, sin_x = jnp.asarray(np.cos(theta), F32), jnp.asarray(np.sin(theta), F32)
     forward = forward_tables()
@@ -563,15 +598,15 @@
     weights = jnp.transpose(spectral_weights, (0, 1, 3, 4, 2))
 
     lines, half = forward_modes(field, forward, weights, length_x)
-    lines = swap(lines)
+    lines = swap(lines, core)
     folded = fold_rest(weights, half, length_x)
-    spectrum, mixed = mix(cos_x, sin_x, lines, folded, norm)
+    spectrum, mixed = mix(core[None], cos_x, sin_x, lines, folded, norm)
     field_late, mixed = lax.optimization_barrier((field, mixed))
-    modes = swap(mixed)
+    modes = swap(mixed, core)
     pre = pointwise(field_late, summing, point_weights, point_bias)
-    activated, slope_lines = cell_stage(inverse, forward, summing, modes, pre, slopes_in, field)
-    slope_lines = swap(slope_lines)
-    grad, grad_point, grad_bias = gradient(cos_x, sin_x, spectrum, slope_lines, norm, MX)
+    activated, slope_lines = cell_stage(core[None], inverse, forward, summing, modes, pre, slopes_in, field)
+    slope_lines = swap(slope_lines, core)
+    grad, grad_point, grad_bias = gradient(core[None], cos_x, sin_x, spectrum, slope_lines, norm, MX)
     return (
         activated.reshape(cotangent.shape),
         jnp.transpose(grad, (0, 1, 4, 2, 3)),

time: 98.9 us -> 114 us (1.15)
  waiting for transfers between devices: 0.17 us -> 18.6 us
  starting transfers between devices: 13.2 us -> 11.1 us
  blocking collectives: 18.3 us -> 16.3 us
    all_to_all x2, waiting for transfers between devices: 0.17 us -> 17.1 us  [swap(): lax.all_to_all(lines.reshape(chips, CORES * rows, lanes), 'space', split_...]
    all_to_all x2, starting transfers between devices: 13.2 us -> 10.9 us  [swap(): lax.all_to_all(lines.reshape(chips, CORES * rows, lanes), 'space', split_...]
    all_to_all x1, blocking collectives: 18.3 us -> 16.3 us  [swap(): lax.all_to_all(lines.reshape(chips, CORES * rows, lanes), 'space', split_...]
    ppermute x0 -> x3, waiting for transfers between devices: none -> 1.43 us  [swap(): far = lax.ppermute(give, 'space', [(d, d ^ 1) for d in range(devices)])]
    unnamed x9 -> x17, local copies, waits for them, and re-layouts: 2.08 us -> 2.67 us
  transfers between devices with their start and end apart: 2 -> 5, of which waited for: 1 -> 3; matrix products, arithmetic and copies ran while one was open for 1% -> 1% of each run, Pallas kernels for 19% -> 16%
where the time goes in v3:
time: 114 us; the launch traced here: 113 us
  Pallas kernels  63.3 us (56%)
  waiting for transfers between devices  18.6 us (16%)
  blocking collectives  16.3 us (14%)
  starting transfers between devices  11.1 us (10%)
  local copies, waits for them, and re-layouts  3.39 us (3%)
    all_to_all x2, waiting for transfers between devices, swap(): lax.all_to_all(lines.reshape(chips, CORES * rows, lanes), 'space', split_...  17.1 us
    all_to_all x1, blocking collectives, swap(): lax.all_to_all(lines.reshape(chips, CORES * rows, lanes), 'space', split_...  16.3 us
    pallas_call x1, Pallas kernels, gradient(): pl.pallas_call(functools.partial(gradient_kernel, points=points, channels...  15.5 us
    pallas_call x1, Pallas kernels, cell_stage(): pl.pallas_call(functools.partial(cell_kernel, channels=channels, step_cha...  12.8 us
    all_to_all x2, starting transfers between devices, swap(): lax.all_to_all(lines.reshape(chips, CORES * rows, lanes), 'space', split_...  10.9 us
    pallas_call x1, Pallas kernels, forward_modes(): pl.pallas_call(functools.partial(forward_kernel, channels=channels, step_...  10.5 us
    pallas_call x1, Pallas kernels, fold_rest(): pl.pallas_call(fold_kernel, grid=(unique - first,), in_specs=pieces + [pl...  9.87 us
    pallas_call x1, Pallas kernels, pointwise(): pl.pallas_call(functools.partial(pointwise_kernel, channels=channels, blo...  8.7 us
  transfers between devices with their start and end apart: 5, of which 3 were waited for; matrix products, arithmetic and copies ran while one was open for 1% of the time, Pallas kernels for 16%

profile of v3, /device:TPU:0, one launch (start us, length us, event | category | flops | bytes accessed | tf_op | source)
XLA Modules:
  0.0 113.3 jit_solution(11380225113806112092)
XLA Ops:
  0.6 10.5 %forward_yz.1 = (f32[512,128]{1,0:T(8,128)}, f32[16,32,32,128]{3,2,1,0:T(8,128)}) custom-call(bf16[512,256]{1,0:T(8,128)(2,1)} %constant.51.clone.z_high, bf16[512,256]{1,0:T(8,128)(2,1)} %constant.52.clone.z_low, bf16[64,256]{1,0:T(8,128)(2,1)} %constant.53.clone.y_both, f32[32,128,256]{2,1,0:T(8,128)} %bitcast.27, f32[2,32,32,32,64]{4,3,2,1,0:T(8,128)} %bitcast.23, ...), custom_call_target="tpu_custom_call" | custom-call | flops 2000000000 | bytes 27262976 | tf_op jit(solution)/shard_map/forward_yz/pallas_call | solution.py:183
  11.1 7.3 %all-to-all-start = ((f32[8,64,128]{2,1,0:T(8,128)}), f32[8,64,128]{2,1,0:T(8,128)S(1)}, u32[]{:S(2)}, u32[]{:S(2)}) async-start(f32[8,64,128]{2,1,0:T(8,128)} %bitcast.37), calls=%async_computation | async-start | bytes 524288 | tf_op jit(solution)/shard_map/all_to_all | solution.py:552
  18.4 8.9 %all-to-all-done = f32[8,64,128]{2,1,0:T(8,128)S(1)} async-done(((f32[8,64,128]{2,1,0:T(8,128)}), f32[8,64,128]{2,1,0:T(8,128)S(1)}, u32[]{:S(2)}, u32[]{:S(2)}) %all-to-all-start) | async-done | bytes 262176 | tf_op jit(solution)/shard_map/all_to_all | solution.py:552
  27.3 0.0 copy-start.1
  27.3 0.1 collective-permute-start
  27.4 9.9 %fold_weights.1.weights_ref = f32[16,32,32,128]{3,2,1,0:T(8,128)} custom-call(f32[2,32,32,32,64]{4,3,2,1,0:T(8,128)} %bitcast.25, f32[2,32,32,32,64]{4,3,2,1,0:T(8,128)} %bitcast.26, f32[16,32,32,128]{3,2,1,0:T(8,128)} %get-tuple-element.16.refs_2_), custom_call_target="tpu_custom_call", output_to_operand_aliasing={{}: (2, {})} | custom-call | flops 4000000 | bytes 20971520 | tf_op jit(solution)/shard_map/fold_weights/pallas_call | solution.py:206
  37.3 0.0 copy-done.1
  37.3 0.0 copy-start.5
  37.3 0.0 copy-start.6
  37.3 0.0 collective-permute-done.far_ref
  37.3 0.0 copy-start.4
  37.3 0.6 copy-done.4
  38.0 5.9 %mix_modes.1 = (f32[16,32,128]{2,1,0:T(8,128)}, f32[16,32,128]{2,1,0:T(8,128)}) custom-call(s32[1]{0:T(128)} %bitcast.core_ref, f32[16,16]{1,0:T(8,128)} %constant.48.clone.cos_ref, f32[16,16]{1,0:T(8,128)} %constant.49.clone.sin_ref, f32[8,2,32,128]{3,2,1,0:T(8,128)} %bitcast.33, f32[8,32,128]{2,1,0:T(8,128)} %copy-done.4, ...), custom_call_target="tpu_custom_call" | custom-call | flops 20000000 | bytes 9437184 | tf_op jit(solution)/shard_map/mix_modes/pallas_call | solution.py:294
  43.9 3.6 %all-to-all-start.1 = ((f32[8,64,128]{2,1,0:T(8,128)}), f32[8,64,128]{2,1,0:T(8,128)S(1)}, u32[]{:S(2)}, u32[]{:S(2)}) async-start(f32[8,64,128]{2,1,0:T(8,128)} %bitcast.38), calls=%async_computation.1 | async-start | bytes 524288 | tf_op jit(solution)/shard_map/all_to_all | solution.py:552
  47.5 0.0 copy-done.5
  47.5 0.7 copy.19
  48.2 0.0 copy-done.6
  48.2 0.7 copy.20.bias_in_ref
  48.9 8.2 %all-to-all-done.1 = f32[8,64,128]{2,1,0:T(8,128)S(1)} async-done(((f32[8,64,128]{2,1,0:T(8,128)}), f32[8,64,128]{2,1,0:T(8,128)S(1)}, u32[]{:S(2)}, u32[]{:S(2)}) %all-to-all-start.1) | async-done | bytes 262176 | tf_op jit(solution)/shard_map/all_to_all | solution.py:552
  57.1 0.0 copy-start.2
  57.1 0.1 collective-permute-start.1
  57.2 8.7 %pointwise.1.pre_ref = f32[32,128,256]{2,1,0:T(8,128)} custom-call(f32[256,32]{1,0:T(8,128)} %constant.50.clone.sum_ref, f32[32,32]{1,0:T(8,128)} %bitcast.39, f32[32,1]{1,0:T(8,128)} %copy.20.bias_in_ref, f32[32,128,256]{2,1,0:T(8,128)} %bitcast.28), custom_call_target="tpu_custom_call" | custom-call | flops 4000000000 | bytes 25165824 | tf_op jit(solution)/shard_map/pointwise/pallas_call | solution.py:359
  65.9 0.0 collective-permute-done.1.far_ref
  65.9 0.0 copy-start.7
  65.9 0.0 copy-done.2
  65.9 0.6 copy-done.7
  66.5 12.8 %cells.1 = (bf16[32,128,256]{2,1,0:T(8,128)(2,1)}, f32[768,128]{1,0:T(8,128)}) custom-call(s32[1]{0:T(128)} %bitcast.core_ref, bf16[128,192]{1,0:T(8,128)(2,1)} %constant.54.clone.inv_y, bf16[256,512]{1,0:T(8,128)(2,1)} %constant.55.clone.inv_z, bf16[128,512]{1,0:T(8,128)(2,1)} %constant.56.clone.inv_z_low, bf16[512,256]{1,0:T(8,128)(2,1)} %constant.51.clone.z_high, ...), custom_call_target="tpu_custom_call" | custom-call | flops 8000000000 | bytes 12582912 | tf_op jit(solution)/shard_map/cells/pallas_call | solution.py:441
  79.4 16.3 %all_to_all.15 = f32[8,96,128]{2,1,0:T(8,128)S(1)} all-to-all(f32[8,96,128]{2,1,0:T(8,128)} %bitcast.36), channel_id=1, replica_groups={{0,2,4,6,8,10,12,14},{1,3,5,7,9,11,13,15},{16,18,20,22,24,26,28,30},{17..., dimensions={0} | all-to-all | bytes 786432 | tf_op jit(solution)/shard_map/all_to_all | solution.py:552
  95.7 0.0 copy-start
  95.7 0.1 collective-permute-start.2
  95.8 1.4 %collective-permute-done.2.far_ref = f32[8,48,128]{2,1,0:T(8,128)S(1)} collective-permute-done((f32[8,48,128]{2,1,0:T(8,128)S(1)}, f32[8,48,128]{2,1,0:T(8,128)S(1)}, u32[]{:S(2)}, u32[]{:S(2)}) %collective-permute-start.2) | collective-permute-done | bytes 196640 | tf_op jit(solution)/shard_map/ppermute | solution.py:556
  97.2 0.0 copy-start.3
  97.2 0.0 copy-done
  97.2 0.7 copy-done.3
  97.9 15.5 %weight_gradient.1 = (f32[2,32,32,32,64]{4,3,2,1,0:T(8,128)}, f32[32,32]{1,0:T(8,128)}, f32[1,32]{1,0:T(1,128)}) custom-call(s32[1]{0:T(128)} %bitcast.core_ref, f32[16,16]{1,0:T(8,128)} %constant.48.clone.cos_ref, f32[16,16]{1,0:T(8,128)} %constant.49.clone.sin_ref, f32[16,32,128]{2,1,0:T(8,128)} %get-tuple-element.21.spec_ref, f32[8,2,48,128]{3,2,1,0:T(8,128)} %bitcast.31, ...), custom_call_target="tpu_custom_call" | custom-call | flops 10000000 | bytes 41943040 | tf_op jit(solution)/shard_map/weight_gradient/pallas_call | solution.py:522
  (3 shorter events, 0.0 us)
Async XLA Ops:
  11.1 16.2 %all-to-all-start = ((f32[8,64,128]{2,1,0:T(8,128)}), f32[8,64,128]{2,1,0:T(8,128)S(1)}, u32[]{:S(2)}, u32[]{:S(2)}) async-start(f32[8,64,128]{2,1,0:T(8,128)} %bitcast.37), calls=%async_computation | async-start | bytes 524288 | tf_op jit(solution)/shard_map/all_to_all | solution.py:552
  27.3 10.0 %copy-start.1 = (f32[8,64,128]{2,1,0:T(8,128)}, f32[8,64,128]{2,1,0:T(8,128)S(1)}, u32[]{:S(2)}) copy-start(f32[8,64,128]{2,1,0:T(8,128)S(1)} %all-to-all-done) | copy-start | bytes 786436
  27.3 10.0 %collective-permute-start = (f32[8,32,128]{2,1,0:T(8,128)S(1)}, f32[8,32,128]{2,1,0:T(8,128)S(1)}, u32[]{:S(2)}, u32[]{:S(2)}) collective-permute-start(f32[8,32,128]{2,1,0:T(8,128)S(1)} %dynamic-slice_bitcast_fusion.2), channel_id=1, source_target_pairs={{0,1},{1,0},{2,3},{3,2},{4,5},{5,4},{6,7},{7,6},{8,9},{9,8},{10,11... | collective-permute-start | bytes 393224 | tf_op jit(solution)/shard_map/ppermute | solution.py:556
  37.3 10.2 %copy-start.5 = (f32[32,32]{1,0:T(8,128)S(1)}, f32[32,32]{1,0:T(8,128)}, u32[]{:S(2)}) copy-start(f32[32,32]{1,0:T(8,128)} %param.17) | copy-start | bytes 12292
  37.3 10.9 %copy-start.6 = (f32[32]{0:T(128)S(1)}, f32[32]{0:T(128)}, u32[]{:S(2)}) copy-start(f32[32]{0:T(128)} %param.18) | copy-start | bytes 388
  37.3 0.6 copy-start.4
  43.9 13.2 %all-to-all-start.1 = ((f32[8,64,128]{2,1,0:T(8,128)}), f32[8,64,128]{2,1,0:T(8,128)S(1)}, u32[]{:S(2)}, u32[]{:S(2)}) async-start(f32[8,64,128]{2,1,0:T(8,128)} %bitcast.38), calls=%async_computation.1 | async-start | bytes 524288 | tf_op jit(solution)/shard_map/all_to_all | solution.py:552
  57.1 8.8 %copy-start.2 = (f32[8,64,128]{2,1,0:T(8,128)}, f32[8,64,128]{2,1,0:T(8,128)S(1)}, u32[]{:S(2)}) copy-start(f32[8,64,128]{2,1,0:T(8,128)S(1)} %all-to-all-done.1) | copy-start | bytes 786436
  57.1 8.8 %collective-permute-start.1 = (f32[8,32,128]{2,1,0:T(8,128)S(1)}, f32[8,32,128]{2,1,0:T(8,128)S(1)}, u32[]{:S(2)}, u32[]{:S(2)}) collective-permute-start(f32[8,32,128]{2,1,0:T(8,128)S(1)} %dynamic-slice_bitcast_fusion.1), channel_id=1, source_target_pairs={{0,1},{1,0},{2,3},{3,2},{4,5},{5,4},{6,7},{7,6},{8,9},{9,8},{10,11... | collective-permute-start | bytes 393224 | tf_op jit(solution)/shard_map/ppermute | solution.py:556
  65.9 0.7 copy-start.7
  95.7 1.5 %copy-start = (f32[8,96,128]{2,1,0:T(8,128)}, f32[8,96,128]{2,1,0:T(8,128)S(1)}, u32[]{:S(2)}) copy-start(f32[8,96,128]{2,1,0:T(8,128)S(1)} %all_to_all.15) | copy-start | bytes 1179652
  95.7 1.5 %collective-permute-start.2 = (f32[8,48,128]{2,1,0:T(8,128)S(1)}, f32[8,48,128]{2,1,0:T(8,128)S(1)}, u32[]{:S(2)}, u32[]{:S(2)}) collective-permute-start(f32[8,48,128]{2,1,0:T(8,128)S(1)} %dynamic-slice_bitcast_fusion), channel_id=1, source_target_pairs={{0,1},{1,0},{2,3},{3,2},{4,5},{5,4},{6,7},{7,6},{8,9},{9,8},{10,11... | collective-permute-start | bytes 589832 | tf_op jit(solution)/shard_map/ppermute | solution.py:556
  97.2 0.7 copy-start.3

commit v4 on v2

--- a/solution.py
+++ b/solution.py
@@ -136,6 +136,15 @@
     return [lines[:, q * LANES : (q + 1) * LANES] for q in range(GROUP // 2)]
 
 
+def join(me, piece_refs, lines_ref):
+    for s, piece in enumerate(piece_refs):
+        lines_ref[me ^ s] = piece[...]
+
+
+def part(me, s, lines_ref, rows):
+    return lines_ref[pl.ds(pl.multiple_of((me ^ s) * rows, 8), rows), :]
+
+
 def full(shape):
     return pl.BlockSpec(shape, lambda *_: (0,) * len(shape))
 
@@ -164,35 +173,44 @@
     return pieces, out, jax.ShapeDtypeStruct(shape, F32)
 
 
-def forward_kernel(z_high, z_low, y_both, field_ref, *refs, channels, step_channels, per_step):
-    *pieces, out_ref, folded_ref = refs
+def forward_kernel(me_ref, z_high, z_low, y_both, field_ref, *refs, channels, step_channels, per_step, copies):
+    pieces, (folded_ref, *out_refs, out_ref) = refs[:copies], refs[copies:]
     step = pl.program_id(0)
     for at in range(per_step):
         fold_block(pieces, folded_ref, at)
     fields = [field_ref[q] for q in range(step_channels)]
     forward_group(fields, z_high[...], z_low[...], y_both[...], out_ref, step * step_channels, channels)
 
-
-def forward_modes(field, tables, weights, unique):
+    @pl.when(step == pl.num_programs(0) - 1)
+    def _():
+        for s, ref in enumerate(out_refs):
+            ref[...] = part(me_ref[0], s, out_ref, channels)
+
+
+def forward_modes(me, field, tables, weights, unique):
     channels = field.shape[0]
     step_channels = 8
     steps = channels // step_channels
     per_step = unique // 2 // steps
     pieces, folded, folded_shape = fold_specs(weights, unique, per_step, 0)
     owners = MY // 2
-    out, half = pl.pallas_call(
-        functools.partial(forward_kernel, channels=channels, step_channels=step_channels, per_step=per_step),
+    half, *out = pl.pallas_call(
+        functools.partial(
+            forward_kernel, channels=channels, step_channels=step_channels, per_step=per_step, copies=len(pieces)
+        ),
         grid=(steps,),
-        in_specs=[full(t.shape) for t in tables]
+        in_specs=[smem()]
+        + [full(t.shape) for t in tables]
         + [pl.BlockSpec((step_channels, NY, NZ), lambda s: (s, 0, 0))]
         + pieces,
-        out_specs=[full((owners * channels, LANES)), folded],
-        out_shape=[jax.ShapeDtypeStruct((owners * channels, LANES), F32), folded_shape],
+        out_specs=[folded] + [full((channels, LANES))] * owners,
+        out_shape=[folded_shape] + [jax.ShapeDtypeStruct((channels, LANES), F32)] * owners,
+        scratch_shapes=[pltpu.VMEM((owners * channels, LANES), F32)],
         compiler_params=params(60),
         cost_estimate=pl.CostEstimate(flops=2 * 10**9, bytes_accessed=26 * MIB, transcendentals=0),
         name="forward_yz",
-    )(*tables, field, *([weights] * len(pieces)))
-    return out.reshape(owners, channels, LANES), half
+    )(me, *tables, field, *([weights] * len(pieces)))
+    return out, half
 
 
 def fold_kernel(*refs):
@@ -240,14 +258,16 @@
 
 
 def mix_kernel(
-    cos_ref, sin_ref, lines_ref, weights_ref, spec_ref, out_ref, sums_ref, total_ref, real_ref, imag_ref,
-    *, points, channels, per_step, norm,
+    me_ref, cos_ref, sin_ref, weights_ref, *refs, points, channels, per_step, norm,
 ):
+    piece_refs, spec_ref, out_refs = refs[:points], refs[points], refs[points + 1 : 2 * points + 1]
+    lines_ref, sums_ref, total_ref, real_ref, imag_ref = refs[2 * points + 1 :]
     step = pl.program_id(0)
     half = points // 2
 
     @pl.when(step == 0)
     def _():
+        join(me_ref[0], piece_refs, lines_ref)
         halve_lines(lines_ref, sums_ref, points, channels)
         total_ref[...] = jnp.zeros_like(total_ref)
 
@@ -274,46 +294,41 @@
     @pl.when(step == pl.num_programs(0) - 1)
     def _():
         for x in range(half):
-            out_ref[x] = total_ref[0, x] + total_ref[1, x]
-            out_ref[x + half] = total_ref[0, x] - total_ref[1, x]
+            lines_ref[x] = total_ref[0, x] + total_ref[1, x]
+            lines_ref[x + half] = total_ref[0, x] - total_ref[1, x]
+        for s, ref in enumerate(out_refs):
+            ref[...] = lines_ref[me_ref[0] ^ s]
 
 
 def smem():
     return pl.BlockSpec(memory_space=pltpu.SMEM)
 
 
-def mix(cos_x, sin_x, lines, weights, norm):
-    points, channels, _ = lines.shape
+def mix(me, cos_x, sin_x, pieces, weights, norm):
+    points = len(pieces)
+    channels = pieces[0].shape[0]
     unique = weights.shape[0]
     per_step = min(unique, 4)
-    shape = (points, channels, LANES)
-    return pl.pallas_call(
+    flat = (channels, LANES)
+    spectrum, *out = pl.pallas_call(
         functools.partial(mix_kernel, points=points, channels=channels, per_step=per_step, norm=norm),
         grid=(unique // per_step,),
-        in_specs=[
-            smem(),
-            smem(),
-            full(shape),
-            pl.BlockSpec((per_step,) + weights.shape[1:], lambda s: (s, 0, 0, 0)),
-        ],
-        out_specs=[
-            pl.BlockSpec((per_step, channels, LANES), lambda s: (s, 0, 0)),
-            full(shape),
-        ],
-        out_shape=[
-            jax.ShapeDtypeStruct((unique, channels, LANES), F32),
-            jax.ShapeDtypeStruct(shape, F32),
-        ],
+        in_specs=[smem(), smem(), smem(), pl.BlockSpec((per_step,) + weights.shape[1:], lambda s: (s, 0, 0, 0))]
+        + [full(flat)] * points,
+        out_specs=[pl.BlockSpec((per_step,) + flat, lambda s: (s, 0, 0))] + [full(flat)] * points,
+        out_shape=[jax.ShapeDtypeStruct((unique,) + flat, F32)] + [jax.ShapeDtypeStruct(flat, F32)] * points,
         scratch_shapes=[
-            pltpu.VMEM((2, 2, points // 2, channels, LANES), F32),
-            pltpu.VMEM((2, points // 2, channels, LANES), F32),
-            pltpu.VMEM((per_step, channels, LANES), F32),
-            pltpu.VMEM((per_step, channels, LANES), F32),
+            pltpu.VMEM((points,) + flat, F32),
+            pltpu.VMEM((2, 2, points // 2) + flat, F32),
+            pltpu.VMEM((2, points // 2) + flat, F32),
+            pltpu.VMEM((per_step,) + flat, F32),
+            pltpu.VMEM((per_step,) + flat, F32),
         ],
         compiler_params=params(60),
         cost_estimate=pl.CostEstimate(flops=2 * 10**7, bytes_accessed=9 * MIB, transcendentals=0),
         name="mix_modes",
-    )(cos_x, sin_x, lines, weights)
+    )(me, cos_x, sin_x, weights, *pieces)
+    return spectrum, out
 
 
 def exact_dot(left, right):
@@ -363,16 +378,20 @@
 
 
 def cell_kernel(
-    inv_y, inv_z, inv_z_low, z_high, z_low, y_both, sum_ref, modes_ref, pre_ref, cot_ref, field_hbm,
-    act_ref, out_ref, field_ref, slope_ref, sem, *, channels, step_channels, rows, owners,
+    me_ref, inv_y, inv_z, inv_z_low, z_high, z_low, y_both, sum_ref, pre_ref, cot_ref, field_hbm, *refs,
+    channels, step_channels, owners,
 ):
+    piece_refs, act_ref, out_refs = refs[:owners], refs[owners], refs[owners + 1 : 2 * owners + 1]
+    lines_ref, out_ref, field_ref, slope_ref, sem = refs[2 * owners + 1 :]
     step = pl.program_id(0)
     copy = pltpu.make_async_copy(field_hbm, field_ref, sem)
 
     @pl.when(step == 0)
     def _():
         copy.start()
-
+        join(me_ref[0], piece_refs, lines_ref)
+
+    modes_ref = lines_ref.reshape(owners * channels, LANES)
     first = step * step_channels
     lines = []
     for g in range(0, step_channels, GROUP):
@@ -390,7 +409,7 @@
         slope = cot_ref[q].astype(F32) * (cdf + before * pdf)
         slopes.append(slope)
         slope_ref[first + q] = slope
-    forward_group(slopes, z_high[...], z_low[...], y_both[...], out_ref, first, rows)
+    forward_group(slopes, z_high[...], z_low[...], y_both[...], out_ref, first, channels)
 
     @pl.when(step == pl.num_programs(0) - 1)
     def _():
@@ -416,29 +435,32 @@
         eye = lax.broadcasted_iota(jnp.int32, (channels, LANES), 0) == lane_index((channels, LANES))
         bias = jnp.sum(jnp.where(eye, dc, 0.0), axis=0, keepdims=True)
         extra = jnp.where(lax.broadcasted_iota(jnp.int32, (8, LANES), 0) == 0, jnp.broadcast_to(bias, (8, LANES)), 0.0)
-        for d in range(owners):
-            out_ref[d * rows + channels : d * rows + channels + 8, :] = packed
-            out_ref[d * rows + channels + 8 : (d + 1) * rows, :] = extra
-
-
-def cell_stage(inverse, forward, summing, modes, pre, cotangent, field):
+        for s, ref in enumerate(out_refs):
+            ref[:channels, :] = part(me_ref[0], s, out_ref, channels)
+            ref[channels : channels + 8, :] = packed
+            ref[channels + 8 :, :] = extra
+
+
+def cell_stage(me, inverse, forward, summing, pieces, pre, cotangent, field):
     channels = field.shape[0]
-    owners = MY // 2
+    owners = len(pieces)
+    step_channels = STEP
     rows = channels + 16
-    step_channels = STEP
     block = pl.BlockSpec((step_channels, NY, NZ), lambda s: (s, 0, 0))
     tables = (*inverse, *forward, summing)
-    act, out = pl.pallas_call(
-        functools.partial(cell_kernel, channels=channels, step_channels=step_channels, rows=rows, owners=owners),
+    act, *out = pl.pallas_call(
+        functools.partial(cell_kernel, channels=channels, step_channels=step_channels, owners=owners),
         grid=(channels // step_channels,),
-        in_specs=[full(t.shape) for t in tables]
-        + [full((owners * channels, LANES)), block, block, pl.BlockSpec(memory_space=pl.ANY)],
-        out_specs=[block, full((owners * rows, LANES))],
-        out_shape=[
-            jax.ShapeDtypeStruct((channels, NY, NZ), BF16),
-            jax.ShapeDtypeStruct((owners * rows, LANES), F32),
-        ],
+        in_specs=[smem()]
+        + [full(t.shape) for t in tables]
+        + [block, block, pl.BlockSpec(memory_space=pl.ANY)]
+        + [full((channels, LANES))] * owners,
+        out_specs=[block] + [full((rows, LANES))] * owners,
+        out_shape=[jax.ShapeDtypeStruct((channels, NY, NZ), BF16)]
+        + [jax.ShapeDtypeStruct((rows, LANES), F32)] * owners,
         scratch_shapes=[
+            pltpu.VMEM((owners, channels, LANES), F32),
+            pltpu.VMEM((owners * channels, LANES), F32),
             pltpu.VMEM((channels, NY, NZ), F32),
             pltpu.VMEM((channels, NY, NZ), F32),
             pltpu.SemaphoreType.DMA,
@@ -446,14 +468,16 @@
         compiler_params=params(60),
         cost_estimate=pl.CostEstimate(flops=8 * 10**9, bytes_accessed=12 * MIB, transcendentals=2 * 10**6),
         name="cells",
-    )(*tables, modes.reshape(owners * channels, LANES), pre, cotangent, field)
-    return act, out.reshape(owners, rows, LANES)
+    )(me, *tables, pre, cotangent, field, *pieces)
+    return act, out
 
 
 def gradient_kernel(
-    cos_ref, sin_ref, spec_ref, lines_ref, out_hbm, point_ref, bias_ref,
-    sums_ref, real_ref, imag_ref, buffer, sems, *, points, channels, unique, copies, norm,
+    me_ref, cos_ref, sin_ref, spec_ref, *refs, points, channels, unique, copies, norm,
 ):
+    piece_refs, (out_hbm, point_ref, bias_ref) = refs[:points], refs[points : points + 3]
+    lines_ref, sums_ref, real_ref, imag_ref, buffer, sems = refs[points + 3 :]
+    join(me_ref[0], piece_refs, lines_ref)
     halve_lines(lines_ref, sums_ref, points, channels)
     half = LANES // 2
     lane = lane_index((channels, LANES))
@@ -498,15 +522,16 @@
             copy.wait()
 
 
-def gradient(cos_x, sin_x, spectrum, lines, norm, kept_x):
-    points, rows, _ = lines.shape
+def gradient(me, cos_x, sin_x, spectrum, pieces, norm, kept_x):
+    points = len(pieces)
+    rows = pieces[0].shape[0]
     unique, channels, _ = spectrum.shape
     half = LANES // 2
     copies = kept_x // unique
     flat = (channels, LANES)
     return pl.pallas_call(
         functools.partial(gradient_kernel, points=points, channels=channels, unique=unique, copies=copies, norm=norm),
-        in_specs=[smem(), smem(), full(spectrum.shape), full(lines.shape)],
+        in_specs=[smem(), smem(), smem(), full(spectrum.shape)] + [full((rows, LANES))] * points,
         out_specs=[pl.BlockSpec(memory_space=pl.ANY), full((channels, channels)), full((1, channels))],
         out_shape=[
             jax.ShapeDtypeStruct((2, kept_x, channels, channels, half), F32),
@@ -514,6 +539,7 @@
             jax.ShapeDtypeStruct((1, channels), F32),
         ],
         scratch_shapes=[
+            pltpu.VMEM((points, rows, LANES), F32),
             pltpu.VMEM((2, 2, points // 2, channels, LANES), F32),
             pltpu.VMEM((2,) + flat, F32),
             pltpu.VMEM((2,) + flat, F32),
@@ -523,11 +549,14 @@
         compiler_params=params(60),
         cost_estimate=pl.CostEstimate(flops=10**7, bytes_accessed=40 * MIB, transcendentals=0),
         name="weight_gradient",
-    )(cos_x, sin_x, spectrum, lines)
-
-
-def swap(lines):
-    return lax.all_to_all(lines, "space", split_axis=0, concat_axis=0, tiled=True)
+    )(me, cos_x, sin_x, spectrum, *pieces)
+
+
+def swap(pieces):
+    count = len(pieces)
+    return pieces[:1] + [
+        lax.ppermute(pieces[s], "space", [(d, d ^ s) for d in range(count)]) for s in range(1, count)
+    ]
 
 
 def suits(width_x, length_x, devices, channels, weights):
@@ -540,6 +569,7 @@
         and 2 * held == LANES
         and MX % length_x == 0
         and length_x % 8 == 0
+        and devices & (devices - 1) == 0
         and even
         and channels == MZ
     )
@@ -562,16 +592,17 @@
     slopes_in = cotangent.reshape(channels, NY, NZ)
     weights = jnp.transpose(spectral_weights, (0, 1, 3, 4, 2))
 
-    lines, half = forward_modes(field, forward, weights, length_x)
+    me = lax.axis_index("space")[None]
+    lines, half = forward_modes(me, field, forward, weights, length_x)
     lines = swap(lines)
     folded = fold_rest(weights, half, length_x)
-    spectrum, mixed = mix(cos_x, sin_x, lines, folded, norm)
-    field_late, mixed = lax.optimization_barrier((field, mixed))
+    spectrum, mixed = mix(me, cos_x, sin_x, lines, folded, norm)
+    field_late, *mixed = lax.optimization_barrier((field, *mixed))
     modes = swap(mixed)
     pre = pointwise(field_late, summing, point_weights, point_bias)
-    activated, slope_lines = cell_stage(inverse, forward, summing, modes, pre, slopes_in, field)
+    activated, slope_lines = cell_stage(me, inverse, forward, summing, modes, pre, slopes_in, field)
     slope_lines = swap(slope_lines)
-    grad, grad_point, grad_bias = gradient(cos_x, sin_x, spectrum, slope_lines, norm, MX)
+    grad, grad_point, grad_bias = gradient(me, cos_x, sin_x, spectrum, slope_lines, norm, MX)
     return (
         activated.reshape(cotangent.shape),
         jnp.transpose(grad, (0, 1, 4, 2, 3)),

time: 98.9 us -> 138 us (1.40)
  starting transfers between devices: 13.2 us -> 63.6 us
  blocking collectives: 18.3 us -> 0 us
  waiting for transfers between devices: 0.17 us -> 6.43 us
    ppermute x0 -> x45, starting transfers between devices: none -> 63.6 us  [swap(): lax.ppermute(pieces[s], 'space', [(d, d ^ s) for d in range(count)])]
    all_to_all x1 -> x0, blocking collectives: 18.3 us -> none  [swap(): lax.all_to_all(lines, 'space', split_axis=0, concat_axis=0, tiled=True)]
    all_to_all x2 -> x0, starting transfers between devices: 13.2 us -> none  [swap(): lax.all_to_all(lines, 'space', split_axis=0, concat_axis=0, tiled=True)]
    ppermute x0 -> x45, waiting for transfers between devices: none -> 6.43 us  [swap(): lax.ppermute(pieces[s], 'space', [(d, d ^ s) for d in range(count)])]
  transfers between devices with their start and end apart: 2 -> 45, of which waited for: 1 -> 3; matrix products, arithmetic and copies ran while one was open for 1% -> 1% of each run, Pallas kernels for 19% -> 13%
where the time goes in v4:
time: 138 us
  Pallas kernels  63.6 us (46%)
  starting transfers between devices  63.6 us (46%)
  waiting for transfers between devices  6.43 us (5%)
  local copies, waits for them, and re-layouts  3.1 us (2%)
    ppermute x45, starting transfers between devices, swap(): lax.ppermute(pieces[s], 'space', [(d, d ^ s) for d in range(count)])  63.6 us
    pallas_call x1, Pallas kernels, gradient(): pl.pallas_call(functools.partial(gradient_kernel, points=points, channels...  15.4 us
    pallas_call x1, Pallas kernels, cell_stage(): pl.pallas_call(functools.partial(cell_kernel, channels=channels, step_cha...  13 us
    pallas_call x1, Pallas kernels, forward_modes(): pl.pallas_call(functools.partial(forward_kernel, channels=channels, step_...  10.5 us
    pallas_call x1, Pallas kernels, fold_rest(): pl.pallas_call(fold_kernel, grid=(unique - first,), in_specs=pieces + [pl...  9.85 us
    pallas_call x1, Pallas kernels, pointwise(): pl.pallas_call(functools.partial(pointwise_kernel, channels=channels, blo...  8.69 us
    ppermute x45, waiting for transfers between devices, swap(): lax.ppermute(pieces[s], 'space', [(d, d ^ s) for d in range(count)])  6.43 us
    pallas_call x1, Pallas kernels, mix(): pl.pallas_call(functools.partial(mix_kernel, points=points, channels=chan...  6.12 us
  transfers between devices with their start and end apart: 45, of which 3 were waited for; matrix products, arithmetic and copies ran while one was open for 1% of the time, Pallas kernels for 13%

profile of v4, /device:TPU:0, one launch (start us, length us, event | category | flops | bytes accessed | tf_op | source)
XLA Modules:
  0.0 137.9 jit_solution(6447853419986780777)
XLA Ops:
  0.6 10.5 %forward_yz.1 = (f32[16,32,32,128]{3,2,1,0:T(8,128)}, f32[32,128]{1,0:T(8,128)}, f32[32,128]{1,0:T(8,128)}, f32[32,128]{1,0:T(8,128)}, f32[32,128]{1,0:T(8,128)}...) custom-call(s32[1]{0:T(128)} %bitcast.me_ref, ...), custom_call_target="tpu_custom_call" | custom-call | flops 2000000000 | bytes 27262976 | tf_op jit(solution)/shard_map/forward_yz/pallas_call | solution.py:197
  11.2 0.5 collective-permute-start
  11.7 2.6 %collective-permute-start.1 = (f32[32,128]{1,0:T(8,128)}, f32[32,128]{1,0:T(8,128)S(1)}, u32[]{:S(2)}, u32[]{:S(2)}) collective-permute-start(f32[32,128]{1,0:T(8,128)} %get-tuple-element.78), channel_id=1, source_target_pairs={{0,2},{1,3},{2,0},{3,1},{4,6},{5,7},{6,4},{7,5},{8,10},{9,11},{10,... | collective-permute-start | bytes 49160 | tf_op jit(solution)/shard_map/ppermute | solution.py:558
  14.3 1.8 %collective-permute-start.3 = (f32[32,128]{1,0:T(8,128)}, f32[32,128]{1,0:T(8,128)S(1)}, u32[]{:S(2)}, u32[]{:S(2)}) collective-permute-start(f32[32,128]{1,0:T(8,128)} %get-tuple-element.80), channel_id=1, source_target_pairs={{0,4},{1,5},{2,6},{3,7},{4,0},{5,1},{6,2},{7,3},{8,12},{9,13},{10,... | collective-permute-start | bytes 49160 | tf_op jit(solution)/shard_map/ppermute | solution.py:558
  16.1 2.6 %collective-permute-start.5 = (f32[32,128]{1,0:T(8,128)}, f32[32,128]{1,0:T(8,128)S(1)}, u32[]{:S(2)}, u32[]{:S(2)}) collective-permute-start(f32[32,128]{1,0:T(8,128)} %get-tuple-element.82), channel_id=1, source_target_pairs={{0,6},{1,7},{2,4},{3,5},{4,2},{5,3},{6,0},{7,1},{8,14},{9,15},{10,... | collective-permute-start | bytes 49160 | tf_op jit(solution)/shard_map/ppermute | solution.py:558
  18.8 0.1 collective-permute-start.6
  18.9 2.6 %collective-permute-start.7 = (f32[32,128]{1,0:T(8,128)}, f32[32,128]{1,0:T(8,128)S(1)}, u32[]{:S(2)}, u32[]{:S(2)}) collective-permute-start(f32[32,128]{1,0:T(8,128)} %get-tuple-element.84), channel_id=1, source_target_pairs={{0,8},{1,9},{2,10},{3,11},{4,12},{5,13},{6,14},{7,15},{8,0},{9,1},... | collective-permute-start | bytes 49160 | tf_op jit(solution)/shard_map/ppermute | solution.py:558
  21.5 0.2 collective-permute-start.8
  21.8 3.4 %collective-permute-start.9 = (f32[32,128]{1,0:T(8,128)}, f32[32,128]{1,0:T(8,128)S(1)}, u32[]{:S(2)}, u32[]{:S(2)}) collective-permute-start(f32[32,128]{1,0:T(8,128)} %get-tuple-element.86), channel_id=1, source_target_pairs={{0,10},{1,11},{2,8},{3,9},{4,14},{5,15},{6,12},{7,13},{8,2},{9,3},... | collective-permute-start | bytes 49160 | tf_op jit(solution)/shard_map/ppermute | solution.py:558
  25.1 0.1 collective-permute-start.10
  25.3 3.5 %collective-permute-start.11 = (f32[32,128]{1,0:T(8,128)}, f32[32,128]{1,0:T(8,128)S(1)}, u32[]{:S(2)}, u32[]{:S(2)}) collective-permute-start(f32[32,128]{1,0:T(8,128)} %get-tuple-element.88), channel_id=1, source_target_pairs={{0,12},{1,13},{2,14},{3,15},{4,8},{5,9},{6,10},{7,11},{8,4},{9,5},... | collective-permute-start | bytes 49160 | tf_op jit(solution)/shard_map/ppermute | solution.py:558
  28.9 4.4 %collective-permute-start.13 = (f32[32,128]{1,0:T(8,128)}, f32[32,128]{1,0:T(8,128)S(1)}, u32[]{:S(2)}, u32[]{:S(2)}) collective-permute-start(f32[32,128]{1,0:T(8,128)} %get-tuple-element.90), channel_id=1, source_target_pairs={{0,14},{1,15},{2,12},{3,13},{4,10},{5,11},{6,8},{7,9},{8,6},{9,7},... | collective-permute-start | bytes 49160 | tf_op jit(solution)/shard_map/ppermute | solution.py:558
  33.4 9.8 %fold_weights.1.weights_ref = f32[16,32,32,128]{3,2,1,0:T(8,128)} custom-call(f32[2,32,32,32,64]{4,3,2,1,0:T(8,128)} %bitcast.13, f32[2,32,32,32,64]{4,3,2,1,0:T(8,128)} %bitcast.14, f32[16,32,32,128]{3,2,1,0:T(8,128)} %get-tuple-element.75.refs_2_), custom_call_target="tpu_custom_call", output_to_operand_aliasing={{}: (2, {})} | custom-call | flops 4000000 | bytes 20971520 | tf_op jit(solution)/shard_map/fold_weights/pallas_call | solution.py:224
  43.4 0.5 copy-done.25
  44.0 6.1 %mix_modes.1 = (f32[16,32,128]{2,1,0:T(8,128)}, f32[32,128]{1,0:T(8,128)}, f32[32,128]{1,0:T(8,128)}, f32[32,128]{1,0:T(8,128)}, f32[32,128]{1,0:T(8,128)}, /*in...) custom-call(s32[1]{0:T(128)} %bitcast.me_ref, ...), custom_call_target="tpu_custom_call" | custom-call | flops 20000000 | bytes 9437184 | tf_op jit(solution)/shard_map/mix_modes/pallas_call | solution.py:313
  50.1 0.4 collective-permute-start.15
  50.6 1.5 %collective-permute-start.16 = (f32[32,128]{1,0:T(8,128)}, f32[32,128]{1,0:T(8,128)S(1)}, u32[]{:S(2)}, u32[]{:S(2)}) collective-permute-start(f32[32,128]{1,0:T(8,128)} %get-tuple-element.111), channel_id=1, source_target_pairs={{0,2},{1,3},{2,0},{3,1},{4,6},{5,7},{6,4},{7,5},{8,10},{9,11},{10,... | collective-permute-start | bytes 49160 | tf_op jit(solution)/shard_map/ppermute | solution.py:558
  52.1 1.9 %collective-permute-start.19 = (f32[32,128]{1,0:T(8,128)}, f32[32,128]{1,0:T(8,128)S(1)}, u32[]{:S(2)}, u32[]{:S(2)}) collective-permute-start(f32[32,128]{1,0:T(8,128)} %get-tuple-element.114), channel_id=1, source_target_pairs={{0,5},{1,4},{2,7},{3,6},{4,1},{5,0},{6,3},{7,2},{8,13},{9,12},{10,... | collective-permute-start | bytes 49160 | tf_op jit(solution)/shard_map/ppermute | solution.py:558
  54.1 1.3 collective-permute-start.20
  55.3 1.2 collective-permute-start.21
  56.5 2.6 %collective-permute-start.22 = (f32[32,128]{1,0:T(8,128)}, f32[32,128]{1,0:T(8,128)S(1)}, u32[]{:S(2)}, u32[]{:S(2)}) collective-permute-start(f32[32,128]{1,0:T(8,128)} %get-tuple-element.117), channel_id=1, source_target_pairs={{0,8},{1,9},{2,10},{3,11},{4,12},{5,13},{6,14},{7,15},{8,0},{9,1},... | collective-permute-start | bytes 49160 | tf_op jit(solution)/shard_map/ppermute | solution.py:558
  59.1 0.2 collective-permute-start.23
  59.4 3.2 %collective-permute-start.24 = (f32[32,128]{1,0:T(8,128)}, f32[32,128]{1,0:T(8,128)S(1)}, u32[]{:S(2)}, u32[]{:S(2)}) collective-permute-start(f32[32,128]{1,0:T(8,128)} %get-tuple-element.119), channel_id=1, source_target_pairs={{0,10},{1,11},{2,8},{3,9},{4,14},{5,15},{6,12},{7,13},{8,2},{9,3},... | collective-permute-start | bytes 49160 | tf_op jit(solution)/shard_map/ppermute | solution.py:558
  62.6 0.7 copy.19
  63.3 0.7 copy.20.bias_in_ref
  64.1 3.4 %collective-permute-start.26 = (f32[32,128]{1,0:T(8,128)}, f32[32,128]{1,0:T(8,128)S(1)}, u32[]{:S(2)}, u32[]{:S(2)}) collective-permute-start(f32[32,128]{1,0:T(8,128)} %get-tuple-element.121), channel_id=1, source_target_pairs={{0,12},{1,13},{2,14},{3,15},{4,8},{5,9},{6,10},{7,11},{8,4},{9,5},... | collective-permute-start | bytes 49160 | tf_op jit(solution)/shard_map/ppermute | solution.py:558
  67.5 0.3 collective-permute-start.27
  67.9 4.4 %collective-permute-start.28 = (f32[32,128]{1,0:T(8,128)}, f32[32,128]{1,0:T(8,128)S(1)}, u32[]{:S(2)}, u32[]{:S(2)}) collective-permute-start(f32[32,128]{1,0:T(8,128)} %get-tuple-element.123), channel_id=1, source_target_pairs={{0,14},{1,15},{2,12},{3,13},{4,10},{5,11},{6,8},{7,9},{8,6},{9,7},... | collective-permute-start | bytes 49160 | tf_op jit(solution)/shard_map/ppermute | solution.py:558
  72.3 8.7 %pointwise.1.pre_ref = f32[32,128,256]{2,1,0:T(8,128)} custom-call(f32[256,32]{1,0:T(8,128)} %constant.24.clone.sum_ref, f32[32,32]{1,0:T(8,128)} %bitcast.18, f32[32,1]{1,0:T(8,128)} %copy.20.bias_in_ref, f32[32,128,256]{2,1,0:T(8,128)} %bitcast.16), custom_call_target="tpu_custom_call" | custom-call | flops 4000000000 | bytes 25165824 | tf_op jit(solution)/shard_map/pointwise/pallas_call | solution.py:367
  81.1 0.4 copy-done.42
  81.6 13.0 %cells.1 = (bf16[32,128,256]{2,1,0:T(8,128)(2,1)}, f32[48,128]{1,0:T(8,128)}, f32[48,128]{1,0:T(8,128)}, f32[48,128]{1,0:T(8,128)}, f32[48,128]{1,0:T(8,128)}, /...) custom-call(s32[1]{0:T(128)} %bitcast.me_ref, ...), custom_call_target="tpu_custom_call" | custom-call | flops 8000000000 | bytes 12582912 | tf_op jit(solution)/shard_map/cells/pallas_call | solution.py:451
  94.6 0.5 collective-permute-start.30
  95.1 1.5 %collective-permute-start.31 = (f32[48,128]{1,0:T(8,128)}, f32[48,128]{1,0:T(8,128)S(1)}, u32[]{:S(2)}, u32[]{:S(2)}) collective-permute-start(f32[48,128]{1,0:T(8,128)} %get-tuple-element.129), channel_id=1, source_target_pairs={{0,2},{1,3},{2,0},{3,1},{4,6},{5,7},{6,4},{7,5},{8,10},{9,11},{10,... | collective-permute-start | bytes 73736 | tf_op jit(solution)/shard_map/ppermute | solution.py:558
  96.7 2.0 %collective-permute-start.34 = (f32[48,128]{1,0:T(8,128)}, f32[48,128]{1,0:T(8,128)S(1)}, u32[]{:S(2)}, u32[]{:S(2)}) collective-permute-start(f32[48,128]{1,0:T(8,128)} %get-tuple-element.132), channel_id=1, source_target_pairs={{0,5},{1,4},{2,7},{3,6},{4,1},{5,0},{6,3},{7,2},{8,13},{9,12},{10,... | collective-permute-start | bytes 73736 | tf_op jit(solution)/shard_map/ppermute | solution.py:558
  98.6 1.3 collective-permute-start.35
  99.9 1.2 collective-permute-start.36
  101.1 2.6 %collective-permute-start.37 = (f32[48,128]{1,0:T(8,128)}, f32[48,128]{1,0:T(8,128)S(1)}, u32[]{:S(2)}, u32[]{:S(2)}) collective-permute-start(f32[48,128]{1,0:T(8,128)} %get-tuple-element.135), channel_id=1, source_target_pairs={{0,8},{1,9},{2,10},{3,11},{4,12},{5,13},{6,14},{7,15},{8,0},{9,1},... | collective-permute-start | bytes 73736 | tf_op jit(solution)/shard_map/ppermute | solution.py:558
  103.7 0.4 collective-permute-start.38
  104.1 3.1 %collective-permute-start.39 = (f32[48,128]{1,0:T(8,128)}, f32[48,128]{1,0:T(8,128)S(1)}, u32[]{:S(2)}, u32[]{:S(2)}) collective-permute-start(f32[48,128]{1,0:T(8,128)} %get-tuple-element.137), channel_id=1, source_target_pairs={{0,10},{1,11},{2,8},{3,9},{4,14},{5,15},{6,12},{7,13},{8,2},{9,3},... | collective-permute-start | bytes 73736 | tf_op jit(solution)/shard_map/ppermute | solution.py:558
  107.2 0.2 collective-permute-start.40
  107.4 3.3 %collective-permute-start.41 = (f32[48,128]{1,0:T(8,128)}, f32[48,128]{1,0:T(8,128)S(1)}, u32[]{:S(2)}, u32[]{:S(2)}) collective-permute-start(f32[48,128]{1,0:T(8,128)} %get-tuple-element.139), channel_id=1, source_target_pairs={{0,12},{1,13},{2,14},{3,15},{4,8},{5,9},{6,10},{7,11},{8,4},{9,5},... | collective-permute-start | bytes 73736 | tf_op jit(solution)/shard_map/ppermute | solution.py:558
  110.7 0.5 collective-permute-start.42
  111.2 4.2 %collective-permute-start.43 = (f32[48,128]{1,0:T(8,128)}, f32[48,128]{1,0:T(8,128)S(1)}, u32[]{:S(2)}, u32[]{:S(2)}) collective-permute-start(f32[48,128]{1,0:T(8,128)} %get-tuple-element.141), channel_id=1, source_target_pairs={{0,14},{1,15},{2,12},{3,13},{4,10},{5,11},{6,8},{7,9},{8,6},{9,7},... | collective-permute-start | bytes 73736 | tf_op jit(solution)/shard_map/ppermute | solution.py:558
  115.5 0.5 collective-permute-done.42.refs_13_
  116.0 2.0 %collective-permute-done.43.refs_14_ = f32[48,128]{1,0:T(8,128)S(1)} collective-permute-done((f32[48,128]{1,0:T(8,128)}, f32[48,128]{1,0:T(8,128)S(1)}, u32[]{:S(2)}, u32[]{:S(2)}) %collective-permute-start.43) | collective-permute-done | bytes 24608 | tf_op jit(solution)/shard_map/ppermute | solution.py:558
  118.0 3.9 %collective-permute-done.44.refs_15_ = f32[48,128]{1,0:T(8,128)S(1)} collective-permute-done((f32[48,128]{1,0:T(8,128)}, f32[48,128]{1,0:T(8,128)S(1)}, u32[]{:S(2)}, u32[]{:S(2)}) %collective-permute-start.44) | collective-permute-done | bytes 24608 | tf_op jit(solution)/shard_map/ppermute | solution.py:558
  122.0 0.5 copy-done.14
  122.5 15.4 %weight_gradient.1 = (f32[2,32,32,32,64]{4,3,2,1,0:T(8,128)}, f32[32,32]{1,0:T(8,128)}, f32[1,32]{1,0:T(1,128)}) custom-call(s32[1]{0:T(128)} %bitcast.me_ref, f32[16,16]{1,0:T(8,128)} %constant.22.clone.cos_ref, f32[16,16]{1,0:T(8,128)} %constant.23.clone.sin_ref, f32[16,32,128]{2,1,0:T(8,128)} %get-tuple-element.126.spec_ref, ...), custom_call_target="tpu_custom_call" | custom-call | flops 10000000 | bytes 41943040 | tf_op jit(solution)/shard_map/weight_gradient/pallas_call | solution.py:532
  (144 shorter events, 0.9 us)
Async XLA Ops:
  11.2 5.0 %collective-permute-start = (f32[32,128]{1,0:T(8,128)}, f32[32,128]{1,0:T(8,128)S(1)}, u32[]{:S(2)}, u32[]{:S(2)}) collective-permute-start(f32[32,128]{1,0:T(8,128)} %get-tuple-element.77), channel_id=1, source_target_pairs={{0,1},{1,0},{2,3},{3,2},{4,5},{5,4},{6,7},{7,6},{8,9},{9,8},{10,11... | collective-permute-start | bytes 49160 | tf_op jit(solution)/shard_map/ppermute | solution.py:558
  11.7 7.1 %collective-permute-start.1 = (f32[32,128]{1,0:T(8,128)}, f32[32,128]{1,0:T(8,128)S(1)}, u32[]{:S(2)}, u32[]{:S(2)}) collective-permute-start(f32[32,128]{1,0:T(8,128)} %get-tuple-element.78), channel_id=1, source_target_pairs={{0,2},{1,3},{2,0},{3,1},{4,6},{5,7},{6,4},{7,5},{8,10},{9,11},{10,... | collective-permute-start | bytes 49160 | tf_op jit(solution)/shard_map/ppermute | solution.py:558
  14.3 4.7 %collective-permute-start.2 = (f32[32,128]{1,0:T(8,128)}, f32[32,128]{1,0:T(8,128)S(1)}, u32[]{:S(2)}, u32[]{:S(2)}) collective-permute-start(f32[32,128]{1,0:T(8,128)} %get-tuple-element.79), channel_id=1, source_target_pairs={{0,3},{1,2},{2,1},{3,0},{4,7},{5,6},{6,5},{7,4},{8,11},{9,10},{10,... | collective-permute-start | bytes 49160 | tf_op jit(solution)/shard_map/ppermute | solution.py:558
  14.3 7.2 %collective-permute-start.3 = (f32[32,128]{1,0:T(8,128)}, f32[32,128]{1,0:T(8,128)S(1)}, u32[]{:S(2)}, u32[]{:S(2)}) collective-permute-start(f32[32,128]{1,0:T(8,128)} %get-tuple-element.80), channel_id=1, source_target_pairs={{0,4},{1,5},{2,6},{3,7},{4,0},{5,1},{6,2},{7,3},{8,12},{9,13},{10,... | collective-permute-start | bytes 49160 | tf_op jit(solution)/shard_map/ppermute | solution.py:558
  16.1 5.6 %collective-permute-start.4 = (f32[32,128]{1,0:T(8,128)}, f32[32,128]{1,0:T(8,128)S(1)}, u32[]{:S(2)}, u32[]{:S(2)}) collective-permute-start(f32[32,128]{1,0:T(8,128)} %get-tuple-element.81), channel_id=1, source_target_pairs={{0,5},{1,4},{2,7},{3,6},{4,1},{5,0},{6,3},{7,2},{8,13},{9,12},{10,... | collective-permute-start | bytes 49160 | tf_op jit(solution)/shard_map/ppermute | solution.py:558
  16.1 27.1 %copy-start.15 = (f32[32,128]{1,0:T(8,128)}, f32[32,128]{1,0:T(8,128)S(1)}, u32[]{:S(2)}) copy-start(f32[32,128]{1,0:T(8,128)S(1)} %collective-permute-done.refs_1_) | copy-start | bytes 49156
  16.1 9.0 %collective-permute-start.5 = (f32[32,128]{1,0:T(8,128)}, f32[32,128]{1,0:T(8,128)S(1)}, u32[]{:S(2)}, u32[]{:S(2)}) collective-permute-start(f32[32,128]{1,0:T(8,128)} %get-tuple-element.82), channel_id=1, source_target_pairs={{0,6},{1,7},{2,4},{3,5},{4,2},{5,3},{6,0},{7,1},{8,14},{9,15},{10,... | collective-permute-start | bytes 49160 | tf_op jit(solution)/shard_map/ppermute | solution.py:558
  18.8 6.5 %collective-permute-start.6 = (f32[32,128]{1,0:T(8,128)}, f32[32,128]{1,0:T(8,128)S(1)}, u32[]{:S(2)}, u32[]{:S(2)}) collective-permute-start(f32[32,128]{1,0:T(8,128)} %get-tuple-element.83), channel_id=1, source_target_pairs={{0,7},{1,6},{2,5},{3,4},{4,3},{5,2},{6,1},{7,0},{8,15},{9,14},{10,... | collective-permute-start | bytes 49160 | tf_op jit(solution)/shard_map/ppermute | solution.py:558
  18.9 9.8 %collective-permute-start.7 = (f32[32,128]{1,0:T(8,128)}, f32[32,128]{1,0:T(8,128)S(1)}, u32[]{:S(2)}, u32[]{:S(2)}) collective-permute-start(f32[32,128]{1,0:T(8,128)} %get-tuple-element.84), channel_id=1, source_target_pairs={{0,8},{1,9},{2,10},{3,11},{4,12},{5,13},{6,14},{7,15},{8,0},{9,1},... | collective-permute-start | bytes 49160 | tf_op jit(solution)/shard_map/ppermute | solution.py:558
  21.5 7.3 %collective-permute-start.8 = (f32[32,128]{1,0:T(8,128)}, f32[32,128]{1,0:T(8,128)S(1)}, u32[]{:S(2)}, u32[]{:S(2)}) collective-permute-start(f32[32,128]{1,0:T(8,128)} %get-tuple-element.85), channel_id=1, source_target_pairs={{0,9},{1,8},{2,11},{3,10},{4,13},{5,12},{6,15},{7,14},{8,1},{9,0},... | collective-permute-start | bytes 49160 | tf_op jit(solution)/shard_map/ppermute | solution.py:558
  21.8 11.5 %collective-permute-start.9 = (f32[32,128]{1,0:T(8,128)}, f32[32,128]{1,0:T(8,128)S(1)}, u32[]{:S(2)}, u32[]{:S(2)}) collective-permute-start(f32[32,128]{1,0:T(8,128)} %get-tuple-element.86), channel_id=1, source_target_pairs={{0,10},{1,11},{2,8},{3,9},{4,14},{5,15},{6,12},{7,13},{8,2},{9,3},... | collective-permute-start | bytes 49160 | tf_op jit(solution)/shard_map/ppermute | solution.py:558
  25.1 18.2 %collective-permute-start.10 = (f32[32,128]{1,0:T(8,128)}, f32[32,128]{1,0:T(8,128)S(1)}, u32[]{:S(2)}, u32[]{:S(2)}) collective-permute-start(f32[32,128]{1,0:T(8,128)} %get-tuple-element.87), channel_id=1, source_target_pairs={{0,11},{1,10},{2,9},{3,8},{4,15},{5,14},{6,13},{7,12},{8,3},{9,2},... | collective-permute-start | bytes 49160 | tf_op jit(solution)/shard_map/ppermute | solution.py:558
  25.3 18.1 %collective-permute-start.11 = (f32[32,128]{1,0:T(8,128)}, f32[32,128]{1,0:T(8,128)S(1)}, u32[]{:S(2)}, u32[]{:S(2)}) collective-permute-start(f32[32,128]{1,0:T(8,128)} %get-tuple-element.88), channel_id=1, source_target_pairs={{0,12},{1,13},{2,14},{3,15},{4,8},{5,9},{6,10},{7,11},{8,4},{9,5},... | collective-permute-start | bytes 49160 | tf_op jit(solution)/shard_map/ppermute | solution.py:558
  28.8 14.6 %collective-permute-start.12 = (f32[32,128]{1,0:T(8,128)}, f32[32,128]{1,0:T(8,128)S(1)}, u32[]{:S(2)}, u32[]{:S(2)}) collective-permute-start(f32[32,128]{1,0:T(8,128)} %get-tuple-element.89), channel_id=1, source_target_pairs={{0,13},{1,12},{2,15},{3,14},{4,9},{5,8},{6,11},{7,10},{8,5},{9,4},... | collective-permute-start | bytes 49160 | tf_op jit(solution)/shard_map/ppermute | solution.py:558
  28.9 14.5 %collective-permute-start.13 = (f32[32,128]{1,0:T(8,128)}, f32[32,128]{1,0:T(8,128)S(1)}, u32[]{:S(2)}, u32[]{:S(2)}) collective-permute-start(f32[32,128]{1,0:T(8,128)} %get-tuple-element.90), channel_id=1, source_target_pairs={{0,14},{1,15},{2,12},{3,13},{4,10},{5,11},{6,8},{7,9},{8,6},{9,7},... | collective-permute-start | bytes 49160 | tf_op jit(solution)/shard_map/ppermute | solution.py:558
  33.2 10.2 %collective-permute-start.14 = (f32[32,128]{1,0:T(8,128)}, f32[32,128]{1,0:T(8,128)S(1)}, u32[]{:S(2)}, u32[]{:S(2)}) collective-permute-start(f32[32,128]{1,0:T(8,128)} %get-tuple-element.91), channel_id=1, source_target_pairs={{0,15},{1,14},{2,13},{3,12},{4,11},{5,10},{6,9},{7,8},{8,7},{9,6},... | collective-permute-start | bytes 49160 | tf_op jit(solution)/shard_map/ppermute | solution.py:558
  50.1 3.9 %collective-permute-start.15 = (f32[32,128]{1,0:T(8,128)}, f32[32,128]{1,0:T(8,128)S(1)}, u32[]{:S(2)}, u32[]{:S(2)}) collective-permute-start(f32[32,128]{1,0:T(8,128)} %get-tuple-element.110), channel_id=1, source_target_pairs={{0,1},{1,0},{2,3},{3,2},{4,5},{5,4},{6,7},{7,6},{8,9},{9,8},{10,11... | collective-permute-start | bytes 49160 | tf_op jit(solution)/shard_map/ppermute | solution.py:558
  50.6 4.8 %collective-permute-start.16 = (f32[32,128]{1,0:T(8,128)}, f32[32,128]{1,0:T(8,128)S(1)}, u32[]{:S(2)}, u32[]{:S(2)}) collective-permute-start(f32[32,128]{1,0:T(8,128)} %get-tuple-element.111), channel_id=1, source_target_pairs={{0,2},{1,3},{2,0},{3,1},{4,6},{5,7},{6,4},{7,5},{8,10},{9,11},{10,... | collective-permute-start | bytes 49160 | tf_op jit(solution)/shard_map/ppermute | solution.py:558
  52.1 4.4 %collective-permute-start.17 = (f32[32,128]{1,0:T(8,128)}, f32[32,128]{1,0:T(8,128)S(1)}, u32[]{:S(2)}, u32[]{:S(2)}) collective-permute-start(f32[32,128]{1,0:T(8,128)} %get-tuple-element.112), channel_id=1, source_target_pairs={{0,3},{1,2},{2,1},{3,0},{4,7},{5,6},{6,5},{7,4},{8,11},{9,10},{10,... | collective-permute-start | bytes 49160 | tf_op jit(solution)/shard_map/ppermute | solution.py:558
  52.1 7.0 %collective-permute-start.18 = (f32[32,128]{1,0:T(8,128)}, f32[32,128]{1,0:T(8,128)S(1)}, u32[]{:S(2)}, u32[]{:S(2)}) collective-permute-start(f32[32,128]{1,0:T(8,128)} %get-tuple-element.113), channel_id=1, source_target_pairs={{0,4},{1,5},{2,6},{3,7},{4,0},{5,1},{6,2},{7,3},{8,12},{9,13},{10,... | collective-permute-start | bytes 49160 | tf_op jit(solution)/shard_map/ppermute | solution.py:558
  52.1 7.3 %collective-permute-start.19 = (f32[32,128]{1,0:T(8,128)}, f32[32,128]{1,0:T(8,128)S(1)}, u32[]{:S(2)}, u32[]{:S(2)}) collective-permute-start(f32[32,128]{1,0:T(8,128)} %get-tuple-element.114), channel_id=1, source_target_pairs={{0,5},{1,4},{2,7},{3,6},{4,1},{5,0},{6,3},{7,2},{8,13},{9,12},{10,... | collective-permute-start | bytes 49160 | tf_op jit(solution)/shard_map/ppermute | solution.py:558
  54.0 27.0 %copy-start.32 = (f32[32,128]{1,0:T(8,128)}, f32[32,128]{1,0:T(8,128)S(1)}, u32[]{:S(2)}) copy-start(f32[32,128]{1,0:T(8,128)S(1)} %collective-permute-done.15.refs_1_) | copy-start | bytes 49156
  54.1 9.9 %collective-permute-start.20 = (f32[32,128]{1,0:T(8,128)}, f32[32,128]{1,0:T(8,128)S(1)}, u32[]{:S(2)}, u32[]{:S(2)}) collective-permute-start(f32[32,128]{1,0:T(8,128)} %get-tuple-element.115), channel_id=1, source_target_pairs={{0,6},{1,7},{2,4},{3,5},{4,2},{5,3},{6,0},{7,1},{8,14},{9,15},{10,... | collective-permute-start | bytes 49160 | tf_op jit(solution)/shard_map/ppermute | solution.py:558
  55.3 25.7 %copy-start.33 = (f32[32,128]{1,0:T(8,128)}, f32[32,128]{1,0:T(8,128)S(1)}, u32[]{:S(2)}) copy-start(f32[32,128]{1,0:T(8,128)S(1)} %collective-permute-done.16.refs_2_) | copy-start | bytes 49156
  55.3 8.8 %collective-permute-start.21 = (f32[32,128]{1,0:T(8,128)}, f32[32,128]{1,0:T(8,128)S(1)}, u32[]{:S(2)}, u32[]{:S(2)}) collective-permute-start(f32[32,128]{1,0:T(8,128)} %get-tuple-element.116), channel_id=1, source_target_pairs={{0,7},{1,6},{2,5},{3,4},{4,3},{5,2},{6,1},{7,0},{8,15},{9,14},{10,... | collective-permute-start | bytes 49160 | tf_op jit(solution)/shard_map/ppermute | solution.py:558
  56.5 11.0 %collective-permute-start.22 = (f32[32,128]{1,0:T(8,128)}, f32[32,128]{1,0:T(8,128)S(1)}, u32[]{:S(2)}, u32[]{:S(2)}) collective-permute-start(f32[32,128]{1,0:T(8,128)} %get-tuple-element.117), channel_id=1, source_target_pairs={{0,8},{1,9},{2,10},{3,11},{4,12},{5,13},{6,14},{7,15},{8,0},{9,1},... | collective-permute-start | bytes 49160 | tf_op jit(solution)/shard_map/ppermute | solution.py:558
  59.1 8.7 %collective-permute-start.23 = (f32[32,128]{1,0:T(8,128)}, f32[32,128]{1,0:T(8,128)S(1)}, u32[]{:S(2)}, u32[]{:S(2)}) collective-permute-start(f32[32,128]{1,0:T(8,128)} %get-tuple-element.118), channel_id=1, source_target_pairs={{0,9},{1,8},{2,11},{3,10},{4,13},{5,12},{6,15},{7,14},{8,1},{9,0},... | collective-permute-start | bytes 49160 | tf_op jit(solution)/shard_map/ppermute | solution.py:558
  59.4 12.9 %collective-permute-start.24 = (f32[32,128]{1,0:T(8,128)}, f32[32,128]{1,0:T(8,128)S(1)}, u32[]{:S(2)}, u32[]{:S(2)}) collective-permute-start(f32[32,128]{1,0:T(8,128)} %get-tuple-element.119), channel_id=1, source_target_pairs={{0,10},{1,11},{2,8},{3,9},{4,14},{5,15},{6,12},{7,13},{8,2},{9,3},... | collective-permute-start | bytes 49160 | tf_op jit(solution)/shard_map/ppermute | solution.py:558
  64.0 17.0 %collective-permute-start.25 = (f32[32,128]{1,0:T(8,128)}, f32[32,128]{1,0:T(8,128)S(1)}, u32[]{:S(2)}, u32[]{:S(2)}) collective-permute-start(f32[32,128]{1,0:T(8,128)} %get-tuple-element.120), channel_id=1, source_target_pairs={{0,11},{1,10},{2,9},{3,8},{4,15},{5,14},{6,13},{7,12},{8,3},{9,2},... | collective-permute-start | bytes 49160 | tf_op jit(solution)/shard_map/ppermute | solution.py:558
  64.1 16.9 %collective-permute-start.26 = (f32[32,128]{1,0:T(8,128)}, f32[32,128]{1,0:T(8,128)S(1)}, u32[]{:S(2)}, u32[]{:S(2)}) collective-permute-start(f32[32,128]{1,0:T(8,128)} %get-tuple-element.121), channel_id=1, source_target_pairs={{0,12},{1,13},{2,14},{3,15},{4,8},{5,9},{6,10},{7,11},{8,4},{9,5},... | collective-permute-start | bytes 49160 | tf_op jit(solution)/shard_map/ppermute | solution.py:558
  67.5 13.5 %collective-permute-start.27 = (f32[32,128]{1,0:T(8,128)}, f32[32,128]{1,0:T(8,128)S(1)}, u32[]{:S(2)}, u32[]{:S(2)}) collective-permute-start(f32[32,128]{1,0:T(8,128)} %get-tuple-element.122), channel_id=1, source_target_pairs={{0,13},{1,12},{2,15},{3,14},{4,9},{5,8},{6,11},{7,10},{8,5},{9,4},... | collective-permute-start | bytes 49160 | tf_op jit(solution)/shard_map/ppermute | solution.py:558
  67.9 13.1 %collective-permute-start.28 = (f32[32,128]{1,0:T(8,128)}, f32[32,128]{1,0:T(8,128)S(1)}, u32[]{:S(2)}, u32[]{:S(2)}) collective-permute-start(f32[32,128]{1,0:T(8,128)} %get-tuple-element.123), channel_id=1, source_target_pairs={{0,14},{1,15},{2,12},{3,13},{4,10},{5,11},{6,8},{7,9},{8,6},{9,7},... | collective-permute-start | bytes 49160 | tf_op jit(solution)/shard_map/ppermute | solution.py:558
  72.3 8.8 %collective-permute-start.29 = (f32[32,128]{1,0:T(8,128)}, f32[32,128]{1,0:T(8,128)S(1)}, u32[]{:S(2)}, u32[]{:S(2)}) collective-permute-start(f32[32,128]{1,0:T(8,128)} %get-tuple-element.124), channel_id=1, source_target_pairs={{0,15},{1,14},{2,13},{3,12},{4,11},{5,10},{6,9},{7,8},{8,7},{9,6},... | collective-permute-start | bytes 49160 | tf_op jit(solution)/shard_map/ppermute | solution.py:558
  94.6 4.0 %collective-permute-start.30 = (f32[48,128]{1,0:T(8,128)}, f32[48,128]{1,0:T(8,128)S(1)}, u32[]{:S(2)}, u32[]{:S(2)}) collective-permute-start(f32[48,128]{1,0:T(8,128)} %get-tuple-element.128), channel_id=1, source_target_pairs={{0,1},{1,0},{2,3},{3,2},{4,5},{5,4},{6,7},{7,6},{8,9},{9,8},{10,11... | collective-permute-start | bytes 73736 | tf_op jit(solution)/shard_map/ppermute | solution.py:558
  95.1 4.8 %collective-permute-start.31 = (f32[48,128]{1,0:T(8,128)}, f32[48,128]{1,0:T(8,128)S(1)}, u32[]{:S(2)}, u32[]{:S(2)}) collective-permute-start(f32[48,128]{1,0:T(8,128)} %get-tuple-element.129), channel_id=1, source_target_pairs={{0,2},{1,3},{2,0},{3,1},{4,6},{5,7},{6,4},{7,5},{8,10},{9,11},{10,... | collective-permute-start | bytes 73736 | tf_op jit(solution)/shard_map/ppermute | solution.py:558
  96.7 4.4 %collective-permute-start.32 = (f32[48,128]{1,0:T(8,128)}, f32[48,128]{1,0:T(8,128)S(1)}, u32[]{:S(2)}, u32[]{:S(2)}) collective-permute-start(f32[48,128]{1,0:T(8,128)} %get-tuple-element.130), channel_id=1, source_target_pairs={{0,3},{1,2},{2,1},{3,0},{4,7},{5,6},{6,5},{7,4},{8,11},{9,10},{10,... | collective-permute-start | bytes 73736 | tf_op jit(solution)/shard_map/ppermute | solution.py:558
  96.7 7.0 %collective-permute-start.33 = (f32[48,128]{1,0:T(8,128)}, f32[48,128]{1,0:T(8,128)S(1)}, u32[]{:S(2)}, u32[]{:S(2)}) collective-permute-start(f32[48,128]{1,0:T(8,128)} %get-tuple-element.131), channel_id=1, source_target_pairs={{0,4},{1,5},{2,6},{3,7},{4,0},{5,1},{6,2},{7,3},{8,12},{9,13},{10,... | collective-permute-start | bytes 73736 | tf_op jit(solution)/shard_map/ppermute | solution.py:558
  96.7 7.4 %collective-permute-start.34 = (f32[48,128]{1,0:T(8,128)}, f32[48,128]{1,0:T(8,128)S(1)}, u32[]{:S(2)}, u32[]{:S(2)}) collective-permute-start(f32[48,128]{1,0:T(8,128)} %get-tuple-element.132), channel_id=1, source_target_pairs={{0,5},{1,4},{2,7},{3,6},{4,1},{5,0},{6,3},{7,2},{8,13},{9,12},{10,... | collective-permute-start | bytes 73736 | tf_op jit(solution)/shard_map/ppermute | solution.py:558
  98.6 8.6 %collective-permute-start.35 = (f32[48,128]{1,0:T(8,128)}, f32[48,128]{1,0:T(8,128)S(1)}, u32[]{:S(2)}, u32[]{:S(2)}) collective-permute-start(f32[48,128]{1,0:T(8,128)} %get-tuple-element.133), channel_id=1, source_target_pairs={{0,6},{1,7},{2,4},{3,5},{4,2},{5,3},{6,0},{7,1},{8,14},{9,15},{10,... | collective-permute-start | bytes 73736 | tf_op jit(solution)/shard_map/ppermute | solution.py:558
  99.9 7.5 %collective-permute-start.36 = (f32[48,128]{1,0:T(8,128)}, f32[48,128]{1,0:T(8,128)S(1)}, u32[]{:S(2)}, u32[]{:S(2)}) collective-permute-start(f32[48,128]{1,0:T(8,128)} %get-tuple-element.134), channel_id=1, source_target_pairs={{0,7},{1,6},{2,5},{3,4},{4,3},{5,2},{6,1},{7,0},{8,15},{9,14},{10,... | collective-permute-start | bytes 73736 | tf_op jit(solution)/shard_map/ppermute | solution.py:558
  101.1 9.6 %collective-permute-start.37 = (f32[48,128]{1,0:T(8,128)}, f32[48,128]{1,0:T(8,128)S(1)}, u32[]{:S(2)}, u32[]{:S(2)}) collective-permute-start(f32[48,128]{1,0:T(8,128)} %get-tuple-element.135), channel_id=1, source_target_pairs={{0,8},{1,9},{2,10},{3,11},{4,12},{5,13},{6,14},{7,15},{8,0},{9,1},... | collective-permute-start | bytes 73736 | tf_op jit(solution)/shard_map/ppermute | solution.py:558
  103.7 7.5 %collective-permute-start.38 = (f32[48,128]{1,0:T(8,128)}, f32[48,128]{1,0:T(8,128)S(1)}, u32[]{:S(2)}, u32[]{:S(2)}) collective-permute-start(f32[48,128]{1,0:T(8,128)} %get-tuple-element.136), channel_id=1, source_target_pairs={{0,9},{1,8},{2,11},{3,10},{4,13},{5,12},{6,15},{7,14},{8,1},{9,0},... | collective-permute-start | bytes 73736 | tf_op jit(solution)/shard_map/ppermute | solution.py:558
  104.1 11.4 %collective-permute-start.39 = (f32[48,128]{1,0:T(8,128)}, f32[48,128]{1,0:T(8,128)S(1)}, u32[]{:S(2)}, u32[]{:S(2)}) collective-permute-start(f32[48,128]{1,0:T(8,128)} %get-tuple-element.137), channel_id=1, source_target_pairs={{0,10},{1,11},{2,8},{3,9},{4,14},{5,15},{6,12},{7,13},{8,2},{9,3},... | collective-permute-start | bytes 73736 | tf_op jit(solution)/shard_map/ppermute | solution.py:558
  107.2 8.3 %collective-permute-start.40 = (f32[48,128]{1,0:T(8,128)}, f32[48,128]{1,0:T(8,128)S(1)}, u32[]{:S(2)}, u32[]{:S(2)}) collective-permute-start(f32[48,128]{1,0:T(8,128)} %get-tuple-element.138), channel_id=1, source_target_pairs={{0,11},{1,10},{2,9},{3,8},{4,15},{5,14},{6,13},{7,12},{8,3},{9,2},... | collective-permute-start | bytes 73736 | tf_op jit(solution)/shard_map/ppermute | solution.py:558
  107.4 8.1 %collective-permute-start.41 = (f32[48,128]{1,0:T(8,128)}, f32[48,128]{1,0:T(8,128)S(1)}, u32[]{:S(2)}, u32[]{:S(2)}) collective-permute-start(f32[48,128]{1,0:T(8,128)} %get-tuple-element.139), channel_id=1, source_target_pairs={{0,12},{1,13},{2,14},{3,15},{4,8},{5,9},{6,10},{7,11},{8,4},{9,5},... | collective-permute-start | bytes 73736 | tf_op jit(solution)/shard_map/ppermute | solution.py:558
  110.7 5.3 %collective-permute-start.42 = (f32[48,128]{1,0:T(8,128)}, f32[48,128]{1,0:T(8,128)S(1)}, u32[]{:S(2)}, u32[]{:S(2)}) collective-permute-start(f32[48,128]{1,0:T(8,128)} %get-tuple-element.140), channel_id=1, source_target_pairs={{0,13},{1,12},{2,15},{3,14},{4,9},{5,8},{6,11},{7,10},{8,5},{9,4},... | collective-permute-start | bytes 73736 | tf_op jit(solution)/shard_map/ppermute | solution.py:558
  111.2 6.7 %collective-permute-start.43 = (f32[48,128]{1,0:T(8,128)}, f32[48,128]{1,0:T(8,128)S(1)}, u32[]{:S(2)}, u32[]{:S(2)}) collective-permute-start(f32[48,128]{1,0:T(8,128)} %get-tuple-element.141), channel_id=1, source_target_pairs={{0,14},{1,15},{2,12},{3,13},{4,10},{5,11},{6,8},{7,9},{8,6},{9,7},... | collective-permute-start | bytes 73736 | tf_op jit(solution)/shard_map/ppermute | solution.py:558
  115.5 6.4 %collective-permute-start.44 = (f32[48,128]{1,0:T(8,128)}, f32[48,128]{1,0:T(8,128)S(1)}, u32[]{:S(2)}, u32[]{:S(2)}) collective-permute-start(f32[48,128]{1,0:T(8,128)} %get-tuple-element.142), channel_id=1, source_target_pairs={{0,15},{1,14},{2,13},{3,12},{4,11},{5,10},{6,9},{7,8},{8,7},{9,6},... | collective-permute-start | bytes 73736 | tf_op jit(solution)/shard_map/ppermute | solution.py:558
  (44 other events, 533.3 us)

commit v5 on v2

--- a/solution.py
+++ b/solution.py
@@ -22,7 +22,7 @@
 MIB = 1 << 20
 LANES = 128
 GROUP = 4
-STEP = 16
+STEP = 8
 
 
 def kept(kept_count, length):
@@ -362,77 +362,132 @@
     )(summing, turned, bias, field)
 
 
-def cell_kernel(
-    inv_y, inv_z, inv_z_low, z_high, z_low, y_both, sum_ref, modes_ref, pre_ref, cot_ref, field_hbm,
-    act_ref, out_ref, field_ref, slope_ref, sem, *, channels, step_channels, rows, owners,
-):
-    step = pl.program_id(0)
-    copy = pltpu.make_async_copy(field_hbm, field_ref, sem)
-
-    @pl.when(step == 0)
-    def _():
-        copy.start()
-
-    first = step * step_channels
+def cell_group(inv_y, inv_z, inv_z_low, modes_ref, pre_ref, cot_ref, act_ref, first, count, channels):
     lines = []
-    for g in range(0, step_channels, GROUP):
-        lines += inverse_y_group(modes_ref, inv_y[...], first + g, channels)
+    for g in range(0, count, GROUP):
+        lines += inverse_y_group(modes_ref, inv_y, first + g, channels)
     high, low = split(jnp.concatenate(lines, axis=0))
-    spectral = dot(jnp.concatenate([high, low], axis=1), inv_z[...]) + dot(high, inv_z_low[...])
+    spectral = dot(jnp.concatenate([high, low], axis=1), inv_z) + dot(high, inv_z_low)
     slopes = []
-    for q in range(step_channels):
+    for q in range(count):
         r = q // 2 * NY
         c = q % 2 * NZ
         before = spectral[r : r + NY, c : c + NZ] + pre_ref[q]
         cdf = 0.5 + 0.5 * lax.erf(before * INV_SQRT_TWO)
         act_ref[q] = (before * cdf).astype(BF16)
         pdf = jnp.exp(-0.5 * before * before) * INV_SQRT_TWO_PI
-        slope = cot_ref[q].astype(F32) * (cdf + before * pdf)
-        slopes.append(slope)
-        slope_ref[first + q] = slope
-    forward_group(slopes, z_high[...], z_low[...], y_both[...], out_ref, first, rows)
+        slopes.append(cot_ref[q].astype(F32) * (cdf + before * pdf))
+    return slopes
+
+
+def early_cell_kernel(
+    inv_y, inv_z, inv_z_low, z_high, z_low, y_both, modes_ref, pre_ref, cot_ref, act_ref, slope_ref, out_ref,
+    *, channels, count, rows,
+):
+    step = pl.program_id(0)
+    slopes = cell_group(
+        inv_y[...], inv_z[...], inv_z_low[...], modes_ref, pre_ref, cot_ref, act_ref, step * count, count, channels
+    )
+    for q in range(count):
+        slope_ref[q] = slopes[q]
+    forward_group(slopes, z_high[...], z_low[...], y_both[...], out_ref, step * count, rows)
+
+
+def point_gradient(field_ref, slope_ref, sum_ref, channels):
+    size = 8 * channels
+    total = jnp.zeros((size, size), F32)
+    for b in range(NY // 8):
+        at = slice(8 * b, 8 * b + 8)
+        f_h, f_l = split(field_ref[:, at, :].reshape(size, NZ))
+        s_h, s_l = split(slope_ref[:, at, :].reshape(size, NZ))
+        total += lax.dot_general(
+            jnp.concatenate([f_h, f_h, f_l], axis=1),
+            jnp.concatenate([s_h, s_l, s_h], axis=1),
+            (((1,), (1,)), ((), ())),
+            preferred_element_type=F32,
+        )
+    row = lax.broadcasted_iota(jnp.int32, (size, size), 0) % 8
+    total = jnp.where(row == lane_index((size, size)) % 8, total, 0.0)
+    return exact_dot(jnp.sum(total.reshape(channels, 8, size), axis=1), sum_ref[...])
+
+
+def late_cell_kernel(
+    inv_y, inv_z, inv_z_low, z_high, z_low, y_both, sum_ref, modes_ref, pre_ref, cot_ref, early_ref,
+    slope_hbm, field_hbm, _, act_ref, out_ref, field_ref, slope_ref, sems, *, channels, count, rows, owners,
+):
+    step = pl.program_id(0)
+    half = channels // 2
+    copies = [
+        pltpu.make_async_copy(field_hbm, field_ref, sems.at[0]),
+        pltpu.make_async_copy(slope_hbm, slope_ref.at[pl.ds(0, half)], sems.at[1]),
+    ]
+
+    @pl.when(step == 0)
+    def _():
+        for copy in copies:
+            copy.start()
+
+    first = half + step * count
+    slopes = cell_group(
+        inv_y[...], inv_z[...], inv_z_low[...], modes_ref, pre_ref, cot_ref, act_ref, first, count, channels
+    )
+    for q in range(count):
+        slope_ref[first + q] = slopes[q]
+    forward_group(slopes, z_high[...], z_low[...], y_both[...], out_ref, step * count, rows)
 
     @pl.when(step == pl.num_programs(0) - 1)
     def _():
-        copy.wait()
-        size = 8 * channels
-        total = jnp.zeros((size, size), F32)
-        for b in range(NY // 8):
-            at = slice(8 * b, 8 * b + 8)
-            f_h, f_l = split(field_ref[:, at, :].reshape(size, NZ))
-            s_h, s_l = split(slope_ref[:, at, :].reshape(size, NZ))
-            total += lax.dot_general(
-                jnp.concatenate([f_h, f_h, f_l], axis=1),
-                jnp.concatenate([s_h, s_l, s_h], axis=1),
-                (((1,), (1,)), ((), ())),
-                preferred_element_type=F32,
-            )
-        row = lax.broadcasted_iota(jnp.int32, (size, size), 0) % 8
-        total = jnp.where(row == lane_index((size, size)) % 8, total, 0.0)
-        folded = jnp.sum(total.reshape(channels, 8, size), axis=1)
-        point = exact_dot(folded, sum_ref[...])
+        for copy in copies:
+            copy.wait()
+        point = point_gradient(field_ref, slope_ref, sum_ref, channels)
         packed = jnp.concatenate([point[8 * q : 8 * q + 8] for q in range(channels // 8)], axis=1)
-        dc = jnp.broadcast_to(out_ref[0:channels, 0:1], (channels, LANES))
+        zero_mode = jnp.concatenate([early_ref[0:half, 0:1], out_ref[0:half, 0:1]], axis=0)
         eye = lax.broadcasted_iota(jnp.int32, (channels, LANES), 0) == lane_index((channels, LANES))
-        bias = jnp.sum(jnp.where(eye, dc, 0.0), axis=0, keepdims=True)
+        bias = jnp.sum(jnp.where(eye, jnp.broadcast_to(zero_mode, (channels, LANES)), 0.0), axis=0, keepdims=True)
         extra = jnp.where(lax.broadcasted_iota(jnp.int32, (8, LANES), 0) == 0, jnp.broadcast_to(bias, (8, LANES)), 0.0)
         for d in range(owners):
-            out_ref[d * rows + channels : d * rows + channels + 8, :] = packed
-            out_ref[d * rows + channels + 8 : (d + 1) * rows, :] = extra
-
-
-def cell_stage(inverse, forward, summing, modes, pre, cotangent, field):
+            out_ref[d * rows + half : d * rows + half + 8, :] = packed
+            out_ref[d * rows + half + 8 : (d + 1) * rows, :] = extra
+
+
+def early_cells(inverse, forward, modes, pre, cotangent):
+    channels = pre.shape[0]
+    owners = MY // 2
+    half = channels // 2
+    block = pl.BlockSpec((STEP, NY, NZ), lambda s: (s, 0, 0))
+    tables = (*inverse, *forward)
+    act, slope, out = pl.pallas_call(
+        functools.partial(early_cell_kernel, channels=channels, count=STEP, rows=half),
+        grid=(half // STEP,),
+        in_specs=[full(t.shape) for t in tables] + [full((owners * channels, LANES)), block, block],
+        out_specs=[block, block, full((owners * half, LANES))],
+        out_shape=[
+            jax.ShapeDtypeStruct((channels, NY, NZ), BF16),
+            jax.ShapeDtypeStruct((half, NY, NZ), F32),
+            jax.ShapeDtypeStruct((owners * half, LANES), F32),
+        ],
+        compiler_params=params(60),
+        cost_estimate=pl.CostEstimate(flops=3 * 10**9, bytes_accessed=7 * MIB, transcendentals=10**6),
+        name="early_cells",
+    )(*tables, modes.reshape(owners * channels, LANES), pre, cotangent)
+    return act, slope, out.reshape(owners, half, LANES)
+
+
+def late_cells(inverse, forward, summing, modes, pre, cotangent, field, early, slope, act):
     channels = field.shape[0]
     owners = MY // 2
-    rows = channels + 16
-    step_channels = STEP
-    block = pl.BlockSpec((step_channels, NY, NZ), lambda s: (s, 0, 0))
+    half = channels // 2
+    rows = half + 16
+    start = half // STEP
+    block = pl.BlockSpec((STEP, NY, NZ), lambda s: (start + s, 0, 0))
+    anywhere = pl.BlockSpec(memory_space=pl.ANY)
     tables = (*inverse, *forward, summing)
     act, out = pl.pallas_call(
-        functools.partial(cell_kernel, channels=channels, step_channels=step_channels, rows=rows, owners=owners),
-        grid=(channels // step_channels,),
+        functools.partial(late_cell_kernel, channels=channels, count=STEP, rows=rows, owners=owners),
+        grid=(start,),
         in_specs=[full(t.shape) for t in tables]
-        + [full((owners * channels, LANES)), block, block, pl.BlockSpec(memory_space=pl.ANY)],
+        + [full((owners * channels, LANES)), block, block, full((owners * half, LANES))]
+        + [anywhere] * 3,
         out_specs=[block, full((owners * rows, LANES))],
         out_shape=[
             jax.ShapeDtypeStruct((channels, NY, NZ), BF16),
@@ -441,34 +496,37 @@
         scratch_shapes=[
             pltpu.VMEM((channels, NY, NZ), F32),
             pltpu.VMEM((channels, NY, NZ), F32),
-            pltpu.SemaphoreType.DMA,
+            pltpu.SemaphoreType.DMA((2,)),
         ],
+        input_output_aliases={len(tables) + 6: 0},
         compiler_params=params(60),
-        cost_estimate=pl.CostEstimate(flops=8 * 10**9, bytes_accessed=12 * MIB, transcendentals=2 * 10**6),
-        name="cells",
-    )(*tables, modes.reshape(owners * channels, LANES), pre, cotangent, field)
+        cost_estimate=pl.CostEstimate(flops=6 * 10**9, bytes_accessed=11 * MIB, transcendentals=10**6),
+        name="late_cells",
+    )(
+        *tables, modes.reshape(owners * channels, LANES), pre, cotangent, early.reshape(owners * half, LANES),
+        slope, field, act,
+    )
     return act, out.reshape(owners, rows, LANES)
 
 
-def gradient_kernel(
-    cos_ref, sin_ref, spec_ref, lines_ref, out_hbm, point_ref, bias_ref,
-    sums_ref, real_ref, imag_ref, buffer, sems, *, points, channels, unique, copies, norm,
-):
-    halve_lines(lines_ref, sums_ref, points, channels)
+def gradient_kernel(cos_ref, sin_ref, spec_ref, lines_ref, *refs, points, channels, unique, copies, norm, part):
+    if part == 1:
+        _, out_hbm, point_ref, bias_ref, sums_ref, real_ref, imag_ref, buffer, sems = refs
+    else:
+        out_hbm, sums_ref, real_ref, imag_ref, buffer, sems = refs
+    outputs = channels // 2
+    halve_lines(lines_ref, sums_ref, points, outputs)
     half = LANES // 2
-    lane = lane_index((channels, LANES))
+    lane = lane_index((outputs, LANES))
     scale = jnp.where(lane % MZ == 0, norm, 2.0 * norm)
-    packed = lines_ref[0, channels : channels + 16, :]
-    for x in range(1, points):
-        packed += lines_ref[x, channels : channels + 16, :]
-    packed = norm * packed
-    for q in range(channels // 8):
-        point_ref[8 * q : 8 * q + 8, :] = packed[:8, q * channels : (q + 1) * channels]
-    bias_ref[...] = packed[8:9, :channels]
 
     def writes(at, slot):
         return [
-            pltpu.make_async_copy(buffer.at[slot], out_hbm.at[:, at + r * unique], sems.at[slot, r])
+            pltpu.make_async_copy(
+                buffer.at[slot],
+                out_hbm.at[:, at + r * unique, :, pl.ds(part * outputs, outputs), :],
+                sems.at[slot, r],
+            )
             for r in range(copies)
         ]
 
@@ -493,37 +551,47 @@
             for copy in writes(at, slot):
                 copy.start()
 
+    if part == 1:
+        packed = lines_ref[0, outputs : outputs + 16, :]
+        for x in range(1, points):
+            packed += lines_ref[x, outputs : outputs + 16, :]
+        packed = norm * packed
+        for q in range(channels // 8):
+            point_ref[8 * q : 8 * q + 8, :] = packed[:8, q * channels : (q + 1) * channels]
+        bias_ref[...] = packed[8:9, :channels]
+
     for at in range(unique - 2, unique):
         for copy in writes(at, at % 2):
             copy.wait()
 
 
-def gradient(cos_x, sin_x, spectrum, lines, norm, kept_x):
+def gradient(cos_x, sin_x, spectrum, lines, norm, kept_x, part, before=()):
     points, rows, _ = lines.shape
     unique, channels, _ = spectrum.shape
     half = LANES // 2
     copies = kept_x // unique
-    flat = (channels, LANES)
+    anywhere = pl.BlockSpec(memory_space=pl.ANY)
+    shape = jax.ShapeDtypeStruct((2, kept_x, channels, channels, half), F32)
+    sums = [(channels, channels), (1, channels)] if part == 1 else []
     return pl.pallas_call(
-        functools.partial(gradient_kernel, points=points, channels=channels, unique=unique, copies=copies, norm=norm),
-        in_specs=[smem(), smem(), full(spectrum.shape), full(lines.shape)],
-        out_specs=[pl.BlockSpec(memory_space=pl.ANY), full((channels, channels)), full((1, channels))],
-        out_shape=[
-            jax.ShapeDtypeStruct((2, kept_x, channels, channels, half), F32),
-            jax.ShapeDtypeStruct((channels, channels), F32),
-            jax.ShapeDtypeStruct((1, channels), F32),
-        ],
+        functools.partial(
+            gradient_kernel, points=points, channels=channels, unique=unique, copies=copies, norm=norm, part=part
+        ),
+        in_specs=[smem(), smem(), full(spectrum.shape), full(lines.shape)] + [anywhere] * len(before),
+        out_specs=[anywhere] + [full(each) for each in sums],
+        out_shape=[shape] + [jax.ShapeDtypeStruct(each, F32) for each in sums],
         scratch_shapes=[
-            pltpu.VMEM((2, 2, points // 2, channels, LANES), F32),
-            pltpu.VMEM((2,) + flat, F32),
-            pltpu.VMEM((2,) + flat, F32),
-            pltpu.VMEM((2, 2, channels, channels, half), F32),
+            pltpu.VMEM((2, 2, points // 2, channels // 2, LANES), F32),
+            pltpu.VMEM((2, channels, LANES), F32),
+            pltpu.VMEM((2, channels, LANES), F32),
+            pltpu.VMEM((2, 2, channels, channels // 2, half), F32),
             pltpu.SemaphoreType.DMA((2, copies)),
         ],
+        input_output_aliases={4: 0} if before else {},
         compiler_params=params(60),
-        cost_estimate=pl.CostEstimate(flops=10**7, bytes_accessed=40 * MIB, transcendentals=0),
+        cost_estimate=pl.CostEstimate(flops=5 * 10**6, bytes_accessed=32 * MIB, transcendentals=0),
         name="weight_gradient",
-    )(cos_x, sin_x, spectrum, lines)
+    )(cos_x, sin_x, spectrum, lines, *before)
 
 
 def swap(lines):
@@ -569,9 +637,12 @@
     field_late, mixed = lax.optimization_barrier((field, mixed))
     modes = swap(mixed)
     pre = pointwise(field_late, summing, point_weights, point_bias)
-    activated, slope_lines = cell_stage(inverse, forward, summing, modes, pre, slopes_in, field)
-    slope_lines = swap(slope_lines)
-    grad, grad_point, grad_bias = gradient(cos_x, sin_x, spectrum, slope_lines, norm, MX)
+    act, slope, early = early_cells(inverse, forward, modes, pre, slopes_in)
+    early_lines = swap(early)
+    activated, late = late_cells(inverse, forward, summing, modes, pre, slopes_in, field, early, slope, act)
+    late_lines = swap(late)
+    (grad,) = gradient(cos_x, sin_x, spectrum, early_lines, norm, MX, 0)
+    grad, grad_point, grad_bias = gradient(cos_x, sin_x, spectrum, late_lines, norm, MX, 1, (grad,))
     return (
         activated.reshape(cotangent.shape),
         jnp.transpose(grad, (0, 1, 4, 2, 3)),

time: 98.9 us -> 104 us (1.052)
  blocking collectives: 18.3 us -> 0 us
  starting transfers between devices: 13.2 us -> 25.2 us
  Pallas kernels: 63 us -> 73.9 us
    all_to_all x1 -> x0, blocking collectives: 18.3 us -> none  [swap(): lax.all_to_all(lines, 'space', split_axis=0, concat_axis=0, tiled=True)]
    all_to_all x2 -> x4, starting transfers between devices: 13.2 us -> 25.2 us  [swap(): lax.all_to_all(lines, 'space', split_axis=0, concat_axis=0, tiled=True)]
    pallas_call x1 -> x2, Pallas kernels: 15.4 us -> 22.5 us  [gradient(): pl.pallas_call(functools.partial(gradient_kernel, points=points, channels...]
    pallas_call x1 -> x2, Pallas kernels: 12.7 us -> 16.4 us  [the longest x1 9.34 us: late_cells(): pl.pallas_call(functools.partial(late_cell_kernel, channels=channels, cou...]
    unnamed x9 -> x13, local copies, waits for them, and re-layouts: 2.08 us -> 2.82 us
  transfers between devices with their start and end apart: 2 -> 4, of which waited for: 1 -> 1; matrix products, arithmetic and copies ran while one was open for 1% -> 1% of each run, Pallas kernels for 19% -> 38%
where the time goes in v5:
time: 104 us
  Pallas kernels  73.9 us (71%)
  starting transfers between devices  25.2 us (24%)
  local copies, waits for them, and re-layouts  3.51 us (3%)
    all_to_all x4, starting transfers between devices, swap(): lax.all_to_all(lines, 'space', split_axis=0, concat_axis=0, tiled=True)  25.2 us
    pallas_call x2, Pallas kernels, gradient(): pl.pallas_call(functools.partial(gradient_kernel, points=points, channels...  22.5 us
    pallas_call x1, Pallas kernels, forward_modes(): pl.pallas_call(functools.partial(forward_kernel, channels=channels, step_...  10.5 us
    pallas_call x1, Pallas kernels, fold_rest(): pl.pallas_call(fold_kernel, grid=(unique - first,), in_specs=pieces + [pl...  9.87 us
    pallas_call x1, Pallas kernels, late_cells(): pl.pallas_call(functools.partial(late_cell_kernel, channels=channels, cou...  9.34 us
    pallas_call x1, Pallas kernels, pointwise(): pl.pallas_call(functools.partial(pointwise_kernel, channels=channels, blo...  8.68 us
    pallas_call x1, Pallas kernels, early_cells(): pl.pallas_call(functools.partial(early_cell_kernel, channels=channels, co...  7.06 us
    pallas_call x1, Pallas kernels, mix(): pl.pallas_call(functools.partial(mix_kernel, points=points, channels=chan...  5.9 us
  transfers between devices with their start and end apart: 4, of which 1 were waited for; matrix products, arithmetic and copies ran while one was open for 1% of the time, Pallas kernels for 38%

profile of v5, /device:TPU:0, one launch (start us, length us, event | category | flops | bytes accessed | tf_op | source)
XLA Modules:
  0.0 103.5 jit_solution(7841363429660905202)
XLA Ops:
  0.6 10.5 %forward_yz.1 = (f32[512,128]{1,0:T(8,128)}, f32[16,32,32,128]{3,2,1,0:T(8,128)}) custom-call(bf16[512,256]{1,0:T(8,128)(2,1)} %constant.21.clone.z_high, bf16[512,256]{1,0:T(8,128)(2,1)} %constant.22.clone.z_low, bf16[64,256]{1,0:T(8,128)(2,1)} %constant.23.clone.y_both, f32[32,128,256]{2,1,0:T(8,128)} %bitcast.19, f32[2,32,32,32,64]{4,3,2,1,0:T(8,128)} %bitcast.14, ...), custom_call_target="tpu_custom_call" | custom-call | flops 2000000000 | bytes 27262976 | tf_op jit(solution)/shard_map/forward_yz/pallas_call | solution.py:183
  11.1 7.4 %all-to-all-start = ((f32[16,32,128]{2,1,0:T(8,128)}), f32[16,32,128]{2,1,0:T(8,128)S(1)}, u32[]{:S(2)}, u32[]{:S(2)}) async-start(f32[16,32,128]{2,1,0:T(8,128)} %bitcast.25), calls=%async_computation | async-start | bytes 524288 | tf_op jit(solution)/shard_map/all_to_all | solution.py:598
  18.5 9.9 %fold_weights.1.weights_ref = f32[16,32,32,128]{3,2,1,0:T(8,128)} custom-call(f32[2,32,32,32,64]{4,3,2,1,0:T(8,128)} %bitcast.16, f32[2,32,32,32,64]{4,3,2,1,0:T(8,128)} %bitcast.17, f32[16,32,32,128]{3,2,1,0:T(8,128)} %get-tuple-element.19.refs_2_), custom_call_target="tpu_custom_call", output_to_operand_aliasing={{}: (2, {})} | custom-call | flops 4000000 | bytes 20971520 | tf_op jit(solution)/shard_map/fold_weights/pallas_call | solution.py:206
  28.4 0.0 copy-start.4
  28.4 0.0 copy-start.5
  28.4 0.2 all-to-all-done.lines_ref
  28.6 0.0 copy-start.1
  28.6 0.7 copy-done.1
  29.3 5.9 %mix_modes.1 = (f32[16,32,128]{2,1,0:T(8,128)}, f32[16,32,128]{2,1,0:T(8,128)}) custom-call(f32[16,16]{1,0:T(8,128)} %constant.18.clone.cos_ref, f32[16,16]{1,0:T(8,128)} %constant.19.clone.sin_ref, f32[16,32,128]{2,1,0:T(8,128)} %copy-done.1, f32[16,32,32,128]{3,2,1,0:T(8,128)} %fold_weights.1.weights_ref), custom_call_target="tpu_custom_call" | custom-call | flops 20000000 | bytes 9437184 | tf_op jit(solution)/shard_map/mix_modes/pallas_call | solution.py:290
  35.2 5.8 %all-to-all-start.1 = ((f32[16,32,128]{2,1,0:T(8,128)}), f32[16,32,128]{2,1,0:T(8,128)S(1)}, u32[]{:S(2)}, u32[]{:S(2)}) async-start(f32[16,32,128]{2,1,0:T(8,128)} %get-tuple-element.21), calls=%async_computation.1 | async-start | bytes 524288 | tf_op jit(solution)/shard_map/all_to_all | solution.py:598
  41.0 0.0 copy-done.4
  41.0 0.7 copy.21
  41.7 0.0 copy-done.5
  41.7 0.7 copy.22.bias_in_ref
  42.4 8.7 %pointwise.1.pre_ref = f32[32,128,256]{2,1,0:T(8,128)} custom-call(f32[256,32]{1,0:T(8,128)} %constant.20.clone.sum_ref, f32[32,32]{1,0:T(8,128)} %bitcast.27, f32[32,1]{1,0:T(8,128)} %copy.22.bias_in_ref, f32[32,128,256]{2,1,0:T(8,128)} %bitcast.20), custom_call_target="tpu_custom_call" | custom-call | flops 4000000000 | bytes 25165824 | tf_op jit(solution)/shard_map/pointwise/pallas_call | solution.py:352
  51.1 0.0 all-to-all-done.1
  51.1 0.0 copy-start.3
  51.1 0.7 copy-done.3
  51.8 7.1 %early_cells.1 = (bf16[32,128,256]{2,1,0:T(8,128)(2,1)}, f32[16,128,256]{2,1,0:T(8,128)}, f32[256,128]{1,0:T(8,128)}) custom-call(bf16[128,192]{1,0:T(8,128)(2,1)} %constant.24.clone.inv_y, bf16[256,512]{1,0:T(8,128)(2,1)} %constant.25.clone.inv_z, bf16[128,512]{1,0:T(8,128)(2,1)} %constant.26.clone.inv_z_low, bf16[512,256]{1,0:T(8,128)(2,1)} %constant.21.clone.z_high, ...), custom_call_target="tpu_custom_call" | custom-call | flops 3000000000 | bytes 7340032 | tf_op jit(solution)/shard_map/early_cells/pallas_call | solution.py:459
  58.9 6.0 %all-to-all-start.3 = ((f32[16,16,128]{2,1,0:T(8,128)}), f32[16,16,128]{2,1,0:T(8,128)S(1)}, u32[]{:S(2)}, u32[]{:S(2)}) async-start(f32[16,16,128]{2,1,0:T(8,128)} %bitcast.26), calls=%async_computation.3 | async-start | bytes 262144 | tf_op jit(solution)/shard_map/all_to_all | solution.py:598
  64.9 9.3 %late_cells.1 = (bf16[32,128,256]{2,1,0:T(8,128)(2,1)}, f32[512,128]{1,0:T(8,128)}) custom-call(bf16[128,192]{1,0:T(8,128)(2,1)} %constant.24.clone.inv_y, bf16[256,512]{1,0:T(8,128)(2,1)} %constant.25.clone.inv_z, bf16[128,512]{1,0:T(8,128)(2,1)} %constant.26.clone.inv_z_low, ...), custom_call_target="tpu_custom_call", output_to_operand_aliasing={{0}: (13, {})} | custom-call | flops 6000000000 | bytes 11534336 | tf_op jit(solution)/shard_map/late_cells/pallas_call | solution.py:485
  74.2 0.0 all-to-all-done.3.lines_ref
  74.2 0.0 copy-start.2
  74.2 6.0 %all-to-all-start.2 = ((f32[16,32,128]{2,1,0:T(8,128)}), f32[16,32,128]{2,1,0:T(8,128)S(1)}, u32[]{:S(2)}, u32[]{:S(2)}) async-start(f32[16,32,128]{2,1,0:T(8,128)} %bitcast.24), calls=%async_computation.2 | async-start | bytes 524288 | tf_op jit(solution)/shard_map/all_to_all | solution.py:598
  80.2 0.0 copy-done.2
  80.3 10.9 %weight_gradient.2.refs_0_ = f32[2,32,32,32,64]{4,3,2,1,0:T(8,128)} custom-call(f32[16,16]{1,0:T(8,128)} %constant.18.clone.cos_ref, f32[16,16]{1,0:T(8,128)} %constant.19.clone.sin_ref, f32[16,32,128]{2,1,0:T(8,128)} %get-tuple-element.27.spec_ref, f32[16,16,128]{2,1,0:T(8,128)} %copy-done.2), custom_call_target="tpu_custom_call" | custom-call | flops 5000000 | bytes 33554432 | tf_op jit(solution)/shard_map/weight_gradient/pallas_call | solution.py:576
  91.2 0.0 all-to-all-done.2.lines_ref
  91.2 0.0 copy-start
  91.2 0.7 copy-done
  91.9 11.6 %weight_gradient.3 = (f32[2,32,32,32,64]{4,3,2,1,0:T(8,128)}, f32[32,32]{1,0:T(8,128)}, f32[1,32]{1,0:T(1,128)}) custom-call(f32[16,16]{1,0:T(8,128)} %constant.18.clone.cos_ref, f32[16,16]{1,0:T(8,128)} %constant.19.clone.sin_ref, f32[16,32,128]{2,1,0:T(8,128)} %get-tuple-element.27.spec_ref, ...), custom_call_target="tpu_custom_call", output_to_operand_aliasing={{0}: (4, {})} | custom-call | flops 5000000 | bytes 33554432 | tf_op jit(solution)/shard_map/weight_gradient/pallas_call | solution.py:576
Async XLA Ops:
  11.1 17.4 %all-to-all-start = ((f32[16,32,128]{2,1,0:T(8,128)}), f32[16,32,128]{2,1,0:T(8,128)S(1)}, u32[]{:S(2)}, u32[]{:S(2)}) async-start(f32[16,32,128]{2,1,0:T(8,128)} %bitcast.25), calls=%async_computation | async-start | bytes 524288 | tf_op jit(solution)/shard_map/all_to_all | solution.py:598
  28.4 12.6 %copy-start.4 = (f32[32,32]{1,0:T(8,128)S(1)}, f32[32,32]{1,0:T(8,128)}, u32[]{:S(2)}) copy-start(f32[32,32]{1,0:T(8,128)} %param.17) | copy-start | bytes 12292
  28.4 13.3 %copy-start.5 = (f32[32]{0:T(128)S(1)}, f32[32]{0:T(128)}, u32[]{:S(2)}) copy-start(f32[32]{0:T(128)} %param.18) | copy-start | bytes 388
  28.6 0.7 copy-start.1
  35.2 15.9 %all-to-all-start.1 = ((f32[16,32,128]{2,1,0:T(8,128)}), f32[16,32,128]{2,1,0:T(8,128)S(1)}, u32[]{:S(2)}, u32[]{:S(2)}) async-start(f32[16,32,128]{2,1,0:T(8,128)} %get-tuple-element.21), calls=%async_computation.1 | async-start | bytes 524288 | tf_op jit(solution)/shard_map/all_to_all | solution.py:598
  51.1 0.7 copy-start.3
  58.9 15.4 %all-to-all-start.3 = ((f32[16,16,128]{2,1,0:T(8,128)}), f32[16,16,128]{2,1,0:T(8,128)S(1)}, u32[]{:S(2)}, u32[]{:S(2)}) async-start(f32[16,16,128]{2,1,0:T(8,128)} %bitcast.26), calls=%async_computation.3 | async-start | bytes 262144 | tf_op jit(solution)/shard_map/all_to_all | solution.py:598
  74.2 6.0 %copy-start.2 = (f32[16,16,128]{2,1,0:T(8,128)}, f32[16,16,128]{2,1,0:T(8,128)S(1)}, u32[]{:S(2)}) copy-start(f32[16,16,128]{2,1,0:T(8,128)S(1)} %all-to-all-done.3.lines_ref) | copy-start | bytes 393220
  74.2 17.0 %all-to-all-start.2 = ((f32[16,32,128]{2,1,0:T(8,128)}), f32[16,32,128]{2,1,0:T(8,128)S(1)}, u32[]{:S(2)}, u32[]{:S(2)}) async-start(f32[16,32,128]{2,1,0:T(8,128)} %bitcast.24), calls=%async_computation.2 | async-start | bytes 524288 | tf_op jit(solution)/shard_map/all_to_all | solution.py:598
  91.2 0.7 copy-start

commit v6 on v5

--- a/solution.py
+++ b/solution.py
@@ -20,8 +20,10 @@
 INV_SQRT_TWO = 0.7071067811865476
 INV_SQRT_TWO_PI = 0.3989422804014327
 MIB = 1 << 20
+LIMIT = 48
 LANES = 128
 GROUP = 4
+SLOTS = 4
 STEP = 8
 
 
@@ -136,6 +138,14 @@
     return [lines[:, q * LANES : (q + 1) * LANES] for q in range(GROUP // 2)]
 
 
+def in_hbm(*arrays):
+    return [pltpu.with_memory_space_constraint(each, pltpu.HBM) for each in arrays]
+
+
+def in_vmem(*arrays):
+    return [pltpu.with_memory_space_constraint(each, pltpu.VMEM) for each in arrays]
+
+
 def full(shape):
     return pl.BlockSpec(shape, lambda *_: (0,) * len(shape))
 
@@ -156,12 +166,15 @@
 def fold_specs(weights, unique, per_step, first):
     block = (2, per_step) + weights.shape[2:]
     pieces = [
-        pl.BlockSpec(block, functools.partial(lambda s, r: (0, first + s + r, 0, 0, 0), r=r * (unique // per_step)))
+        pl.BlockSpec(
+            block,
+            functools.partial(lambda s, r: (0, first + s + r, 0, 0, 0), r=r * (unique // per_step)),
+        )
         for r in range(weights.shape[1] // unique)
     ]
     shape = (unique,) + weights.shape[2:4] + (2 * weights.shape[4],)
     out = pl.BlockSpec((per_step,) + shape[1:], lambda s: (first + s, 0, 0, 0))
-    return pieces, out, jax.ShapeDtypeStruct(shape, F32)
+    return pieces, out, pltpu.HBM(shape, F32)
 
 
 def forward_kernel(z_high, z_low, y_both, field_ref, *refs, channels, step_channels, per_step):
@@ -187,11 +200,11 @@
         + [pl.BlockSpec((step_channels, NY, NZ), lambda s: (s, 0, 0))]
         + pieces,
         out_specs=[full((owners * channels, LANES)), folded],
-        out_shape=[jax.ShapeDtypeStruct((owners * channels, LANES), F32), folded_shape],
-        compiler_params=params(60),
+        out_shape=[pltpu.VMEM((owners * channels, LANES), F32), folded_shape],
+        compiler_params=params(LIMIT),
         cost_estimate=pl.CostEstimate(flops=2 * 10**9, bytes_accessed=26 * MIB, transcendentals=0),
         name="forward_yz",
-    )(*tables, field, *([weights] * len(pieces)))
+    )(*in_hbm(*tables, field, *([weights] * len(pieces))))
     return out.reshape(owners, channels, LANES), half
 
 
@@ -210,10 +223,10 @@
         out_specs=folded,
         out_shape=folded_shape,
         input_output_aliases={len(pieces): 0},
-        compiler_params=params(60),
+        compiler_params=params(LIMIT),
         cost_estimate=pl.CostEstimate(flops=4 * 10**6, bytes_accessed=20 * MIB, transcendentals=0),
         name="fold_weights",
-    )(*([weights] * len(pieces)), half)
+    )(*in_hbm(*([weights] * len(pieces)), half))
 
 
 def halve_lines(lines_ref, sums_ref, points, channels):
@@ -301,8 +314,8 @@
             full(shape),
         ],
         out_shape=[
-            jax.ShapeDtypeStruct((unique, channels, LANES), F32),
-            jax.ShapeDtypeStruct(shape, F32),
+            pltpu.VMEM((unique, channels, LANES), F32),
+            pltpu.VMEM(shape, F32),
         ],
         scratch_shapes=[
             pltpu.VMEM((2, 2, points // 2, channels, LANES), F32),
@@ -310,10 +323,10 @@
             pltpu.VMEM((per_step, channels, LANES), F32),
             pltpu.VMEM((per_step, channels, LANES), F32),
         ],
-        compiler_params=params(60),
+        compiler_params=params(LIMIT),
         cost_estimate=pl.CostEstimate(flops=2 * 10**7, bytes_accessed=9 * MIB, transcendentals=0),
         name="mix_modes",
-    )(cos_x, sin_x, lines, weights)
+    )(cos_x, sin_x, *in_vmem(lines), *in_hbm(weights))
 
 
 def exact_dot(left, right):
@@ -354,12 +367,12 @@
         grid=(NY // (8 * blocks),),
         in_specs=[full(summing.shape), full(turned.shape), full(bias.shape), block],
         out_specs=block,
-        out_shape=jax.ShapeDtypeStruct(field.shape, F32),
+        out_shape=pltpu.HBM(field.shape, F32),
         scratch_shapes=[pltpu.VMEM((2 * size, size), BF16), pltpu.VMEM((size, 1), F32)],
-        compiler_params=params(60),
+        compiler_params=params(LIMIT),
         cost_estimate=pl.CostEstimate(flops=4 * 10**9, bytes_accessed=24 * MIB, transcendentals=0),
         name="pointwise",
-    )(summing, turned, bias, field)
+    )(*in_hbm(summing, turned, bias, field))
 
 
 def cell_group(inv_y, inv_z, inv_z_low, modes_ref, pre_ref, cot_ref, act_ref, first, count, channels):
@@ -462,14 +475,14 @@
         in_specs=[full(t.shape) for t in tables] + [full((owners * channels, LANES)), block, block],
         out_specs=[block, block, full((owners * half, LANES))],
         out_shape=[
-            jax.ShapeDtypeStruct((channels, NY, NZ), BF16),
-            jax.ShapeDtypeStruct((half, NY, NZ), F32),
-            jax.ShapeDtypeStruct((owners * half, LANES), F32),
+            pltpu.HBM((channels, NY, NZ), BF16),
+            pltpu.HBM((half, NY, NZ), F32),
+            pltpu.VMEM((owners * half, LANES), F32),
         ],
-        compiler_params=params(60),
+        compiler_params=params(LIMIT),
         cost_estimate=pl.CostEstimate(flops=3 * 10**9, bytes_accessed=7 * MIB, transcendentals=10**6),
         name="early_cells",
-    )(*tables, modes.reshape(owners * channels, LANES), pre, cotangent)
+    )(*in_hbm(*tables), *in_vmem(modes.reshape(owners * channels, LANES)), *in_hbm(pre, cotangent))
     return act, slope, out.reshape(owners, half, LANES)
 
 
@@ -490,8 +503,8 @@
         + [anywhere] * 3,
         out_specs=[block, full((owners * rows, LANES))],
         out_shape=[
-            jax.ShapeDtypeStruct((channels, NY, NZ), BF16),
-            jax.ShapeDtypeStruct((owners * rows, LANES), F32),
+            pltpu.HBM((channels, NY, NZ), BF16),
+            pltpu.VMEM((owners * rows, LANES), F32),
         ],
         scratch_shapes=[
             pltpu.VMEM((channels, NY, NZ), F32),
@@ -499,12 +512,15 @@
             pltpu.SemaphoreType.DMA((2,)),
         ],
         input_output_aliases={len(tables) + 6: 0},
-        compiler_params=params(60),
+        compiler_params=params(LIMIT),
         cost_estimate=pl.CostEstimate(flops=6 * 10**9, bytes_accessed=11 * MIB, transcendentals=10**6),
         name="late_cells",
     )(
-        *tables, modes.reshape(owners * channels, LANES), pre, cotangent, early.reshape(owners * half, LANES),
-        slope, field, act,
+        *in_hbm(*tables),
+        *in_vmem(modes.reshape(owners * channels, LANES)),
+        *in_hbm(pre, cotangent),
+        *in_vmem(early.reshape(owners * half, LANES)),
+        *in_hbm(slope, field, act),
     )
     return act, out.reshape(owners, rows, LANES)
 
@@ -523,24 +539,25 @@
     def writes(at, slot):
         return [
             pltpu.make_async_copy(
-                buffer.at[slot],
-                out_hbm.at[:, at + r * unique, :, pl.ds(part * outputs, outputs), :],
-                sems.at[slot, r],
+                buffer.at[slot, c],
+                out_hbm.at[c, at + r * unique, :, pl.ds(part * outputs, outputs), :],
+                sems.at[slot, c, r],
             )
             for r in range(copies)
+            for c in range(2)
         ]
 
-    @pl.loop(0, unique // 2)
-    def _(pair):
-        for slot in range(2):
-            at = 2 * pair + slot
-
-            @pl.when(pair > 0)
+    @pl.loop(0, unique // SLOTS)
+    def _(turn):
+        for slot in range(SLOTS):
+            at = SLOTS * turn + slot
+
+            @pl.when(turn > 0)
             def _():
-                for copy in writes(at - 2, slot):
+                for copy in writes(at - SLOTS, slot):
                     copy.wait()
 
-            slope = scale * spectrum_row(cos_ref, sin_ref, sums_ref, at, slot, points // 2)
+            slope = scale * spectrum_row(cos_ref, sin_ref, sums_ref, at, slot % 2, points // 2)
             other = roll(slope, 64)
             flipped = jnp.where(lane < half, other, -other)
             real_ref[slot], imag_ref[slot] = doubled(spec_ref[at])
@@ -560,8 +577,8 @@
             point_ref[8 * q : 8 * q + 8, :] = packed[:8, q * channels : (q + 1) * channels]
         bias_ref[...] = packed[8:9, :channels]
 
-    for at in range(unique - 2, unique):
-        for copy in writes(at, at % 2):
+    for at in range(unique - SLOTS, unique):
+        for copy in writes(at, at % SLOTS):
             copy.wait()
 
 
@@ -582,16 +599,16 @@
         out_shape=[shape] + [jax.ShapeDtypeStruct(each, F32) for each in sums],
         scratch_shapes=[
             pltpu.VMEM((2, 2, points // 2, channels // 2, LANES), F32),
-            pltpu.VMEM((2, channels, LANES), F32),
-            pltpu.VMEM((2, channels, LANES), F32),
-            pltpu.VMEM((2, 2, channels, channels // 2, half), F32),
-            pltpu.SemaphoreType.DMA((2, copies)),
+            pltpu.VMEM((SLOTS, channels, LANES), F32),
+            pltpu.VMEM((SLOTS, channels, LANES), F32),
+            pltpu.VMEM((SLOTS, 2, channels, channels // 2, half), F32),
+            pltpu.SemaphoreType.DMA((SLOTS, 2, copies)),
         ],
         input_output_aliases={4: 0} if before else {},
-        compiler_params=params(60),
+        compiler_params=params(LIMIT),
         cost_estimate=pl.CostEstimate(flops=5 * 10**6, bytes_accessed=32 * MIB, transcendentals=0),
         name="weight_gradient",
-    )(cos_x, sin_x, spectrum, lines, *before)
+    )(cos_x, sin_x, *in_vmem(spectrum, lines), *before)
 
 
 def swap(lines):

time: 104 us -> 97 us (0.933)
  Pallas kernels: 73.9 us -> 65.8 us
  waiting for transfers between devices: 0.18 us -> 3.16 us
  local copies, waits for them, and re-layouts: 3.51 us -> 1.38 us
    pallas_call x2, Pallas kernels: 22.5 us -> 14.7 us  [gradient(): pl.pallas_call(functools.partial(gradient_kernel, points=points, channels...]
    all_to_all x4, waiting for transfers between devices: 0.18 us -> 3.16 us  [swap(): lax.all_to_all(lines, 'space', split_axis=0, concat_axis=0, tiled=True)]
    unnamed x13 -> x9, local copies, waits for them, and re-layouts: 2.82 us -> 0.7 us
  transfers between devices with their start and end apart: 4 -> 4, of which waited for: 1 -> 2; matrix products, arithmetic and copies ran while one was open for 1% -> 1% of each run, Pallas kernels for 38% -> 36%
where the time goes in v6:
time: 97 us; the launch traced here: 96.3 us
  Pallas kernels  65.8 us (68%)
  starting transfers between devices  25.3 us (26%)
  waiting for transfers between devices  3.16 us (3%)
  local copies, waits for them, and re-layouts  1.38 us (1%)
    all_to_all x4, starting transfers between devices, swap(): lax.all_to_all(lines, 'space', split_axis=0, concat_axis=0, tiled=True)  25.3 us
    pallas_call x2, Pallas kernels, gradient(): pl.pallas_call(functools.partial(gradient_kernel, points=points, channels...  14.7 us
    pallas_call x1, Pallas kernels, forward_modes(): pl.pallas_call(functools.partial(forward_kernel, channels=channels, step_...  10.5 us
    pallas_call x1, Pallas kernels, fold_rest(): pl.pallas_call(fold_kernel, grid=(unique - first,), in_specs=pieces + [pl...  9.87 us
    pallas_call x1, Pallas kernels, late_cells(): pl.pallas_call(functools.partial(late_cell_kernel, channels=channels, cou...  9.25 us
    pallas_call x1, Pallas kernels, pointwise(): pl.pallas_call(functools.partial(pointwise_kernel, channels=channels, blo...  8.68 us
    pallas_call x1, Pallas kernels, early_cells(): pl.pallas_call(functools.partial(early_cell_kernel, channels=channels, co...  6.97 us
    pallas_call x1, Pallas kernels, mix(): pl.pallas_call(functools.partial(mix_kernel, points=points, channels=chan...  5.83 us
  transfers between devices with their start and end apart: 4, of which 2 were waited for; matrix products, arithmetic and copies ran while one was open for 1% of the time, Pallas kernels for 36%

profile of v6, /device:TPU:0, one launch (start us, length us, event | category | flops | bytes accessed | tf_op | source)
XLA Modules:
  0.0 96.3 jit_solution(18348100181445992679)
XLA Ops:
  0.6 10.5 %forward_yz.1 = (f32[512,128]{1,0:T(8,128)}, f32[16,32,32,128]{3,2,1,0:T(8,128)}) custom-call(bf16[512,256]{1,0:T(8,128)(2,1)} %constant.21.clone.z_high, bf16[512,256]{1,0:T(8,128)(2,1)} %constant.22.clone.z_low, bf16[64,256]{1,0:T(8,128)(2,1)} %constant.23.clone.y_both, f32[32,128,256]{2,1,0:T(8,128)} %bitcast.21, f32[2,32,32,32,64]{4,3,2,1,0:T(8,128)} %bitcast.16, ...), custom_call_target="tpu_custom_call" | custom-call | flops 2000000000 | bytes 27262976 | tf_op jit(solution)/shard_map/forward_yz/pallas_call | solution.py:196
  11.1 7.4 %all-to-all-start = ((f32[16,32,128]{2,1,0:T(8,128)}), f32[16,32,128]{2,1,0:T(8,128)S(1)}, u32[]{:S(2)}, u32[]{:S(2)}) async-start(f32[16,32,128]{2,1,0:T(8,128)} %bitcast.2), calls=%async_computation | async-start | bytes 524288 | tf_op jit(solution)/shard_map/all_to_all | solution.py:615
  18.5 0.0 copy-start
  18.5 0.0 copy-start.1
  18.5 9.9 %fold_weights.1.weights_ref = f32[16,32,32,128]{3,2,1,0:T(8,128)} custom-call(f32[2,32,32,32,64]{4,3,2,1,0:T(8,128)} %bitcast.18, f32[2,32,32,32,64]{4,3,2,1,0:T(8,128)} %bitcast.19, f32[16,32,32,128]{3,2,1,0:T(8,128)} %get-tuple-element.19.refs_2_), custom_call_target="tpu_custom_call", output_to_operand_aliasing={{}: (2, {})} | custom-call | flops 4000000 | bytes 20971520 | tf_op jit(solution)/shard_map/fold_weights/pallas_call | solution.py:219
  28.4 0.0 copy-start.2
  28.4 0.0 copy-start.3
  28.4 0.1 all-to-all-done.lines_ref
  28.6 0.0 copy-done
  28.6 0.0 copy-done.1
  28.6 5.8 %mix_modes.1 = (f32[16,32,128]{2,1,0:T(8,128)S(1)}, f32[16,32,128]{2,1,0:T(8,128)}) custom-call(f32[16,16]{1,0:T(8,128)S(1)} %copy-done.1, f32[16,16]{1,0:T(8,128)S(1)} %copy-done, f32[16,32,128]{2,1,0:T(8,128)S(1)} %all-to-all-done.lines_ref, f32[16,32,32,128]{3,2,1,0:T(8,128)} %fold_weights.1.weights_ref), custom_call_target="tpu_custom_call" | custom-call | flops 20000000 | bytes 9437184 | tf_op jit(solution)/shard_map/mix_modes/pallas_call | solution.py:303
  34.4 5.9 %all-to-all-start.1 = ((f32[16,32,128]{2,1,0:T(8,128)}), f32[16,32,128]{2,1,0:T(8,128)S(1)}, u32[]{:S(2)}, u32[]{:S(2)}) async-start(f32[16,32,128]{2,1,0:T(8,128)} %get-tuple-element.21), calls=%async_computation.1 | async-start | bytes 524288 | tf_op jit(solution)/shard_map/all_to_all | solution.py:615
  40.3 0.0 copy-done.2
  40.3 0.7 copy.21
  41.0 0.0 copy-done.3
  41.0 0.7 copy.22.bias_in_ref
  41.7 8.7 %pointwise.1.pre_ref = f32[32,128,256]{2,1,0:T(8,128)} custom-call(f32[256,32]{1,0:T(8,128)} %constant.20.clone.sum_ref, f32[32,32]{1,0:T(8,128)} %bitcast.24, f32[32,1]{1,0:T(8,128)} %copy.22.bias_in_ref, f32[32,128,256]{2,1,0:T(8,128)} %bitcast.22), custom_call_target="tpu_custom_call" | custom-call | flops 4000000000 | bytes 25165824 | tf_op jit(solution)/shard_map/pointwise/pallas_call | solution.py:365
  50.3 0.0 all-to-all-done.1
  50.3 7.0 %early_cells.1 = (bf16[32,128,256]{2,1,0:T(8,128)(2,1)}, f32[16,128,256]{2,1,0:T(8,128)}, f32[256,128]{1,0:T(8,128)}) custom-call(bf16[128,192]{1,0:T(8,128)(2,1)} %constant.24.clone.inv_y, bf16[256,512]{1,0:T(8,128)(2,1)} %constant.25.clone.inv_z, bf16[128,512]{1,0:T(8,128)(2,1)} %constant.26.clone.inv_z_low, bf16[512,256]{1,0:T(8,128)(2,1)} %constant.21.clone.z_high, ...), custom_call_target="tpu_custom_call" | custom-call | flops 3000000000 | bytes 7340032 | tf_op jit(solution)/shard_map/early_cells/pallas_call | solution.py:472
  57.3 6.0 %all-to-all-start.3 = ((f32[16,16,128]{2,1,0:T(8,128)}), f32[16,16,128]{2,1,0:T(8,128)S(1)}, u32[]{:S(2)}, u32[]{:S(2)}) async-start(f32[16,16,128]{2,1,0:T(8,128)} %bitcast.10), calls=%async_computation.3 | async-start | bytes 262144 | tf_op jit(solution)/shard_map/all_to_all | solution.py:615
  63.3 9.3 %late_cells.1 = (bf16[32,128,256]{2,1,0:T(8,128)(2,1)}, f32[512,128]{1,0:T(8,128)}) custom-call(bf16[128,192]{1,0:T(8,128)(2,1)} %constant.24.clone.inv_y, bf16[256,512]{1,0:T(8,128)(2,1)} %constant.25.clone.inv_z, bf16[128,512]{1,0:T(8,128)(2,1)} %constant.26.clone.inv_z_low, ...), custom_call_target="tpu_custom_call", output_to_operand_aliasing={{0}: (13, {})} | custom-call | flops 6000000000 | bytes 11534336 | tf_op jit(solution)/shard_map/late_cells/pallas_call | solution.py:498
  72.6 0.0 all-to-all-done.3.lines_ref
  72.6 6.0 %all-to-all-start.2 = ((f32[16,32,128]{2,1,0:T(8,128)}), f32[16,32,128]{2,1,0:T(8,128)S(1)}, u32[]{:S(2)}, u32[]{:S(2)}) async-start(f32[16,32,128]{2,1,0:T(8,128)} %bitcast.9), calls=%async_computation.2 | async-start | bytes 524288 | tf_op jit(solution)/shard_map/all_to_all | solution.py:615
  78.6 7.0 %weight_gradient.2.refs_0_ = f32[2,32,32,32,64]{4,3,2,1,0:T(8,128)} custom-call(f32[16,16]{1,0:T(8,128)S(1)} %copy-done.1, f32[16,16]{1,0:T(8,128)S(1)} %copy-done, f32[16,32,128]{2,1,0:T(8,128)S(1)} %get-tuple-element.27.spec_ref, f32[16,16,128]{2,1,0:T(8,128)S(1)} %all-to-all-done.3.lines_ref), custom_call_target="tpu_custom_call" | custom-call | flops 5000000 | bytes 33554432 | tf_op jit(solution)/shard_map/weight_gradient/pallas_call | solution.py:593
  85.7 3.0 %all-to-all-done.2.lines_ref = f32[16,32,128]{2,1,0:T(8,128)S(1)} async-done(((f32[16,32,128]{2,1,0:T(8,128)}), f32[16,32,128]{2,1,0:T(8,128)S(1)}, u32[]{:S(2)}, u32[]{:S(2)}) %all-to-all-start.2) | async-done | bytes 262176 | tf_op jit(solution)/shard_map/all_to_all | solution.py:615
  88.7 7.6 %weight_gradient.3 = (f32[2,32,32,32,64]{4,3,2,1,0:T(8,128)}, f32[32,32]{1,0:T(8,128)}, f32[1,32]{1,0:T(1,128)}) custom-call(f32[16,16]{1,0:T(8,128)S(1)} %copy-done.1, f32[16,16]{1,0:T(8,128)S(1)} %copy-done, f32[16,32,128]{2,1,0:T(8,128)S(1)} %get-tuple-element.27.spec_ref, ...), custom_call_target="tpu_custom_call", output_to_operand_aliasing={{0}: (4, {})} | custom-call | flops 5000000 | bytes 33554432 | tf_op jit(solution)/shard_map/weight_gradient/pallas_call | solution.py:593
Async XLA Ops:
  11.1 17.4 %all-to-all-start = ((f32[16,32,128]{2,1,0:T(8,128)}), f32[16,32,128]{2,1,0:T(8,128)S(1)}, u32[]{:S(2)}, u32[]{:S(2)}) async-start(f32[16,32,128]{2,1,0:T(8,128)} %bitcast.2), calls=%async_computation | async-start | bytes 524288 | tf_op jit(solution)/shard_map/all_to_all | solution.py:615
  18.5 10.0 %copy-start = (f32[16,16]{1,0:T(8,128)S(1)}, f32[16,16]{1,0:T(8,128)}, u32[]{:S(2)}) copy-start(f32[16,16]{1,0:T(8,128)} %constant.19.clone.sin_ref) | copy-start | bytes 3076
  18.5 10.0 %copy-start.1 = (f32[16,16]{1,0:T(8,128)S(1)}, f32[16,16]{1,0:T(8,128)}, u32[]{:S(2)}) copy-start(f32[16,16]{1,0:T(8,128)} %constant.18.clone.cos_ref) | copy-start | bytes 3076
  28.4 11.9 %copy-start.2 = (f32[32,32]{1,0:T(8,128)S(1)}, f32[32,32]{1,0:T(8,128)}, u32[]{:S(2)}) copy-start(f32[32,32]{1,0:T(8,128)} %param.17) | copy-start | bytes 12292
  28.4 12.6 %copy-start.3 = (f32[32]{0:T(128)S(1)}, f32[32]{0:T(128)}, u32[]{:S(2)}) copy-start(f32[32]{0:T(128)} %param.18) | copy-start | bytes 388
  34.4 16.0 %all-to-all-start.1 = ((f32[16,32,128]{2,1,0:T(8,128)}), f32[16,32,128]{2,1,0:T(8,128)S(1)}, u32[]{:S(2)}, u32[]{:S(2)}) async-start(f32[16,32,128]{2,1,0:T(8,128)} %get-tuple-element.21), calls=%async_computation.1 | async-start | bytes 524288 | tf_op jit(solution)/shard_map/all_to_all | solution.py:615
  57.3 15.3 %all-to-all-start.3 = ((f32[16,16,128]{2,1,0:T(8,128)}), f32[16,16,128]{2,1,0:T(8,128)S(1)}, u32[]{:S(2)}, u32[]{:S(2)}) async-start(f32[16,16,128]{2,1,0:T(8,128)} %bitcast.10), calls=%async_computation.3 | async-start | bytes 262144 | tf_op jit(solution)/shard_map/all_to_all | solution.py:615
  72.6 16.1 %all-to-all-start.2 = ((f32[16,32,128]{2,1,0:T(8,128)}), f32[16,32,128]{2,1,0:T(8,128)S(1)}, u32[]{:S(2)}, u32[]{:S(2)}) async-start(f32[16,32,128]{2,1,0:T(8,128)} %bitcast.9), calls=%async_computation.2 | async-start | bytes 524288 | tf_op jit(solution)/shard_map/all_to_all | solution.py:615

commit v7 on v6

--- a/solution.py
+++ b/solution.py
@@ -23,7 +23,6 @@
 LIMIT = 48
 LANES = 128
 GROUP = 4
-SLOTS = 4
 STEP = 8
 
 
@@ -155,78 +154,128 @@
 
 
 def fold_block(pieces, out_ref, at):
-    real, imag = pieces[0][0, at], pieces[0][1, at]
-    for piece in pieces[1:]:
-        real, imag = real + piece[0, at], imag + piece[1, at]
+    copies = pieces.shape[0]
+    real, imag = pieces[0, 0], pieces[0, 1]
+    for r in range(1, copies):
+        real, imag = real + pieces[r, 0], imag + pieces[r, 1]
     modes = real.shape[-1]
     out_ref[at, :, :, :modes] = real
     out_ref[at, :, :, modes:] = imag
 
 
-def fold_specs(weights, unique, per_step, first):
-    block = (2, per_step) + weights.shape[2:]
-    pieces = [
-        pl.BlockSpec(
-            block,
-            functools.partial(lambda s, r: (0, first + s + r, 0, 0, 0), r=r * (unique // per_step)),
-        )
-        for r in range(weights.shape[1] // unique)
+def fetches(weights_hbm, ring_ref, sems, at, slot, unique):
+    copies = ring_ref.shape[1]
+    return [
+        pltpu.make_async_copy(weights_hbm.at[c, at + r * unique], ring_ref.at[slot, r, c], sems.at[slot, r, c])
+        for r in range(copies)
+        for c in range(2)
     ]
+
+
+def fold_shapes(weights, unique, slots):
+    copies = weights.shape[1] // unique
     shape = (unique,) + weights.shape[2:4] + (2 * weights.shape[4],)
-    out = pl.BlockSpec((per_step,) + shape[1:], lambda s: (first + s, 0, 0, 0))
-    return pieces, out, pltpu.HBM(shape, F32)
-
-
-def forward_kernel(z_high, z_low, y_both, field_ref, *refs, channels, step_channels, per_step):
-    *pieces, out_ref, folded_ref = refs
+    ring = [pltpu.VMEM((slots, copies, 2) + weights.shape[2:], F32), pltpu.SemaphoreType.DMA((slots, copies, 2))]
+    return pltpu.HBM(shape, F32), ring
+
+
+def forward_kernel(
+    z_high, z_low, y_both, field_ref, weights_hbm, out_ref, folded_ref, ring_ref, sems,
+    *, channels, step_channels, per_step, unique, slots,
+):
     step = pl.program_id(0)
-    for at in range(per_step):
-        fold_block(pieces, folded_ref, at)
-    fields = [field_ref[q] for q in range(step_channels)]
-    forward_group(fields, z_high[...], z_low[...], y_both[...], out_ref, step * step_channels, channels)
+
+    def transform():
+        fields = [field_ref[q] for q in range(step_channels)]
+        forward_group(fields, z_high[...], z_low[...], y_both[...], out_ref, step * step_channels, channels)
+
+    @pl.when(step == 0)
+    def _():
+        for at in range(slots):
+            for copy in fetches(weights_hbm, ring_ref, sems, at, at, unique):
+                copy.start()
+        transform()
+
+    @pl.when(step > 0)
+    def _():
+        for q in range(per_step):
+            at = (step - 1) * per_step + q
+            for copy in fetches(weights_hbm, ring_ref, sems, at, at, unique):
+                copy.wait()
+            fold_block(ring_ref.at[at], folded_ref, q)
+        transform()
+
+
+FOLD_STEP = 2
+FIELD_STEP = 8
+
+
+def folded_early(channels):
+    return (channels // FIELD_STEP - 1) * FOLD_STEP
 
 
 def forward_modes(field, tables, weights, unique):
     channels = field.shape[0]
-    step_channels = 8
-    steps = channels // step_channels
-    per_step = unique // 2 // steps
-    pieces, folded, folded_shape = fold_specs(weights, unique, per_step, 0)
+    slots = folded_early(channels)
+    folded_shape, ring = fold_shapes(weights, unique, slots)
     owners = MY // 2
-    out, half = pl.pallas_call(
-        functools.partial(forward_kernel, channels=channels, step_channels=step_channels, per_step=per_step),
-        grid=(steps,),
+    out, some = pl.pallas_call(
+        functools.partial(
+            forward_kernel, channels=channels, step_channels=FIELD_STEP, per_step=FOLD_STEP, unique=unique, slots=slots
+        ),
+        grid=(channels // FIELD_STEP,),
         in_specs=[full(t.shape) for t in tables]
-        + [pl.BlockSpec((step_channels, NY, NZ), lambda s: (s, 0, 0))]
-        + pieces,
-        out_specs=[full((owners * channels, LANES)), folded],
+        + [pl.BlockSpec((FIELD_STEP, NY, NZ), lambda s: (s, 0, 0)), pl.BlockSpec(memory_space=pl.ANY)],
+        out_specs=[
+            full((owners * channels, LANES)),
+            pl.BlockSpec((FOLD_STEP,) + folded_shape.shape[1:], lambda s: (jnp.maximum(s - 1, 0), 0, 0, 0)),
+        ],
         out_shape=[pltpu.VMEM((owners * channels, LANES), F32), folded_shape],
+        scratch_shapes=ring,
         compiler_params=params(LIMIT),
-        cost_estimate=pl.CostEstimate(flops=2 * 10**9, bytes_accessed=26 * MIB, transcendentals=0),
+        cost_estimate=pl.CostEstimate(flops=2 * 10**9, bytes_accessed=22 * MIB, transcendentals=0),
         name="forward_yz",
-    )(*in_hbm(*tables, field, *([weights] * len(pieces))))
-    return out.reshape(owners, channels, LANES), half
-
-
-def fold_kernel(*refs):
-    *pieces, _, out_ref = refs
-    fold_block(pieces, out_ref, 0)
-
-
-def fold_rest(weights, half, unique):
-    first = unique // 2
-    pieces, folded, folded_shape = fold_specs(weights, unique, 1, first)
+    )(*in_hbm(*tables, field, weights))
+    return out.reshape(owners, channels, LANES), some
+
+
+def fold_kernel(weights_hbm, _, out_ref, ring_ref, sems, *, first, unique, slots):
+    step = pl.program_id(0)
+    slot = step % slots
+
+    @pl.when(step == 0)
+    def _():
+        for ahead in range(slots):
+            for copy in fetches(weights_hbm, ring_ref, sems, first + ahead, ahead, unique):
+                copy.start()
+
+    for copy in fetches(weights_hbm, ring_ref, sems, first + step, slot, unique):
+        copy.wait()
+    fold_block(ring_ref.at[slot], out_ref, 0)
+
+    @pl.when(step + slots < pl.num_programs(0))
+    def _():
+        for copy in fetches(weights_hbm, ring_ref, sems, first + step + slots, slot, unique):
+            copy.start()
+
+
+def fold_rest(weights, some, unique):
+    first = folded_early(weights.shape[2])
+    slots = min(4, unique - first)
+    folded_shape, ring = fold_shapes(weights, unique, slots)
+    anywhere = pl.BlockSpec(memory_space=pl.ANY)
     return pl.pallas_call(
-        fold_kernel,
+        functools.partial(fold_kernel, first=first, unique=unique, slots=slots),
         grid=(unique - first,),
-        in_specs=pieces + [pl.BlockSpec(memory_space=pl.ANY)],
-        out_specs=folded,
+        in_specs=[anywhere, anywhere],
+        out_specs=pl.BlockSpec((1,) + folded_shape.shape[1:], lambda s: (first + s, 0, 0, 0)),
         out_shape=folded_shape,
-        input_output_aliases={len(pieces): 0},
+        scratch_shapes=ring,
+        input_output_aliases={1: 0},
         compiler_params=params(LIMIT),
-        cost_estimate=pl.CostEstimate(flops=4 * 10**6, bytes_accessed=20 * MIB, transcendentals=0),
+        cost_estimate=pl.CostEstimate(flops=4 * 10**6, bytes_accessed=25 * MIB, transcendentals=0),
         name="fold_weights",
-    )(*in_hbm(*([weights] * len(pieces)), half))
+    )(*in_hbm(weights, some))
 
 
 def halve_lines(lines_ref, sums_ref, points, channels):
@@ -253,14 +302,19 @@
 
 
 def mix_kernel(
-    cos_ref, sin_ref, lines_ref, weights_ref, spec_ref, out_ref, sums_ref, total_ref, real_ref, imag_ref,
-    *, points, channels, per_step, norm,
+    cos_ref, sin_ref, lines_ref, weights_hbm, spec_ref, out_ref,
+    sums_ref, total_ref, real_ref, imag_ref, weights_ref, sems, *, points, channels, per_step, norm,
 ):
     step = pl.program_id(0)
     half = points // 2
 
+    def fetch(at):
+        return pltpu.make_async_copy(weights_hbm.at[at], weights_ref.at[at], sems.at[at])
+
     @pl.when(step == 0)
     def _():
+        for at in range(points):
+            fetch(at).start()
         halve_lines(lines_ref, sums_ref, points, channels)
         total_ref[...] = jnp.zeros_like(total_ref)
 
@@ -273,8 +327,9 @@
         real_ref[q], imag_ref[q] = doubled(spec)
         by_real = jnp.zeros((channels, LANES), F32)
         by_imag = jnp.zeros((channels, LANES), F32)
+        fetch(at).wait()
         for i in range(channels):
-            weight = weights_ref[q, i]
+            weight = weights_ref[at, i]
             by_real += real_ref[q, pl.ds(i, 1), :] * weight
             by_imag += imag_ref[q, pl.ds(i, 1), :] * weight
         other = roll(by_imag, 64)
@@ -307,7 +362,7 @@
             smem(),
             smem(),
             full(shape),
-            pl.BlockSpec((per_step,) + weights.shape[1:], lambda s: (s, 0, 0, 0)),
+            pl.BlockSpec(memory_space=pl.ANY),
         ],
         out_specs=[
             pl.BlockSpec((per_step, channels, LANES), lambda s: (s, 0, 0)),
@@ -322,6 +377,8 @@
             pltpu.VMEM((2, points // 2, channels, LANES), F32),
             pltpu.VMEM((per_step, channels, LANES), F32),
             pltpu.VMEM((per_step, channels, LANES), F32),
+            pltpu.VMEM(weights.shape, F32),
+            pltpu.SemaphoreType.DMA((unique,)),
         ],
         compiler_params=params(LIMIT),
         cost_estimate=pl.CostEstimate(flops=2 * 10**7, bytes_accessed=9 * MIB, transcendentals=0),
@@ -429,10 +486,11 @@
     slope_hbm, field_hbm, _, act_ref, out_ref, field_ref, slope_ref, sems, *, channels, count, rows, owners,
 ):
     step = pl.program_id(0)
-    half = channels // 2
+    early = early_count(channels)
+    late = channels - early
     copies = [
         pltpu.make_async_copy(field_hbm, field_ref, sems.at[0]),
-        pltpu.make_async_copy(slope_hbm, slope_ref.at[pl.ds(0, half)], sems.at[1]),
+        pltpu.make_async_copy(slope_hbm, slope_ref.at[pl.ds(0, early)], sems.at[1]),
     ]
 
     @pl.when(step == 0)
@@ -440,7 +498,7 @@
         for copy in copies:
             copy.start()
 
-    first = half + step * count
+    first = early + step * count
     slopes = cell_group(
         inv_y[...], inv_z[...], inv_z_low[...], modes_ref, pre_ref, cot_ref, act_ref, first, count, channels
     )
@@ -454,52 +512,56 @@
             copy.wait()
         point = point_gradient(field_ref, slope_ref, sum_ref, channels)
         packed = jnp.concatenate([point[8 * q : 8 * q + 8] for q in range(channels // 8)], axis=1)
-        zero_mode = jnp.concatenate([early_ref[0:half, 0:1], out_ref[0:half, 0:1]], axis=0)
+        zero_mode = jnp.concatenate([early_ref[0:early, 0:1], out_ref[0:late, 0:1]], axis=0)
         eye = lax.broadcasted_iota(jnp.int32, (channels, LANES), 0) == lane_index((channels, LANES))
         bias = jnp.sum(jnp.where(eye, jnp.broadcast_to(zero_mode, (channels, LANES)), 0.0), axis=0, keepdims=True)
         extra = jnp.where(lax.broadcasted_iota(jnp.int32, (8, LANES), 0) == 0, jnp.broadcast_to(bias, (8, LANES)), 0.0)
         for d in range(owners):
-            out_ref[d * rows + half : d * rows + half + 8, :] = packed
-            out_ref[d * rows + half + 8 : (d + 1) * rows, :] = extra
+            out_ref[d * rows + late : d * rows + late + 8, :] = packed
+            out_ref[d * rows + late + 8 : (d + 1) * rows, :] = extra
+
+
+def early_count(channels):
+    return channels * 3 // 4
 
 
 def early_cells(inverse, forward, modes, pre, cotangent):
     channels = pre.shape[0]
     owners = MY // 2
-    half = channels // 2
+    early = early_count(channels)
     block = pl.BlockSpec((STEP, NY, NZ), lambda s: (s, 0, 0))
     tables = (*inverse, *forward)
     act, slope, out = pl.pallas_call(
-        functools.partial(early_cell_kernel, channels=channels, count=STEP, rows=half),
-        grid=(half // STEP,),
+        functools.partial(early_cell_kernel, channels=channels, count=STEP, rows=early),
+        grid=(early // STEP,),
         in_specs=[full(t.shape) for t in tables] + [full((owners * channels, LANES)), block, block],
-        out_specs=[block, block, full((owners * half, LANES))],
+        out_specs=[block, block, full((owners * early, LANES))],
         out_shape=[
             pltpu.HBM((channels, NY, NZ), BF16),
-            pltpu.HBM((half, NY, NZ), F32),
-            pltpu.VMEM((owners * half, LANES), F32),
+            pltpu.HBM((early, NY, NZ), F32),
+            pltpu.VMEM((owners * early, LANES), F32),
         ],
         compiler_params=params(LIMIT),
         cost_estimate=pl.CostEstimate(flops=3 * 10**9, bytes_accessed=7 * MIB, transcendentals=10**6),
         name="early_cells",
     )(*in_hbm(*tables), *in_vmem(modes.reshape(owners * channels, LANES)), *in_hbm(pre, cotangent))
-    return act, slope, out.reshape(owners, half, LANES)
+    return act, slope, out.reshape(owners, early, LANES)
 
 
 def late_cells(inverse, forward, summing, modes, pre, cotangent, field, early, slope, act):
     channels = field.shape[0]
     owners = MY // 2
-    half = channels // 2
-    rows = half + 16
-    start = half // STEP
+    first = early_count(channels)
+    rows = channels - first + 16
+    start = first // STEP
     block = pl.BlockSpec((STEP, NY, NZ), lambda s: (start + s, 0, 0))
     anywhere = pl.BlockSpec(memory_space=pl.ANY)
     tables = (*inverse, *forward, summing)
     act, out = pl.pallas_call(
         functools.partial(late_cell_kernel, channels=channels, count=STEP, rows=rows, owners=owners),
-        grid=(start,),
+        grid=((channels - first) // STEP,),
         in_specs=[full(t.shape) for t in tables]
-        + [full((owners * channels, LANES)), block, block, full((owners * half, LANES))]
+        + [full((owners * channels, LANES)), block, block, full((owners * first, LANES))]
         + [anywhere] * 3,
         out_specs=[block, full((owners * rows, LANES))],
         out_shape=[
@@ -519,18 +581,18 @@
         *in_hbm(*tables),
         *in_vmem(modes.reshape(owners * channels, LANES)),
         *in_hbm(pre, cotangent),
-        *in_vmem(early.reshape(owners * half, LANES)),
+        *in_vmem(early.reshape(owners * first, LANES)),
         *in_hbm(slope, field, act),
     )
     return act, out.reshape(owners, rows, LANES)
 
 
-def gradient_kernel(cos_ref, sin_ref, spec_ref, lines_ref, *refs, points, channels, unique, copies, norm, part):
-    if part == 1:
+def gradient_kernel(cos_ref, sin_ref, spec_ref, lines_ref, *refs, points, channels, unique, copies, norm, first, outputs, slots):
+    last = first > 0
+    if last:
         _, out_hbm, point_ref, bias_ref, sums_ref, real_ref, imag_ref, buffer, sems = refs
     else:
         out_hbm, sums_ref, real_ref, imag_ref, buffer, sems = refs
-    outputs = channels // 2
     halve_lines(lines_ref, sums_ref, points, outputs)
     half = LANES // 2
     lane = lane_index((outputs, LANES))
@@ -540,21 +602,21 @@
         return [
             pltpu.make_async_copy(
                 buffer.at[slot, c],
-                out_hbm.at[c, at + r * unique, :, pl.ds(part * outputs, outputs), :],
+                out_hbm.at[c, at + r * unique, :, pl.ds(first, outputs), :],
                 sems.at[slot, c, r],
             )
             for r in range(copies)
             for c in range(2)
         ]
 
-    @pl.loop(0, unique // SLOTS)
+    @pl.loop(0, unique // slots)
     def _(turn):
-        for slot in range(SLOTS):
-            at = SLOTS * turn + slot
+        for slot in range(slots):
+            at = slots * turn + slot
 
             @pl.when(turn > 0)
             def _():
-                for copy in writes(at - SLOTS, slot):
+                for copy in writes(at - slots, slot):
                     copy.wait()
 
             slope = scale * spectrum_row(cos_ref, sin_ref, sums_ref, at, slot % 2, points // 2)
@@ -568,7 +630,7 @@
             for copy in writes(at, slot):
                 copy.start()
 
-    if part == 1:
+    if last:
         packed = lines_ref[0, outputs : outputs + 16, :]
         for x in range(1, points):
             packed += lines_ref[x, outputs : outputs + 16, :]
@@ -577,32 +639,36 @@
             point_ref[8 * q : 8 * q + 8, :] = packed[:8, q * channels : (q + 1) * channels]
         bias_ref[...] = packed[8:9, :channels]
 
-    for at in range(unique - SLOTS, unique):
-        for copy in writes(at, at % SLOTS):
+    for at in range(unique - slots, unique):
+        for copy in writes(at, at % slots):
             copy.wait()
 
 
-def gradient(cos_x, sin_x, spectrum, lines, norm, kept_x, part, before=()):
+def gradient(cos_x, sin_x, spectrum, lines, norm, kept_x, before=()):
     points, rows, _ = lines.shape
     unique, channels, _ = spectrum.shape
     half = LANES // 2
     copies = kept_x // unique
+    first = early_count(channels) if before else 0
+    outputs = channels - first if before else early_count(channels)
+    slots = 8 if before else 4
     anywhere = pl.BlockSpec(memory_space=pl.ANY)
     shape = jax.ShapeDtypeStruct((2, kept_x, channels, channels, half), F32)
-    sums = [(channels, channels), (1, channels)] if part == 1 else []
+    sums = [(channels, channels), (1, channels)] if before else []
     return pl.pallas_call(
         functools.partial(
-            gradient_kernel, points=points, channels=channels, unique=unique, copies=copies, norm=norm, part=part
+            gradient_kernel, points=points, channels=channels, unique=unique, copies=copies, norm=norm,
+            first=first, outputs=outputs, slots=slots,
         ),
         in_specs=[smem(), smem(), full(spectrum.shape), full(lines.shape)] + [anywhere] * len(before),
         out_specs=[anywhere] + [full(each) for each in sums],
         out_shape=[shape] + [jax.ShapeDtypeStruct(each, F32) for each in sums],
         scratch_shapes=[
-            pltpu.VMEM((2, 2, points // 2, channels // 2, LANES), F32),
-            pltpu.VMEM((SLOTS, channels, LANES), F32),
-            pltpu.VMEM((SLOTS, channels, LANES), F32),
-            pltpu.VMEM((SLOTS, 2, channels, channels // 2, half), F32),
-            pltpu.SemaphoreType.DMA((SLOTS, 2, copies)),
+            pltpu.VMEM((2, 2, points // 2, outputs, LANES), F32),
+            pltpu.VMEM((slots, channels, LANES), F32),
+            pltpu.VMEM((slots, channels, LANES), F32),
+            pltpu.VMEM((slots, 2, channels, outputs, half), F32),
+            pltpu.SemaphoreType.DMA((slots, 2, copies)),
         ],
         input_output_aliases={4: 0} if before else {},
         compiler_params=params(LIMIT),
@@ -647,9 +713,9 @@
     slopes_in = cotangent.reshape(channels, NY, NZ)
     weights = jnp.transpose(spectral_weights, (0, 1, 3, 4, 2))
 
-    lines, half = forward_modes(field, forward, weights, length_x)
+    lines, some = forward_modes(field, forward, weights, length_x)
     lines = swap(lines)
-    folded = fold_rest(weights, half, length_x)
+    folded = fold_rest(weights, some, length_x)
     spectrum, mixed = mix(cos_x, sin_x, lines, folded, norm)
     field_late, mixed = lax.optimization_barrier((field, mixed))
     modes = swap(mixed)
@@ -658,8 +724,8 @@
     early_lines = swap(early)
     activated, late = late_cells(inverse, forward, summing, modes, pre, slopes_in, field, early, slope, act)
     late_lines = swap(late)
-    (grad,) = gradient(cos_x, sin_x, spectrum, early_lines, norm, MX, 0)
-    grad, grad_point, grad_bias = gradient(cos_x, sin_x, spectrum, late_lines, norm, MX, 1, (grad,))
+    (grad,) = gradient(cos_x, sin_x, spectrum, early_lines, norm, MX)
+    grad, grad_point, grad_bias = gradient(cos_x, sin_x, spectrum, late_lines, norm, MX, (grad,))
     return (
         activated.reshape(cotangent.shape),
         jnp.transpose(grad, (0, 1, 4, 2, 3)),

time: 97 us -> 97.1 us (level)
  Pallas kernels: 65.8 us -> 68.8 us
  waiting for transfers between devices: 3.16 us -> 0.77 us
    all_to_all x4, waiting for transfers between devices: 3.16 us -> 0.77 us  [swap(): lax.all_to_all(lines, 'space', split_axis=0, concat_axis=0, tiled=True)]
    pallas_call x1, Pallas kernels: 6.97 us -> 9.16 us  [early_cells(): pl.pallas_call(functools.partial(early_cell_kernel, channels=channels, co...]
    pallas_call x1, Pallas kernels: 5.83 us -> 7.06 us  [mix(): pl.pallas_call(functools.partial(mix_kernel, points=points, channels=chan...]
  transfers between devices with their start and end apart: 4 -> 4, of which waited for: 2 -> 2; matrix products, arithmetic and copies ran while one was open for 1% -> 1% of each run, Pallas kernels for 36% -> 38%
where the time goes in v7:
time: 97.1 us; the launch traced here: 96.5 us
  Pallas kernels  68.8 us (71%)
  starting transfers between devices  24.7 us (25%)
  local copies, waits for them, and re-layouts  1.39 us (1%)
    all_to_all x4, starting transfers between devices, swap(): lax.all_to_all(lines, 'space', split_axis=0, concat_axis=0, tiled=True)  24.7 us
    pallas_call x2, Pallas kernels, gradient(): pl.pallas_call(functools.partial(gradient_kernel, points=points, channels...  15.3 us
    pallas_call x1, Pallas kernels, forward_modes(): pl.pallas_call(functools.partial(forward_kernel, channels=channels, step_...  10.4 us
    pallas_call x1, Pallas kernels, fold_rest(): pl.pallas_call(functools.partial(fold_kernel, first=first, unique=unique,...  9.77 us
    pallas_call x1, Pallas kernels, early_cells(): pl.pallas_call(functools.partial(early_cell_kernel, channels=channels, co...  9.16 us
    pallas_call x1, Pallas kernels, pointwise(): pl.pallas_call(functools.partial(pointwise_kernel, channels=channels, blo...  8.68 us
    pallas_call x1, Pallas kernels, late_cells(): pl.pallas_call(functools.partial(late_cell_kernel, channels=channels, cou...  8.43 us
    pallas_call x1, Pallas kernels, mix(): pl.pallas_call(functools.partial(mix_kernel, points=points, channels=chan...  7.06 us
  transfers between devices with their start and end apart: 4, of which 2 were waited for; matrix products, arithmetic and copies ran while one was open for 1% of the time, Pallas kernels for 38%

profile of v7, /device:TPU:0, one launch (start us, length us, event | category | flops | bytes accessed | tf_op | source)
XLA Modules:
  0.0 96.5 jit_solution(3731746978119685312)
XLA Ops:
  0.6 10.4 %forward_yz.1 = (f32[512,128]{1,0:T(8,128)}, f32[16,32,32,128]{3,2,1,0:T(8,128)}) custom-call(bf16[512,256]{1,0:T(8,128)(2,1)} %constant.21.clone.z_high, bf16[512,256]{1,0:T(8,128)(2,1)} %constant.22.clone.z_low, bf16[64,256]{1,0:T(8,128)(2,1)} %constant.23.clone.y_both, f32[32,128,256]{2,1,0:T(8,128)} %bitcast.19, f32[2,32,32,32,64]{4,3,2,1,0:T(8,128)} %bitcast.16), custom_call_target="tpu_custom_call" | custom-call | flops 2000000000 | bytes 23068672 | tf_op jit(solution)/shard_map/forward_yz/pallas_call | solution.py:222
  11.1 7.4 %all-to-all-start = ((f32[16,32,128]{2,1,0:T(8,128)}), f32[16,32,128]{2,1,0:T(8,128)S(1)}, u32[]{:S(2)}, u32[]{:S(2)}) async-start(f32[16,32,128]{2,1,0:T(8,128)} %bitcast.2), calls=%async_computation | async-start | bytes 524288 | tf_op jit(solution)/shard_map/all_to_all | solution.py:681
  18.5 0.0 copy-start
  18.5 0.0 copy-start.1
  18.5 9.8 %fold_weights.1.weights_hbm = f32[16,32,32,128]{3,2,1,0:T(8,128)} custom-call(f32[2,32,32,32,64]{4,3,2,1,0:T(8,128)} %bitcast.17, f32[16,32,32,128]{3,2,1,0:T(8,128)} %get-tuple-element.19._), custom_call_target="tpu_custom_call", output_to_operand_aliasing={{}: (1, {})} | custom-call | flops 4000000 | bytes 26214400 | tf_op jit(solution)/shard_map/fold_weights/pallas_call | solution.py:267
  28.3 0.0 copy-start.2
  28.3 0.0 copy-start.3
  28.3 0.2 all-to-all-done.lines_ref
  28.5 0.0 copy-done
  28.5 0.0 copy-done.1
  28.5 7.1 %mix_modes.1 = (f32[16,32,128]{2,1,0:T(8,128)S(1)}, f32[16,32,128]{2,1,0:T(8,128)}) custom-call(f32[16,16]{1,0:T(8,128)S(1)} %copy-done.1, f32[16,16]{1,0:T(8,128)S(1)} %copy-done, f32[16,32,128]{2,1,0:T(8,128)S(1)} %all-to-all-done.lines_ref, f32[16,32,32,128]{3,2,1,0:T(8,128)} %fold_weights.1.weights_hbm), custom_call_target="tpu_custom_call" | custom-call | flops 20000000 | bytes 9437184 | tf_op jit(solution)/shard_map/mix_modes/pallas_call | solution.py:358
  35.6 5.8 %all-to-all-start.1 = ((f32[16,32,128]{2,1,0:T(8,128)}), f32[16,32,128]{2,1,0:T(8,128)S(1)}, u32[]{:S(2)}, u32[]{:S(2)}) async-start(f32[16,32,128]{2,1,0:T(8,128)} %get-tuple-element.21), calls=%async_computation.1 | async-start | bytes 524288 | tf_op jit(solution)/shard_map/all_to_all | solution.py:681
  41.5 0.0 copy-done.2
  41.5 0.7 copy.21
  42.2 0.0 copy-done.3
  42.2 0.7 copy.22.bias_in_ref
  42.8 8.7 %pointwise.1.pre_ref = f32[32,128,256]{2,1,0:T(8,128)} custom-call(f32[256,32]{1,0:T(8,128)} %constant.20.clone.sum_ref, f32[32,32]{1,0:T(8,128)} %bitcast.22, f32[32,1]{1,0:T(8,128)} %copy.22.bias_in_ref, f32[32,128,256]{2,1,0:T(8,128)} %bitcast.20), custom_call_target="tpu_custom_call" | custom-call | flops 4000000000 | bytes 25165824 | tf_op jit(solution)/shard_map/pointwise/pallas_call | solution.py:422
  51.5 0.0 all-to-all-done.1
  51.5 9.2 %early_cells.1 = (bf16[32,128,256]{2,1,0:T(8,128)(2,1)}, f32[24,128,256]{2,1,0:T(8,128)}, f32[384,128]{1,0:T(8,128)}) custom-call(bf16[128,192]{1,0:T(8,128)(2,1)} %constant.24.clone.inv_y, bf16[256,512]{1,0:T(8,128)(2,1)} %constant.25.clone.inv_z, bf16[128,512]{1,0:T(8,128)(2,1)} %constant.26.clone.inv_z_low, bf16[512,256]{1,0:T(8,128)(2,1)} %constant.21.clone.z_high, ...), custom_call_target="tpu_custom_call" | custom-call | flops 3000000000 | bytes 7340032 | tf_op jit(solution)/shard_map/early_cells/pallas_call | solution.py:534
  60.7 6.0 %all-to-all-start.3 = ((f32[16,24,128]{2,1,0:T(8,128)}), f32[16,24,128]{2,1,0:T(8,128)S(1)}, u32[]{:S(2)}, u32[]{:S(2)}) async-start(f32[16,24,128]{2,1,0:T(8,128)} %bitcast.10), calls=%async_computation.3 | async-start | bytes 393216 | tf_op jit(solution)/shard_map/all_to_all | solution.py:681
  66.7 8.4 %late_cells.1 = (bf16[32,128,256]{2,1,0:T(8,128)(2,1)}, f32[384,128]{1,0:T(8,128)}) custom-call(bf16[128,192]{1,0:T(8,128)(2,1)} %constant.24.clone.inv_y, bf16[256,512]{1,0:T(8,128)(2,1)} %constant.25.clone.inv_z, bf16[128,512]{1,0:T(8,128)(2,1)} %constant.26.clone.inv_z_low, ...), custom_call_target="tpu_custom_call", output_to_operand_aliasing={{0}: (13, {})} | custom-call | flops 6000000000 | bytes 11534336 | tf_op jit(solution)/shard_map/late_cells/pallas_call | solution.py:560
  75.2 0.6 all-to-all-done.3.lines_ref
  75.7 5.5 %all-to-all-start.2 = ((f32[16,24,128]{2,1,0:T(8,128)}), f32[16,24,128]{2,1,0:T(8,128)S(1)}, u32[]{:S(2)}, u32[]{:S(2)}) async-start(f32[16,24,128]{2,1,0:T(8,128)} %bitcast.9), calls=%async_computation.2 | async-start | bytes 393216 | tf_op jit(solution)/shard_map/all_to_all | solution.py:681
  81.2 9.6 %weight_gradient.2.refs_0_ = f32[2,32,32,32,64]{4,3,2,1,0:T(8,128)} custom-call(f32[16,16]{1,0:T(8,128)S(1)} %copy-done.1, f32[16,16]{1,0:T(8,128)S(1)} %copy-done, f32[16,32,128]{2,1,0:T(8,128)S(1)} %get-tuple-element.27.spec_ref, f32[16,24,128]{2,1,0:T(8,128)S(1)} %all-to-all-done.3.lines_ref), custom_call_target="tpu_custom_call" | custom-call | flops 5000000 | bytes 33554432 | tf_op jit(solution)/shard_map/weight_gradient/pallas_call | solution.py:658
  90.8 0.0 all-to-all-done.2.lines_ref
  90.8 5.6 %weight_gradient.3 = (f32[2,32,32,32,64]{4,3,2,1,0:T(8,128)}, f32[32,32]{1,0:T(8,128)}, f32[1,32]{1,0:T(1,128)}) custom-call(f32[16,16]{1,0:T(8,128)S(1)} %copy-done.1, f32[16,16]{1,0:T(8,128)S(1)} %copy-done, f32[16,32,128]{2,1,0:T(8,128)S(1)} %get-tuple-element.27.spec_ref, ...), custom_call_target="tpu_custom_call", output_to_operand_aliasing={{0}: (4, {})} | custom-call | flops 5000000 | bytes 33554432 | tf_op jit(solution)/shard_map/weight_gradient/pallas_call | solution.py:658
Async XLA Ops:
  11.1 17.4 %all-to-all-start = ((f32[16,32,128]{2,1,0:T(8,128)}), f32[16,32,128]{2,1,0:T(8,128)S(1)}, u32[]{:S(2)}, u32[]{:S(2)}) async-start(f32[16,32,128]{2,1,0:T(8,128)} %bitcast.2), calls=%async_computation | async-start | bytes 524288 | tf_op jit(solution)/shard_map/all_to_all | solution.py:681
  18.5 10.0 %copy-start = (f32[16,16]{1,0:T(8,128)S(1)}, f32[16,16]{1,0:T(8,128)}, u32[]{:S(2)}) copy-start(f32[16,16]{1,0:T(8,128)} %constant.19.clone.sin_ref) | copy-start | bytes 3076
  18.5 10.0 %copy-start.1 = (f32[16,16]{1,0:T(8,128)S(1)}, f32[16,16]{1,0:T(8,128)}, u32[]{:S(2)}) copy-start(f32[16,16]{1,0:T(8,128)} %constant.18.clone.cos_ref) | copy-start | bytes 3076
  28.3 13.2 %copy-start.2 = (f32[32,32]{1,0:T(8,128)S(1)}, f32[32,32]{1,0:T(8,128)}, u32[]{:S(2)}) copy-start(f32[32,32]{1,0:T(8,128)} %param.17) | copy-start | bytes 12292
  28.3 13.9 %copy-start.3 = (f32[32]{0:T(128)S(1)}, f32[32]{0:T(128)}, u32[]{:S(2)}) copy-start(f32[32]{0:T(128)} %param.18) | copy-start | bytes 388
  35.6 15.9 %all-to-all-start.1 = ((f32[16,32,128]{2,1,0:T(8,128)}), f32[16,32,128]{2,1,0:T(8,128)S(1)}, u32[]{:S(2)}, u32[]{:S(2)}) async-start(f32[16,32,128]{2,1,0:T(8,128)} %get-tuple-element.21), calls=%async_computation.1 | async-start | bytes 524288 | tf_op jit(solution)/shard_map/all_to_all | solution.py:681
  60.7 15.0 %all-to-all-start.3 = ((f32[16,24,128]{2,1,0:T(8,128)}), f32[16,24,128]{2,1,0:T(8,128)S(1)}, u32[]{:S(2)}, u32[]{:S(2)}) async-start(f32[16,24,128]{2,1,0:T(8,128)} %bitcast.10), calls=%async_computation.3 | async-start | bytes 393216 | tf_op jit(solution)/shard_map/all_to_all | solution.py:681
  75.7 15.1 %all-to-all-start.2 = ((f32[16,24,128]{2,1,0:T(8,128)}), f32[16,24,128]{2,1,0:T(8,128)S(1)}, u32[]{:S(2)}, u32[]{:S(2)}) async-start(f32[16,24,128]{2,1,0:T(8,128)} %bitcast.9), calls=%async_computation.2 | async-start | bytes 393216 | tf_op jit(solution)/shard_map/all_to_all | solution.py:681

commit v8 on v7

--- a/solution.py
+++ b/solution.py
@@ -49,16 +49,18 @@
 
 def forward_tables():
     theta = angles(np.arange(NZ), np.arange(MZ), NZ)
-    cos_z, sin_z = np.cos(theta), np.sin(theta)
-    plain = [lane_spread(f, s, cos_z, -sin_z) for f, s in ((1, 0), (0, 1))]
-    turned = [lane_spread(f, s, -sin_z, -cos_z) for f, s in ((1, 0), (0, 1))]
-    table_z = np.concatenate([np.concatenate(plain, 0), np.concatenate(turned, 0)], axis=1)
-    theta = angles(np.arange(NY), kept(MY, NY), NY)
-    both = np.concatenate([np.cos(theta).T, np.sin(theta).T], axis=1)
-    table_y = np.concatenate([both[0::2], both[1::2]], axis=0)
-    z_high, z_low = split_table(table_z)
-    y_high, y_low = split_table(table_y)
-    return z_high, z_low, np.concatenate([y_high, y_low], axis=0)
+    table = np.concatenate([lane_spread(f, s, np.cos(theta), -np.sin(theta)) for f, s in ((1, 0), (0, 1))], axis=0)
+    high, low = split_table(table)
+    table_z = np.concatenate(
+        [np.concatenate([high, low], axis=1), np.concatenate([high, np.zeros_like(low)], axis=1)], axis=0
+    )
+    theta = angles(np.arange(NY), kept(MY, NY), NY).T
+    table = np.concatenate([np.cos(theta)[0::2], np.cos(theta)[1::2], np.sin(theta)[0::2], np.sin(theta)[1::2]], axis=0)
+    high, low = split_table(table)
+    table_y = np.concatenate(
+        [np.concatenate([high, high], axis=1), np.concatenate([low, np.zeros_like(low)], axis=1)], axis=0
+    )
+    return table_z, table_y
 
 
 def inverse_tables(norm):
@@ -68,14 +70,13 @@
     y_high, y_low = split_table(table_y)
     theta = angles(np.arange(NZ), np.arange(MZ), NZ)
     weight = np.where(np.arange(MZ) == 0, 1.0, 2.0) * norm
-    cos_z, sin_z = np.cos(theta) * weight, -np.sin(theta) * weight
-    table_z = np.concatenate([lane_spread(f, s, cos_z, sin_z).T for f, s in ((1, 0), (0, 1))], axis=1)
-    z_high, z_low = split_table(table_z)
-    return (
-        np.concatenate([y_high, y_high, y_low], axis=1),
-        np.concatenate([z_high, z_high], axis=0),
-        z_low,
-    )
+    parts = (np.cos(theta) * weight, -np.sin(theta) * weight)
+    own, other = lane_spread(1, 0, *parts).T, lane_spread(0, 1, *parts).T
+    tables_z = []
+    for mine, theirs in ((own, other), (other, own)):
+        high = split_table(mine)[0]
+        tables_z.append(np.concatenate([high, high + split_table(theirs)[1]], axis=0))
+    return np.concatenate([y_high, y_high, y_low], axis=1), *tables_z
 
 
 def dot(left, right):
@@ -95,24 +96,22 @@
     return pltpu.roll(values, shift % LANES, len(values.shape) - 1)
 
 
-def forward_group(fields, z_high, z_low, y_both, out_ref, first, rows):
+def forward_group(fields, table_z, table_y, out_ref, first, rows):
     left = jnp.concatenate(
         [jnp.concatenate([fields[q], fields[q + 1]], axis=1) for q in range(0, len(fields), 2)], axis=0
     )
-    high, low = split(left)
-    lines = dot(high, z_high) + dot(high, z_low) + dot(low, z_high)
+    lines = dot(jnp.concatenate(split(left), axis=1), table_z)
+    lines = lines[:, :LANES] + lines[:, LANES:]
     half = MY // 2
     for g in range(0, len(fields) // 2, GROUP // 2):
-        pairs = []
-        for q in range(g, g + GROUP // 2):
-            part = lines[q * NY : (q + 1) * NY]
-            pairs.append(jnp.concatenate([part[:, :LANES], part[:, LANES:]], axis=0))
-        high, low = split(jnp.concatenate(pairs, axis=1))
-        wide = dot(y_both, high)
-        modes = wide[:MY] + wide[MY:] + dot(y_both[:MY], low)
+        quad = jnp.concatenate([lines[q * NY : (q + 1) * NY] for q in range(g, g + GROUP // 2)], axis=1)
+        wide = dot(table_y, jnp.concatenate(split(quad), axis=0))
+        wide = wide[: 2 * MY] + wide[2 * MY :]
         for q in range(GROUP // 2):
-            even = modes[:half, q * LANES : (q + 1) * LANES]
-            odd = modes[half:, q * LANES : (q + 1) * LANES]
+            by_cos = wide[:MY, q * LANES : (q + 1) * LANES]
+            by_sin = roll(wide[MY:, q * LANES : (q + 1) * LANES], 64)
+            modes = by_cos + jnp.where(lane_index(by_sin.shape) < LANES // 2, by_sin, -by_sin)
+            even, odd = modes[:half], modes[half:]
             at_even = (lane_index(even.shape) // MZ) % 2 == 0
             at = first + 2 * (g + q)
             out_ref[pl.ds(at, half, stride=rows), :] = jnp.where(at_even, even, roll(odd, MZ))
@@ -180,14 +179,14 @@
 
 
 def forward_kernel(
-    z_high, z_low, y_both, field_ref, weights_hbm, out_ref, folded_ref, ring_ref, sems,
+    table_z, table_y, field_ref, weights_hbm, out_ref, folded_ref, ring_ref, sems,
     *, channels, step_channels, per_step, unique, slots,
 ):
     step = pl.program_id(0)
 
     def transform():
         fields = [field_ref[q] for q in range(step_channels)]
-        forward_group(fields, z_high[...], z_low[...], y_both[...], out_ref, step * step_channels, channels)
+        forward_group(fields, table_z[...], table_y[...], out_ref, step * step_channels, channels)
 
     @pl.when(step == 0)
     def _():
@@ -302,19 +301,14 @@
 
 
 def mix_kernel(
-    cos_ref, sin_ref, lines_ref, weights_hbm, spec_ref, out_ref,
-    sums_ref, total_ref, real_ref, imag_ref, weights_ref, sems, *, points, channels, per_step, norm,
+    cos_ref, sin_ref, lines_ref, weights_ref, spec_ref, out_ref, sums_ref, total_ref, real_ref, imag_ref,
+    *, points, channels, per_step, norm,
 ):
     step = pl.program_id(0)
     half = points // 2
 
-    def fetch(at):
-        return pltpu.make_async_copy(weights_hbm.at[at], weights_ref.at[at], sems.at[at])
-
     @pl.when(step == 0)
     def _():
-        for at in range(points):
-            fetch(at).start()
         halve_lines(lines_ref, sums_ref, points, channels)
         total_ref[...] = jnp.zeros_like(total_ref)
 
@@ -327,9 +321,8 @@
         real_ref[q], imag_ref[q] = doubled(spec)
         by_real = jnp.zeros((channels, LANES), F32)
         by_imag = jnp.zeros((channels, LANES), F32)
-        fetch(at).wait()
         for i in range(channels):
-            weight = weights_ref[at, i]
+            weight = weights_ref[q, i]
             by_real += real_ref[q, pl.ds(i, 1), :] * weight
             by_imag += imag_ref[q, pl.ds(i, 1), :] * weight
         other = roll(by_imag, 64)
@@ -362,7 +355,7 @@
             smem(),
             smem(),
             full(shape),
-            pl.BlockSpec(memory_space=pl.ANY),
+            pl.BlockSpec((per_step,) + weights.shape[1:], lambda s: (s, 0, 0, 0)),
         ],
         out_specs=[
             pl.BlockSpec((per_step, channels, LANES), lambda s: (s, 0, 0)),
@@ -377,8 +370,6 @@
             pltpu.VMEM((2, points // 2, channels, LANES), F32),
             pltpu.VMEM((per_step, channels, LANES), F32),
             pltpu.VMEM((per_step, channels, LANES), F32),
-            pltpu.VMEM(weights.shape, F32),
-            pltpu.SemaphoreType.DMA((unique,)),
         ],
         compiler_params=params(LIMIT),
         cost_estimate=pl.CostEstimate(flops=2 * 10**7, bytes_accessed=9 * MIB, transcendentals=0),
@@ -432,35 +423,54 @@
     )(*in_hbm(summing, turned, bias, field))
 
 
-def cell_group(inv_y, inv_z, inv_z_low, modes_ref, pre_ref, cot_ref, act_ref, first, count, channels):
+TAIL = (
+    0.28208447628636224, 0.2824095107622592, 0.24285420127949567, 0.20367621235863168, -0.028966708844937322,
+    0.28146769954808826, -0.490173103351073, 0.2860108822904108, -0.0593632144096072,
+)
+
+
+def normal(values):
+    bell = jnp.exp(-0.5 * values * values)
+    t = 1.0 / (1.0 + (0.5 * INV_SQRT_TWO) * jnp.abs(values))
+    tail = 0.5 * TAIL[-1]
+    for factor in TAIL[-2::-1]:
+        tail = tail * t + 0.5 * factor
+    tail = tail * t * bell
+    return jnp.where(values < 0.0, tail, 1.0 - tail), values * bell * INV_SQRT_TWO_PI
+
+
+def cell_group(inv_y, inv_z, modes_ref, pre_ref, cot_ref, act_ref, first, count, channels):
     lines = []
     for g in range(0, count, GROUP):
         lines += inverse_y_group(modes_ref, inv_y, first + g, channels)
-    high, low = split(jnp.concatenate(lines, axis=0))
-    spectral = dot(jnp.concatenate([high, low], axis=1), inv_z) + dot(high, inv_z_low)
+    lines = jnp.concatenate(lines, axis=0)
+    high = lines.astype(BF16).astype(F32)
+    low = lines - high
+    at_even = (lane_index(lines.shape) // MZ) % 2 == 0
+    spectral = [
+        dot(jnp.concatenate([high, side], axis=1).astype(BF16), table)
+        for side, table in zip((jnp.where(at_even, low, roll(high, MZ)), jnp.where(at_even, roll(high, -MZ), low)), inv_z)
+    ]
     slopes = []
     for q in range(count):
-        r = q // 2 * NY
-        c = q % 2 * NZ
-        before = spectral[r : r + NY, c : c + NZ] + pre_ref[q]
-        cdf = 0.5 + 0.5 * lax.erf(before * INV_SQRT_TWO)
+        before = spectral[q % 2][q // 2 * NY : (q // 2 + 1) * NY] + pre_ref[q]
+        cdf, bent = normal(before)
         act_ref[q] = (before * cdf).astype(BF16)
-        pdf = jnp.exp(-0.5 * before * before) * INV_SQRT_TWO_PI
-        slopes.append(cot_ref[q].astype(F32) * (cdf + before * pdf))
+        slopes.append(cot_ref[q].astype(F32) * (cdf + bent))
     return slopes
 
 
 def early_cell_kernel(
-    inv_y, inv_z, inv_z_low, z_high, z_low, y_both, modes_ref, pre_ref, cot_ref, act_ref, slope_ref, out_ref,
+    inv_y, inv_z0, inv_z1, table_z, table_y, modes_ref, pre_ref, cot_ref, act_ref, slope_ref, out_ref,
     *, channels, count, rows,
 ):
     step = pl.program_id(0)
     slopes = cell_group(
-        inv_y[...], inv_z[...], inv_z_low[...], modes_ref, pre_ref, cot_ref, act_ref, step * count, count, channels
+        inv_y[...], (inv_z0[...], inv_z1[...]), modes_ref, pre_ref, cot_ref, act_ref, step * count, count, channels
     )
     for q in range(count):
         slope_ref[q] = slopes[q]
-    forward_group(slopes, z_high[...], z_low[...], y_both[...], out_ref, step * count, rows)
+    forward_group(slopes, table_z[...], table_y[...], out_ref, step * count, rows)
 
 
 def point_gradient(field_ref, slope_ref, sum_ref, channels):
@@ -482,7 +492,7 @@
 
 
 def late_cell_kernel(
-    inv_y, inv_z, inv_z_low, z_high, z_low, y_both, sum_ref, modes_ref, pre_ref, cot_ref, early_ref,
+    inv_y, inv_z0, inv_z1, table_z, table_y, sum_ref, modes_ref, pre_ref, cot_ref, early_ref,
     slope_hbm, field_hbm, _, act_ref, out_ref, field_ref, slope_ref, sems, *, channels, count, rows, owners,
 ):
     step = pl.program_id(0)
@@ -500,11 +510,11 @@
 
     first = early + step * count
     slopes = cell_group(
-        inv_y[...], inv_z[...], inv_z_low[...], modes_ref, pre_ref, cot_ref, act_ref, first, count, channels
+        inv_y[...], (inv_z0[...], inv_z1[...]), modes_ref, pre_ref, cot_ref, act_ref, first, count, channels
     )
     for q in range(count):
         slope_ref[first + q] = slopes[q]
-    forward_group(slopes, z_high[...], z_low[...], y_both[...], out_ref, step * count, rows)
+    forward_group(slopes, table_z[...], table_y[...], out_ref, step * count, rows)
 
     @pl.when(step == pl.num_programs(0) - 1)
     def _():

time: 97.1 us -> 96.8 us (level)
    pallas_call x1, Pallas kernels: 7.06 us -> 5.83 us  [mix(): pl.pallas_call(functools.partial(mix_kernel, points=points, channels=chan...]
    pallas_call x1, Pallas kernels: 9.16 us -> 10.1 us  [early_cells(): pl.pallas_call(functools.partial(early_cell_kernel, channels=channels, co...]
where the time goes in v8:
time: 96.8 us; the launch traced here: 96.1 us
  Pallas kernels  68.4 us (71%)
  starting transfers between devices  24.6 us (25%)
  local copies, waits for them, and re-layouts  1.39 us (1%)
    all_to_all x4, starting transfers between devices, swap(): lax.all_to_all(lines, 'space', split_axis=0, concat_axis=0, tiled=True)  24.6 us
    pallas_call x2, Pallas kernels, gradient(): pl.pallas_call(functools.partial(gradient_kernel, points=points, channels...  15.3 us
    pallas_call x1, Pallas kernels, forward_modes(): pl.pallas_call(functools.partial(forward_kernel, channels=channels, step_...  10.5 us
    pallas_call x1, Pallas kernels, early_cells(): pl.pallas_call(functools.partial(early_cell_kernel, channels=channels, co...  10.1 us
    pallas_call x1, Pallas kernels, fold_rest(): pl.pallas_call(functools.partial(fold_kernel, first=first, unique=unique,...  9.77 us
    pallas_call x1, Pallas kernels, pointwise(): pl.pallas_call(functools.partial(pointwise_kernel, channels=channels, blo...  8.67 us
    pallas_call x1, Pallas kernels, late_cells(): pl.pallas_call(functools.partial(late_cell_kernel, channels=channels, cou...  8.33 us
    pallas_call x1, Pallas kernels, mix(): pl.pallas_call(functools.partial(mix_kernel, points=points, channels=chan...  5.83 us
  transfers between devices with their start and end apart: 4, of which 2 were waited for; matrix products, arithmetic and copies ran while one was open for 1% of the time, Pallas kernels for 38%

profile of v8, /device:TPU:0, one launch (start us, length us, event | category | flops | bytes accessed | tf_op | source)
XLA Modules:
  0.0 96.1 jit_solution(14876114366516830670)
XLA Ops:
  0.6 10.5 %forward_yz.1 = (f32[512,128]{1,0:T(8,128)}, f32[16,32,32,128]{3,2,1,0:T(8,128)}) custom-call(bf16[1024,256]{1,0:T(8,128)(2,1)} %constant.19.clone.table_z, bf16[128,256]{1,0:T(8,128)(2,1)} %constant.20.clone.table_y, f32[32,128,256]{2,1,0:T(8,128)} %bitcast.19, f32[2,32,32,32,64]{4,3,2,1,0:T(8,128)} %bitcast.16), custom_call_target="tpu_custom_call" | custom-call | flops 2000000000 | bytes 23068672 | tf_op jit(solution)/shard_map/forward_yz/pallas_call | solution.py:221
  11.1 7.4 %all-to-all-start = ((f32[16,32,128]{2,1,0:T(8,128)}), f32[16,32,128]{2,1,0:T(8,128)S(1)}, u32[]{:S(2)}, u32[]{:S(2)}) async-start(f32[16,32,128]{2,1,0:T(8,128)} %bitcast.2), calls=%async_computation | async-start | bytes 524288 | tf_op jit(solution)/shard_map/all_to_all | solution.py:691
  18.5 0.0 copy-start
  18.5 0.0 copy-start.1
  18.5 9.8 %fold_weights.1.weights_ref = f32[16,32,32,128]{3,2,1,0:T(8,128)} custom-call(f32[2,32,32,32,64]{4,3,2,1,0:T(8,128)} %bitcast.17, f32[16,32,32,128]{3,2,1,0:T(8,128)} %get-tuple-element.19._), custom_call_target="tpu_custom_call", output_to_operand_aliasing={{}: (1, {})} | custom-call | flops 4000000 | bytes 26214400 | tf_op jit(solution)/shard_map/fold_weights/pallas_call | solution.py:266
  28.3 0.0 copy-start.2
  28.3 0.0 copy-start.3
  28.3 0.2 all-to-all-done.lines_ref
  28.6 0.0 copy-done
  28.6 0.0 copy-done.1
  28.6 5.8 %mix_modes.1 = (f32[16,32,128]{2,1,0:T(8,128)S(1)}, f32[16,32,128]{2,1,0:T(8,128)}) custom-call(f32[16,16]{1,0:T(8,128)S(1)} %copy-done.1, f32[16,16]{1,0:T(8,128)S(1)} %copy-done, f32[16,32,128]{2,1,0:T(8,128)S(1)} %all-to-all-done.lines_ref, f32[16,32,32,128]{3,2,1,0:T(8,128)} %fold_weights.1.weights_ref), custom_call_target="tpu_custom_call" | custom-call | flops 20000000 | bytes 9437184 | tf_op jit(solution)/shard_map/mix_modes/pallas_call | solution.py:351
  34.4 5.8 %all-to-all-start.1 = ((f32[16,32,128]{2,1,0:T(8,128)}), f32[16,32,128]{2,1,0:T(8,128)S(1)}, u32[]{:S(2)}, u32[]{:S(2)}) async-start(f32[16,32,128]{2,1,0:T(8,128)} %get-tuple-element.21), calls=%async_computation.1 | async-start | bytes 524288 | tf_op jit(solution)/shard_map/all_to_all | solution.py:691
  40.2 0.0 copy-done.2
  40.2 0.7 copy.20
  40.9 0.0 copy-done.3
  40.9 0.7 copy.21.bias_in_ref
  41.6 8.7 %pointwise.1.pre_ref = f32[32,128,256]{2,1,0:T(8,128)} custom-call(f32[256,32]{1,0:T(8,128)} %constant.18.clone.sum_ref, f32[32,32]{1,0:T(8,128)} %bitcast.22, f32[32,1]{1,0:T(8,128)} %copy.21.bias_in_ref, f32[32,128,256]{2,1,0:T(8,128)} %bitcast.20), custom_call_target="tpu_custom_call" | custom-call | flops 4000000000 | bytes 25165824 | tf_op jit(solution)/shard_map/pointwise/pallas_call | solution.py:413
  50.3 0.0 all-to-all-done.1
  50.3 10.1 %early_cells.1 = (bf16[32,128,256]{2,1,0:T(8,128)(2,1)}, f32[24,128,256]{2,1,0:T(8,128)}, f32[384,128]{1,0:T(8,128)}) custom-call(bf16[128,192]{1,0:T(8,128)(2,1)} %constant.21.clone.inv_y, bf16[256,256]{1,0:T(8,128)(2,1)} %constant.22.clone.inv_z0, bf16[256,256]{1,0:T(8,128)(2,1)} %constant.23.clone.inv_z1, bf16[1024,256]{1,0:T(8,128)(2,1)} %constant.19.clone.table_z, ...), custom_call_target="tpu_custom_call" | custom-call | flops 3000000000 | bytes 7340032 | tf_op jit(solution)/shard_map/early_cells/pallas_call | solution.py:544
  60.4 6.0 %all-to-all-start.3 = ((f32[16,24,128]{2,1,0:T(8,128)}), f32[16,24,128]{2,1,0:T(8,128)S(1)}, u32[]{:S(2)}, u32[]{:S(2)}) async-start(f32[16,24,128]{2,1,0:T(8,128)} %bitcast.10), calls=%async_computation.3 | async-start | bytes 393216 | tf_op jit(solution)/shard_map/all_to_all | solution.py:691
  66.4 8.3 %late_cells.1 = (bf16[32,128,256]{2,1,0:T(8,128)(2,1)}, f32[384,128]{1,0:T(8,128)}) custom-call(bf16[128,192]{1,0:T(8,128)(2,1)} %constant.21.clone.inv_y, bf16[256,256]{1,0:T(8,128)(2,1)} %constant.22.clone.inv_z0, bf16[256,256]{1,0:T(8,128)(2,1)} %constant.23.clone.inv_z1, ...), custom_call_target="tpu_custom_call", output_to_operand_aliasing={{0}: (12, {})} | custom-call | flops 6000000000 | bytes 11534336 | tf_op jit(solution)/shard_map/late_cells/pallas_call | solution.py:570
  74.8 0.7 all-to-all-done.3.lines_ref
  75.4 5.4 %all-to-all-start.2 = ((f32[16,24,128]{2,1,0:T(8,128)}), f32[16,24,128]{2,1,0:T(8,128)S(1)}, u32[]{:S(2)}, u32[]{:S(2)}) async-start(f32[16,24,128]{2,1,0:T(8,128)} %bitcast.9), calls=%async_computation.2 | async-start | bytes 393216 | tf_op jit(solution)/shard_map/all_to_all | solution.py:691
  80.8 9.6 %weight_gradient.2.refs_0_ = f32[2,32,32,32,64]{4,3,2,1,0:T(8,128)} custom-call(f32[16,16]{1,0:T(8,128)S(1)} %copy-done.1, f32[16,16]{1,0:T(8,128)S(1)} %copy-done, f32[16,32,128]{2,1,0:T(8,128)S(1)} %get-tuple-element.27.spec_ref, f32[16,24,128]{2,1,0:T(8,128)S(1)} %all-to-all-done.3.lines_ref), custom_call_target="tpu_custom_call" | custom-call | flops 5000000 | bytes 33554432 | tf_op jit(solution)/shard_map/weight_gradient/pallas_call | solution.py:668
  90.4 0.0 all-to-all-done.2.lines_ref
  90.4 5.6 %weight_gradient.3 = (f32[2,32,32,32,64]{4,3,2,1,0:T(8,128)}, f32[32,32]{1,0:T(8,128)}, f32[1,32]{1,0:T(1,128)}) custom-call(f32[16,16]{1,0:T(8,128)S(1)} %copy-done.1, f32[16,16]{1,0:T(8,128)S(1)} %copy-done, f32[16,32,128]{2,1,0:T(8,128)S(1)} %get-tuple-element.27.spec_ref, ...), custom_call_target="tpu_custom_call", output_to_operand_aliasing={{0}: (4, {})} | custom-call | flops 5000000 | bytes 33554432 | tf_op jit(solution)/shard_map/weight_gradient/pallas_call | solution.py:668
Async XLA Ops:
  11.1 17.4 %all-to-all-start = ((f32[16,32,128]{2,1,0:T(8,128)}), f32[16,32,128]{2,1,0:T(8,128)S(1)}, u32[]{:S(2)}, u32[]{:S(2)}) async-start(f32[16,32,128]{2,1,0:T(8,128)} %bitcast.2), calls=%async_computation | async-start | bytes 524288 | tf_op jit(solution)/shard_map/all_to_all | solution.py:691
  18.5 10.0 %copy-start = (f32[16,16]{1,0:T(8,128)S(1)}, f32[16,16]{1,0:T(8,128)}, u32[]{:S(2)}) copy-start(f32[16,16]{1,0:T(8,128)} %constant.17.clone.sin_ref) | copy-start | bytes 3076
  18.5 10.0 %copy-start.1 = (f32[16,16]{1,0:T(8,128)S(1)}, f32[16,16]{1,0:T(8,128)}, u32[]{:S(2)}) copy-start(f32[16,16]{1,0:T(8,128)} %constant.16.clone.cos_ref) | copy-start | bytes 3076
  28.3 11.9 %copy-start.2 = (f32[32,32]{1,0:T(8,128)S(1)}, f32[32,32]{1,0:T(8,128)}, u32[]{:S(2)}) copy-start(f32[32,32]{1,0:T(8,128)} %param.16) | copy-start | bytes 12292
  28.3 12.6 %copy-start.3 = (f32[32]{0:T(128)S(1)}, f32[32]{0:T(128)}, u32[]{:S(2)}) copy-start(f32[32]{0:T(128)} %param.17) | copy-start | bytes 388
  34.4 15.9 %all-to-all-start.1 = ((f32[16,32,128]{2,1,0:T(8,128)}), f32[16,32,128]{2,1,0:T(8,128)S(1)}, u32[]{:S(2)}, u32[]{:S(2)}) async-start(f32[16,32,128]{2,1,0:T(8,128)} %get-tuple-element.21), calls=%async_computation.1 | async-start | bytes 524288 | tf_op jit(solution)/shard_map/all_to_all | solution.py:691
  60.4 15.0 %all-to-all-start.3 = ((f32[16,24,128]{2,1,0:T(8,128)}), f32[16,24,128]{2,1,0:T(8,128)S(1)}, u32[]{:S(2)}, u32[]{:S(2)}) async-start(f32[16,24,128]{2,1,0:T(8,128)} %bitcast.10), calls=%async_computation.3 | async-start | bytes 393216 | tf_op jit(solution)/shard_map/all_to_all | solution.py:691
  75.4 15.0 %all-to-all-start.2 = ((f32[16,24,128]{2,1,0:T(8,128)}), f32[16,24,128]{2,1,0:T(8,128)S(1)}, u32[]{:S(2)}, u32[]{:S(2)}) async-start(f32[16,24,128]{2,1,0:T(8,128)} %bitcast.9), calls=%async_computation.2 | async-start | bytes 393216 | tf_op jit(solution)/shard_map/all_to_all | solution.py:691

commit v9 on v8

--- a/solution.py
+++ b/solution.py
@@ -179,30 +179,41 @@
 
 
 def forward_kernel(
-    table_z, table_y, field_ref, weights_hbm, out_ref, folded_ref, ring_ref, sems,
-    *, channels, step_channels, per_step, unique, slots,
+    table_z, table_y, block_ref, field_hbm, weights_hbm, out_ref, folded_hbm,
+    field_ref, ring_ref, folded_ref, field_sems, sems, folded_sems, *, channels, step_channels, unique, slots,
 ):
-    step = pl.program_id(0)
-
-    def transform():
-        fields = [field_ref[q] for q in range(step_channels)]
-        forward_group(fields, table_z[...], table_y[...], out_ref, step * step_channels, channels)
-
-    @pl.when(step == 0)
-    def _():
-        for at in range(slots):
-            for copy in fetches(weights_hbm, ring_ref, sems, at, at, unique):
-                copy.start()
-        transform()
-
-    @pl.when(step > 0)
-    def _():
-        for q in range(per_step):
-            at = (step - 1) * per_step + q
-            for copy in fetches(weights_hbm, ring_ref, sems, at, at, unique):
-                copy.wait()
-            fold_block(ring_ref.at[at], folded_ref, q)
-        transform()
+    steps = channels // step_channels
+    per_step = slots // (steps - 1)
+    fields = [
+        pltpu.make_async_copy(
+            field_hbm.at[pl.ds(s * step_channels, step_channels)],
+            field_ref.at[pl.ds((s - 1) * step_channels, step_channels)],
+            field_sems.at[s - 1],
+        )
+        for s in range(1, steps)
+    ]
+    weights = [fetches(weights_hbm, ring_ref, sems, at, at, unique) for at in range(slots)]
+    stores = [pltpu.make_async_copy(folded_ref.at[at], folded_hbm.at[at], folded_sems.at[at]) for at in range(slots)]
+    for copy in fields:
+        copy.start()
+    for each in weights:
+        for copy in each:
+            copy.start()
+    for s in range(steps):
+        if s > 0:
+            fields[s - 1].wait()
+            for at in range((s - 1) * per_step, s * per_step):
+                for copy in weights[at]:
+                    copy.wait()
+                fold_block(ring_ref.at[at], folded_ref, at)
+        base = (s - 1) * step_channels
+        part = [block_ref[q] if s == 0 else field_ref[base + q] for q in range(step_channels)]
+        forward_group(part, table_z[...], table_y[...], out_ref, s * step_channels, channels)
+        if s > 0:
+            for at in range((s - 1) * per_step, s * per_step):
+                stores[at].start()
+    for copy in stores:
+        copy.wait()
 
 
 FOLD_STEP = 2
@@ -218,23 +229,26 @@
     slots = folded_early(channels)
     folded_shape, ring = fold_shapes(weights, unique, slots)
     owners = MY // 2
+    anywhere = pl.BlockSpec(memory_space=pl.ANY)
     out, some = pl.pallas_call(
-        functools.partial(
-            forward_kernel, channels=channels, step_channels=FIELD_STEP, per_step=FOLD_STEP, unique=unique, slots=slots
-        ),
-        grid=(channels // FIELD_STEP,),
+        functools.partial(forward_kernel, channels=channels, step_channels=FIELD_STEP, unique=unique, slots=slots),
+        grid=(1,),
         in_specs=[full(t.shape) for t in tables]
-        + [pl.BlockSpec((FIELD_STEP, NY, NZ), lambda s: (s, 0, 0)), pl.BlockSpec(memory_space=pl.ANY)],
-        out_specs=[
-            full((owners * channels, LANES)),
-            pl.BlockSpec((FOLD_STEP,) + folded_shape.shape[1:], lambda s: (jnp.maximum(s - 1, 0), 0, 0, 0)),
+        + [pl.BlockSpec((FIELD_STEP, NY, NZ), lambda s: (0, 0, 0)), anywhere, anywhere],
+        out_specs=[full((owners * channels, LANES)), anywhere],
+        out_shape=[pltpu.VMEM((owners * channels, LANES), F32), folded_shape],
+        scratch_shapes=[
+            pltpu.VMEM((channels - FIELD_STEP, NY, NZ), F32),
+            ring[0],
+            pltpu.VMEM((slots,) + folded_shape.shape[1:], F32),
+            pltpu.SemaphoreType.DMA((channels // FIELD_STEP - 1,)),
+            ring[1],
+            pltpu.SemaphoreType.DMA((slots,)),
         ],
-        out_shape=[pltpu.VMEM((owners * channels, LANES), F32), folded_shape],
-        scratch_shapes=ring,
         compiler_params=params(LIMIT),
         cost_estimate=pl.CostEstimate(flops=2 * 10**9, bytes_accessed=22 * MIB, transcendentals=0),
         name="forward_yz",
-    )(*in_hbm(*tables, field, weights))
+    )(*in_hbm(*tables, field, field, weights))
     return out.reshape(owners, channels, LANES), some
 
 
@@ -423,22 +437,6 @@
     )(*in_hbm(summing, turned, bias, field))
 
 
-TAIL = (
-    0.28208447628636224, 0.2824095107622592, 0.24285420127949567, 0.20367621235863168, -0.028966708844937322,
-    0.28146769954808826, -0.490173103351073, 0.2860108822904108, -0.0593632144096072,
-)
-
-
-def normal(values):
-    bell = jnp.exp(-0.5 * values * values)
-    t = 1.0 / (1.0 + (0.5 * INV_SQRT_TWO) * jnp.abs(values))
-    tail = 0.5 * TAIL[-1]
-    for factor in TAIL[-2::-1]:
-        tail = tail * t + 0.5 * factor
-    tail = tail * t * bell
-    return jnp.where(values < 0.0, tail, 1.0 - tail), values * bell * INV_SQRT_TWO_PI
-
-
 def cell_group(inv_y, inv_z, modes_ref, pre_ref, cot_ref, act_ref, first, count, channels):
     lines = []
     for g in range(0, count, GROUP):
@@ -454,9 +452,10 @@
     slopes = []
     for q in range(count):
         before = spectral[q % 2][q // 2 * NY : (q // 2 + 1) * NY] + pre_ref[q]
-        cdf, bent = normal(before)
+        cdf = 0.5 + 0.5 * lax.erf(before * INV_SQRT_TWO)
         act_ref[q] = (before * cdf).astype(BF16)
-        slopes.append(cot_ref[q].astype(F32) * (cdf + bent))
+        pdf = jnp.exp(-0.5 * before * before) * INV_SQRT_TWO_PI
+        slopes.append(cot_ref[q].astype(F32) * (cdf + before * pdf))
     return slopes
 
 

time: 96.8 us -> 95.6 us (0.988)
  Pallas kernels: 68.4 us -> 67.3 us
    pallas_call x1, Pallas kernels: 10.1 us -> 7.95 us  [early_cells(): pl.pallas_call(functools.partial(early_cell_kernel, channels=channels, co...]
    pallas_call x1, Pallas kernels: 10.5 us -> 11.5 us  [forward_modes(): pl.pallas_call(functools.partial(forward_kernel, channels=channels, step_...]
where the time goes in v9:
time: 95.6 us; the launch traced here: 94.9 us
  Pallas kernels  67.3 us (70%)
  starting transfers between devices  24.6 us (26%)
  local copies, waits for them, and re-layouts  1.39 us (1%)
    all_to_all x4, starting transfers between devices, swap(): lax.all_to_all(lines, 'space', split_axis=0, concat_axis=0, tiled=True)  24.6 us
    pallas_call x2, Pallas kernels, gradient(): pl.pallas_call(functools.partial(gradient_kernel, points=points, channels...  15.3 us
    pallas_call x1, Pallas kernels, forward_modes(): pl.pallas_call(functools.partial(forward_kernel, channels=channels, step_...  11.5 us
    pallas_call x1, Pallas kernels, fold_rest(): pl.pallas_call(functools.partial(fold_kernel, first=first, unique=unique,...  9.77 us
    pallas_call x1, Pallas kernels, pointwise(): pl.pallas_call(functools.partial(pointwise_kernel, channels=channels, blo...  8.67 us
    pallas_call x1, Pallas kernels, late_cells(): pl.pallas_call(functools.partial(late_cell_kernel, channels=channels, cou...  8.33 us
    pallas_call x1, Pallas kernels, early_cells(): pl.pallas_call(functools.partial(early_cell_kernel, channels=channels, co...  7.95 us
    pallas_call x1, Pallas kernels, mix(): pl.pallas_call(functools.partial(mix_kernel, points=points, channels=chan...  5.83 us
  transfers between devices with their start and end apart: 4, of which 2 were waited for; matrix products, arithmetic and copies ran while one was open for 1% of the time, Pallas kernels for 38%

profile of v9, /device:TPU:0, one launch (start us, length us, event | category | flops | bytes accessed | tf_op | source)
XLA Modules:
  0.0 94.9 jit_solution(5903768015610228310)
XLA Ops:
  0.6 11.5 %forward_yz.1 = (f32[512,128]{1,0:T(8,128)}, f32[16,32,32,128]{3,2,1,0:T(8,128)}) custom-call(bf16[1024,256]{1,0:T(8,128)(2,1)} %constant.19.clone.table_z, bf16[128,256]{1,0:T(8,128)(2,1)} %constant.20.clone.table_y, f32[32,128,256]{2,1,0:T(8,128)} %bitcast.19, f32[32,128,256]{2,1,0:T(8,128)} %bitcast.20, f32[2,32,32,32,64]{4,3,2,1,0:T(8,128)} %bitcast.16), custom_call_target="tpu_custom_call" | custom-call | flops 2000000000 | bytes 23068672 | tf_op jit(solution)/shard_map/forward_yz/pallas_call | solution.py:233
  12.1 7.4 %all-to-all-start = ((f32[16,32,128]{2,1,0:T(8,128)}), f32[16,32,128]{2,1,0:T(8,128)S(1)}, u32[]{:S(2)}, u32[]{:S(2)}) async-start(f32[16,32,128]{2,1,0:T(8,128)} %bitcast.2), calls=%async_computation | async-start | bytes 524288 | tf_op jit(solution)/shard_map/all_to_all | solution.py:690
  19.5 0.0 copy-start
  19.6 0.0 copy-start.1
  19.6 9.8 %fold_weights.1.weights_ref = f32[16,32,32,128]{3,2,1,0:T(8,128)} custom-call(f32[2,32,32,32,64]{4,3,2,1,0:T(8,128)} %bitcast.17, f32[16,32,32,128]{3,2,1,0:T(8,128)} %get-tuple-element.19._), custom_call_target="tpu_custom_call", output_to_operand_aliasing={{}: (1, {})} | custom-call | flops 4000000 | bytes 26214400 | tf_op jit(solution)/shard_map/fold_weights/pallas_call | solution.py:280
  29.3 0.0 copy-start.2
  29.4 0.0 copy-start.3
  29.4 0.2 all-to-all-done.lines_ref
  29.6 0.0 copy-done
  29.6 0.0 copy-done.1
  29.6 5.8 %mix_modes.1 = (f32[16,32,128]{2,1,0:T(8,128)S(1)}, f32[16,32,128]{2,1,0:T(8,128)}) custom-call(f32[16,16]{1,0:T(8,128)S(1)} %copy-done.1, f32[16,16]{1,0:T(8,128)S(1)} %copy-done, f32[16,32,128]{2,1,0:T(8,128)S(1)} %all-to-all-done.lines_ref, f32[16,32,32,128]{3,2,1,0:T(8,128)} %fold_weights.1.weights_ref), custom_call_target="tpu_custom_call" | custom-call | flops 20000000 | bytes 9437184 | tf_op jit(solution)/shard_map/mix_modes/pallas_call | solution.py:365
  35.4 5.8 %all-to-all-start.1 = ((f32[16,32,128]{2,1,0:T(8,128)}), f32[16,32,128]{2,1,0:T(8,128)S(1)}, u32[]{:S(2)}, u32[]{:S(2)}) async-start(f32[16,32,128]{2,1,0:T(8,128)} %get-tuple-element.21), calls=%async_computation.1 | async-start | bytes 524288 | tf_op jit(solution)/shard_map/all_to_all | solution.py:690
  41.3 0.0 copy-done.2
  41.3 0.7 copy.20
  41.9 0.0 copy-done.3
  41.9 0.7 copy.21.bias_in_ref
  42.6 8.7 %pointwise.1.pre_ref = f32[32,128,256]{2,1,0:T(8,128)} custom-call(f32[256,32]{1,0:T(8,128)} %constant.18.clone.sum_ref, f32[32,32]{1,0:T(8,128)} %bitcast.23, f32[32,1]{1,0:T(8,128)} %copy.21.bias_in_ref, f32[32,128,256]{2,1,0:T(8,128)} %bitcast.21), custom_call_target="tpu_custom_call" | custom-call | flops 4000000000 | bytes 25165824 | tf_op jit(solution)/shard_map/pointwise/pallas_call | solution.py:427
  51.3 0.0 all-to-all-done.1
  51.3 8.0 %early_cells.1 = (bf16[32,128,256]{2,1,0:T(8,128)(2,1)}, f32[24,128,256]{2,1,0:T(8,128)}, f32[384,128]{1,0:T(8,128)}) custom-call(bf16[128,192]{1,0:T(8,128)(2,1)} %constant.21.clone.inv_y, bf16[256,256]{1,0:T(8,128)(2,1)} %constant.22.clone.inv_z0, bf16[256,256]{1,0:T(8,128)(2,1)} %constant.23.clone.inv_z1, bf16[1024,256]{1,0:T(8,128)(2,1)} %constant.19.clone.table_z, ...), custom_call_target="tpu_custom_call" | custom-call | flops 3000000000 | bytes 7340032 | tf_op jit(solution)/shard_map/early_cells/pallas_call | solution.py:543
  59.3 6.0 %all-to-all-start.3 = ((f32[16,24,128]{2,1,0:T(8,128)}), f32[16,24,128]{2,1,0:T(8,128)S(1)}, u32[]{:S(2)}, u32[]{:S(2)}) async-start(f32[16,24,128]{2,1,0:T(8,128)} %bitcast.10), calls=%async_computation.3 | async-start | bytes 393216 | tf_op jit(solution)/shard_map/all_to_all | solution.py:690
  65.3 8.3 %late_cells.1 = (bf16[32,128,256]{2,1,0:T(8,128)(2,1)}, f32[384,128]{1,0:T(8,128)}) custom-call(bf16[128,192]{1,0:T(8,128)(2,1)} %constant.21.clone.inv_y, bf16[256,256]{1,0:T(8,128)(2,1)} %constant.22.clone.inv_z0, bf16[256,256]{1,0:T(8,128)(2,1)} %constant.23.clone.inv_z1, ...), custom_call_target="tpu_custom_call", output_to_operand_aliasing={{0}: (12, {})} | custom-call | flops 6000000000 | bytes 11534336 | tf_op jit(solution)/shard_map/late_cells/pallas_call | solution.py:569
  73.6 0.7 all-to-all-done.3.lines_ref
  74.3 5.4 %all-to-all-start.2 = ((f32[16,24,128]{2,1,0:T(8,128)}), f32[16,24,128]{2,1,0:T(8,128)S(1)}, u32[]{:S(2)}, u32[]{:S(2)}) async-start(f32[16,24,128]{2,1,0:T(8,128)} %bitcast.9), calls=%async_computation.2 | async-start | bytes 393216 | tf_op jit(solution)/shard_map/all_to_all | solution.py:690
  79.7 9.6 %weight_gradient.2.refs_0_ = f32[2,32,32,32,64]{4,3,2,1,0:T(8,128)} custom-call(f32[16,16]{1,0:T(8,128)S(1)} %copy-done.1, f32[16,16]{1,0:T(8,128)S(1)} %copy-done, f32[16,32,128]{2,1,0:T(8,128)S(1)} %get-tuple-element.27.spec_ref, f32[16,24,128]{2,1,0:T(8,128)S(1)} %all-to-all-done.3.lines_ref), custom_call_target="tpu_custom_call" | custom-call | flops 5000000 | bytes 33554432 | tf_op jit(solution)/shard_map/weight_gradient/pallas_call | solution.py:667
  89.3 0.0 all-to-all-done.2.lines_ref
  89.3 5.6 %weight_gradient.3 = (f32[2,32,32,32,64]{4,3,2,1,0:T(8,128)}, f32[32,32]{1,0:T(8,128)}, f32[1,32]{1,0:T(1,128)}) custom-call(f32[16,16]{1,0:T(8,128)S(1)} %copy-done.1, f32[16,16]{1,0:T(8,128)S(1)} %copy-done, f32[16,32,128]{2,1,0:T(8,128)S(1)} %get-tuple-element.27.spec_ref, ...), custom_call_target="tpu_custom_call", output_to_operand_aliasing={{0}: (4, {})} | custom-call | flops 5000000 | bytes 33554432 | tf_op jit(solution)/shard_map/weight_gradient/pallas_call | solution.py:667
Async XLA Ops:
  12.1 17.5 %all-to-all-start = ((f32[16,32,128]{2,1,0:T(8,128)}), f32[16,32,128]{2,1,0:T(8,128)S(1)}, u32[]{:S(2)}, u32[]{:S(2)}) async-start(f32[16,32,128]{2,1,0:T(8,128)} %bitcast.2), calls=%async_computation | async-start | bytes 524288 | tf_op jit(solution)/shard_map/all_to_all | solution.py:690
  19.5 10.0 %copy-start = (f32[16,16]{1,0:T(8,128)S(1)}, f32[16,16]{1,0:T(8,128)}, u32[]{:S(2)}) copy-start(f32[16,16]{1,0:T(8,128)} %constant.17.clone.sin_ref) | copy-start | bytes 3076
  19.6 10.0 %copy-start.1 = (f32[16,16]{1,0:T(8,128)S(1)}, f32[16,16]{1,0:T(8,128)}, u32[]{:S(2)}) copy-start(f32[16,16]{1,0:T(8,128)} %constant.16.clone.cos_ref) | copy-start | bytes 3076
  29.3 11.9 %copy-start.2 = (f32[32,32]{1,0:T(8,128)S(1)}, f32[32,32]{1,0:T(8,128)}, u32[]{:S(2)}) copy-start(f32[32,32]{1,0:T(8,128)} %param.16) | copy-start | bytes 12292
  29.4 12.6 %copy-start.3 = (f32[32]{0:T(128)S(1)}, f32[32]{0:T(128)}, u32[]{:S(2)}) copy-start(f32[32]{0:T(128)} %param.17) | copy-start | bytes 388
  35.4 15.9 %all-to-all-start.1 = ((f32[16,32,128]{2,1,0:T(8,128)}), f32[16,32,128]{2,1,0:T(8,128)S(1)}, u32[]{:S(2)}, u32[]{:S(2)}) async-start(f32[16,32,128]{2,1,0:T(8,128)} %get-tuple-element.21), calls=%async_computation.1 | async-start | bytes 524288 | tf_op jit(solution)/shard_map/all_to_all | solution.py:690
  59.3 15.0 %all-to-all-start.3 = ((f32[16,24,128]{2,1,0:T(8,128)}), f32[16,24,128]{2,1,0:T(8,128)S(1)}, u32[]{:S(2)}, u32[]{:S(2)}) async-start(f32[16,24,128]{2,1,0:T(8,128)} %bitcast.10), calls=%async_computation.3 | async-start | bytes 393216 | tf_op jit(solution)/shard_map/all_to_all | solution.py:690
  74.3 15.0 %all-to-all-start.2 = ((f32[16,24,128]{2,1,0:T(8,128)}), f32[16,24,128]{2,1,0:T(8,128)S(1)}, u32[]{:S(2)}, u32[]{:S(2)}) async-start(f32[16,24,128]{2,1,0:T(8,128)} %bitcast.9), calls=%async_computation.2 | async-start | bytes 393216 | tf_op jit(solution)/shard_map/all_to_all | solution.py:690

commit v10 on v8

--- a/solution.py
+++ b/solution.py
@@ -346,7 +346,7 @@
 def mix(cos_x, sin_x, lines, weights, norm):
     points, channels, _ = lines.shape
     unique = weights.shape[0]
-    per_step = min(unique, 4)
+    per_step = 2
     shape = (points, channels, LANES)
     return pl.pallas_call(
         functools.partial(mix_kernel, points=points, channels=channels, per_step=per_step, norm=norm),
@@ -423,22 +423,6 @@
     )(*in_hbm(summing, turned, bias, field))
 
 
-TAIL = (
-    0.28208447628636224, 0.2824095107622592, 0.24285420127949567, 0.20367621235863168, -0.028966708844937322,
-    0.28146769954808826, -0.490173103351073, 0.2860108822904108, -0.0593632144096072,
-)
-
-
-def normal(values):
-    bell = jnp.exp(-0.5 * values * values)
-    t = 1.0 / (1.0 + (0.5 * INV_SQRT_TWO) * jnp.abs(values))
-    tail = 0.5 * TAIL[-1]
-    for factor in TAIL[-2::-1]:
-        tail = tail * t + 0.5 * factor
-    tail = tail * t * bell
-    return jnp.where(values < 0.0, tail, 1.0 - tail), values * bell * INV_SQRT_TWO_PI
-
-
 def cell_group(inv_y, inv_z, modes_ref, pre_ref, cot_ref, act_ref, first, count, channels):
     lines = []
     for g in range(0, count, GROUP):
@@ -454,9 +438,10 @@
     slopes = []
     for q in range(count):
         before = spectral[q % 2][q // 2 * NY : (q // 2 + 1) * NY] + pre_ref[q]
-        cdf, bent = normal(before)
+        cdf = 0.5 + 0.5 * lax.erf(before * INV_SQRT_TWO)
         act_ref[q] = (before * cdf).astype(BF16)
-        slopes.append(cot_ref[q].astype(F32) * (cdf + bent))
+        pdf = jnp.exp(-0.5 * before * before) * INV_SQRT_TWO_PI
+        slopes.append(cot_ref[q].astype(F32) * (cdf + before * pdf))
     return slopes
 
 
@@ -597,12 +582,20 @@
     return act, out.reshape(owners, rows, LANES)
 
 
-def gradient_kernel(cos_ref, sin_ref, spec_ref, lines_ref, *refs, points, channels, unique, copies, norm, first, outputs, slots):
+def join(core, near_ref, far_ref, lines_ref):
+    chips, cores = near_ref.shape[:2]
+    for p in range(chips):
+        lines_ref[cores * p + core] = near_ref[p, core]
+        lines_ref[cores * p + 1 - core] = far_ref[p, core]
+
+
+def gradient_kernel(core_ref, cos_ref, sin_ref, spec_ref, near_ref, far_ref, *refs, points, channels, unique, copies, norm, first, outputs, slots):
     last = first > 0
     if last:
-        _, out_hbm, point_ref, bias_ref, sums_ref, real_ref, imag_ref, buffer, sems = refs
+        _, out_hbm, point_ref, bias_ref, lines_ref, sums_ref, real_ref, imag_ref, buffer, sems = refs
     else:
-        out_hbm, sums_ref, real_ref, imag_ref, buffer, sems = refs
+        out_hbm, lines_ref, sums_ref, real_ref, imag_ref, buffer, sems = refs
+    join(core_ref[0], near_ref, far_ref, lines_ref)
     halve_lines(lines_ref, sums_ref, points, outputs)
     half = LANES // 2
     lane = lane_index((outputs, LANES))
@@ -654,8 +647,9 @@
             copy.wait()
 
 
-def gradient(cos_x, sin_x, spectrum, lines, norm, kept_x, before=()):
-    points, rows, _ = lines.shape
+def gradient(core, cos_x, sin_x, spectrum, near, far, norm, kept_x, before=()):
+    chips, cores, rows, _ = near.shape
+    points = chips * cores
     unique, channels, _ = spectrum.shape
     half = LANES // 2
     copies = kept_x // unique
@@ -670,25 +664,44 @@
             gradient_kernel, points=points, channels=channels, unique=unique, copies=copies, norm=norm,
             first=first, outputs=outputs, slots=slots,
         ),
-        in_specs=[smem(), smem(), full(spectrum.shape), full(lines.shape)] + [anywhere] * len(before),
+        in_specs=[smem(), smem(), smem(), full(spectrum.shape), full(near.shape), full(far.shape)]
+        + [anywhere] * len(before),
         out_specs=[anywhere] + [full(each) for each in sums],
         out_shape=[shape] + [jax.ShapeDtypeStruct(each, F32) for each in sums],
         scratch_shapes=[
+            pltpu.VMEM((points, rows, LANES), F32),
             pltpu.VMEM((2, 2, points // 2, outputs, LANES), F32),
             pltpu.VMEM((slots, channels, LANES), F32),
             pltpu.VMEM((slots, channels, LANES), F32),
             pltpu.VMEM((slots, 2, channels, outputs, half), F32),
             pltpu.SemaphoreType.DMA((slots, 2, copies)),
         ],
-        input_output_aliases={4: 0} if before else {},
+        input_output_aliases={6: 0} if before else {},
         compiler_params=params(LIMIT),
         cost_estimate=pl.CostEstimate(flops=5 * 10**6, bytes_accessed=32 * MIB, transcendentals=0),
         name="weight_gradient",
-    )(cos_x, sin_x, *in_vmem(spectrum, lines), *before)
+    )(core, cos_x, sin_x, *in_vmem(spectrum, near, far), *before)
 
 
 def swap(lines):
     return lax.all_to_all(lines, "space", split_axis=0, concat_axis=0, tiled=True)
+
+
+CORES = 2
+
+
+def swap_chips(lines):
+    devices, rows, lanes = lines.shape
+    chips = devices // CORES
+    groups = [[p * CORES + q for p in range(chips)] for q in range(CORES)]
+    near = lax.all_to_all(
+        lines.reshape(chips, CORES * rows, lanes), "space", split_axis=0, concat_axis=0, tiled=True, axis_index_groups=groups
+    )
+    return near.reshape(chips, CORES, rows, lanes)
+
+
+def swap_cores(near, devices):
+    return lax.ppermute(near, "space", [(d, d ^ 1) for d in range(devices)])
 
 
 def suits(width_x, length_x, devices, channels, weights):
@@ -731,11 +744,16 @@
     modes = swap(mixed)
     pre = pointwise(field_late, summing, point_weights, point_bias)
     act, slope, early = early_cells(inverse, forward, modes, pre, slopes_in)
-    early_lines = swap(early)
+    early_near = swap_chips(early)
     activated, late = late_cells(inverse, forward, summing, modes, pre, slopes_in, field, early, slope, act)
-    late_lines = swap(late)
-    (grad,) = gradient(cos_x, sin_x, spectrum, early_lines, norm, MX)
-    grad, grad_point, grad_bias = gradient(cos_x, sin_x, spectrum, late_lines, norm, MX, (grad,))
+    early_near, late = lax.optimization_barrier((early_near, late))
+    early_far = swap_cores(early_near, devices)
+    late_near = swap_chips(late)
+    core = lax.axis_index("space")[None] & (CORES - 1)
+    (grad,) = gradient(core, cos_x, sin_x, spectrum, early_near, early_far, norm, MX)
+    late_near, grad = lax.optimization_barrier((late_near, grad))
+    late_far = swap_cores(late_near, devices)
+    grad, grad_point, grad_bias = gradient(core, cos_x, sin_x, spectrum, late_near, late_far, norm, MX, (grad,))
     return (
         activated.reshape(cotangent.shape),
         jnp.transpose(grad, (0, 1, 4, 2, 3)),

time: 96.8 us -> 99.7 us (1.030)
  waiting for transfers between devices: 0.88 us -> 2.96 us
    all_to_all x0 -> x2, starting transfers between devices: none -> 11.9 us  [swap_chips(): lax.all_to_all(lines.reshape(chips, CORES * rows, lanes), 'space', split_...]
    all_to_all x4 -> x2, starting transfers between devices: 24.6 us -> 13.2 us  [swap(): lax.all_to_all(lines, 'space', split_axis=0, concat_axis=0, tiled=True)]
    ppermute x0 -> x2, waiting for transfers between devices: none -> 2.73 us  [swap_cores(): return lax.ppermute(near, 'space', [(d, d ^ 1) for d in range(devices)])]
    pallas_call x1, Pallas kernels: 10.1 us -> 7.94 us  [early_cells(): pl.pallas_call(functools.partial(early_cell_kernel, channels=channels, co...]
    pallas_call x1, Pallas kernels: 5.83 us -> 7.93 us  [mix(): pl.pallas_call(functools.partial(mix_kernel, points=points, channels=chan...]
  transfers between devices with their start and end apart: 4 -> 6, of which waited for: 2 -> 3; matrix products, arithmetic and copies ran while one was open for 1% -> 1% of each run, Pallas kernels for 38% -> 37%
where the time goes in v10:
time: 99.7 us; the launch traced here: 98.9 us
  Pallas kernels  68.4 us (69%)
  starting transfers between devices  25.4 us (25%)
  waiting for transfers between devices  2.96 us (3%)
  local copies, waits for them, and re-layouts  1.39 us (1%)
    pallas_call x2, Pallas kernels, gradient(): pl.pallas_call(functools.partial(gradient_kernel, points=points, channels...  15.3 us
    all_to_all x2, starting transfers between devices, swap(): lax.all_to_all(lines, 'space', split_axis=0, concat_axis=0, tiled=True)  13.2 us
    all_to_all x2, starting transfers between devices, swap_chips(): lax.all_to_all(lines.reshape(chips, CORES * rows, lanes), 'space', split_...  11.9 us
    pallas_call x1, Pallas kernels, forward_modes(): pl.pallas_call(functools.partial(forward_kernel, channels=channels, step_...  10.5 us
    pallas_call x1, Pallas kernels, fold_rest(): pl.pallas_call(functools.partial(fold_kernel, first=first, unique=unique,...  9.77 us
    pallas_call x1, Pallas kernels, pointwise(): pl.pallas_call(functools.partial(pointwise_kernel, channels=channels, blo...  8.66 us
    pallas_call x1, Pallas kernels, late_cells(): pl.pallas_call(functools.partial(late_cell_kernel, channels=channels, cou...  8.33 us
    pallas_call x1, Pallas kernels, early_cells(): pl.pallas_call(functools.partial(early_cell_kernel, channels=channels, co...  7.94 us
  transfers between devices with their start and end apart: 6, of which 3 were waited for; matrix products, arithmetic and copies ran while one was open for 1% of the time, Pallas kernels for 37%

profile of v10, /device:TPU:0, one launch (start us, length us, event | category | flops | bytes accessed | tf_op | source)
XLA Modules:
  0.0 98.9 jit_solution(14496039714507997385)
XLA Ops:
  0.6 10.5 %forward_yz.1 = (f32[512,128]{1,0:T(8,128)}, f32[16,32,32,128]{3,2,1,0:T(8,128)}) custom-call(bf16[1024,256]{1,0:T(8,128)(2,1)} %constant.26.clone.table_z, bf16[128,256]{1,0:T(8,128)(2,1)} %constant.27.clone.table_y, f32[32,128,256]{2,1,0:T(8,128)} %bitcast.27, f32[2,32,32,32,64]{4,3,2,1,0:T(8,128)} %bitcast.24), custom_call_target="tpu_custom_call" | custom-call | flops 2000000000 | bytes 23068672 | tf_op jit(solution)/shard_map/forward_yz/pallas_call | solution.py:221
  11.1 7.4 %all-to-all-start = ((f32[16,32,128]{2,1,0:T(8,128)}), f32[16,32,128]{2,1,0:T(8,128)S(1)}, u32[]{:S(2)}, u32[]{:S(2)}) async-start(f32[16,32,128]{2,1,0:T(8,128)} %bitcast.2), calls=%async_computation | async-start | bytes 524288 | tf_op jit(solution)/shard_map/all_to_all | solution.py:687
  18.5 0.0 copy-start
  18.5 0.0 copy-start.1
  18.5 9.8 %fold_weights.1.weights_ref = f32[16,32,32,128]{3,2,1,0:T(8,128)} custom-call(f32[2,32,32,32,64]{4,3,2,1,0:T(8,128)} %bitcast.25, f32[16,32,32,128]{3,2,1,0:T(8,128)} %get-tuple-element.23._), custom_call_target="tpu_custom_call", output_to_operand_aliasing={{}: (1, {})} | custom-call | flops 4000000 | bytes 26214400 | tf_op jit(solution)/shard_map/fold_weights/pallas_call | solution.py:266
  28.3 0.0 copy-start.2
  28.3 0.0 copy-start.3
  28.3 0.2 all-to-all-done.lines_ref
  28.6 0.0 copy-done
  28.6 0.0 copy-done.1
  28.6 7.9 %mix_modes.1 = (f32[16,32,128]{2,1,0:T(8,128)S(1)}, f32[16,32,128]{2,1,0:T(8,128)}) custom-call(f32[16,16]{1,0:T(8,128)S(1)} %copy-done.1, f32[16,16]{1,0:T(8,128)S(1)} %copy-done, f32[16,32,128]{2,1,0:T(8,128)S(1)} %all-to-all-done.lines_ref, f32[16,32,32,128]{3,2,1,0:T(8,128)} %fold_weights.1.weights_ref), custom_call_target="tpu_custom_call" | custom-call | flops 20000000 | bytes 9437184 | tf_op jit(solution)/shard_map/mix_modes/pallas_call | solution.py:351
  36.5 5.8 %all-to-all-start.1 = ((f32[16,32,128]{2,1,0:T(8,128)}), f32[16,32,128]{2,1,0:T(8,128)S(1)}, u32[]{:S(2)}, u32[]{:S(2)}) async-start(f32[16,32,128]{2,1,0:T(8,128)} %get-tuple-element.25), calls=%async_computation.1 | async-start | bytes 524288 | tf_op jit(solution)/shard_map/all_to_all | solution.py:687
  42.3 0.0 copy-done.2
  42.3 0.7 copy.20
  43.0 0.0 copy-done.3
  43.0 0.7 copy.21.bias_in_ref
  43.7 8.7 %pointwise.1.pre_ref = f32[32,128,256]{2,1,0:T(8,128)} custom-call(f32[256,32]{1,0:T(8,128)} %constant.25.clone.sum_ref, f32[32,32]{1,0:T(8,128)} %bitcast.30, f32[32,1]{1,0:T(8,128)} %copy.21.bias_in_ref, f32[32,128,256]{2,1,0:T(8,128)} %bitcast.28), custom_call_target="tpu_custom_call" | custom-call | flops 4000000000 | bytes 25165824 | tf_op jit(solution)/shard_map/pointwise/pallas_call | solution.py:413
  52.4 0.0 all-to-all-done.1
  52.4 7.9 %early_cells.1 = (bf16[32,128,256]{2,1,0:T(8,128)(2,1)}, f32[24,128,256]{2,1,0:T(8,128)}, f32[384,128]{1,0:T(8,128)}) custom-call(bf16[128,192]{1,0:T(8,128)(2,1)} %constant.28.clone.inv_y, bf16[256,256]{1,0:T(8,128)(2,1)} %constant.29.clone.inv_z0, bf16[256,256]{1,0:T(8,128)(2,1)} %constant.30.clone.inv_z1, bf16[1024,256]{1,0:T(8,128)(2,1)} %constant.26.clone.table_z, ...), custom_call_target="tpu_custom_call" | custom-call | flops 3000000000 | bytes 7340032 | tf_op jit(solution)/shard_map/early_cells/pallas_call | solution.py:529
  60.3 5.9 %all-to-all-start.2 = ((f32[8,48,128]{2,1,0:T(8,128)}), f32[8,48,128]{2,1,0:T(8,128)S(1)}, u32[]{:S(2)}, u32[]{:S(2)}) async-start(f32[8,48,128]{2,1,0:T(8,128)} %bitcast.10), calls=%async_computation.2 | async-start | bytes 393216 | tf_op jit(solution)/shard_map/all_to_all | solution.py:697
  66.2 8.3 %late_cells.1 = (bf16[32,128,256]{2,1,0:T(8,128)(2,1)}, f32[384,128]{1,0:T(8,128)}) custom-call(bf16[128,192]{1,0:T(8,128)(2,1)} %constant.28.clone.inv_y, bf16[256,256]{1,0:T(8,128)(2,1)} %constant.29.clone.inv_z0, bf16[256,256]{1,0:T(8,128)(2,1)} %constant.30.clone.inv_z1, ...), custom_call_target="tpu_custom_call", output_to_operand_aliasing={{0}: (12, {})} | custom-call | flops 6000000000 | bytes 11534336 | tf_op jit(solution)/shard_map/late_cells/pallas_call | solution.py:555
  74.6 0.0 all-to-all-done.2
  74.6 6.0 %all-to-all-start.3 = ((f32[8,48,128]{2,1,0:T(8,128)}), f32[8,48,128]{2,1,0:T(8,128)S(1)}, u32[]{:S(2)}, u32[]{:S(2)}) async-start(f32[8,48,128]{2,1,0:T(8,128)} %bitcast.13), calls=%async_computation.3 | async-start | bytes 393216 | tf_op jit(solution)/shard_map/all_to_all | solution.py:697
  80.6 0.0 collective-permute-start
  80.6 1.4 %collective-permute-done.far_ref = f32[8,2,24,128]{3,2,1,0:T(8,128)S(1)} collective-permute-done((f32[8,2,24,128]{3,2,1,0:T(8,128)S(1)}, f32[8,2,24,128]{3,2,1,0:T(8,128)S(1)}, u32[]{:S(2)}, u32[]{:S(2)}) %collective-permute-start) | collective-permute-done | bytes 196640 | tf_op jit(solution)/shard_map/ppermute | solution.py:704
  82.1 9.6 %weight_gradient.2.refs_0_ = f32[2,32,32,32,64]{4,3,2,1,0:T(8,128)} custom-call(s32[1]{0:T(128)} %bitcast.9.core_ref, f32[16,16]{1,0:T(8,128)S(1)} %copy-done.1, f32[16,16]{1,0:T(8,128)S(1)} %copy-done, f32[16,32,128]{2,1,0:T(8,128)S(1)} %get-tuple-element.31.spec_ref, f32[8,2,24,128]{3,2,1,0:T(8,128)S(1)} %bitcast.19, ...), custom_call_target="tpu_custom_call" | custom-call | flops 5000000 | bytes 33554432 | tf_op jit(solution)/shard_map/weight_gradient/pallas_call | solution.py:662
  91.7 0.0 all-to-all-done.3
  91.7 0.2 collective-permute-start.1
  91.9 1.3 %collective-permute-done.1.far_ref = f32[8,2,24,128]{3,2,1,0:T(8,128)S(1)} collective-permute-done((f32[8,2,24,128]{3,2,1,0:T(8,128)S(1)}, f32[8,2,24,128]{3,2,1,0:T(8,128)S(1)}, u32[]{:S(2)}, u32[]{:S(2)}) %collective-permute-start.1) | collective-permute-done | bytes 196640 | tf_op jit(solution)/shard_map/ppermute | solution.py:704
  93.2 5.6 %weight_gradient.3 = (f32[2,32,32,32,64]{4,3,2,1,0:T(8,128)}, f32[32,32]{1,0:T(8,128)}, f32[1,32]{1,0:T(1,128)}) custom-call(s32[1]{0:T(128)} %bitcast.9.core_ref, f32[16,16]{1,0:T(8,128)S(1)} %copy-done.1, f32[16,16]{1,0:T(8,128)S(1)} %copy-done, f32[16,32,128]{2,1,0:T(8,128)S(1)} %get-tuple-element.31.spec_ref, ...), custom_call_target="tpu_custom_call", output_to_operand_aliasing={{0}: (6, {})} | custom-call | flops 5000000 | bytes 33554432 | tf_op jit(solution)/shard_map/weight_gradient/pallas_call | solution.py:662
Async XLA Ops:
  11.1 17.4 %all-to-all-start = ((f32[16,32,128]{2,1,0:T(8,128)}), f32[16,32,128]{2,1,0:T(8,128)S(1)}, u32[]{:S(2)}, u32[]{:S(2)}) async-start(f32[16,32,128]{2,1,0:T(8,128)} %bitcast.2), calls=%async_computation | async-start | bytes 524288 | tf_op jit(solution)/shard_map/all_to_all | solution.py:687
  18.5 10.0 %copy-start = (f32[16,16]{1,0:T(8,128)S(1)}, f32[16,16]{1,0:T(8,128)}, u32[]{:S(2)}) copy-start(f32[16,16]{1,0:T(8,128)} %constant.24.clone.sin_ref) | copy-start | bytes 3076
  18.5 10.0 %copy-start.1 = (f32[16,16]{1,0:T(8,128)S(1)}, f32[16,16]{1,0:T(8,128)}, u32[]{:S(2)}) copy-start(f32[16,16]{1,0:T(8,128)} %constant.23.clone.cos_ref) | copy-start | bytes 3076
  28.3 14.0 %copy-start.2 = (f32[32,32]{1,0:T(8,128)S(1)}, f32[32,32]{1,0:T(8,128)}, u32[]{:S(2)}) copy-start(f32[32,32]{1,0:T(8,128)} %param.16) | copy-start | bytes 12292
  28.3 14.7 %copy-start.3 = (f32[32]{0:T(128)S(1)}, f32[32]{0:T(128)}, u32[]{:S(2)}) copy-start(f32[32]{0:T(128)} %param.17) | copy-start | bytes 388
  36.5 15.9 %all-to-all-start.1 = ((f32[16,32,128]{2,1,0:T(8,128)}), f32[16,32,128]{2,1,0:T(8,128)S(1)}, u32[]{:S(2)}, u32[]{:S(2)}) async-start(f32[16,32,128]{2,1,0:T(8,128)} %get-tuple-element.25), calls=%async_computation.1 | async-start | bytes 524288 | tf_op jit(solution)/shard_map/all_to_all | solution.py:687
  60.3 14.3 %all-to-all-start.2 = ((f32[8,48,128]{2,1,0:T(8,128)}), f32[8,48,128]{2,1,0:T(8,128)S(1)}, u32[]{:S(2)}, u32[]{:S(2)}) async-start(f32[8,48,128]{2,1,0:T(8,128)} %bitcast.10), calls=%async_computation.2 | async-start | bytes 393216 | tf_op jit(solution)/shard_map/all_to_all | solution.py:697
  74.6 17.1 %all-to-all-start.3 = ((f32[8,48,128]{2,1,0:T(8,128)}), f32[8,48,128]{2,1,0:T(8,128)S(1)}, u32[]{:S(2)}, u32[]{:S(2)}) async-start(f32[8,48,128]{2,1,0:T(8,128)} %bitcast.13), calls=%async_computation.3 | async-start | bytes 393216 | tf_op jit(solution)/shard_map/all_to_all | solution.py:697
  80.6 1.4 %collective-permute-start = (f32[8,2,24,128]{3,2,1,0:T(8,128)S(1)}, f32[8,2,24,128]{3,2,1,0:T(8,128)S(1)}, u32[]{:S(2)}, u32[]{:S(2)}) collective-permute-start(f32[8,2,24,128]{3,2,1,0:T(8,128)S(1)} %bitcast.18), channel_id=1, source_target_pairs={{0,1},{1,0},{2,3},{3,2},{4,5},{5,4},{6,7},{7,6},{8,9},{9,8},{10,11... | collective-permute-start | bytes 589832 | tf_op jit(solution)/shard_map/ppermute | solution.py:704
  91.7 1.5 %collective-permute-start.1 = (f32[8,2,24,128]{3,2,1,0:T(8,128)S(1)}, f32[8,2,24,128]{3,2,1,0:T(8,128)S(1)}, u32[]{:S(2)}, u32[]{:S(2)}) collective-permute-start(f32[8,2,24,128]{3,2,1,0:T(8,128)S(1)} %bitcast.20), channel_id=1, source_target_pairs={{0,1},{1,0},{2,3},{3,2},{4,5},{5,4},{6,7},{7,6},{8,9},{9,8},{10,11... | collective-permute-start | bytes 589832 | tf_op jit(solution)/shard_map/ppermute | solution.py:704

commit v11 on v8

--- a/solution.py
+++ b/solution.py
@@ -23,6 +23,7 @@
 LIMIT = 48
 LANES = 128
 GROUP = 4
+EARLY_STEP = 12
 STEP = 8
 
 
@@ -346,7 +347,7 @@
 def mix(cos_x, sin_x, lines, weights, norm):
     points, channels, _ = lines.shape
     unique = weights.shape[0]
-    per_step = min(unique, 4)
+    per_step = min(unique, 8)
     shape = (points, channels, LANES)
     return pl.pallas_call(
         functools.partial(mix_kernel, points=points, channels=channels, per_step=per_step, norm=norm),
@@ -423,22 +424,6 @@
     )(*in_hbm(summing, turned, bias, field))
 
 
-TAIL = (
-    0.28208447628636224, 0.2824095107622592, 0.24285420127949567, 0.20367621235863168, -0.028966708844937322,
-    0.28146769954808826, -0.490173103351073, 0.2860108822904108, -0.0593632144096072,
-)
-
-
-def normal(values):
-    bell = jnp.exp(-0.5 * values * values)
-    t = 1.0 / (1.0 + (0.5 * INV_SQRT_TWO) * jnp.abs(values))
-    tail = 0.5 * TAIL[-1]
-    for factor in TAIL[-2::-1]:
-        tail = tail * t + 0.5 * factor
-    tail = tail * t * bell
-    return jnp.where(values < 0.0, tail, 1.0 - tail), values * bell * INV_SQRT_TWO_PI
-
-
 def cell_group(inv_y, inv_z, modes_ref, pre_ref, cot_ref, act_ref, first, count, channels):
     lines = []
     for g in range(0, count, GROUP):
@@ -454,9 +439,10 @@
     slopes = []
     for q in range(count):
         before = spectral[q % 2][q // 2 * NY : (q // 2 + 1) * NY] + pre_ref[q]
-        cdf, bent = normal(before)
+        cdf = 0.5 + 0.5 * lax.erf(before * INV_SQRT_TWO)
         act_ref[q] = (before * cdf).astype(BF16)
-        slopes.append(cot_ref[q].astype(F32) * (cdf + bent))
+        pdf = jnp.exp(-0.5 * before * before) * INV_SQRT_TWO_PI
+        slopes.append(cot_ref[q].astype(F32) * (cdf + before * pdf))
     return slopes
 
 
@@ -539,11 +525,11 @@
     channels = pre.shape[0]
     owners = MY // 2
     early = early_count(channels)
-    block = pl.BlockSpec((STEP, NY, NZ), lambda s: (s, 0, 0))
+    block = pl.BlockSpec((EARLY_STEP, NY, NZ), lambda s: (s, 0, 0))
     tables = (*inverse, *forward)
     act, slope, out = pl.pallas_call(
-        functools.partial(early_cell_kernel, channels=channels, count=STEP, rows=early),
-        grid=(early // STEP,),
+        functools.partial(early_cell_kernel, channels=channels, count=EARLY_STEP, rows=early),
+        grid=(early // EARLY_STEP,),
         in_specs=[full(t.shape) for t in tables] + [full((owners * channels, LANES)), block, block],
         out_specs=[block, block, full((owners * early, LANES))],
         out_shape=[
@@ -661,7 +647,7 @@
     copies = kept_x // unique
     first = early_count(channels) if before else 0
     outputs = channels - first if before else early_count(channels)
-    slots = 8 if before else 4
+    slots = 8
     anywhere = pl.BlockSpec(memory_space=pl.ANY)
     shape = jax.ShapeDtypeStruct((2, kept_x, channels, channels, half), F32)
     sums = [(channels, channels), (1, channels)] if before else []

time: 96.8 us -> 94.2 us (0.973)
  Pallas kernels: 68.4 us -> 65.7 us
    pallas_call x1, Pallas kernels: 10.1 us -> 7.79 us  [early_cells(): pl.pallas_call(functools.partial(early_cell_kernel, channels=channels, co...]
  transfers between devices with their start and end apart: 4 -> 4, of which waited for: 2 -> 2; matrix products, arithmetic and copies ran while one was open for 1% -> 1% of each run, Pallas kernels for 38% -> 39%
where the time goes in v11:
time: 94.2 us; the launch traced here: 93.5 us
  Pallas kernels  65.7 us (70%)
  starting transfers between devices  24.6 us (26%)
  local copies, waits for them, and re-layouts  1.39 us (1%)
    all_to_all x4, starting transfers between devices, swap(): lax.all_to_all(lines, 'space', split_axis=0, concat_axis=0, tiled=True)  24.6 us
    pallas_call x2, Pallas kernels, gradient(): pl.pallas_call(functools.partial(gradient_kernel, points=points, channels...  15.4 us
    pallas_call x1, Pallas kernels, forward_modes(): pl.pallas_call(functools.partial(forward_kernel, channels=channels, step_...  10.5 us
    pallas_call x1, Pallas kernels, fold_rest(): pl.pallas_call(functools.partial(fold_kernel, first=first, unique=unique,...  9.77 us
    pallas_call x1, Pallas kernels, pointwise(): pl.pallas_call(functools.partial(pointwise_kernel, channels=channels, blo...  8.67 us
    pallas_call x1, Pallas kernels, late_cells(): pl.pallas_call(functools.partial(late_cell_kernel, channels=channels, cou...  8.33 us
    pallas_call x1, Pallas kernels, early_cells(): pl.pallas_call(functools.partial(early_cell_kernel, channels=channels, co...  7.79 us
    pallas_call x1, Pallas kernels, mix(): pl.pallas_call(functools.partial(mix_kernel, points=points, channels=chan...  5.33 us
  transfers between devices with their start and end apart: 4, of which 2 were waited for; matrix products, arithmetic and copies ran while one was open for 1% of the time, Pallas kernels for 39%

profile of v11, /device:TPU:0, one launch (start us, length us, event | category | flops | bytes accessed | tf_op | source)
XLA Modules:
  0.0 93.5 jit_solution(452012344507741529)
XLA Ops:
  0.6 10.5 %forward_yz.1 = (f32[512,128]{1,0:T(8,128)}, f32[16,32,32,128]{3,2,1,0:T(8,128)}) custom-call(bf16[1024,256]{1,0:T(8,128)(2,1)} %constant.19.clone.table_z, bf16[128,256]{1,0:T(8,128)(2,1)} %constant.20.clone.table_y, f32[32,128,256]{2,1,0:T(8,128)} %bitcast.19, f32[2,32,32,32,64]{4,3,2,1,0:T(8,128)} %bitcast.16), custom_call_target="tpu_custom_call" | custom-call | flops 2000000000 | bytes 23068672 | tf_op jit(solution)/shard_map/forward_yz/pallas_call | solution.py:222
  11.1 7.4 %all-to-all-start = ((f32[16,32,128]{2,1,0:T(8,128)}), f32[16,32,128]{2,1,0:T(8,128)S(1)}, u32[]{:S(2)}, u32[]{:S(2)}) async-start(f32[16,32,128]{2,1,0:T(8,128)} %bitcast.2), calls=%async_computation | async-start | bytes 524288 | tf_op jit(solution)/shard_map/all_to_all | solution.py:677
  18.5 0.0 copy-start
  18.5 0.0 copy-start.1
  18.5 9.8 %fold_weights.1.weights_ref = f32[16,32,32,128]{3,2,1,0:T(8,128)} custom-call(f32[2,32,32,32,64]{4,3,2,1,0:T(8,128)} %bitcast.17, f32[16,32,32,128]{3,2,1,0:T(8,128)} %get-tuple-element.19._), custom_call_target="tpu_custom_call", output_to_operand_aliasing={{}: (1, {})} | custom-call | flops 4000000 | bytes 26214400 | tf_op jit(solution)/shard_map/fold_weights/pallas_call | solution.py:267
  28.3 0.0 copy-start.2
  28.3 0.0 copy-start.3
  28.3 0.2 all-to-all-done.lines_ref
  28.6 0.0 copy-done
  28.6 0.0 copy-done.1
  28.6 5.3 %mix_modes.1 = (f32[16,32,128]{2,1,0:T(8,128)S(1)}, f32[16,32,128]{2,1,0:T(8,128)}) custom-call(f32[16,16]{1,0:T(8,128)S(1)} %copy-done.1, f32[16,16]{1,0:T(8,128)S(1)} %copy-done, f32[16,32,128]{2,1,0:T(8,128)S(1)} %all-to-all-done.lines_ref, f32[16,32,32,128]{3,2,1,0:T(8,128)} %fold_weights.1.weights_ref), custom_call_target="tpu_custom_call" | custom-call | flops 20000000 | bytes 9437184 | tf_op jit(solution)/shard_map/mix_modes/pallas_call | solution.py:352
  33.9 5.8 %all-to-all-start.1 = ((f32[16,32,128]{2,1,0:T(8,128)}), f32[16,32,128]{2,1,0:T(8,128)S(1)}, u32[]{:S(2)}, u32[]{:S(2)}) async-start(f32[16,32,128]{2,1,0:T(8,128)} %get-tuple-element.21), calls=%async_computation.1 | async-start | bytes 524288 | tf_op jit(solution)/shard_map/all_to_all | solution.py:677
  39.7 0.0 copy-done.2
  39.7 0.7 copy.20
  40.4 0.0 copy-done.3
  40.4 0.7 copy.21.bias_in_ref
  41.1 8.7 %pointwise.1.pre_ref = f32[32,128,256]{2,1,0:T(8,128)} custom-call(f32[256,32]{1,0:T(8,128)} %constant.18.clone.sum_ref, f32[32,32]{1,0:T(8,128)} %bitcast.22, f32[32,1]{1,0:T(8,128)} %copy.21.bias_in_ref, f32[32,128,256]{2,1,0:T(8,128)} %bitcast.20), custom_call_target="tpu_custom_call" | custom-call | flops 4000000000 | bytes 25165824 | tf_op jit(solution)/shard_map/pointwise/pallas_call | solution.py:414
  49.8 0.0 all-to-all-done.1
  49.8 7.8 %early_cells.1 = (bf16[32,128,256]{2,1,0:T(8,128)(2,1)}, f32[24,128,256]{2,1,0:T(8,128)}, f32[384,128]{1,0:T(8,128)}) custom-call(bf16[128,192]{1,0:T(8,128)(2,1)} %constant.21.clone.inv_y, bf16[256,256]{1,0:T(8,128)(2,1)} %constant.22.clone.inv_z0, bf16[256,256]{1,0:T(8,128)(2,1)} %constant.23.clone.inv_z1, bf16[1024,256]{1,0:T(8,128)(2,1)} %constant.19.clone.table_z, ...), custom_call_target="tpu_custom_call" | custom-call | flops 3000000000 | bytes 7340032 | tf_op jit(solution)/shard_map/early_cells/pallas_call | solution.py:530
  57.6 6.0 %all-to-all-start.3 = ((f32[16,24,128]{2,1,0:T(8,128)}), f32[16,24,128]{2,1,0:T(8,128)S(1)}, u32[]{:S(2)}, u32[]{:S(2)}) async-start(f32[16,24,128]{2,1,0:T(8,128)} %bitcast.10), calls=%async_computation.3 | async-start | bytes 393216 | tf_op jit(solution)/shard_map/all_to_all | solution.py:677
  63.6 8.3 %late_cells.1 = (bf16[32,128,256]{2,1,0:T(8,128)(2,1)}, f32[384,128]{1,0:T(8,128)}) custom-call(bf16[128,192]{1,0:T(8,128)(2,1)} %constant.21.clone.inv_y, bf16[256,256]{1,0:T(8,128)(2,1)} %constant.22.clone.inv_z0, bf16[256,256]{1,0:T(8,128)(2,1)} %constant.23.clone.inv_z1, ...), custom_call_target="tpu_custom_call", output_to_operand_aliasing={{0}: (12, {})} | custom-call | flops 6000000000 | bytes 11534336 | tf_op jit(solution)/shard_map/late_cells/pallas_call | solution.py:556
  71.9 0.7 all-to-all-done.3.lines_ref
  72.6 5.4 %all-to-all-start.2 = ((f32[16,24,128]{2,1,0:T(8,128)}), f32[16,24,128]{2,1,0:T(8,128)S(1)}, u32[]{:S(2)}, u32[]{:S(2)}) async-start(f32[16,24,128]{2,1,0:T(8,128)} %bitcast.9), calls=%async_computation.2 | async-start | bytes 393216 | tf_op jit(solution)/shard_map/all_to_all | solution.py:677
  78.0 9.8 %weight_gradient.2.refs_0_ = f32[2,32,32,32,64]{4,3,2,1,0:T(8,128)} custom-call(f32[16,16]{1,0:T(8,128)S(1)} %copy-done.1, f32[16,16]{1,0:T(8,128)S(1)} %copy-done, f32[16,32,128]{2,1,0:T(8,128)S(1)} %get-tuple-element.27.spec_ref, f32[16,24,128]{2,1,0:T(8,128)S(1)} %all-to-all-done.3.lines_ref), custom_call_target="tpu_custom_call" | custom-call | flops 5000000 | bytes 33554432 | tf_op jit(solution)/shard_map/weight_gradient/pallas_call | solution.py:654
  87.7 0.0 all-to-all-done.2.lines_ref
  87.7 5.6 %weight_gradient.3 = (f32[2,32,32,32,64]{4,3,2,1,0:T(8,128)}, f32[32,32]{1,0:T(8,128)}, f32[1,32]{1,0:T(1,128)}) custom-call(f32[16,16]{1,0:T(8,128)S(1)} %copy-done.1, f32[16,16]{1,0:T(8,128)S(1)} %copy-done, f32[16,32,128]{2,1,0:T(8,128)S(1)} %get-tuple-element.27.spec_ref, ...), custom_call_target="tpu_custom_call", output_to_operand_aliasing={{0}: (4, {})} | custom-call | flops 5000000 | bytes 33554432 | tf_op jit(solution)/shard_map/weight_gradient/pallas_call | solution.py:654
Async XLA Ops:
  11.1 17.5 %all-to-all-start = ((f32[16,32,128]{2,1,0:T(8,128)}), f32[16,32,128]{2,1,0:T(8,128)S(1)}, u32[]{:S(2)}, u32[]{:S(2)}) async-start(f32[16,32,128]{2,1,0:T(8,128)} %bitcast.2), calls=%async_computation | async-start | bytes 524288 | tf_op jit(solution)/shard_map/all_to_all | solution.py:677
  18.5 10.0 %copy-start = (f32[16,16]{1,0:T(8,128)S(1)}, f32[16,16]{1,0:T(8,128)}, u32[]{:S(2)}) copy-start(f32[16,16]{1,0:T(8,128)} %constant.17.clone.sin_ref) | copy-start | bytes 3076
  18.5 10.0 %copy-start.1 = (f32[16,16]{1,0:T(8,128)S(1)}, f32[16,16]{1,0:T(8,128)}, u32[]{:S(2)}) copy-start(f32[16,16]{1,0:T(8,128)} %constant.16.clone.cos_ref) | copy-start | bytes 3076
  28.3 11.4 %copy-start.2 = (f32[32,32]{1,0:T(8,128)S(1)}, f32[32,32]{1,0:T(8,128)}, u32[]{:S(2)}) copy-start(f32[32,32]{1,0:T(8,128)} %param.16) | copy-start | bytes 12292
  28.3 12.1 %copy-start.3 = (f32[32]{0:T(128)S(1)}, f32[32]{0:T(128)}, u32[]{:S(2)}) copy-start(f32[32]{0:T(128)} %param.17) | copy-start | bytes 388
  33.9 15.9 %all-to-all-start.1 = ((f32[16,32,128]{2,1,0:T(8,128)}), f32[16,32,128]{2,1,0:T(8,128)S(1)}, u32[]{:S(2)}, u32[]{:S(2)}) async-start(f32[16,32,128]{2,1,0:T(8,128)} %get-tuple-element.21), calls=%async_computation.1 | async-start | bytes 524288 | tf_op jit(solution)/shard_map/all_to_all | solution.py:677
  57.6 15.0 %all-to-all-start.3 = ((f32[16,24,128]{2,1,0:T(8,128)}), f32[16,24,128]{2,1,0:T(8,128)S(1)}, u32[]{:S(2)}, u32[]{:S(2)}) async-start(f32[16,24,128]{2,1,0:T(8,128)} %bitcast.10), calls=%async_computation.3 | async-start | bytes 393216 | tf_op jit(solution)/shard_map/all_to_all | solution.py:677
  72.6 15.2 %all-to-all-start.2 = ((f32[16,24,128]{2,1,0:T(8,128)}), f32[16,24,128]{2,1,0:T(8,128)S(1)}, u32[]{:S(2)}, u32[]{:S(2)}) async-start(f32[16,24,128]{2,1,0:T(8,128)} %bitcast.9), calls=%async_computation.2 | async-start | bytes 393216 | tf_op jit(solution)/shard_map/all_to_all | solution.py:677

commit v12 on v11

--- a/solution.py
+++ b/solution.py
@@ -189,14 +189,19 @@
         fields = [field_ref[q] for q in range(step_channels)]
         forward_group(fields, table_z[...], table_y[...], out_ref, step * step_channels, channels)
 
+    folding = (step > 0) & (step <= slots // per_step)
+
     @pl.when(step == 0)
     def _():
         for at in range(slots):
             for copy in fetches(weights_hbm, ring_ref, sems, at, at, unique):
                 copy.start()
+
+    @pl.when(jnp.logical_not(folding))
+    def _():
         transform()
 
-    @pl.when(step > 0)
+    @pl.when(folding)
     def _():
         for q in range(per_step):
             at = (step - 1) * per_step + q
@@ -211,7 +216,7 @@
 
 
 def folded_early(channels):
-    return (channels // FIELD_STEP - 1) * FOLD_STEP
+    return (channels // FIELD_STEP - 2) * FOLD_STEP
 
 
 def forward_modes(field, tables, weights, unique):
@@ -228,7 +233,7 @@
         + [pl.BlockSpec((FIELD_STEP, NY, NZ), lambda s: (s, 0, 0)), pl.BlockSpec(memory_space=pl.ANY)],
         out_specs=[
             full((owners * channels, LANES)),
-            pl.BlockSpec((FOLD_STEP,) + folded_shape.shape[1:], lambda s: (jnp.maximum(s - 1, 0), 0, 0, 0)),
+            pl.BlockSpec((FOLD_STEP,) + folded_shape.shape[1:], lambda s: (jnp.clip(s - 1, 0, slots // FOLD_STEP - 1), 0, 0, 0)),
         ],
         out_shape=[pltpu.VMEM((owners * channels, LANES), F32), folded_shape],
         scratch_shapes=ring,
@@ -241,39 +246,48 @@
 
 def fold_kernel(weights_hbm, _, out_ref, ring_ref, sems, *, first, unique, slots):
     step = pl.program_id(0)
-    slot = step % slots
+
+    def fetch(turn):
+        slot = turn % slots
+        return [
+            copy
+            for q in range(FOLD_STEP)
+            for copy in fetches(weights_hbm, ring_ref, sems, first + turn * FOLD_STEP + q, slot * FOLD_STEP + q, unique)
+        ]
 
     @pl.when(step == 0)
     def _():
         for ahead in range(slots):
-            for copy in fetches(weights_hbm, ring_ref, sems, first + ahead, ahead, unique):
+            for copy in fetch(ahead):
                 copy.start()
 
-    for copy in fetches(weights_hbm, ring_ref, sems, first + step, slot, unique):
+    for copy in fetch(step):
         copy.wait()
-    fold_block(ring_ref.at[slot], out_ref, 0)
+    for q in range(FOLD_STEP):
+        fold_block(ring_ref.at[step % slots * FOLD_STEP + q], out_ref, q)
 
     @pl.when(step + slots < pl.num_programs(0))
     def _():
-        for copy in fetches(weights_hbm, ring_ref, sems, first + step + slots, slot, unique):
+        for copy in fetch(step + slots):
             copy.start()
 
 
 def fold_rest(weights, some, unique):
     first = folded_early(weights.shape[2])
-    slots = min(4, unique - first)
-    folded_shape, ring = fold_shapes(weights, unique, slots)
+    steps = (unique - first) // FOLD_STEP
+    slots = min(3, steps)
+    folded_shape, ring = fold_shapes(weights, unique, slots * FOLD_STEP)
     anywhere = pl.BlockSpec(memory_space=pl.ANY)
     return pl.pallas_call(
         functools.partial(fold_kernel, first=first, unique=unique, slots=slots),
-        grid=(unique - first,),
+        grid=(steps,),
         in_specs=[anywhere, anywhere],
-        out_specs=pl.BlockSpec((1,) + folded_shape.shape[1:], lambda s: (first + s, 0, 0, 0)),
+        out_specs=pl.BlockSpec((FOLD_STEP,) + folded_shape.shape[1:], lambda s: (first // FOLD_STEP + s, 0, 0, 0)),
         out_shape=folded_shape,
         scratch_shapes=ring,
         input_output_aliases={1: 0},
         compiler_params=params(LIMIT),
-        cost_estimate=pl.CostEstimate(flops=4 * 10**6, bytes_accessed=25 * MIB, transcendentals=0),
+        cost_estimate=pl.CostEstimate(flops=4 * 10**6, bytes_accessed=30 * MIB, transcendentals=0),
         name="fold_weights",
     )(*in_hbm(weights, some))
 

time: 94.2 us -> 93.7 us (level)
    pallas_call x1, Pallas kernels: 10.5 us -> 8.36 us  [forward_modes(): pl.pallas_call(functools.partial(forward_kernel, channels=channels, step_...]
    pallas_call x1, Pallas kernels: 9.77 us -> 11.4 us  [fold_rest(): pl.pallas_call(functools.partial(fold_kernel, first=first, unique=unique,...]
  transfers between devices with their start and end apart: 4 -> 4, of which waited for: 2 -> 1; matrix products, arithmetic and copies ran while one was open for 1% -> 1% of each run, Pallas kernels for 39% -> 41%
where the time goes in v12:
time: 93.7 us; the launch traced here: 93.1 us
  Pallas kernels  65.3 us (70%)
  starting transfers between devices  24.8 us (26%)
  local copies, waits for them, and re-layouts  1.39 us (1%)
    all_to_all x4, starting transfers between devices, swap(): lax.all_to_all(lines, 'space', split_axis=0, concat_axis=0, tiled=True)  24.8 us
    pallas_call x2, Pallas kernels, gradient(): pl.pallas_call(functools.partial(gradient_kernel, points=points, channels...  15.4 us
    pallas_call x1, Pallas kernels, fold_rest(): pl.pallas_call(functools.partial(fold_kernel, first=first, unique=unique,...  11.4 us
    pallas_call x1, Pallas kernels, pointwise(): pl.pallas_call(functools.partial(pointwise_kernel, channels=channels, blo...  8.67 us
    pallas_call x1, Pallas kernels, forward_modes(): pl.pallas_call(functools.partial(forward_kernel, channels=channels, step_...  8.36 us
    pallas_call x1, Pallas kernels, late_cells(): pl.pallas_call(functools.partial(late_cell_kernel, channels=channels, cou...  8.33 us
    pallas_call x1, Pallas kernels, early_cells(): pl.pallas_call(functools.partial(early_cell_kernel, channels=channels, co...  7.79 us
    pallas_call x1, Pallas kernels, mix(): pl.pallas_call(functools.partial(mix_kernel, points=points, channels=chan...  5.34 us
  transfers between devices with their start and end apart: 4, of which 1 were waited for; matrix products, arithmetic and copies ran while one was open for 1% of the time, Pallas kernels for 41%

profile of v12, /device:TPU:0, one launch (start us, length us, event | category | flops | bytes accessed | tf_op | source)
XLA Modules:
  0.0 93.1 jit_solution(13163453703012234049)
XLA Ops:
  0.6 8.4 %forward_yz.1 = (f32[512,128]{1,0:T(8,128)}, f32[16,32,32,128]{3,2,1,0:T(8,128)}) custom-call(bf16[1024,256]{1,0:T(8,128)(2,1)} %constant.19.clone.table_z, bf16[128,256]{1,0:T(8,128)(2,1)} %constant.20.clone.table_y, f32[32,128,256]{2,1,0:T(8,128)} %bitcast.19, f32[2,32,32,32,64]{4,3,2,1,0:T(8,128)} %bitcast.16), custom_call_target="tpu_custom_call" | custom-call | flops 2000000000 | bytes 23068672 | tf_op jit(solution)/shard_map/forward_yz/pallas_call | solution.py:227
  9.0 7.4 %all-to-all-start = ((f32[16,32,128]{2,1,0:T(8,128)}), f32[16,32,128]{2,1,0:T(8,128)S(1)}, u32[]{:S(2)}, u32[]{:S(2)}) async-start(f32[16,32,128]{2,1,0:T(8,128)} %bitcast.2), calls=%async_computation | async-start | bytes 524288 | tf_op jit(solution)/shard_map/all_to_all | solution.py:691
  16.4 0.0 copy-start
  16.4 0.0 copy-start.1
  16.4 11.4 %fold_weights.1.weights_ref = f32[16,32,32,128]{3,2,1,0:T(8,128)} custom-call(f32[2,32,32,32,64]{4,3,2,1,0:T(8,128)} %bitcast.17, f32[16,32,32,128]{3,2,1,0:T(8,128)} %get-tuple-element.19._), custom_call_target="tpu_custom_call", output_to_operand_aliasing={{}: (1, {})} | custom-call | flops 4000000 | bytes 31457280 | tf_op jit(solution)/shard_map/fold_weights/pallas_call | solution.py:281
  27.8 0.0 copy-start.2
  27.8 0.0 copy-start.3
  27.9 0.0 all-to-all-done.lines_ref
  27.9 0.0 copy-done
  27.9 0.0 copy-done.1
  27.9 5.3 %mix_modes.1 = (f32[16,32,128]{2,1,0:T(8,128)S(1)}, f32[16,32,128]{2,1,0:T(8,128)}) custom-call(f32[16,16]{1,0:T(8,128)S(1)} %copy-done.1, f32[16,16]{1,0:T(8,128)S(1)} %copy-done, f32[16,32,128]{2,1,0:T(8,128)S(1)} %all-to-all-done.lines_ref, f32[16,32,32,128]{3,2,1,0:T(8,128)} %fold_weights.1.weights_ref), custom_call_target="tpu_custom_call" | custom-call | flops 20000000 | bytes 9437184 | tf_op jit(solution)/shard_map/mix_modes/pallas_call | solution.py:366
  33.2 6.0 %all-to-all-start.1 = ((f32[16,32,128]{2,1,0:T(8,128)}), f32[16,32,128]{2,1,0:T(8,128)S(1)}, u32[]{:S(2)}, u32[]{:S(2)}) async-start(f32[16,32,128]{2,1,0:T(8,128)} %get-tuple-element.21), calls=%async_computation.1 | async-start | bytes 524288 | tf_op jit(solution)/shard_map/all_to_all | solution.py:691
  39.2 0.0 copy-done.2
  39.2 0.7 copy.20
  39.9 0.0 copy-done.3
  39.9 0.7 copy.21.bias_in_ref
  40.6 8.7 %pointwise.1.pre_ref = f32[32,128,256]{2,1,0:T(8,128)} custom-call(f32[256,32]{1,0:T(8,128)} %constant.18.clone.sum_ref, f32[32,32]{1,0:T(8,128)} %bitcast.22, f32[32,1]{1,0:T(8,128)} %copy.21.bias_in_ref, f32[32,128,256]{2,1,0:T(8,128)} %bitcast.20), custom_call_target="tpu_custom_call" | custom-call | flops 4000000000 | bytes 25165824 | tf_op jit(solution)/shard_map/pointwise/pallas_call | solution.py:428
  49.3 0.0 all-to-all-done.1
  49.3 7.8 %early_cells.1 = (bf16[32,128,256]{2,1,0:T(8,128)(2,1)}, f32[24,128,256]{2,1,0:T(8,128)}, f32[384,128]{1,0:T(8,128)}) custom-call(bf16[128,192]{1,0:T(8,128)(2,1)} %constant.21.clone.inv_y, bf16[256,256]{1,0:T(8,128)(2,1)} %constant.22.clone.inv_z0, bf16[256,256]{1,0:T(8,128)(2,1)} %constant.23.clone.inv_z1, bf16[1024,256]{1,0:T(8,128)(2,1)} %constant.19.clone.table_z, ...), custom_call_target="tpu_custom_call" | custom-call | flops 3000000000 | bytes 7340032 | tf_op jit(solution)/shard_map/early_cells/pallas_call | solution.py:544
  57.1 6.0 %all-to-all-start.3 = ((f32[16,24,128]{2,1,0:T(8,128)}), f32[16,24,128]{2,1,0:T(8,128)S(1)}, u32[]{:S(2)}, u32[]{:S(2)}) async-start(f32[16,24,128]{2,1,0:T(8,128)} %bitcast.10), calls=%async_computation.3 | async-start | bytes 393216 | tf_op jit(solution)/shard_map/all_to_all | solution.py:691
  63.1 8.3 %late_cells.1 = (bf16[32,128,256]{2,1,0:T(8,128)(2,1)}, f32[384,128]{1,0:T(8,128)}) custom-call(bf16[128,192]{1,0:T(8,128)(2,1)} %constant.21.clone.inv_y, bf16[256,256]{1,0:T(8,128)(2,1)} %constant.22.clone.inv_z0, bf16[256,256]{1,0:T(8,128)(2,1)} %constant.23.clone.inv_z1, ...), custom_call_target="tpu_custom_call", output_to_operand_aliasing={{0}: (12, {})} | custom-call | flops 6000000000 | bytes 11534336 | tf_op jit(solution)/shard_map/late_cells/pallas_call | solution.py:570
  71.4 0.7 all-to-all-done.3.lines_ref
  72.1 5.4 %all-to-all-start.2 = ((f32[16,24,128]{2,1,0:T(8,128)}), f32[16,24,128]{2,1,0:T(8,128)S(1)}, u32[]{:S(2)}, u32[]{:S(2)}) async-start(f32[16,24,128]{2,1,0:T(8,128)} %bitcast.9), calls=%async_computation.2 | async-start | bytes 393216 | tf_op jit(solution)/shard_map/all_to_all | solution.py:691
  77.5 9.8 %weight_gradient.2.refs_0_ = f32[2,32,32,32,64]{4,3,2,1,0:T(8,128)} custom-call(f32[16,16]{1,0:T(8,128)S(1)} %copy-done.1, f32[16,16]{1,0:T(8,128)S(1)} %copy-done, f32[16,32,128]{2,1,0:T(8,128)S(1)} %get-tuple-element.27.spec_ref, f32[16,24,128]{2,1,0:T(8,128)S(1)} %all-to-all-done.3.lines_ref), custom_call_target="tpu_custom_call" | custom-call | flops 5000000 | bytes 33554432 | tf_op jit(solution)/shard_map/weight_gradient/pallas_call | solution.py:668
  87.3 0.0 all-to-all-done.2.lines_ref
  87.3 5.6 %weight_gradient.3 = (f32[2,32,32,32,64]{4,3,2,1,0:T(8,128)}, f32[32,32]{1,0:T(8,128)}, f32[1,32]{1,0:T(1,128)}) custom-call(f32[16,16]{1,0:T(8,128)S(1)} %copy-done.1, f32[16,16]{1,0:T(8,128)S(1)} %copy-done, f32[16,32,128]{2,1,0:T(8,128)S(1)} %get-tuple-element.27.spec_ref, ...), custom_call_target="tpu_custom_call", output_to_operand_aliasing={{0}: (4, {})} | custom-call | flops 5000000 | bytes 33554432 | tf_op jit(solution)/shard_map/weight_gradient/pallas_call | solution.py:668
Async XLA Ops:
  9.0 18.9 %all-to-all-start = ((f32[16,32,128]{2,1,0:T(8,128)}), f32[16,32,128]{2,1,0:T(8,128)S(1)}, u32[]{:S(2)}, u32[]{:S(2)}) async-start(f32[16,32,128]{2,1,0:T(8,128)} %bitcast.2), calls=%async_computation | async-start | bytes 524288 | tf_op jit(solution)/shard_map/all_to_all | solution.py:691
  16.4 11.5 %copy-start = (f32[16,16]{1,0:T(8,128)S(1)}, f32[16,16]{1,0:T(8,128)}, u32[]{:S(2)}) copy-start(f32[16,16]{1,0:T(8,128)} %constant.17.clone.sin_ref) | copy-start | bytes 3076
  16.4 11.5 %copy-start.1 = (f32[16,16]{1,0:T(8,128)S(1)}, f32[16,16]{1,0:T(8,128)}, u32[]{:S(2)}) copy-start(f32[16,16]{1,0:T(8,128)} %constant.16.clone.cos_ref) | copy-start | bytes 3076
  27.8 11.4 %copy-start.2 = (f32[32,32]{1,0:T(8,128)S(1)}, f32[32,32]{1,0:T(8,128)}, u32[]{:S(2)}) copy-start(f32[32,32]{1,0:T(8,128)} %param.16) | copy-start | bytes 12292
  27.8 12.1 %copy-start.3 = (f32[32]{0:T(128)S(1)}, f32[32]{0:T(128)}, u32[]{:S(2)}) copy-start(f32[32]{0:T(128)} %param.17) | copy-start | bytes 388
  33.2 16.1 %all-to-all-start.1 = ((f32[16,32,128]{2,1,0:T(8,128)}), f32[16,32,128]{2,1,0:T(8,128)S(1)}, u32[]{:S(2)}, u32[]{:S(2)}) async-start(f32[16,32,128]{2,1,0:T(8,128)} %get-tuple-element.21), calls=%async_computation.1 | async-start | bytes 524288 | tf_op jit(solution)/shard_map/all_to_all | solution.py:691
  57.1 15.0 %all-to-all-start.3 = ((f32[16,24,128]{2,1,0:T(8,128)}), f32[16,24,128]{2,1,0:T(8,128)S(1)}, u32[]{:S(2)}, u32[]{:S(2)}) async-start(f32[16,24,128]{2,1,0:T(8,128)} %bitcast.10), calls=%async_computation.3 | async-start | bytes 393216 | tf_op jit(solution)/shard_map/all_to_all | solution.py:691
  72.1 15.2 %all-to-all-start.2 = ((f32[16,24,128]{2,1,0:T(8,128)}), f32[16,24,128]{2,1,0:T(8,128)S(1)}, u32[]{:S(2)}, u32[]{:S(2)}) async-start(f32[16,24,128]{2,1,0:T(8,128)} %bitcast.9), calls=%async_computation.2 | async-start | bytes 393216 | tf_op jit(solution)/shard_map/all_to_all | solution.py:691

commit v13 on v12

--- a/solution.py
+++ b/solution.py
@@ -316,42 +316,55 @@
 
 
 def mix_kernel(
-    cos_ref, sin_ref, lines_ref, weights_ref, spec_ref, out_ref, sums_ref, total_ref, real_ref, imag_ref,
-    *, points, channels, per_step, norm,
+    cos_ref, sin_ref, lines_ref, weights_hbm, spec_ref, out_ref,
+    sums_ref, total_ref, real_ref, imag_ref, weights_ref, sems, *, points, channels, per_step, norm,
 ):
-    step = pl.program_id(0)
     half = points // 2
-
-    @pl.when(step == 0)
-    def _():
-        halve_lines(lines_ref, sums_ref, points, channels)
-        total_ref[...] = jnp.zeros_like(total_ref)
-
+    steps = points // per_step
+
+    def fetch(step):
+        count = channels // 2
+        return [
+            pltpu.make_async_copy(
+                weights_hbm.at[pl.ds(step * per_step, per_step), pl.ds(h * count, count)],
+                weights_ref.at[step % 2, :, pl.ds(h * count, count)],
+                sems.at[step % 2, h],
+            )
+            for h in range(2)
+        ]
+
+    for copy in fetch(0):
+        copy.start()
+    halve_lines(lines_ref, sums_ref, points, channels)
+    total_ref[...] = jnp.zeros_like(total_ref)
     low = lane_index((channels, LANES)) < LANES // 2
-    for q in range(per_step):
-        at = step * per_step + q
-        parity = q % 2
-        spec = norm * spectrum_row(cos_ref, sin_ref, sums_ref, at, parity, half)
-        spec_ref[q] = spec
-        real_ref[q], imag_ref[q] = doubled(spec)
-        by_real = jnp.zeros((channels, LANES), F32)
-        by_imag = jnp.zeros((channels, LANES), F32)
-        for i in range(channels):
-            weight = weights_ref[q, i]
-            by_real += real_ref[q, pl.ds(i, 1), :] * weight
-            by_imag += imag_ref[q, pl.ds(i, 1), :] * weight
-        other = roll(by_imag, 64)
-        mixed = by_real + jnp.where(low, -other, other)
-        other = roll(mixed, 64)
-        turned = jnp.where(low, -other, other)
-        for x in range(half):
-            total_ref[parity, x] += cos_ref[at, x] * mixed + sin_ref[at, x] * turned
-
-    @pl.when(step == pl.num_programs(0) - 1)
-    def _():
-        for x in range(half):
-            out_ref[x] = total_ref[0, x] + total_ref[1, x]
-            out_ref[x + half] = total_ref[0, x] - total_ref[1, x]
+    for step in range(steps):
+        for copy in fetch(step):
+            copy.wait()
+        if step + 1 < steps:
+            for copy in fetch(step + 1):
+                copy.start()
+        for q in range(per_step):
+            at = step * per_step + q
+            parity = q % 2
+            spec = norm * spectrum_row(cos_ref, sin_ref, sums_ref, at, parity, half)
+            spec_ref[at] = spec
+            real_ref[q], imag_ref[q] = doubled(spec)
+            by_real = jnp.zeros((channels, LANES), F32)
+            by_imag = jnp.zeros((channels, LANES), F32)
+            for i in range(channels):
+                weight = weights_ref[step % 2, q, i]
+                by_real += real_ref[q, pl.ds(i, 1), :] * weight
+                by_imag += imag_ref[q, pl.ds(i, 1), :] * weight
+            other = roll(by_imag, 64)
+            mixed = by_real + jnp.where(low, -other, other)
+            other = roll(mixed, 64)
+            turned = jnp.where(low, -other, other)
+            for x in range(half):
+                total_ref[parity, x] += cos_ref[at, x] * mixed + sin_ref[at, x] * turned
+    for x in range(half):
+        out_ref[x] = total_ref[0, x] + total_ref[1, x]
+        out_ref[x + half] = total_ref[0, x] - total_ref[1, x]
 
 
 def smem():
@@ -361,19 +374,19 @@
 def mix(cos_x, sin_x, lines, weights, norm):
     points, channels, _ = lines.shape
     unique = weights.shape[0]
-    per_step = min(unique, 8)
+    per_step = 4
     shape = (points, channels, LANES)
     return pl.pallas_call(
         functools.partial(mix_kernel, points=points, channels=channels, per_step=per_step, norm=norm),
-        grid=(unique // per_step,),
+        grid=(1,),
         in_specs=[
             smem(),
             smem(),
             full(shape),
-            pl.BlockSpec((per_step,) + weights.shape[1:], lambda s: (s, 0, 0, 0)),
+            pl.BlockSpec(memory_space=pl.ANY),
         ],
         out_specs=[
-            pl.BlockSpec((per_step, channels, LANES), lambda s: (s, 0, 0)),
+            full((unique, channels, LANES)),
             full(shape),
         ],
         out_shape=[
@@ -385,6 +398,8 @@
             pltpu.VMEM((2, points // 2, channels, LANES), F32),
             pltpu.VMEM((per_step, channels, LANES), F32),
             pltpu.VMEM((per_step, channels, LANES), F32),
+            pltpu.VMEM((2, per_step) + weights.shape[1:], F32),
+            pltpu.SemaphoreType.DMA((2, 2)),
         ],
         compiler_params=params(LIMIT),
         cost_estimate=pl.CostEstimate(flops=2 * 10**7, bytes_accessed=9 * MIB, transcendentals=0),
@@ -661,7 +676,7 @@
     copies = kept_x // unique
     first = early_count(channels) if before else 0
     outputs = channels - first if before else early_count(channels)
-    slots = 8
+    slots = unique
     anywhere = pl.BlockSpec(memory_space=pl.ANY)
     shape = jax.ShapeDtypeStruct((2, kept_x, channels, channels, half), F32)
     sums = [(channels, channels), (1, channels)] if before else []

time: 93.7 us -> 97.3 us (1.038)
  Pallas kernels: 65.3 us -> 68.7 us
    pallas_call x1, Pallas kernels: 5.34 us -> 8.39 us  [mix(): pl.pallas_call(functools.partial(mix_kernel, points=points, channels=chan...]
  transfers between devices with their start and end apart: 4 -> 4, of which waited for: 1 -> 1; matrix products, arithmetic and copies ran while one was open for 1% -> 1% of each run, Pallas kernels for 41% -> 40%
where the time goes in v13:
time: 97.3 us; the launch traced here: 96.5 us
  Pallas kernels  68.7 us (71%)
  starting transfers between devices  24.8 us (25%)
  local copies, waits for them, and re-layouts  1.39 us (1%)
    all_to_all x4, starting transfers between devices, swap(): lax.all_to_all(lines, 'space', split_axis=0, concat_axis=0, tiled=True)  24.8 us
    pallas_call x2, Pallas kernels, gradient(): pl.pallas_call(functools.partial(gradient_kernel, points=points, channels...  15.8 us
    pallas_call x1, Pallas kernels, fold_rest(): pl.pallas_call(functools.partial(fold_kernel, first=first, unique=unique,...  11.4 us
    pallas_call x1, Pallas kernels, pointwise(): pl.pallas_call(functools.partial(pointwise_kernel, channels=channels, blo...  8.68 us
    pallas_call x1, Pallas kernels, mix(): pl.pallas_call(functools.partial(mix_kernel, points=points, channels=chan...  8.39 us
    pallas_call x1, Pallas kernels, forward_modes(): pl.pallas_call(functools.partial(forward_kernel, channels=channels, step_...  8.36 us
    pallas_call x1, Pallas kernels, late_cells(): pl.pallas_call(functools.partial(late_cell_kernel, channels=channels, cou...  8.33 us
    pallas_call x1, Pallas kernels, early_cells(): pl.pallas_call(functools.partial(early_cell_kernel, channels=channels, co...  7.79 us
  transfers between devices with their start and end apart: 4, of which 1 were waited for; matrix products, arithmetic and copies ran while one was open for 1% of the time, Pallas kernels for 40%

profile of v13, /device:TPU:0, one launch (start us, length us, event | category | flops | bytes accessed | tf_op | source)
XLA Modules:
  0.0 96.5 jit_solution(2203103477224093789)
XLA Ops:
  0.6 8.4 %forward_yz.1 = (f32[512,128]{1,0:T(8,128)}, f32[16,32,32,128]{3,2,1,0:T(8,128)}) custom-call(bf16[1024,256]{1,0:T(8,128)(2,1)} %constant.19.clone.table_z, bf16[128,256]{1,0:T(8,128)(2,1)} %constant.20.clone.table_y, f32[32,128,256]{2,1,0:T(8,128)} %bitcast.19, f32[2,32,32,32,64]{4,3,2,1,0:T(8,128)} %bitcast.16), custom_call_target="tpu_custom_call" | custom-call | flops 2000000000 | bytes 23068672 | tf_op jit(solution)/shard_map/forward_yz/pallas_call | solution.py:227
  9.0 7.4 %all-to-all-start = ((f32[16,32,128]{2,1,0:T(8,128)}), f32[16,32,128]{2,1,0:T(8,128)S(1)}, u32[]{:S(2)}, u32[]{:S(2)}) async-start(f32[16,32,128]{2,1,0:T(8,128)} %bitcast.2), calls=%async_computation | async-start | bytes 524288 | tf_op jit(solution)/shard_map/all_to_all | solution.py:706
  16.4 0.0 copy-start
  16.4 0.0 copy-start.1
  16.4 11.4 %fold_weights.1.weights_hbm = f32[16,32,32,128]{3,2,1,0:T(8,128)} custom-call(f32[2,32,32,32,64]{4,3,2,1,0:T(8,128)} %bitcast.17, f32[16,32,32,128]{3,2,1,0:T(8,128)} %get-tuple-element.19._), custom_call_target="tpu_custom_call", output_to_operand_aliasing={{}: (1, {})} | custom-call | flops 4000000 | bytes 31457280 | tf_op jit(solution)/shard_map/fold_weights/pallas_call | solution.py:281
  27.8 0.0 copy-start.2
  27.8 0.0 copy-start.3
  27.9 0.0 all-to-all-done.lines_ref
  27.9 0.0 copy-done
  27.9 0.0 copy-done.1
  27.9 8.4 %mix_modes.1 = (f32[16,32,128]{2,1,0:T(8,128)S(1)}, f32[16,32,128]{2,1,0:T(8,128)}) custom-call(f32[16,16]{1,0:T(8,128)S(1)} %copy-done.1, f32[16,16]{1,0:T(8,128)S(1)} %copy-done, f32[16,32,128]{2,1,0:T(8,128)S(1)} %all-to-all-done.lines_ref, f32[16,32,32,128]{3,2,1,0:T(8,128)} %fold_weights.1.weights_hbm), custom_call_target="tpu_custom_call" | custom-call | flops 20000000 | bytes 9437184 | tf_op jit(solution)/shard_map/mix_modes/pallas_call | solution.py:379
  36.3 6.0 %all-to-all-start.1 = ((f32[16,32,128]{2,1,0:T(8,128)}), f32[16,32,128]{2,1,0:T(8,128)S(1)}, u32[]{:S(2)}, u32[]{:S(2)}) async-start(f32[16,32,128]{2,1,0:T(8,128)} %get-tuple-element.21), calls=%async_computation.1 | async-start | bytes 524288 | tf_op jit(solution)/shard_map/all_to_all | solution.py:706
  42.3 0.0 copy-done.2
  42.3 0.7 copy.20
  43.0 0.0 copy-done.3
  43.0 0.7 copy.21.bias_in_ref
  43.7 8.7 %pointwise.1.pre_ref = f32[32,128,256]{2,1,0:T(8,128)} custom-call(f32[256,32]{1,0:T(8,128)} %constant.18.clone.sum_ref, f32[32,32]{1,0:T(8,128)} %bitcast.22, f32[32,1]{1,0:T(8,128)} %copy.21.bias_in_ref, f32[32,128,256]{2,1,0:T(8,128)} %bitcast.20), custom_call_target="tpu_custom_call" | custom-call | flops 4000000000 | bytes 25165824 | tf_op jit(solution)/shard_map/pointwise/pallas_call | solution.py:443
  52.4 0.0 all-to-all-done.1
  52.4 7.8 %early_cells.1 = (bf16[32,128,256]{2,1,0:T(8,128)(2,1)}, f32[24,128,256]{2,1,0:T(8,128)}, f32[384,128]{1,0:T(8,128)}) custom-call(bf16[128,192]{1,0:T(8,128)(2,1)} %constant.21.clone.inv_y, bf16[256,256]{1,0:T(8,128)(2,1)} %constant.22.clone.inv_z0, bf16[256,256]{1,0:T(8,128)(2,1)} %constant.23.clone.inv_z1, bf16[1024,256]{1,0:T(8,128)(2,1)} %constant.19.clone.table_z, ...), custom_call_target="tpu_custom_call" | custom-call | flops 3000000000 | bytes 7340032 | tf_op jit(solution)/shard_map/early_cells/pallas_call | solution.py:559
  60.2 6.0 %all-to-all-start.3 = ((f32[16,24,128]{2,1,0:T(8,128)}), f32[16,24,128]{2,1,0:T(8,128)S(1)}, u32[]{:S(2)}, u32[]{:S(2)}) async-start(f32[16,24,128]{2,1,0:T(8,128)} %bitcast.10), calls=%async_computation.3 | async-start | bytes 393216 | tf_op jit(solution)/shard_map/all_to_all | solution.py:706
  66.2 8.3 %late_cells.1 = (bf16[32,128,256]{2,1,0:T(8,128)(2,1)}, f32[384,128]{1,0:T(8,128)}) custom-call(bf16[128,192]{1,0:T(8,128)(2,1)} %constant.21.clone.inv_y, bf16[256,256]{1,0:T(8,128)(2,1)} %constant.22.clone.inv_z0, bf16[256,256]{1,0:T(8,128)(2,1)} %constant.23.clone.inv_z1, ...), custom_call_target="tpu_custom_call", output_to_operand_aliasing={{0}: (12, {})} | custom-call | flops 6000000000 | bytes 11534336 | tf_op jit(solution)/shard_map/late_cells/pallas_call | solution.py:585
  74.5 0.7 all-to-all-done.3.lines_ref
  75.2 5.4 %all-to-all-start.2 = ((f32[16,24,128]{2,1,0:T(8,128)}), f32[16,24,128]{2,1,0:T(8,128)S(1)}, u32[]{:S(2)}, u32[]{:S(2)}) async-start(f32[16,24,128]{2,1,0:T(8,128)} %bitcast.9), calls=%async_computation.2 | async-start | bytes 393216 | tf_op jit(solution)/shard_map/all_to_all | solution.py:706
  80.6 10.2 %weight_gradient.2.refs_0_ = f32[2,32,32,32,64]{4,3,2,1,0:T(8,128)} custom-call(f32[16,16]{1,0:T(8,128)S(1)} %copy-done.1, f32[16,16]{1,0:T(8,128)S(1)} %copy-done, f32[16,32,128]{2,1,0:T(8,128)S(1)} %get-tuple-element.27.spec_ref, f32[16,24,128]{2,1,0:T(8,128)S(1)} %all-to-all-done.3.lines_ref), custom_call_target="tpu_custom_call" | custom-call | flops 5000000 | bytes 33554432 | tf_op jit(solution)/shard_map/weight_gradient/pallas_call | solution.py:683
  90.8 0.0 all-to-all-done.2.lines_ref
  90.8 5.6 %weight_gradient.3 = (f32[2,32,32,32,64]{4,3,2,1,0:T(8,128)}, f32[32,32]{1,0:T(8,128)}, f32[1,32]{1,0:T(1,128)}) custom-call(f32[16,16]{1,0:T(8,128)S(1)} %copy-done.1, f32[16,16]{1,0:T(8,128)S(1)} %copy-done, f32[16,32,128]{2,1,0:T(8,128)S(1)} %get-tuple-element.27.spec_ref, ...), custom_call_target="tpu_custom_call", output_to_operand_aliasing={{0}: (4, {})} | custom-call | flops 5000000 | bytes 33554432 | tf_op jit(solution)/shard_map/weight_gradient/pallas_call | solution.py:683
Async XLA Ops:
  9.0 18.9 %all-to-all-start = ((f32[16,32,128]{2,1,0:T(8,128)}), f32[16,32,128]{2,1,0:T(8,128)S(1)}, u32[]{:S(2)}, u32[]{:S(2)}) async-start(f32[16,32,128]{2,1,0:T(8,128)} %bitcast.2), calls=%async_computation | async-start | bytes 524288 | tf_op jit(solution)/shard_map/all_to_all | solution.py:706
  16.4 11.5 %copy-start = (f32[16,16]{1,0:T(8,128)S(1)}, f32[16,16]{1,0:T(8,128)}, u32[]{:S(2)}) copy-start(f32[16,16]{1,0:T(8,128)} %constant.17.clone.sin_ref) | copy-start | bytes 3076
  16.4 11.5 %copy-start.1 = (f32[16,16]{1,0:T(8,128)S(1)}, f32[16,16]{1,0:T(8,128)}, u32[]{:S(2)}) copy-start(f32[16,16]{1,0:T(8,128)} %constant.16.clone.cos_ref) | copy-start | bytes 3076
  27.8 14.5 %copy-start.2 = (f32[32,32]{1,0:T(8,128)S(1)}, f32[32,32]{1,0:T(8,128)}, u32[]{:S(2)}) copy-start(f32[32,32]{1,0:T(8,128)} %param.16) | copy-start | bytes 12292
  27.8 15.2 %copy-start.3 = (f32[32]{0:T(128)S(1)}, f32[32]{0:T(128)}, u32[]{:S(2)}) copy-start(f32[32]{0:T(128)} %param.17) | copy-start | bytes 388
  36.3 16.1 %all-to-all-start.1 = ((f32[16,32,128]{2,1,0:T(8,128)}), f32[16,32,128]{2,1,0:T(8,128)S(1)}, u32[]{:S(2)}, u32[]{:S(2)}) async-start(f32[16,32,128]{2,1,0:T(8,128)} %get-tuple-element.21), calls=%async_computation.1 | async-start | bytes 524288 | tf_op jit(solution)/shard_map/all_to_all | solution.py:706
  60.2 15.0 %all-to-all-start.3 = ((f32[16,24,128]{2,1,0:T(8,128)}), f32[16,24,128]{2,1,0:T(8,128)S(1)}, u32[]{:S(2)}, u32[]{:S(2)}) async-start(f32[16,24,128]{2,1,0:T(8,128)} %bitcast.10), calls=%async_computation.3 | async-start | bytes 393216 | tf_op jit(solution)/shard_map/all_to_all | solution.py:706
  75.2 15.6 %all-to-all-start.2 = ((f32[16,24,128]{2,1,0:T(8,128)}), f32[16,24,128]{2,1,0:T(8,128)S(1)}, u32[]{:S(2)}, u32[]{:S(2)}) async-start(f32[16,24,128]{2,1,0:T(8,128)} %bitcast.9), calls=%async_computation.2 | async-start | bytes 393216 | tf_op jit(solution)/shard_map/all_to_all | solution.py:706
